TPU v7x, 32 devices: a whole 2x2x4 slice. The times are simulated.
32 devices in a mesh: section: 2 (over x), dp: 16 (over z, y, core).
Axes of the slice: x: 2, y: 2, z: 4, core: 2. Of those that a mesh axis runs over, the one named last changes fastest.
Arguments:
- block_input: bfloat16 [2, 16, 96, 768], P(None, 'dp'), may hold values from -6 to 6
- cotangent: bfloat16 [2, 16, 96, 768], P(None, 'dp'), may hold values from -8 to 8
- lengths: int32 [2, 16], P(None, 'dp'), may hold values from 1 to 96, 1152 in all within a row
- leads: int32 [2, 16], P(None, 'dp'), may hold values from 0 to 23
- norm_gain1: float32 [2, 768], P('section', 'dp'), may hold values from 0.25 to 1.75
- norm_bias1: float32 [2, 768], P('section', 'dp'), may hold values from -1.75 to 1.75
- lead_table: float32 [2, 768, 24], P('section', 'dp'), may hold values from -3 to 3
- qkv_weight: float32 [2, 768, 2304], P('section', 'dp'), may hold values from -0.21875 to 0.21875
- query_bias: float32 [2, 768], P('section', 'dp'), may hold values from -1.75 to 1.75
- value_bias: float32 [2, 768], P('section', 'dp'), may hold values from -1.75 to 1.75
- out_weight: float32 [2, 768, 768], P('section', 'dp'), may hold values from -0.875 to 0.875
- out_bias: float32 [2, 768], P('section', 'dp'), may hold values from -1.75 to 1.75
- norm_gain2: float32 [2, 768], P('section', 'dp'), may hold values from 0.25 to 1.75
- norm_bias2: float32 [2, 768], P('section', 'dp'), may hold values from -1.75 to 1.75
- up_weight: float32 [2, 768, 3072], P('section', 'dp'), may hold values from -0.21875 to 0.21875
- up_bias: float32 [2, 3072], P('section', 'dp'), may hold values from -1.75 to 1.75
- down_weight: float32 [2, 3072, 768], P('section', 'dp'), may hold values from -0.109375 to 0.109375
- down_bias: float32 [2, 768], P('section', 'dp'), may hold values from -1.75 to 1.75
Outputs:
- activations: bfloat16 [2, 2, 16, 96, 768], P('section', None, 'dp')
- input_grads: float32 [2, 2, 16, 96, 768], P('section', None, 'dp')
- grad_norm_gain1: float32 [2, 768], P('section', 'dp')
- grad_norm_bias1: float32 [2, 768], P('section', 'dp')
- grad_lead_table: float32 [2, 768, 24], P('section', 'dp')
- grad_qkv_weight: float32 [2, 768, 2304], P('section', 'dp')
- grad_query_bias: float32 [2, 768], P('section', 'dp')
- grad_value_bias: float32 [2, 768], P('section', 'dp')
- grad_out_weight: float32 [2, 768, 768], P('section', 'dp')
- grad_out_bias: float32 [2, 768], P('section', 'dp')
- grad_norm_gain2: float32 [2, 768], P('section', 'dp')
- grad_norm_bias2: float32 [2, 768], P('section', 'dp')
- grad_up_weight: float32 [2, 768, 3072], P('section', 'dp')
- grad_up_bias: float32 [2, 3072], P('section', 'dp')
- grad_down_weight: float32 [2, 3072, 768], P('section', 'dp')
- grad_down_bias: float32 [2, 768], P('section', 'dp')
Inputs may be any that keep to these rules, and one draw needn't show every extreme that they name: In each micro-batch the lengths of the 16 items sum to 1152 and the longest is 96.
All inputs are finite; a program needn't handle non-finite values. No bound on the sum of `lengths` on one device may be relied on, other than what follows from the above.
Results may differ from a plain program's by a relative error of at most 0.013.
The roundings to bfloat16 on the way count: a program that leaves them out, or rounds other values in their place, can miss the bound.
Values may be sent and summed in bfloat16 or wider, within the bound.
No kernel may reach another device: no remote copies, remote signals or barrier semaphores. Data moves between devices by JAX's collectives and lax.ppermute only.
A program may use at most 128 MiB of HBM per device.

v0:
```python
import jax
import jax.numpy as jnp
from jax import lax
from jax.sharding import PartitionSpec as P

HEAD = 64


EPS = 1e-06
SCALE_FACTOR = 0.125


def shifted(value, axis, steps):
    count = lax.axis_size(axis)
    first, last = (max(0, -steps), min(count, count - steps))
    return lax.ppermute(value, axis, [(source, source + steps) for source in range(first, last)])


def layer_norm(values, gain, shift):
    mean = jnp.mean(values, -1, keepdims=True)
    centred = values - mean
    variance = jnp.mean(centred * centred, -1, keepdims=True)
    return centred * lax.rsqrt(variance + EPS) * gain + shift


def gelu_tanh(values):
    return (
        0.5
        * values
        * (1.0 + jnp.tanh(0.7978845608028654 * (values + 0.044715 * values * values * values)))
    )


def split_heads(values):
    return values.reshape(values.shape[0], -1, HEAD)


def masked_scores(query, key_rows, valid_keys):
    product = (
        jnp.einsum(
            "qhd,khd->hqk",
            split_heads(query),
            split_heads(key_rows),
            preferred_element_type=jnp.float32,
        )
        * SCALE_FACTOR
    )
    return jnp.where(valid_keys[None, None, :], product, -1000000000.0)


def forward_layer(weights, inputs, length, lead):
    (
        gain_one,
        shift_one,
        lead_table,
        qkv_weight,
        query_bias,
        value_bias,
        out_weight,
        out_bias,
        gain_two,
        shift_two,
        up_weight,
        up_bias,
        down_weight,
        down_bias,
    ) = weights
    rows = inputs.shape[0]
    width = inputs.shape[1]
    onehot = (jnp.arange(lead_table.shape[1]) == lead).astype(jnp.float32)
    embedded = jnp.dot(lead_table, onehot.astype(jnp.bfloat16), preferred_element_type=jnp.float32)
    normed = (
        layer_norm(inputs, gain_one.astype(jnp.float32), shift_one.astype(jnp.float32))
        + embedded[None, :]
    ).astype(jnp.bfloat16)
    joined = jnp.dot(normed, qkv_weight, preferred_element_type=jnp.float32)
    query = (joined[:, :width] + query_bias.astype(jnp.float32)).astype(jnp.bfloat16)
    key_rows = joined[:, width : 2 * width].astype(jnp.bfloat16)
    value = (joined[:, 2 * width :] + value_bias.astype(jnp.float32)).astype(jnp.bfloat16)
    valid_keys = jnp.arange(rows) < length
    logits = masked_scores(query, key_rows, valid_keys)
    top = jnp.max(logits, -1, keepdims=True)
    expo = jnp.exp(logits - top)
    total = jnp.sum(expo, -1, keepdims=True)
    probs = expo / total
    log_total = top[:, :, 0] + jnp.log(total[:, :, 0])
    mixed = jnp.einsum(
        "hqk,khd->qhd",
        probs.astype(jnp.bfloat16),
        split_heads(value),
        preferred_element_type=jnp.float32,
    )
    attended = mixed.reshape(rows, width).astype(jnp.bfloat16)
    middle = inputs + (
        jnp.dot(attended, out_weight, preferred_element_type=jnp.float32)
        + out_bias.astype(jnp.float32)
    )
    hidden = layer_norm(middle, gain_two.astype(jnp.float32), shift_two.astype(jnp.float32)).astype(
        jnp.bfloat16
    )
    pre_act = jnp.dot(hidden, up_weight, preferred_element_type=jnp.float32) + up_bias.astype(
        jnp.float32
    )
    activated = gelu_tanh(pre_act).astype(jnp.bfloat16)
    output = middle + (
        jnp.dot(activated, down_weight, preferred_element_type=jnp.float32)
        + down_bias.astype(jnp.float32)
    )
    kept = (
        inputs,
        normed,
        query,
        key_rows,
        value,
        attended,
        middle,
        hidden,
        pre_act,
        log_total,
        valid_keys,
        onehot,
    )
    return (output, kept)


def backward_layer(weights, kept, upstream):
    (
        gain_one,
        shift_one,
        lead_table,
        qkv_weight,
        query_bias,
        value_bias,
        out_weight,
        out_bias,
        gain_two,
        shift_two,
        up_weight,
        up_bias,
        down_weight,
        down_bias,
    ) = weights
    (
        inputs,
        normed,
        query,
        key_rows,
        value,
        attended,
        middle,
        hidden,
        pre_act,
        log_total,
        valid_keys,
        onehot,
    ) = kept
    rows = inputs.shape[0]
    width = inputs.shape[1]
    branch_grad = upstream.astype(jnp.bfloat16)
    activated = gelu_tanh(pre_act).astype(jnp.bfloat16)
    grad_down = jnp.einsum("tf,td->fd", activated, branch_grad, preferred_element_type=jnp.float32)
    grad_down_bias = jnp.sum(branch_grad.astype(jnp.float32), 0)
    grad_act = jnp.einsum("td,fd->tf", branch_grad, down_weight, preferred_element_type=jnp.float32)
    grad_pre = jax.vjp(gelu_tanh, pre_act)[1](grad_act)[0].astype(jnp.bfloat16)
    grad_up = jnp.einsum("td,tf->df", hidden, grad_pre, preferred_element_type=jnp.float32)
    grad_up_bias = jnp.sum(grad_pre.astype(jnp.float32), 0)
    grad_hidden = jnp.einsum("tf,df->td", grad_pre, up_weight, preferred_element_type=jnp.float32)
    norm_back_two = jax.vjp(
        layer_norm, middle, gain_two.astype(jnp.float32), shift_two.astype(jnp.float32)
    )[1]
    through_two, grad_gain_two, grad_shift_two = norm_back_two(grad_hidden)
    grad_middle = upstream + through_two
    attn_grad = grad_middle.astype(jnp.bfloat16)
    grad_out = jnp.einsum("td,te->de", attended, attn_grad, preferred_element_type=jnp.float32)
    grad_out_bias = jnp.sum(attn_grad.astype(jnp.float32), 0)
    grad_attended = jnp.einsum(
        "te,de->td", attn_grad, out_weight, preferred_element_type=jnp.float32
    ).astype(jnp.bfloat16)
    logits = masked_scores(query, key_rows, valid_keys)
    probs = jnp.exp(logits - log_total[:, :, None])
    grad_heads = split_heads(grad_attended)
    grad_value = jnp.einsum(
        "hqk,qhd->khd", probs.astype(jnp.bfloat16), grad_heads, preferred_element_type=jnp.float32
    )
    grad_probs = jnp.einsum(
        "qhd,khd->hqk", grad_heads, split_heads(value), preferred_element_type=jnp.float32
    )
    centre = jnp.sum(grad_probs * probs, -1, keepdims=True)
    grad_logits = (probs * (grad_probs - centre)).astype(jnp.bfloat16)
    grad_query = (
        jnp.einsum(
            "hqk,khd->qhd", grad_logits, split_heads(key_rows), preferred_element_type=jnp.float32
        )
        * SCALE_FACTOR
    )
    grad_key = (
        jnp.einsum(
            "hqk,qhd->khd", grad_logits, split_heads(query), preferred_element_type=jnp.float32
        )
        * SCALE_FACTOR
    )
    query_part = grad_query.reshape(rows, width).astype(jnp.bfloat16)
    key_part = grad_key.reshape(rows, width).astype(jnp.bfloat16)
    value_part = grad_value.reshape(rows, width).astype(jnp.bfloat16)
    grad_rows = jnp.concatenate([query_part, key_part, value_part], 1)
    grad_query_bias = jnp.sum(query_part.astype(jnp.float32), 0)
    grad_value_bias = jnp.sum(value_part.astype(jnp.float32), 0)
    grad_qkv = jnp.einsum("td,te->de", normed, grad_rows, preferred_element_type=jnp.float32)
    grad_normed = jnp.einsum("te,de->td", grad_rows, qkv_weight, preferred_element_type=jnp.float32)
    grad_table = jnp.sum(grad_normed, 0)[:, None] * onehot[None, :]
    norm_back_one = jax.vjp(
        layer_norm, inputs, gain_one.astype(jnp.float32), shift_one.astype(jnp.float32)
    )[1]
    through_one, grad_gain_one, grad_shift_one = norm_back_one(grad_normed)
    grads = (
        grad_gain_one,
        grad_shift_one,
        grad_table,
        grad_qkv,
        grad_query_bias,
        grad_value_bias,
        grad_out,
        grad_out_bias,
        grad_gain_two,
        grad_shift_two,
        grad_up,
        grad_up_bias,
        grad_down,
        grad_down_bias,
    )
    return (grad_middle + through_one, grads)


def fetch_forward(parts):
    return (
        lax.all_gather(parts[0], "dp", axis=0, tiled=True),
        lax.all_gather(parts[1], "dp", axis=0, tiled=True),
        lax.all_gather(parts[2], "dp", axis=0, tiled=True),
        lax.all_gather(parts[3], "dp", axis=0, tiled=True),
        lax.all_gather(parts[4], "dp", axis=0, tiled=True),
        lax.all_gather(parts[5], "dp", axis=0, tiled=True),
        lax.all_gather(parts[6], "dp", axis=0, tiled=True),
        lax.all_gather(parts[7], "dp", axis=0, tiled=True),
        lax.all_gather(parts[8], "dp", axis=0, tiled=True),
        lax.all_gather(parts[9], "dp", axis=0, tiled=True),
        lax.all_gather(parts[10], "dp", axis=0, tiled=True),
        lax.all_gather(parts[11], "dp", axis=0, tiled=True),
        lax.all_gather(parts[12], "dp", axis=0, tiled=True),
        lax.all_gather(parts[13], "dp", axis=0, tiled=True),
    )


def fetch_backward(parts):
    return (
        lax.all_gather(parts[0], "dp", axis=0, tiled=True),
        lax.all_gather(parts[1], "dp", axis=0, tiled=True),
        lax.all_gather(parts[2], "dp", axis=0, tiled=True),
        lax.all_gather(parts[3], "dp", axis=0, tiled=True),
        lax.all_gather(parts[4], "dp", axis=0, tiled=True),
        lax.all_gather(parts[5], "dp", axis=0, tiled=True),
        lax.all_gather(parts[6], "dp", axis=0, tiled=True),
        lax.all_gather(parts[7], "dp", axis=0, tiled=True),
        lax.all_gather(parts[8], "dp", axis=0, tiled=True),
        lax.all_gather(parts[9], "dp", axis=0, tiled=True),
        lax.all_gather(parts[10], "dp", axis=0, tiled=True),
        lax.all_gather(parts[11], "dp", axis=0, tiled=True),
        lax.all_gather(parts[12], "dp", axis=0, tiled=True),
        lax.all_gather(parts[13], "dp", axis=0, tiled=True),
    )


def reduce_totals(grads):
    return (
        lax.psum_scatter(grads[0], "dp", scatter_dimension=0, tiled=True),
        lax.psum_scatter(grads[1], "dp", scatter_dimension=0, tiled=True),
        lax.psum_scatter(grads[2], "dp", scatter_dimension=0, tiled=True),
        lax.psum_scatter(grads[3], "dp", scatter_dimension=0, tiled=True),
        lax.psum_scatter(grads[4], "dp", scatter_dimension=0, tiled=True),
        lax.psum_scatter(grads[5], "dp", scatter_dimension=0, tiled=True),
        lax.psum_scatter(grads[6], "dp", scatter_dimension=0, tiled=True),
        lax.psum_scatter(grads[7], "dp", scatter_dimension=0, tiled=True),
        lax.psum_scatter(grads[8], "dp", scatter_dimension=0, tiled=True),
        lax.psum_scatter(grads[9], "dp", scatter_dimension=0, tiled=True),
        lax.psum_scatter(grads[10], "dp", scatter_dimension=0, tiled=True),
        lax.psum_scatter(grads[11], "dp", scatter_dimension=0, tiled=True),
        lax.psum_scatter(grads[12], "dp", scatter_dimension=0, tiled=True),
        lax.psum_scatter(grads[13], "dp", scatter_dimension=0, tiled=True),
    )


def send_forward(values):
    return shifted(values, "section", 1)


def send_backward(values):
    return shifted(values, "section", -1)


def body(
    block_input,
    cotangent,
    lengths,
    leads,
    norm_gain1,
    norm_bias1,
    lead_table,
    qkv_weight,
    query_bias,
    value_bias,
    out_weight,
    out_bias,
    norm_gain2,
    norm_bias2,
    up_weight,
    up_bias,
    down_weight,
    down_bias,
):
    masters = (
        norm_gain1,
        norm_bias1,
        lead_table,
        qkv_weight,
        query_bias,
        value_bias,
        out_weight,
        out_bias,
        norm_gain2,
        norm_bias2,
        up_weight,
        up_bias,
        down_weight,
        down_bias,
    )
    parts = tuple((master[0].astype(jnp.bfloat16) for master in masters))
    first_section = lax.axis_index("section") == 0
    micro = block_input.shape[0]
    rows = block_input.shape[2]
    width = block_input.shape[3]
    weights = fetch_forward(parts)
    kept_steps = []
    produced = []
    incoming = jnp.zeros((rows, width), jnp.bfloat16)
    for step in range(micro + 1):
        early = min(step, micro - 1)
        late = max(step - 1, 0)
        if step > 0:
            incoming = send_forward(produced[-1])
        inputs = jnp.where(
            first_section, block_input[early, 0].astype(jnp.float32), incoming.astype(jnp.float32)
        )
        length = jnp.where(first_section, lengths[early, 0], lengths[late, 0])
        lead = jnp.where(first_section, leads[early, 0], leads[late, 0])
        output, kept = forward_layer(weights, inputs, length, lead)
        kept_steps.append(kept)
        produced.append(output.astype(jnp.bfloat16))
    activations = jnp.stack(
        [
            jnp.where(first_section, produced[batch_index], produced[batch_index + 1])
            for batch_index in range(micro)
        ]
    )
    weights_back = fetch_backward(parts)
    sums = [jnp.zeros(weight.shape, jnp.float32) for weight in weights_back]
    returning = []
    input_list = []
    arriving = jnp.zeros((rows, width), jnp.bfloat16)
    for step in range(micro + 1):
        kept = kept_steps[micro - step]
        if step > 0:
            arriving = send_backward(returning[-1])
        if step < micro:
            own = cotangent[micro - 1 - step, 0].astype(jnp.float32)
        else:
            own = jnp.zeros((rows, width), jnp.float32)
        upstream = jnp.where(first_section, arriving.astype(jnp.float32), own)
        input_grad, step_grads = backward_layer(weights_back, kept, upstream)
        returning.append(input_grad.astype(jnp.bfloat16))
        input_list.append(input_grad)
        sums = [running + grad for running, grad in zip(sums, step_grads)]
    sums = list(reduce_totals(sums))
    input_grads = jnp.stack(
        [
            jnp.where(
                first_section, input_list[micro - batch_index], input_list[micro - 1 - batch_index]
            )
            for batch_index in range(micro)
        ]
    )
    results = [activations[None, :, None], input_grads[None, :, None]] + [
        running[None] for running in sums
    ]
    return tuple(results)


def solution(mesh):
    return jax.shard_map(
        body,
        mesh=mesh,
        in_specs=(
            P(None, "dp", None, None),
            P(None, "dp", None, None),
            P(None, "dp"),
            P(None, "dp"),
            P("section", "dp"),
            P("section", "dp"),
            P("section", "dp", None),
            P("section", "dp", None),
            P("section", "dp"),
            P("section", "dp"),
            P("section", "dp", None),
            P("section", "dp"),
            P("section", "dp"),
            P("section", "dp"),
            P("section", "dp", None),
            P("section", "dp"),
            P("section", "dp", None),
            P("section", "dp"),
        ),
        out_specs=(
            P("section", None, "dp", None, None),
            P("section", None, "dp", None, None),
            P("section", "dp"),
            P("section", "dp"),
            P("section", "dp", None),
            P("section", "dp", None),
            P("section", "dp"),
            P("section", "dp"),
            P("section", "dp", None),
            P("section", "dp"),
            P("section", "dp"),
            P("section", "dp"),
            P("section", "dp", None),
            P("section", "dp"),
            P("section", "dp", None),
            P("section", "dp"),
        ),
        check_vma=False,
    )
```

profile of v0, /device:TPU:0, one launch (start us, length us, event | category | flops | bytes accessed | tf_op | source)
XLA Modules:
  0.0 781.4 jit_solution(14735492907810290699)
XLA Ops:
  7.2 1.8 convert_element_type.519
  9.1 1.6 convert_element_type.533
  16.8 63.5 %all-reduce.19 = (bf16[768]{0:T(1024)(128)(2,1)S(1)}, bf16[768]{0:T(1024)(128)(2,1)S(1)}, bf16[768]{0:T(1024)(128)(2,1)S(1)}, bf16[768]{0:T(1024)(128)(2,1)S(1)}...) all-reduce(bf16[768]{0:T(1024)(128)(2,1)S(1)} %dynamic-update-slice, ...), channel_id=3, replica_groups=mesh['section'=2,'dp'=16] {'dp'}, use_global_device_ids=true, to_apply=%add.1 | all-reduce | flops 9216 | bytes 36864
  80.5 18.9 %all-gather.2 = bf16[1,768,24]{2,0,1:T(2,128)(2,1)S(1)} all-gather(bf16[1,48,24]{2,0,1:T(2,128)(2,1)S(1)} %copy.153), channel_id=4, replica_groups=mesh['section'=2,'dp'=16] {'dp'}, dimensions={1}, use_global_device_ids=true | all-gather | bytes 39168 | tf_op jit(solution)/shard_map/all_gather | solution.py:238
  110.3 2.9 fusion.43
  114.7 1.8 fusion.229
  116.7 41.0 %all-gather.23.cloned.1.call-done = bf16[1,768,3072]{2,1,0:T(8,128)(2,1)} async-done(((bf16[1,48,3072]{2,1,0:T(8,128)(2,1)}), bf16[1,768,3072]{2,1,0:T(8,128)(2,1)}) %all-gather.23.cloned.1.call-update) | async-done | bytes 4718608 | tf_op jit(solution)/shard_map/all_gather | solution.py:246
  157.7 3.3 fusion.24
  161.1 51.4 %all-gather.25.cloned.1.call-done = bf16[1,3072,768]{2,1,0:T(8,128)(2,1)} async-done(((bf16[1,192,768]{2,1,0:T(8,128)(2,1)}), bf16[1,3072,768]{2,1,0:T(8,128)(2,1)}) %all-gather.25.cloned.1.call-update) | async-done | bytes 4718608 | tf_op jit(solution)/shard_map/all_gather | solution.py:248
  212.4 3.5 fusion.135
  216.0 3.4 collective-permute-start
  220.0 2.9 collective-permute-done
  227.7 3.3 fusion.27
  231.0 3.8 fusion.138
  234.9 4.9 collective-permute-start.1
  240.3 1.6 collective-permute-done.1
  249.5 3.4 fusion.30
  252.9 5.3 convert_reduce_fusion.2
  258.3 2.2 multiply_reduce_fusion.5
  264.0 1.7 copy.167
  265.8 2.0 convert_reduce_fusion.5
  271.2 1.9 multiply_reduce_fusion.8
  274.0 1.6 collective-permute-start.2
  275.6 1.9 fusion.234
  277.5 3.7 collective-permute-done.2
  281.9 5.0 convert_reduce_fusion.1
  286.9 2.2 multiply_reduce_fusion.4
  291.2 1.7 copy.171
  292.9 2.0 convert_reduce_fusion.4
  298.3 1.9 multiply_reduce_fusion.7
  302.8 1.8 fusion.235
  304.7 3.9 collective-permute-done.3
  308.5 4.9 convert_reduce_fusion
  313.4 2.2 multiply_reduce_fusion.3
  320.2 1.8 convert_reduce_fusion.3
  325.0 2.6 fusion.214
  329.0 4.2 add_add_fusion.3
  337.1 4.2 add_add_fusion.2
  342.3 2.8 fusion.182
  346.6 5.3 add_add_fusion
  354.7 1.5 fusion.210
  356.2 5.1 add_add_fusion.1
  362.9 3.4 fusion.147
  370.9 58.3 %all-reduce.18 = (f32[768]{0:T(1024)S(1)}, f32[768]{0:T(1024)S(1)}, f32[768]{0:T(1024)S(1)}, f32[768]{0:T(1024)S(1)}, f32[768]{0:T(1024)S(1)}, /*index=5*/f32[76...) all-reduce(f32[768]{0:T(1024)S(1)} %get-tuple-element.214, ...), channel_id=16, replica_groups=mesh['section'=2,'dp'=16] {'dp'}, use_global_device_ids=true, to_apply=%region_36.37.clone | all-reduce | flops 9216 | bytes 73728
  436.8 12.0 %reduce-scatter.10.cloned.1.call-done = f32[48,768]{1,0:T(8,128)} async-done(((f32[768,768]{1,0:T(8,128)}), f32[48,768]{1,0:T(8,128)}) %reduce-scatter.10.cloned.1.call-update) | async-done | bytes 147472 | tf_op jit(solution)/shard_map/reduce_scatter | solution.py:280
  448.8 93.7 %reduce-scatter.8.cloned.1.call-done = f32[48,2304]{1,0:T(8,128)} async-done(((f32[768,2304]{1,0:T(8,128)}), f32[48,2304]{1,0:T(8,128)}) %reduce-scatter.8.cloned.1.call-update) | async-done | bytes 442384 | tf_op jit(solution)/shard_map/reduce_scatter | solution.py:277
  542.5 116.1 %reduce-scatter.14.cloned.1.call-done = f32[192,768]{1,0:T(8,128)} async-done(((f32[3072,768]{1,0:T(8,128)}), f32[192,768]{1,0:T(8,128)}) %reduce-scatter.14.cloned.1.call-update) | async-done | bytes 589840 | tf_op jit(solution)/shard_map/reduce_scatter | solution.py:286
  658.6 115.8 %reduce-scatter.12.cloned.1.call-done = f32[48,3072]{1,0:T(8,128)} async-done(((f32[768,3072]{1,0:T(8,128)}), f32[48,3072]{1,0:T(8,128)}) %reduce-scatter.12.cloned.1.call-update) | async-done | bytes 589840 | tf_op jit(solution)/shard_map/reduce_scatter | solution.py:284
  (609 shorter events, 73.2 us)
Async XLA Ops:
  7.2 103.1 %all-gather.19.cloned.1.call-start = ((), (), s32[]{:S(2)}) async-start(), calls=%async_computation.9 | async-start | bytes 3760128 | tf_op jit(solution)/shard_map/all_gather | solution.py:239
  9.1 105.6 %all-gather.21.cloned.1.call-start = ((), (), s32[]{:S(2)}) async-start(), calls=%async_computation.10 | async-start | bytes 1253376 | tf_op jit(solution)/shard_map/all_gather | solution.py:242
  10.8 5.4 copy-start.198
  10.8 5.7 copy-start.190
  10.8 146.9 %all-gather.23.cloned.1.call-start = ((), (), s32[]{:S(2)}) async-start(), calls=%async_computation.11 | async-start | bytes 5013504 | tf_op jit(solution)/shard_map/all_gather | solution.py:246
  11.7 88.0 %copy-start.172 = (s32[2,1]{0,1:T(1,128)S(1)}, s32[2,1]{0,1:T(1,128)}, u32[]{:S(2)}) copy-start(s32[2,1]{0,1:T(1,128)} %param.20) | copy-start | bytes 28
  11.7 89.9 %copy-start.173 = (s32[2,1]{0,1:T(1,128)S(1)}, s32[2,1]{0,1:T(1,128)}, u32[]{:S(2)}) copy-start(s32[2,1]{0,1:T(1,128)} %param.21) | copy-start | bytes 28
  11.7 98.3 %copy-start.6 = (bf16[2,1,96,768]{3,2,1,0:T(8,128)(2,1)S(1)}, bf16[2,1,96,768]{3,2,1,0:T(8,128)(2,1)}, u32[]{:S(2)}) copy-start(bf16[2,1,96,768]{3,2,1,0:T(8,128)(2,1)} %param.18) | copy-start | bytes 884740
  11.7 200.7 %all-gather.25.cloned.1.call-start = ((), (), s32[]{:S(2)}) async-start(), calls=%async_computation.12 | async-start | bytes 5013504 | tf_op jit(solution)/shard_map/all_gather | solution.py:248
  12.5 422.8 %reduce-scatter.16.cloned.1.call-start = ((), (), s32[]{:S(2)}) async-start(), calls=%async_computation.13 | async-start | bytes 417792
  80.4 145.0 %copy-start.102 = (f32[768]{0:T(1024)}, f32[768]{0:T(1024)S(1)}, u32[]{:S(2)}) copy-start(f32[768]{0:T(1024)S(1)} %convert_element_type.667) | copy-start | bytes 9220
  80.4 132.0 %copy-start.166 = (f32[768]{0:T(1024)}, f32[768]{0:T(1024)S(1)}, u32[]{:S(2)}) copy-start(f32[768]{0:T(1024)S(1)} %convert_element_type.671) | copy-start | bytes 9220
  80.4 146.7 %copy-start.89 = (f32[3072]{0:T(1024)}, f32[3072]{0:T(1024)S(1)}, u32[]{:S(2)}) copy-start(f32[3072]{0:T(1024)S(1)} %convert_element_type.670) | copy-start | bytes 36868
  108.4 114.8 %copy-start.91 = (f32[768]{0:T(1024)}, f32[768]{0:T(1024)S(1)}, u32[]{:S(2)}) copy-start(f32[768]{0:T(1024)S(1)} %convolution_reduce_fusion.1) | copy-start | bytes 9220
  109.2 133.2 %copy-start.93 = (f32[768]{0:T(1024)}, f32[768]{0:T(1024)S(1)}, u32[]{:S(2)}) copy-start(f32[768]{0:T(1024)S(1)} %convolution_reduce_fusion) | copy-start | bytes 9220
  116.4 96.0 %copy-start.9 = (f32[96,768]{1,0:T(8,128)}, f32[96,768]{1,0:T(8,128)S(1)}, u32[]{:S(2)}) copy-start(f32[96,768]{1,0:T(8,128)S(1)} %get-tuple-element.172) | copy-start | bytes 884740
  116.5 44.6 %copy-start.131 = (f32[96]{0:T(128)}, f32[96]{0:T(128)S(1)}, u32[]{:S(2)}) copy-start(f32[96]{0:T(128)S(1)} %broadcast_multiply_fusion.4) | copy-start | bytes 1156
  116.7 44.4 %copy-start.182 = (f32[96]{0:T(128)}, f32[96]{0:T(128)S(1)}, u32[]{:S(2)}) copy-start(f32[96]{0:T(128)S(1)} %multiply_reduce_fusion.19) | copy-start | bytes 1156
  116.7 44.4 %copy-start.153 = (f32[96]{0:T(128)}, f32[96]{0:T(128)S(1)}, u32[]{:S(2)}) copy-start(f32[96]{0:T(128)S(1)} %fusion.194) | copy-start | bytes 1156
  161.1 54.9 %copy-start.22 = (f32[96,3072]{1,0:T(8,128)}, f32[96,3072]{1,0:T(8,128)S(1)}, u32[]{:S(2)}) copy-start(f32[96,3072]{1,0:T(8,128)S(1)} %fusion.24) | copy-start | bytes 3538948
  212.4 10.8 %copy-start.1 = (bf16[1,768,2304]{2,1,0:T(8,128)(2,1)S(1)}, bf16[1,768,2304]{2,1,0:T(8,128)(2,1)}, u32[]{:S(2)}) copy-start(bf16[1,768,2304]{2,1,0:T(8,128)(2,1)} %all-gather.19.cloned.1.call-done) | copy-start | bytes 10616836
  215.9 8.1 %copy-start.95 = (bf16[96,768]{1,0:T(8,128)(2,1)}, bf16[96,768]{1,0:T(8,128)(2,1)S(1)}, u32[]{:S(2)}) copy-start(bf16[96,768]{1,0:T(8,128)(2,1)S(1)} %fusion.135) | copy-start | bytes 442372
  216.0 6.9 collective-permute-start
  225.4 5.6 copy-start.69
  231.0 11.3 %copy-start.2 = (bf16[1,768,2304]{2,1,0:T(8,128)(2,1)S(1)}, bf16[1,768,2304]{2,1,0:T(8,128)(2,1)}, u32[]{:S(2)}) copy-start(bf16[1,768,2304]{2,1,0:T(8,128)(2,1)} %all-gather.19.cloned.1.call-done) | copy-start | bytes 10616836
  234.9 8.3 %copy-start.97 = (bf16[96,768]{1,0:T(8,128)(2,1)}, bf16[96,768]{1,0:T(8,128)(2,1)S(1)}, u32[]{:S(2)}) copy-start(bf16[96,768]{1,0:T(8,128)(2,1)S(1)} %fusion.138) | copy-start | bytes 442372
  234.9 7.1 collective-permute-start.1
  249.2 11.3 %copy-start.7 = (f32[96,768]{1,0:T(8,128)}, f32[96,768]{1,0:T(8,128)S(1)}, u32[]{:S(2)}) copy-start(f32[96,768]{1,0:T(8,128)S(1)} %get-tuple-element.180) | copy-start | bytes 884740
  249.2 11.3 %copy-start.113 = (f32[96]{0:T(128)}, f32[96]{0:T(128)S(1)}, u32[]{:S(2)}) copy-start(f32[96]{0:T(128)S(1)} %broadcast_multiply_fusion) | copy-start | bytes 1156
  249.4 11.1 %copy-start.137 = (f32[96]{0:T(128)}, f32[96]{0:T(128)S(1)}, u32[]{:S(2)}) copy-start(f32[96]{0:T(128)S(1)} %fusion.198) | copy-start | bytes 1156
  249.5 8.8 %slice-start = ((s8[4718592]{0:T(1024)(128)(4,1)}), s8[4194304]{0:T(1024)(128)(4,1)S(1)}, s32[]{:S(2)}) async-start(s8[4718592]{0:T(1024)(128)(4,1)} %bitcast.376), calls=%async_computation.14 | async-start | bytes 8388608
  274.0 7.8 %copy-start.12 = (f32[96,3072]{1,0:T(8,128)S(1)}, f32[96,3072]{1,0:T(8,128)}, u32[]{:S(2)}) copy-start(f32[96,3072]{1,0:T(8,128)} %copy-done.11) | copy-start | bytes 3538948
  274.0 7.2 collective-permute-start.2
  275.6 11.2 %slice-start.2 = ((s8[4718592]{0:T(1024)(128)(4,1)}), s8[4194304]{0:T(1024)(128)(4,1)S(1)}, s32[]{:S(2)}) async-start(s8[4718592]{0:T(1024)(128)(4,1)} %bitcast.378), calls=%async_computation.16 | async-start | bytes 8388608
  301.3 7.2 copy-start.23
  301.3 7.2 collective-permute-start.3
  302.8 10.6 %slice-start.4 = ((s8[4718592]{0:T(1024)(128)(4,1)}), s8[4194304]{0:T(1024)(128)(4,1)S(1)}, s32[]{:S(2)}) async-start(s8[4718592]{0:T(1024)(128)(4,1)} %bitcast.380), calls=%async_computation.18 | async-start | bytes 8388608
  304.6 8.8 %slice-start.5 = ((s8[4718592]{0:T(1024)(128)(4,1)}), s8[524288]{0:T(1024)(128)(4,1)S(1)}, s32[]{:S(2)}) async-start(s8[4718592]{0:T(1024)(128)(4,1)} %bitcast.380), calls=%async_computation.19 | async-start | bytes 1048576
  304.6 8.8 %copy-start.10 = (f32[96,768]{1,0:T(8,128)S(1)}, f32[96,768]{1,0:T(8,128)}, u32[]{:S(2)}) copy-start(f32[96,768]{1,0:T(8,128)} %copy-done.9) | copy-start | bytes 884740
  304.6 8.8 %copy-start.132 = (f32[96]{0:T(128)S(1)}, f32[96]{0:T(128)}, u32[]{:S(2)}) copy-start(f32[96]{0:T(128)} %copy-done.131) | copy-start | bytes 1156
  304.6 8.8 %copy-start.154 = (f32[96]{0:T(128)S(1)}, f32[96]{0:T(128)}, u32[]{:S(2)}) copy-start(f32[96]{0:T(128)} %copy-done.153) | copy-start | bytes 1156
  327.6 5.6 copy-start.123
  328.7 120.1 %reduce-scatter.10.cloned.1.call-start = ((), (), s32[]{:S(2)}) async-start(), calls=%async_computation.6 | async-start | bytes 2506752 | tf_op jit(solution)/shard_map/reduce_scatter | solution.py:280
  333.3 209.2 %reduce-scatter.8.cloned.1.call-start = ((), (), s32[]{:S(2)}) async-start(), calls=%async_computation.5 | async-start | bytes 7520256 | tf_op jit(solution)/shard_map/reduce_scatter | solution.py:277
  341.4 317.3 %reduce-scatter.14.cloned.1.call-start = ((), (), s32[]{:S(2)}) async-start(), calls=%async_computation.8 | async-start | bytes 10027008 | tf_op jit(solution)/shard_map/reduce_scatter | solution.py:286
  352.0 422.4 %reduce-scatter.12.cloned.1.call-start = ((), (), s32[]{:S(2)}) async-start(), calls=%async_computation.7 | async-start | bytes 10027008 | tf_op jit(solution)/shard_map/reduce_scatter | solution.py:284
  362.9 5.8 copy-start.59
  362.9 5.8 copy-start.148
  (170 other events, 383.7 us)
Sparse Core Ops, SparseCore 0:
  10.9 50.6 all-gather.18
  64.4 37.2 all-gather.20
  104.6 53.0 all-gather.22
  160.5 51.9 all-gather.24
  328.8 53.2 reduce-scatter.15
  386.7 61.9 reduce-scatter.9
  453.3 89.1 reduce-scatter.7
  547.7 110.8 reduce-scatter.13
  663.3 111.1 reduce-scatter.11
where the time goes:
time: 791 us; the launch traced here: 781 us
  waiting for transfers between devices  442 us (56%)
  blocking collectives  141 us (18%)
  matrix products  110 us (14%)
  local copies, waits for them, and re-layouts  30.2 us (4%)
  other arithmetic  23.8 us (3%)
  between operations  22.5 us (3%)
  starting transfers between devices  12.1 us (2%)
    unnamed x2, blocking collectives  122 us
    reduce_scatter x1, waiting for transfers between devices, reduce_totals(): lax.psum_scatter(grads[12], 'dp', scatter_dimension=0, tiled=True)  116 us
    reduce_scatter x1, waiting for transfers between devices, reduce_totals(): lax.psum_scatter(grads[10], 'dp', scatter_dimension=0, tiled=True)  116 us
    reduce_scatter x1, waiting for transfers between devices, reduce_totals(): lax.psum_scatter(grads[3], 'dp', scatter_dimension=0, tiled=True)  93.7 us
    all_gather x1, waiting for transfers between devices, fetch_forward(): lax.all_gather(parts[12], 'dp', axis=0, tiled=True)  51.4 us
    all_gather x1, waiting for transfers between devices, fetch_forward(): lax.all_gather(parts[10], 'dp', axis=0, tiled=True)  41 us
    all_gather x1, blocking collectives, fetch_forward(): lax.all_gather(parts[2], 'dp', axis=0, tiled=True)  18.9 us
    unnamed x432, local copies, waits for them, and re-layouts  15.9 us
  transfers between devices with their start and end apart: 13, of which 10 were waited for; matrix products, arithmetic and copies ran while one was open for 9% of the time, Pallas kernels for 0%

commit v1 on v0

v1 whole, which is shorter than its diff:
```python
import functools

import jax
import jax.numpy as jnp
from jax import lax
from jax.experimental import pallas as pl
from jax.experimental.pallas import tpu as pltpu
from jax.sharding import PartitionSpec as P

HEAD = 64
PAIR = 2 * HEAD
EPS = 1e-06
SCALE_FACTOR = 0.125
GELU_A = 0.7978845608028654
GELU_B = 0.044715
LIMIT = 60 * 1024 * 1024
F32 = jnp.float32
BF16 = jnp.bfloat16
BLOCKS = 12
QKV, OUT, UP, DOWN = (0, 3), (3, 1), (4, 4), (8, 4)


def mm(left, right):
    return jnp.dot(left, right, preferred_element_type=F32)


def mm_nt(left, right):
    return lax.dot_general(left, right, (((1,), (1,)), ((), ())), preferred_element_type=F32)


def mm_tn(left, right):
    return lax.dot_general(left, right, (((0,), (0,)), ((), ())), preferred_element_type=F32)


def normalised(values):
    mean = jnp.mean(values, -1, keepdims=True)
    centred = values - mean
    variance = jnp.mean(centred * centred, -1, keepdims=True)
    rstd = lax.rsqrt(variance + EPS)
    return centred * rstd, rstd


def norm_back(grad, xhat, rstd, gain):
    scaled = grad * gain
    first = jnp.mean(scaled, -1, keepdims=True)
    second = jnp.mean(scaled * xhat, -1, keepdims=True)
    return rstd * (scaled - first - xhat * second)


def gelu_both(values):
    square = values * values
    slope = GELU_A * (1.0 + 3.0 * GELU_B * square)
    bend = jnp.tanh(GELU_A * values * (1.0 + GELU_B * square))
    half = 0.5 * (1.0 + bend)
    return values * half, half + 0.5 * values * (1.0 - bend * bend) * slope


def split_pair(rows):
    lane = lax.broadcasted_iota(jnp.int32, rows.shape, 1)
    zero = jnp.zeros_like(rows)
    return jnp.concatenate(
        [jnp.where(lane < HEAD, rows, zero), jnp.where(lane < HEAD, zero, rows)], 0
    )


def join_pair(stacked):
    count = stacked.shape[0] // 2
    lane = lax.broadcasted_iota(jnp.int32, (count, PAIR), 1)
    return jnp.where(lane < HEAD, stacked[:count], stacked[count:])


class Plan:
    def __init__(self, shards, rows, order, items, length, width):
        self.shards, self.rows, self.order = shards, rows, order
        self.items, self.length, self.width = items, length, width
        self.tokens = items * length
        self.pairs = width // PAIR


def weight_copies(plan, gathered, held, sem, group):
    first, count = group
    copies = []
    for place, device in enumerate(plan.order):
        if group is DOWN:
            for block in range(count):
                row = count * device + block
                copies.append(
                    pltpu.make_async_copy(
                        gathered.at[place, first + block],
                        held.at[first + row // plan.shards, row % plan.shards],
                        sem,
                    )
                )
        else:
            copies.append(
                pltpu.make_async_copy(
                    gathered.at[place, pl.ds(first, count)],
                    held.at[pl.ds(first, count), device],
                    sem,
                )
            )
    return copies


def start_weights(plan, gathered, held, sem, group):
    for copy in weight_copies(plan, gathered, held, sem, group):
        copy.start()


def wait_weights(held, sem, group):
    first, count = group
    part = held.at[pl.ds(first, count)]
    pltpu.make_async_copy(part, part, sem).wait()


def block_of(plan, held, index):
    return held[index].reshape(plan.width, plan.width)


def forward(plan, inputs, lengths, vec, gathered, held, sems, scratch, keep):
    width, length = plan.width, plan.length
    normed_ref, qkv_ref, attended_ref, middle_ref, hidden_ref = scratch[:5]
    start_weights(plan, gathered, held, sems.at[0], QKV)
    start_weights(plan, gathered, held, sems.at[1], OUT)
    values = inputs.astype(F32)
    xhat, _ = normalised(values)
    base = xhat * vec[0:1, :] + vec[1:2, :]
    for item in range(plan.items):
        rows = slice(item * length, (item + 1) * length)
        normed_ref[rows, :] = (base[rows] + vec[12 + item : 13 + item, :]).astype(BF16)
    wait_weights(held, sems.at[0], QKV)
    start_weights(plan, gathered, held, sems.at[2], UP)
    for part, bias in enumerate((2, None, 3)):
        joined = mm(normed_ref[...], block_of(plan, held, part))
        if bias is not None:
            joined = joined + vec[bias : bias + 1, :]
        qkv_ref[:, part * width : (part + 1) * width] = joined.astype(BF16)
    start_weights(plan, gathered, held, sems.at[3], DOWN)
    key_index = lax.broadcasted_iota(jnp.int32, (2 * length, length), 1)
    for item in range(plan.items):
        rows = slice(item * length, (item + 1) * length)
        valid = key_index < lengths[item]
        for pair in range(plan.pairs):
            at = pair * PAIR
            query = split_pair(qkv_ref[rows, at : at + PAIR])
            key = qkv_ref[rows, width + at : width + at + PAIR]
            value = qkv_ref[rows, 2 * width + at : 2 * width + at + PAIR]
            logits = jnp.where(valid, mm_nt(query, key) * SCALE_FACTOR, -1000000000.0)
            expo = jnp.exp(logits - jnp.max(logits, -1, keepdims=True))
            probs = expo / jnp.sum(expo, -1, keepdims=True)
            if keep:
                scratch[5][item * plan.pairs + pair] = probs
            attended_ref[rows, at : at + PAIR] = join_pair(mm(probs.astype(BF16), value)).astype(
                BF16
            )
    wait_weights(held, sems.at[1], OUT)
    middle = values + (mm(attended_ref[...], block_of(plan, held, OUT[0])) + vec[4:5, :])
    middle_ref[...] = middle
    xhat, _ = normalised(middle)
    hidden_ref[...] = (xhat * vec[5:6, :] + vec[6:7, :]).astype(BF16)
    wait_weights(held, sems.at[2], UP)
    wait_weights(held, sems.at[3], DOWN)
    total = None
    for part in range(UP[1]):
        pre_act = mm(hidden_ref[...], block_of(plan, held, UP[0] + part)) + vec[8 + part : 9 + part, :]
        act, slope = gelu_both(pre_act)
        act = act.astype(BF16)
        if keep:
            scratch[6][:, part * width : (part + 1) * width] = act
            scratch[7][:, part * width : (part + 1) * width] = slope
        term = mm(act, block_of(plan, held, DOWN[0] + part))
        total = term if total is None else total + term
    return middle_ref[...] + (total + vec[7:8, :])


def attention_back(plan, probs_ref, qkv_ref, grad_attended_ref, rows_ref):
    width, length = plan.width, plan.length
    for item in range(plan.items):
        rows = slice(item * length, (item + 1) * length)
        for pair in range(plan.pairs):
            at = pair * PAIR
            query = split_pair(qkv_ref[rows, at : at + PAIR])
            key = qkv_ref[rows, width + at : width + at + PAIR]
            value = qkv_ref[rows, 2 * width + at : 2 * width + at + PAIR]
            grad = split_pair(grad_attended_ref[rows, at : at + PAIR])
            probs = probs_ref[item * plan.pairs + pair]
            grad_probs = mm_nt(grad, value)
            centre = jnp.sum(grad_probs * probs, -1, keepdims=True)
            grad_logits = (probs * (grad_probs - centre)).astype(BF16)
            grad_query = join_pair(mm(grad_logits, key)) * SCALE_FACTOR
            grad_key = mm_tn(grad_logits, query) * SCALE_FACTOR
            grad_value = mm_tn(probs.astype(BF16), grad)
            rows_ref[rows, at : at + PAIR] = grad_query.astype(BF16)
            rows_ref[rows, width + at : width + at + PAIR] = grad_key.astype(BF16)
            rows_ref[rows, 2 * width + at : 2 * width + at + PAIR] = grad_value.astype(BF16)


def column_sum(values):
    return jnp.sum(values.astype(F32), 0, keepdims=True)


def forward_kernel(plan, lengths, x_ref, vec, gathered, y_ref, held, normed, qkv, attended, middle, hidden, sems):
    out = forward(
        plan, x_ref[...], lengths, vec, gathered, held, sems,
        (normed, qkv, attended, middle, hidden), False,
    )
    y_ref[...] = out.astype(BF16)


def chain_kernel(
    plan, lengths, flag, x_ref, recv_ref, cot_ref, vec, gathered,
    y_ref, xin_ref, dx_ref, normed_out, qkv_out, attended_out, middle_out, hidden_out, probs_out, act_out, slope_out,
    held, normed, qkv, attended, middle, hidden, probs, act, slope, grad_attended, grad_rows, sems, out_sems,
):
    width = plan.width
    xin_ref[...] = jnp.where(flag[0] == 0, x_ref[...], recv_ref[...])
    scratch = (normed, qkv, attended, middle, hidden, probs, act, slope)
    out = forward(plan, xin_ref[...], lengths, vec, gathered, held, sems, scratch, True)
    y_ref[...] = out.astype(BF16)
    outs = (normed_out, qkv_out, attended_out, middle_out, hidden_out, probs_out, act_out, slope_out)
    copies = [
        pltpu.make_async_copy(source, target, out_sems.at[index])
        for index, (source, target) in enumerate(zip(scratch, outs))
    ]
    for copy in copies:
        copy.start()
    branch = cot_ref[...]
    grad_hidden = None
    for part in range(UP[1]):
        grad_act = mm_nt(branch, block_of(plan, held, DOWN[0] + part))
        grad_pre = (slope[:, part * width : (part + 1) * width] * grad_act).astype(BF16)
        term = mm_nt(grad_pre, block_of(plan, held, UP[0] + part))
        grad_hidden = term if grad_hidden is None else grad_hidden + term
    xhat, rstd = normalised(middle[...])
    grad_middle = branch.astype(F32) + norm_back(grad_hidden, xhat, rstd, vec[5:6, :])
    grad_attended[...] = mm_nt(grad_middle.astype(BF16), block_of(plan, held, OUT[0])).astype(BF16)
    attention_back(plan, probs, qkv, grad_attended, grad_rows)
    grad_normed = None
    for part in range(QKV[1]):
        term = mm_nt(grad_rows[:, part * width : (part + 1) * width], block_of(plan, held, part))
        grad_normed = term if grad_normed is None else grad_normed + term
    xhat, rstd = normalised(xin_ref[...].astype(F32))
    dx_ref[...] = (grad_middle + norm_back(grad_normed, xhat, rstd, vec[0:1, :])).astype(BF16)
    for copy in copies:
        copy.wait()


def grad_copies(plan, stage, grads, sem, index):
    copies = []
    for place, device in enumerate(plan.order):
        if index >= DOWN[0]:
            for block in range(DOWN[1]):
                row = DOWN[1] * device + block
                if DOWN[0] + row // plan.shards == index:
                    copies.append(
                        pltpu.make_async_copy(
                            stage.at[row % plan.shards], grads.at[place, DOWN[0] + block], sem
                        )
                    )
        else:
            copies.append(pltpu.make_async_copy(stage.at[device], grads.at[place, index], sem))
    return copies


def backward_kernel(
    plan, flag, arr_ref, cot_ref, xin_ref, vec, gathered,
    normed_in, qkv_in, attended_in, middle_in, hidden_in, probs_in, act_in, slope_in,
    dx_ref, small_ref, grads,
    held, normed, qkv, attended, middle, hidden, probs, act, slope, grad_attended, grad_rows, grad_pre_ref, stage,
    sems, in_sems, stage_sems,
):
    width, length = plan.width, plan.length
    start_weights(plan, gathered, held, sems.at[3], DOWN)
    ins = (normed_in, qkv_in, attended_in, middle_in, hidden_in, probs_in, act_in, slope_in)
    scratch = (normed, qkv, attended, middle, hidden, probs, act, slope)
    copies = [
        pltpu.make_async_copy(source, target, in_sems.at[index])
        for index, (source, target) in enumerate(zip(ins, scratch))
    ]
    copies[7].start()
    copies[6].start()
    start_weights(plan, gathered, held, sems.at[2], UP)
    for index in (4, 3, 2):
        copies[index].start()
    start_weights(plan, gathered, held, sems.at[1], OUT)
    for index in (5, 1, 0):
        copies[index].start()
    start_weights(plan, gathered, held, sems.at[0], QKV)
    branch = jnp.where(flag[0] == 0, arr_ref[...], cot_ref[...])
    used = [False, False]

    def emit(index, value):
        slot = index % 2
        if used[slot]:
            pltpu.make_async_copy(stage.at[slot], stage.at[slot], stage_sems.at[slot]).wait()
        used[slot] = True
        stage[slot] = value.astype(BF16).reshape(plan.shards, plan.rows, width)
        for copy in grad_copies(plan, stage.at[slot], grads, stage_sems.at[slot], index):
            copy.start()

    small_ref[7:8, :] = column_sum(branch)
    wait_weights(held, sems.at[3], DOWN)
    copies[7].wait()
    copies[6].wait()
    wait_weights(held, sems.at[2], UP)
    grad_hidden = None
    for part in range(UP[1]):
        columns = slice(part * width, (part + 1) * width)
        grad_act = mm_nt(branch, block_of(plan, held, DOWN[0] + part))
        grad_pre = (slope[:, columns] * grad_act).astype(BF16)
        grad_pre_ref[:, columns] = grad_pre
        small_ref[8 + part : 9 + part, :] = column_sum(grad_pre)
        term = mm_nt(grad_pre, block_of(plan, held, UP[0] + part))
        grad_hidden = term if grad_hidden is None else grad_hidden + term
        emit(DOWN[0] + part, mm_tn(act[:, columns], branch))
    copies[4].wait()
    for part in range(UP[1]):
        columns = slice(part * width, (part + 1) * width)
        emit(UP[0] + part, mm_tn(hidden[...], grad_pre_ref[:, columns]))
    copies[3].wait()
    copies[2].wait()
    xhat, rstd = normalised(middle[...])
    small_ref[5:6, :] = column_sum(grad_hidden * xhat)
    small_ref[6:7, :] = column_sum(grad_hidden)
    grad_middle = branch.astype(F32) + norm_back(grad_hidden, xhat, rstd, vec[5:6, :])
    middle[...] = grad_middle
    attn_grad = grad_middle.astype(BF16)
    small_ref[4:5, :] = column_sum(attn_grad)
    emit(OUT[0], mm_tn(attended[...], attn_grad))
    wait_weights(held, sems.at[1], OUT)
    grad_attended[...] = mm_nt(attn_grad, block_of(plan, held, OUT[0])).astype(BF16)
    copies[5].wait()
    copies[1].wait()
    attention_back(plan, probs, qkv, grad_attended, grad_rows)
    copies[0].wait()
    wait_weights(held, sems.at[0], QKV)
    grad_normed = None
    for part in range(QKV[1]):
        rows = grad_rows[:, part * width : (part + 1) * width]
        term = mm_nt(rows, block_of(plan, held, part))
        grad_normed = term if grad_normed is None else grad_normed + term
        emit(part, mm_tn(normed[...], rows))
        if part != 1:
            small_ref[2 + part // 2 : 3 + part // 2, :] = column_sum(rows)
    xhat, rstd = normalised(xin_ref[...].astype(F32))
    small_ref[0:1, :] = column_sum(grad_normed * xhat)
    small_ref[1:2, :] = column_sum(grad_normed)
    for item in range(plan.items):
        small_ref[12 + item : 13 + item, :] = column_sum(
            grad_normed[item * length : (item + 1) * length]
        )
    dx_ref[...] = middle[...] + norm_back(grad_normed, xhat, rstd, vec[0:1, :])
    for slot in range(2):
        pltpu.make_async_copy(stage.at[slot], stage.at[slot], stage_sems.at[slot]).wait()


SMEM = pl.BlockSpec(memory_space=pltpu.SMEM)
VMEM = pl.BlockSpec(memory_space=pltpu.VMEM)
ANY = pl.BlockSpec(memory_space=pl.ANY)


def kept_shapes(plan):
    tokens, width = plan.tokens, plan.width
    return [
        ((tokens, width), BF16),
        ((tokens, 3 * width), BF16),
        ((tokens, width), BF16),
        ((tokens, width), F32),
        ((tokens, width), BF16),
        ((plan.items * plan.pairs, 2 * plan.length, plan.length), F32),
        ((tokens, 4 * width), BF16),
        ((tokens, 4 * width), F32),
    ]


def params():
    return pltpu.CompilerParams(vmem_limit_bytes=LIMIT)


def run_forward(plan, lengths, x, vec, gathered):
    kept = [pltpu.VMEM(*shape) for shape in kept_shapes(plan)]
    held = pltpu.VMEM((BLOCKS, plan.shards, plan.rows, plan.width), BF16)
    return pl.pallas_call(
        functools.partial(forward_kernel, plan),
        out_shape=jax.ShapeDtypeStruct(x.shape, BF16),
        in_specs=[SMEM, VMEM, VMEM, ANY],
        out_specs=VMEM,
        scratch_shapes=[held] + kept[:5] + [pltpu.SemaphoreType.DMA((4,))],
        compiler_params=params(),
        name="layer_forward",
    )(lengths, x, vec, gathered)


def run_chain(plan, lengths, flag, x, recv, cot, vec, gathered):
    tokens, width = plan.tokens, plan.width
    shapes = kept_shapes(plan)
    held = pltpu.VMEM((BLOCKS, plan.shards, plan.rows, plan.width), BF16)
    rows = jax.ShapeDtypeStruct((tokens, width), BF16)
    return pl.pallas_call(
        functools.partial(chain_kernel, plan),
        out_shape=[rows] * 3 + [jax.ShapeDtypeStruct(*shape) for shape in shapes],
        in_specs=[SMEM, SMEM, VMEM, VMEM, VMEM, VMEM, ANY],
        out_specs=[VMEM] * 3 + [ANY] * len(shapes),
        scratch_shapes=[held]
        + [pltpu.VMEM(*shape) for shape in shapes]
        + [
            pltpu.VMEM((tokens, width), BF16),
            pltpu.VMEM((tokens, 3 * width), BF16),
            pltpu.SemaphoreType.DMA((4,)),
            pltpu.SemaphoreType.DMA((len(shapes),)),
        ],
        compiler_params=params(),
        name="layer_chain",
    )(lengths, flag, x, recv, cot, vec, gathered)


def run_backward(plan, flag, arriving, cot, xin, vec, gathered, kept):
    tokens, width = plan.tokens, plan.width
    shapes = kept_shapes(plan)
    blocks = (BLOCKS, plan.shards, plan.rows, plan.width)
    return pl.pallas_call(
        functools.partial(backward_kernel, plan),
        out_shape=[
            jax.ShapeDtypeStruct((tokens, width), F32),
            jax.ShapeDtypeStruct((16, width), F32),
            jax.ShapeDtypeStruct((plan.shards, BLOCKS, plan.rows, plan.width), BF16),
        ],
        in_specs=[SMEM, VMEM, VMEM, VMEM, VMEM, ANY] + [ANY] * len(shapes),
        out_specs=[VMEM, VMEM, ANY],
        scratch_shapes=[pltpu.VMEM(blocks, BF16)]
        + [pltpu.VMEM(*shape) for shape in shapes]
        + [
            pltpu.VMEM((tokens, width), BF16),
            pltpu.VMEM((tokens, 3 * width), BF16),
            pltpu.VMEM((tokens, 4 * width), BF16),
            pltpu.VMEM((2,) + blocks[1:], BF16),
            pltpu.SemaphoreType.DMA((4,)),
            pltpu.SemaphoreType.DMA((len(shapes),)),
            pltpu.SemaphoreType.DMA((2,)),
        ],
        compiler_params=params(),
        name="layer_backward",
    )(flag, arriving, cot, xin, vec, gathered, *kept)


def shifted(value, axis, steps):
    count = lax.axis_size(axis)
    first, last = (max(0, -steps), min(count, count - steps))
    return lax.ppermute(value, axis, [(source, source + steps) for source in range(first, last)])


def small_gather(value, count):
    value = value[None]
    if count & (count - 1):
        return lax.all_gather(value, "dp", axis=0, tiled=True)
    index = lax.axis_index("dp")
    step = 1
    while step < count:
        other = lax.ppermute(value, "dp", [(i, i ^ step) for i in range(count)])
        value = jnp.where(
            (index & step) == 0,
            jnp.concatenate([value, other], 0),
            jnp.concatenate([other, value], 0),
        )
        step *= 2
    return value


def small_scatter(value, count):
    if count & (count - 1):
        return lax.psum_scatter(value, "dp", scatter_dimension=0, tiled=True)[0]
    index = lax.axis_index("dp")
    step = count // 2
    while step:
        upper = (index & step) != 0
        keep = jnp.where(upper, value[step:], value[:step])
        send = jnp.where(upper, value[:step], value[step:])
        value = keep + lax.ppermute(send, "dp", [(i, i ^ step) for i in range(count)])
        step //= 2
    return value[0]


def cycle(count):
    chips = count // 2
    walk = list(range(0, chips, 2)) + list(range(chips - 1, 0, -2))
    return [2 * chip + core for chip in walk for core in range(2)]


def body(
    block_input, cotangent, lengths, leads,
    norm_gain1, norm_bias1, lead_table, qkv_weight, query_bias, value_bias, out_weight, out_bias,
    norm_gain2, norm_bias2, up_weight, up_bias, down_weight, down_bias,
):
    count = lax.axis_size("dp")
    micro, local, length, width = block_input.shape
    items = micro * local
    rows = width // count
    leads_count = lead_table.shape[2]
    section = lax.axis_index("section")
    flag = section.astype(jnp.int32).reshape(1)
    flat = lambda value: value.reshape(items * length, width)
    x, cot = flat(block_input), flat(cotangent)
    lens, lead = lengths.reshape(items), leads.reshape(items)

    qkv_part = qkv_weight[0].astype(BF16).reshape(rows, 3, width).transpose(1, 0, 2)
    up_part = up_weight[0].astype(BF16).reshape(rows, 4, width).transpose(1, 0, 2)
    packed = jnp.concatenate(
        [
            qkv_part,
            out_weight.astype(BF16),
            up_part,
            down_weight[0].astype(BF16).reshape(4, rows, width),
        ],
        0,
    )
    aligned = rows % 16 == 0
    order = cycle(count) if aligned else list(range(count))
    if aligned:
        gathered = lax.all_gather(packed, "dp", axis=0, tiled=True, axis_index_groups=[order])
        gathered = gathered.reshape(count, BLOCKS, rows, width)
        plan = Plan(count, rows, order, items, length, width)
    else:
        gathered = lax.all_gather(packed, "dp", axis=0).reshape(count, BLOCKS, rows, width)
        head = gathered[:, :8].transpose(1, 0, 2, 3).reshape(8, width, width)
        tail = gathered[:, 8:].reshape(4, width, width)
        gathered = jnp.concatenate([head, tail], 0)[None]
        plan = Plan(1, width, [0], items, length, width)

    small = jnp.concatenate(
        [
            norm_gain1, norm_bias1, query_bias, value_bias, out_bias, norm_gain2, norm_bias2, down_bias,
            up_bias.reshape(4, rows), lead_table[0].T,
        ],
        0,
    ).astype(BF16)
    small = small_gather(small, count)
    wide = small.transpose(1, 0, 2).reshape(12 + leads_count, width).astype(F32)
    vec = jnp.concatenate(
        [wide[:8], small[:, 8:12].reshape(4, width).astype(F32)]
        + [lax.dynamic_slice_in_dim(wide, 12 + lead[item], 1, 0) for item in range(items)]
        + [jnp.zeros((4 - items, width), F32)],
        0,
    )

    first_out = run_forward(plan, lens, x, vec, gathered)
    recv = shifted(first_out, "section", 1)
    output, xin, first_grad, *kept = run_chain(plan, lens, flag, x, recv, cot, vec, gathered)
    arriving = shifted(first_grad, "section", -1)
    input_grad, sums, grads = run_backward(plan, flag, arriving, cot, xin, vec, gathered, kept)

    if aligned:
        grads = lax.psum_scatter(
            grads.reshape(count * BLOCKS, rows, width),
            "dp", scatter_dimension=0, tiled=True, axis_index_groups=[order],
        )
    else:
        grads = grads.reshape(BLOCKS, width, width)
        head = grads[:8].reshape(8, count, rows, width).transpose(1, 0, 2, 3)
        tail = grads[8:].reshape(count, 4, rows, width)
        grads = lax.psum_scatter(
            jnp.concatenate([head, tail], 1), "dp", scatter_dimension=0, tiled=False
        )
    hot = (jnp.arange(leads_count)[:, None] == lead[None, :]).astype(F32)
    table = sum(hot[:, item : item + 1] * sums[12 + item : 13 + item] for item in range(items))
    spread = jnp.concatenate(
        [
            sums[:8].reshape(8, count, rows).transpose(1, 0, 2),
            sums[8:12].reshape(count, 4, rows),
            table.reshape(leads_count, count, rows).transpose(1, 0, 2),
        ],
        1,
    )
    spread = small_scatter(spread, count)

    grads = grads.astype(F32)
    vector = lambda index: spread[index : index + 1]
    across = lambda value: value.transpose(1, 0, 2).reshape(1, rows, -1)
    shape = (1, micro, local, length, width)
    return (
        output.reshape(shape),
        input_grad.reshape(shape),
        vector(0),
        vector(1),
        spread[12:].T[None],
        across(grads[:3]),
        vector(2),
        vector(3),
        grads[3:4],
        vector(4),
        vector(5),
        vector(6),
        across(grads[4:8]),
        spread[8:12].reshape(1, 4 * rows),
        grads[8:].reshape(1, 4 * rows, width),
        vector(7),
    )


def solution(mesh):
    weights = (
        P("section", "dp"),
        P("section", "dp"),
        P("section", "dp", None),
        P("section", "dp", None),
        P("section", "dp"),
        P("section", "dp"),
        P("section", "dp", None),
        P("section", "dp"),
        P("section", "dp"),
        P("section", "dp"),
        P("section", "dp", None),
        P("section", "dp"),
        P("section", "dp", None),
        P("section", "dp"),
    )
    rows = P(None, "dp", None, None)
    layers = P("section", None, "dp", None, None)
    return jax.shard_map(
        body,
        mesh=mesh,
        in_specs=(rows, rows, P(None, "dp"), P(None, "dp")) + weights,
        out_specs=(layers, layers) + weights,
        check_vma=False,
    )
```

time: 791 us -> 267 us (0.34)
  waiting for transfers between devices: 442 us -> 156 us
  blocking collectives: 141 us -> 0 us
  matrix products: 110 us -> 0 us
  Pallas kernels: 0 us -> 56.3 us
  other arithmetic: 23.8 us -> 3.89 us
  local copies, waits for them, and re-layouts: 30.2 us -> 13.1 us
    reduce_scatter x4 -> x1, waiting for transfers between devices: 338 us -> 56 us  [body(): lax.psum_scatter(grads.reshape(count * BLOCKS, rows, width), 'dp', scatte...]
    unnamed x2 -> x0, blocking collectives: 122 us -> none
    dot_general x57 -> x0, matrix products: 110 us -> none  [the longest x3 15.2 us: backward_layer(): jnp.einsum('td,fd->tf', branch_grad, down_weight, preferred_element_type=...]
    pallas_call x0 -> x3, Pallas kernels: none -> 56.3 us  [the longest x1 26.7 us: run_backward(): pl.pallas_call(functools.partial(backward_kernel, plan), out_shape=[jax.S...]
    all_gather x4 -> x1, waiting for transfers between devices: 92.4 us -> 60.7 us  [body(): lax.all_gather(packed, 'dp', axis=0, tiled=True, axis_index_groups=[order])]
    ppermute x0 -> x8, waiting for transfers between devices: none -> 23.6 us  [the longest x4 17.2 us: small_scatter(): lax.ppermute(send, 'dp', [(i, i ^ step) for i in range(count)])]
    all_gather x1 -> x0, blocking collectives: 18.9 us -> none  [fetch_forward(): lax.all_gather(parts[2], 'dp', axis=0, tiled=True)]
    unnamed x432 -> x36, local copies, waits for them, and re-layouts: 15.9 us -> 2.19 us
  transfers between devices with their start and end apart: 13 -> 12, of which waited for: 10 -> 12; matrix products, arithmetic and copies ran while one was open for 9% -> 2% of each run, Pallas kernels for 0% -> 0%
where the time goes in v1:
time: 267 us; the launch traced here: 265 us
  waiting for transfers between devices  156 us (58%)
  Pallas kernels  56.3 us (21%)
  starting transfers between devices  18.6 us (7%)
  between operations  17.3 us (6%)
  local copies, waits for them, and re-layouts  13.1 us (5%)
  other arithmetic  3.89 us (1%)
    all_gather x1, waiting for transfers between devices, body(): lax.all_gather(packed, 'dp', axis=0, tiled=True, axis_index_groups=[order])  60.7 us
    reduce_scatter x1, waiting for transfers between devices, body(): lax.psum_scatter(grads.reshape(count * BLOCKS, rows, width), 'dp', scatte...  56 us
    pallas_call x1, Pallas kernels, run_backward(): pl.pallas_call(functools.partial(backward_kernel, plan), out_shape=[jax.S...  26.7 us
    pallas_call x1, Pallas kernels, run_chain(): pl.pallas_call(functools.partial(chain_kernel, plan), out_shape=[rows] *...  19.6 us
    ppermute x4, waiting for transfers between devices, small_scatter(): lax.ppermute(send, 'dp', [(i, i ^ step) for i in range(count)])  17.2 us
    ppermute x2, waiting for transfers between devices, shifted(): lax.ppermute(value, axis, [(source, source + steps) for source in range(f...  15.8 us
    pallas_call x1, Pallas kernels, run_forward(): pl.pallas_call(functools.partial(forward_kernel, plan), out_shape=jax.Sha...  10 us
    ppermute x4, starting transfers between devices, small_gather(): other = lax.ppermute(value, 'dp', [(i, i ^ step) for i in range(count)])  8.67 us
  transfers between devices with their start and end apart: 12, of which 12 were waited for; matrix products, arithmetic and copies ran while one was open for 2% of the time, Pallas kernels for 0%

profile of v1, /device:TPU:0, one launch (start us, length us, event | category | flops | bytes accessed | tf_op | source)
XLA Modules:
  0.0 265.3 jit_solution(12100613155798733166)
XLA Ops:
  7.3 1.2 convert_element_type.63
  8.4 0.2 copy.71
  8.6 0.2 convert_element_type.62
  8.9 0.1 copy.70
  9.2 0.8 pad_maximum_fusion
  10.1 1.2 copy.72
  11.6 0.2 concatenate.74
  11.8 0.5 collective-permute-start
  12.3 0.8 collective-permute-done
  13.2 2.9 %collective-permute-start.1 = (bf16[2,36,48]{2,1,0:T(8,128)(2,1)S(1)}, bf16[2,36,48]{2,1,0:T(8,128)(2,1)S(1)}, u32[]{:S(2)}, u32[]{:S(2)}) collective-permute-start(bf16[2,36,48]{2,1,0:T(8,128)(2,1)S(1)} %maximum_select_fusion.3), channel_id=1, source_target_pairs={{0,2},{1,3},{2,0},{3,1},{4,6},{5,7},{6,4},{7,5},{8,10},{9,11},{10,... | collective-permute-start | bytes 20744 | tf_op jit(solution)/shard_map/ppermute | solution.py:459
  16.1 1.8 collective-permute-done.1
  17.9 2.1 collective-permute-start.2
  20.0 2.0 collective-permute-done.2
  22.1 3.1 %collective-permute-start.3 = (bf16[8,36,48]{2,1,0:T(8,128)(2,1)S(1)}, bf16[8,36,48]{2,1,0:T(8,128)(2,1)S(1)}, u32[]{:S(2)}, u32[]{:S(2)}) collective-permute-start(bf16[8,36,48]{2,1,0:T(8,128)(2,1)S(1)} %maximum_select_fusion.1), channel_id=1, source_target_pairs={{0,8},{1,9},{2,10},{3,11},{4,12},{5,13},{6,14},{7,15},{8,0},{9,1},... | collective-permute-start | bytes 82952 | tf_op jit(solution)/shard_map/ppermute | solution.py:459
  25.1 0.6 fusion
  28.3 1.8 collective-permute-done.3
  30.4 0.1 reshape.294
  30.5 0.2 convert_element_type.57
  30.7 1.2 concatenate.83.vec
  31.9 60.7 %all-gather.2.cloned.1.call-done = bf16[192,48,768]{2,1,0:T(8,128)(2,1)} async-done(((bf16[12,48,768]{2,1,0:T(8,128)(2,1)}), bf16[192,48,768]{2,1,0:T(8,128)(2,1)}) %all-gather.2.cloned.1.call-update) | async-done | bytes 14155792 | tf_op jit(solution)/shard_map/all_gather | solution.py:519
  92.7 10.0 %layer_forward.1 = bf16[192,768]{1,0:T(8,128)(2,1)} custom-call(s32[2]{0:T(128)} %bitcast.91, bf16[192,768]{1,0:T(8,128)(2,1)} %bitcast.85, f32[16,768]{1,0:T(8,128)} %concatenate.83.vec, bf16[16,12,48,768]{3,2,1,0:T(8,128)(2,1)} %bitcast.78), custom_call_target="tpu_custom_call" | custom-call | tf_op jit(solution)/shard_map/layer_forward/pallas_call | solution.py:383
  102.7 3.6 %collective-permute-start.4 = (bf16[192,768]{1,0:T(8,128)(2,1)}, bf16[192,768]{1,0:T(8,128)(2,1)S(1)}, u32[]{:S(2)}, u32[]{:S(2)}) collective-permute-start(bf16[192,768]{1,0:T(8,128)(2,1)} %layer_forward.1), channel_id=1, source_target_pairs={{0,16},{1,17},{2,18},{3,19},{4,20},{5,21},{6,22},{7,23},{8,24},{9,... | collective-permute-start | bytes 884744 | tf_op jit(solution)/shard_map/ppermute | solution.py:449
  106.3 6.8 %collective-permute-done.4.recv_ref = bf16[192,768]{1,0:T(8,128)(2,1)S(1)} collective-permute-done((bf16[192,768]{1,0:T(8,128)(2,1)}, bf16[192,768]{1,0:T(8,128)(2,1)S(1)}, u32[]{:S(2)}, u32[]{:S(2)}) %collective-permute-start.4) | collective-permute-done | bytes 294944 | tf_op jit(solution)/shard_map/ppermute | solution.py:449
  113.1 0.7 copy-done.3
  113.8 19.6 %layer_chain.1 = (bf16[192,768]{1,0:T(8,128)(2,1)}, bf16[192,768]{1,0:T(8,128)(2,1)}, bf16[192,768]{1,0:T(8,128)(2,1)}, bf16[192,768]{1,0:T(8,128)(2,1)}, bf16[1...) custom-call(s32[2]{0:T(128)} %bitcast.92, ...), custom_call_target="tpu_custom_call" | custom-call | tf_op jit(solution)/shard_map/layer_chain/pallas_call | solution.py:399
  133.4 1.5 collective-permute-start.5
  134.9 9.0 %collective-permute-done.5.arr_ref = bf16[192,768]{1,0:T(8,128)(2,1)S(1)} collective-permute-done((bf16[192,768]{1,0:T(8,128)(2,1)}, bf16[192,768]{1,0:T(8,128)(2,1)S(1)}, u32[]{:S(2)}, u32[]{:S(2)}) %collective-permute-start.5) | collective-permute-done | bytes 294944 | tf_op jit(solution)/shard_map/ppermute | solution.py:449
  143.9 0.7 copy-done.4
  144.6 26.7 %layer_backward.1 = (f32[192,768]{1,0:T(8,128)}, f32[16,768]{1,0:T(8,128)}, bf16[16,12,48,768]{3,2,1,0:T(8,128)(2,1)}) custom-call(s32[1]{0:T(128)} %bitcast.1.flag, bf16[192,768]{1,0:T(8,128)(2,1)} %copy-done.4, bf16[192,768]{1,0:T(8,128)(2,1)} %bitcast.88, bf16[192,768]{1,0:T(8,128)(2,1)} %get-tuple-element.32.xin_ref, f32[16,768]{1,0:T(8,128)} %concatenate.83.vec, ...), custom_call_target="tpu_custom_call" | custom-call | tf_op jit(solution)/shard_map/layer_backward/pallas_call | solution.py:421
  171.4 0.7 copy-done.6
  172.3 0.1 reshape.288
  172.7 3.1 %collective-permute-start.6 = (f32[8,36,48]{2,1,0:T(8,128)S(1)}, f32[8,36,48]{2,1,0:T(8,128)S(1)}, u32[]{:S(2)}, u32[]{:S(2)}) collective-permute-start(f32[8,36,48]{2,1,0:T(8,128)S(1)} %slice_select_fusion), channel_id=1, source_target_pairs={{0,8},{1,9},{2,10},{3,11},{4,12},{5,13},{6,14},{7,15},{8,0},{9,1},... | collective-permute-start | bytes 165896 | tf_op jit(solution)/shard_map/ppermute | solution.py:478
  175.7 7.6 %collective-permute-done.6 = f32[8,36,48]{2,1,0:T(8,128)S(1)} collective-permute-done((f32[8,36,48]{2,1,0:T(8,128)S(1)}, f32[8,36,48]{2,1,0:T(8,128)S(1)}, u32[]{:S(2)}, u32[]{:S(2)}) %collective-permute-start.6) | collective-permute-done | bytes 55328 | tf_op jit(solution)/shard_map/ppermute | solution.py:478
  183.4 5.4 %collective-permute-done.7 = f32[4,36,48]{2,1,0:T(8,128)S(1)} collective-permute-done((f32[4,36,48]{2,1,0:T(8,128)S(1)}, f32[4,36,48]{2,1,0:T(8,128)S(1)}, u32[]{:S(2)}, u32[]{:S(2)}) %collective-permute-start.7) | collective-permute-done | bytes 27680 | tf_op jit(solution)/shard_map/ppermute | solution.py:478
  188.9 1.6 collective-permute-start.8
  190.4 3.0 %collective-permute-done.8 = f32[2,36,48]{2,1,0:T(8,128)S(1)} collective-permute-done((f32[2,36,48]{2,1,0:T(8,128)S(1)}, f32[2,36,48]{2,1,0:T(8,128)S(1)}, u32[]{:S(2)}, u32[]{:S(2)}) %collective-permute-start.8) | collective-permute-done | bytes 13856 | tf_op jit(solution)/shard_map/ppermute | solution.py:478
  193.6 1.2 collective-permute-done.9
  194.8 0.6 reshape.292
  195.4 0.5 slice_bitcast_fusion.3
  196.0 0.6 slice_bitcast_fusion.2
  196.6 56.0 %reduce-scatter.2.cloned.1.call-done = bf16[12,48,768]{2,1,0:T(8,128)(2,1)} async-done(((bf16[192,48,768]{2,1,0:T(8,128)(2,1)}), bf16[12,48,768]{2,1,0:T(8,128)(2,1)}) %reduce-scatter.2.cloned.1.call-update) | async-done | bytes 884752 | tf_op jit(solution)/shard_map/reduce_scatter | solution.py:552
  252.6 1.3 convert_element_type.66
  254.0 0.3 copy.74
  254.3 1.1 reshape.290
  255.4 0.4 copy.75
  255.8 1.1 reshape.291
  256.9 0.7 slice.195
  257.6 0.9 slice.201
  (83 shorter events, 1.6 us)
Async XLA Ops:
  7.2 1.4 copy-start.1
  7.2 1.7 copy-start.5
  7.2 1.8 copy-start.2
  7.2 85.5 %all-gather.2.cloned.1.call-start = ((), (), s32[]{:S(2)}) async-start(), calls=%async_computation.1 | async-start | bytes 15040512 | tf_op jit(solution)/shard_map/all_gather | solution.py:519
  10.0 1.4 copy-start.17
  10.0 1.5 copy-start.9
  10.0 1.5 copy-start.10
  10.0 1.5 copy-start.11
  10.1 1.5 copy-start.12
  10.1 1.5 copy-start.13
  10.1 1.5 copy-start.14
  10.1 1.5 copy-start.15
  10.1 1.5 copy-start.16
  10.1 1.5 copy-start.7
  10.1 15.0 %copy-start.8 = (s32[2,1]{0,1:T(1,128)S(1)}, s32[2,1]{0,1:T(1,128)}, u32[]{:S(2)}) copy-start(s32[2,1]{0,1:T(1,128)} %param.21) | copy-start | bytes 28
  11.3 241.3 %reduce-scatter.2.cloned.1.call-start = ((), (), s32[]{:S(2)}) async-start(), calls=%async_computation.2 | async-start | bytes 15040512 | tf_op jit(solution)/shard_map/reduce_scatter | solution.py:552
  11.8 1.3 collective-permute-start
  13.2 4.7 %collective-permute-start.1 = (bf16[2,36,48]{2,1,0:T(8,128)(2,1)S(1)}, bf16[2,36,48]{2,1,0:T(8,128)(2,1)S(1)}, u32[]{:S(2)}, u32[]{:S(2)}) collective-permute-start(bf16[2,36,48]{2,1,0:T(8,128)(2,1)S(1)} %maximum_select_fusion.3), channel_id=1, source_target_pairs={{0,2},{1,3},{2,0},{3,1},{4,6},{5,7},{6,4},{7,5},{8,10},{9,11},{10,... | collective-permute-start | bytes 20744 | tf_op jit(solution)/shard_map/ppermute | solution.py:459
  17.9 4.1 %collective-permute-start.2 = (bf16[4,36,48]{2,1,0:T(8,128)(2,1)S(1)}, bf16[4,36,48]{2,1,0:T(8,128)(2,1)S(1)}, u32[]{:S(2)}, u32[]{:S(2)}) collective-permute-start(bf16[4,36,48]{2,1,0:T(8,128)(2,1)S(1)} %maximum_select_fusion.2), channel_id=1, source_target_pairs={{0,4},{1,5},{2,6},{3,7},{4,0},{5,1},{6,2},{7,3},{8,12},{9,13},{10,... | collective-permute-start | bytes 41480 | tf_op jit(solution)/shard_map/ppermute | solution.py:459
  22.1 8.1 %collective-permute-start.3 = (bf16[8,36,48]{2,1,0:T(8,128)(2,1)S(1)}, bf16[8,36,48]{2,1,0:T(8,128)(2,1)S(1)}, u32[]{:S(2)}, u32[]{:S(2)}) collective-permute-start(bf16[8,36,48]{2,1,0:T(8,128)(2,1)S(1)} %maximum_select_fusion.1), channel_id=1, source_target_pairs={{0,8},{1,9},{2,10},{3,11},{4,12},{5,13},{6,14},{7,15},{8,0},{9,1},... | collective-permute-start | bytes 82952 | tf_op jit(solution)/shard_map/ppermute | solution.py:459
  102.7 10.4 %collective-permute-start.4 = (bf16[192,768]{1,0:T(8,128)(2,1)}, bf16[192,768]{1,0:T(8,128)(2,1)S(1)}, u32[]{:S(2)}, u32[]{:S(2)}) collective-permute-start(bf16[192,768]{1,0:T(8,128)(2,1)} %layer_forward.1), channel_id=1, source_target_pairs={{0,16},{1,17},{2,18},{3,19},{4,20},{5,21},{6,22},{7,23},{8,24},{9,... | collective-permute-start | bytes 884744 | tf_op jit(solution)/shard_map/ppermute | solution.py:449
  113.1 0.7 copy-start.3
  133.4 10.5 %collective-permute-start.5 = (bf16[192,768]{1,0:T(8,128)(2,1)}, bf16[192,768]{1,0:T(8,128)(2,1)S(1)}, u32[]{:S(2)}, u32[]{:S(2)}) collective-permute-start(bf16[192,768]{1,0:T(8,128)(2,1)} %get-tuple-element.31), channel_id=1, source_target_pairs={{16,0},{17,1},{18,2},{19,3},{20,4},{21,5},{22,6},{23,7},{24,8},{25... | collective-permute-start | bytes 884744 | tf_op jit(solution)/shard_map/ppermute | solution.py:449
  143.9 0.7 copy-start.4
  171.3 0.8 copy-start.6
  172.7 10.6 %collective-permute-start.6 = (f32[8,36,48]{2,1,0:T(8,128)S(1)}, f32[8,36,48]{2,1,0:T(8,128)S(1)}, u32[]{:S(2)}, u32[]{:S(2)}) collective-permute-start(f32[8,36,48]{2,1,0:T(8,128)S(1)} %slice_select_fusion), channel_id=1, source_target_pairs={{0,8},{1,9},{2,10},{3,11},{4,12},{5,13},{6,14},{7,15},{8,0},{9,1},... | collective-permute-start | bytes 165896 | tf_op jit(solution)/shard_map/ppermute | solution.py:478
  183.4 5.5 %collective-permute-start.7 = (f32[4,36,48]{2,1,0:T(8,128)S(1)}, f32[4,36,48]{2,1,0:T(8,128)S(1)}, u32[]{:S(2)}, u32[]{:S(2)}) collective-permute-start(f32[4,36,48]{2,1,0:T(8,128)S(1)} %slice_select_fusion.1), channel_id=1, source_target_pairs={{0,4},{1,5},{2,6},{3,7},{4,0},{5,1},{6,2},{7,3},{8,12},{9,13},{10,... | collective-permute-start | bytes 82952 | tf_op jit(solution)/shard_map/ppermute | solution.py:478
  188.9 4.6 %collective-permute-start.8 = (f32[2,36,48]{2,1,0:T(8,128)S(1)}, f32[2,36,48]{2,1,0:T(8,128)S(1)}, u32[]{:S(2)}, u32[]{:S(2)}) collective-permute-start(f32[2,36,48]{2,1,0:T(8,128)S(1)} %slice_select_fusion.2), channel_id=1, source_target_pairs={{0,2},{1,3},{2,0},{3,1},{4,6},{5,7},{6,4},{7,5},{8,10},{9,11},{10,... | collective-permute-start | bytes 41480 | tf_op jit(solution)/shard_map/ppermute | solution.py:478
  193.5 1.3 collective-permute-start.9
  254.3 2.6 copy-start
Sparse Core Ops, SparseCore 0:
  11.5 81.1 all-gather.1
  171.4 81.1 reduce-scatter.1

commit v2 on v1

v2 whole, which is shorter than its diff:
```python
import functools

import jax
import jax.numpy as jnp
from jax import lax
from jax.experimental import pallas as pl
from jax.experimental.pallas import tpu as pltpu
from jax.sharding import PartitionSpec as P

HEAD = 64
PAIR = 2 * HEAD
EPS = 1e-06
SCALE_FACTOR = 0.125
GELU_A = 0.7978845608028654
GELU_B = 0.044715
F32 = jnp.float32
BF16 = jnp.bfloat16
OUT = 3
FIRST = 4
SECOND = 8
QUART = 4


def mm(left, right):
    return jnp.dot(left, right, preferred_element_type=F32)


def mm_nt(left, right):
    return lax.dot_general(left, right, (((1,), (1,)), ((), ())), preferred_element_type=F32)


def mm_tn(left, right):
    return lax.dot_general(left, right, (((0,), (0,)), ((), ())), preferred_element_type=F32)


def normalised(values):
    mean = jnp.mean(values, -1, keepdims=True)
    centred = values - mean
    variance = jnp.mean(centred * centred, -1, keepdims=True)
    rstd = lax.rsqrt(variance + EPS)
    return centred * rstd, rstd


def norm_back(grad, xhat, rstd, gain):
    scaled = grad * gain
    first = jnp.mean(scaled, -1, keepdims=True)
    second = jnp.mean(scaled * xhat, -1, keepdims=True)
    return rstd * (scaled - first - xhat * second)


def gelu_both(values):
    square = values * values
    slope = GELU_A * (1.0 + 3.0 * GELU_B * square)
    bend = jnp.tanh(GELU_A * values * (1.0 + GELU_B * square))
    half = 0.5 * (1.0 + bend)
    return values * half, half + 0.5 * values * (1.0 - bend * bend) * slope


def split_pair(rows):
    lane = lax.broadcasted_iota(jnp.int32, rows.shape, 1)
    zero = jnp.zeros_like(rows)
    return jnp.concatenate(
        [jnp.where(lane < HEAD, rows, zero), jnp.where(lane < HEAD, zero, rows)], 0
    )


def join_pair(stacked):
    count = stacked.shape[0] // 2
    lane = lax.broadcasted_iota(jnp.int32, (count, PAIR), 1)
    return jnp.where(lane < HEAD, stacked[:count], stacked[count:])


class Plan:
    def __init__(self, shards, rows, order, items, length, width):
        self.shards, self.rows, self.order = shards, rows, order
        self.items, self.length, self.width = items, length, width
        self.tokens = items * length
        self.pairs = width // PAIR


def first_copies(pieces, devs, held, sem, blocks):
    return [
        pltpu.make_async_copy(piece.at[blocks], held.at[blocks, devs[slot]], sem)
        for slot, piece in enumerate(pieces)
    ]


def down_rows(plan, device):
    whole = plan.shards % QUART == 0
    parts = [(0, QUART)] if whole else [(block, 1) for block in range(QUART)]
    return [
        (first, count, *divmod(QUART * device + first, plan.shards)) for first, count in parts
    ]


def up_copies(plan, gathered, held, sem, part):
    return [
        pltpu.make_async_copy(gathered.at[place, part], held.at[part, device], sem)
        for place, device in enumerate(plan.order)
    ]


def down_copies(plan, gathered, held, sem, part):
    return [
        pltpu.make_async_copy(
            gathered.at[place, pl.ds(QUART + first, count)],
            held.at[QUART + block, pl.ds(row, count)],
            sem,
        )
        for place, device in enumerate(plan.order)
        for first, count, block, row in down_rows(plan, device)
        if block == part
    ]


def start_all(copies):
    for copy in copies:
        copy.start()


def wait_bytes(part, sem):
    pltpu.make_async_copy(part, part, sem).wait()


def block_of(plan, held, index):
    return held[index].reshape(plan.width, plan.width)


def columns_of(plan, index):
    return slice(index * plan.width, (index + 1) * plan.width)


def attention_forward(plan, lengths, qkv_ref, attended_ref, probs_ref):
    width, length = plan.width, plan.length
    key_index = lax.broadcasted_iota(jnp.int32, (2 * length, length), 1)
    for item in range(plan.items):
        rows = slice(item * length, (item + 1) * length)
        valid = key_index < lengths[item]
        for pair in range(plan.pairs):
            at = pair * PAIR
            query = split_pair(qkv_ref[rows, at : at + PAIR])
            key = qkv_ref[rows, width + at : width + at + PAIR]
            value = qkv_ref[rows, 2 * width + at : 2 * width + at + PAIR]
            logits = jnp.where(valid, mm_nt(query, key) * SCALE_FACTOR, -1000000000.0)
            expo = jnp.exp(logits - jnp.max(logits, -1, keepdims=True))
            probs = expo / jnp.sum(expo, -1, keepdims=True)
            if probs_ref is not None:
                probs_ref[item * plan.pairs + pair] = probs
            attended_ref[rows, at : at + PAIR] = join_pair(mm(probs.astype(BF16), value)).astype(
                BF16
            )


def first_half(plan, inputs, lengths, vec, held, wait, normed_ref, qkv_ref, attended_ref, probs_ref, hidden_ref):
    width, length = plan.width, plan.length
    values = inputs.astype(F32)
    xhat, _ = normalised(values)
    base = xhat * vec[0:1, :] + vec[1:2, :]
    for item in range(plan.items):
        rows = slice(item * length, (item + 1) * length)
        normed_ref[rows, :] = (base[rows] + vec[12 + item : 13 + item, :]).astype(BF16)
    wait(0)
    for part, bias in enumerate((2, None, 3)):
        joined = mm(normed_ref[...], block_of(plan, held, part))
        if bias is not None:
            joined = joined + vec[bias : bias + 1, :]
        qkv_ref[:, columns_of(plan, part)] = joined.astype(BF16)
    attention_forward(plan, lengths, qkv_ref, attended_ref, probs_ref)
    wait(1)
    middle = values + (mm(attended_ref[...], block_of(plan, held, OUT)) + vec[4:5, :])
    xhat, _ = normalised(middle)
    hidden_ref[...] = (xhat * vec[5:6, :] + vec[6:7, :]).astype(BF16)
    return middle


def second_half(plan, hidden_ref, vec, held, act_ref=None, slope_ref=None, wait=None):
    total = None
    for part in range(QUART):
        if wait is not None:
            wait(part)
        pre_act = mm(hidden_ref[...], block_of(plan, held, part)) + vec[8 + part : 9 + part, :]
        act, slope = gelu_both(pre_act)
        act = act.astype(BF16)
        if act_ref is not None:
            act_ref[:, columns_of(plan, part)] = act
            slope_ref[:, columns_of(plan, part)] = slope
        if wait is not None:
            wait(QUART + part)
        term = mm(act, block_of(plan, held, QUART + part))
        total = term if total is None else total + term
    return total + vec[7:8, :]


def attention_back(plan, probs_ref, qkv_ref, grad_attended_ref, rows_ref):
    width, length = plan.width, plan.length
    for item in range(plan.items):
        rows = slice(item * length, (item + 1) * length)
        for pair in range(plan.pairs):
            at = pair * PAIR
            query = split_pair(qkv_ref[rows, at : at + PAIR])
            key = qkv_ref[rows, width + at : width + at + PAIR]
            value = qkv_ref[rows, 2 * width + at : 2 * width + at + PAIR]
            grad = split_pair(grad_attended_ref[rows, at : at + PAIR])
            probs = probs_ref[item * plan.pairs + pair]
            grad_probs = mm_nt(grad, value)
            centre = jnp.sum(grad_probs * probs, -1, keepdims=True)
            grad_logits = (probs * (grad_probs - centre)).astype(BF16)
            grad_query = join_pair(mm(grad_logits, key)) * SCALE_FACTOR
            grad_key = mm_tn(grad_logits, query) * SCALE_FACTOR
            grad_value = mm_tn(probs.astype(BF16), grad)
            rows_ref[rows, at : at + PAIR] = grad_query.astype(BF16)
            rows_ref[rows, width + at : width + at + PAIR] = grad_key.astype(BF16)
            rows_ref[rows, 2 * width + at : 2 * width + at + PAIR] = grad_value.astype(BF16)


def column_sum(values):
    return jnp.sum(values.astype(F32), 0, keepdims=True)


def load_first(held, pieces, devs, sems):
    start_all(first_copies(pieces, devs, held, sems.at[0], pl.ds(0, OUT)))
    start_all(first_copies(pieces, devs, held, sems.at[1], pl.ds(OUT, 1)))

    def wait(group):
        blocks = pl.ds(OUT, 1) if group else pl.ds(0, OUT)
        wait_bytes(held.at[blocks], sems.at[group])

    return wait


def attend_kernel(plan, lengths, flag, devs, x_ref, vec, *refs):
    pieces, (middle_ref, hidden_ref, held, normed, qkv, attended, sems) = refs[:-7], refs[-7:]
    wait = load_first(held, pieces, devs, sems)
    middle_ref[...] = first_half(
        plan, x_ref[...], lengths, vec, held, wait, normed, qkv, attended, None, hidden_ref
    )


def mlp_kernel(plan, middle_ref, hidden_ref, vec, gathered, y_ref, held, sems):
    for part in range(QUART):
        start_all(up_copies(plan, gathered, held, sems.at[part], part))
        start_all(down_copies(plan, gathered, held, sems.at[QUART + part], part))

    def wait(block):
        wait_bytes(held.at[block], sems.at[block])

    total = second_half(plan, hidden_ref, vec, held, wait=wait)
    y_ref[...] = (middle_ref[...] + total).astype(BF16)


def load_kernel(plan, devs, after, gathered, *refs):
    pieces, (held1, held2, sems) = refs[:-3], refs[-3:]
    copies = first_copies(pieces, devs, held1, sems.at[0], pl.ds(0, FIRST))
    for part in range(QUART):
        copies += up_copies(plan, gathered, held2, sems.at[1], part)
        copies += down_copies(plan, gathered, held2, sems.at[1], part)
    start_all(copies)
    wait_bytes(held1, sems.at[0])
    wait_bytes(held2, sems.at[1])


def chain_kernel(
    plan, lengths, flag, x_ref, recv_ref, cot_ref, vec, held1, held2,
    y_ref, xin_ref, dx_ref, normed, qkv, attended, middle, hidden, probs, act, slope, grad_attended, grad_rows,
):
    xin_ref[...] = jnp.where(flag[0] == 0, x_ref[...], recv_ref[...])
    middle[...] = first_half(
        plan, xin_ref[...], lengths, vec, held1, lambda group: None, normed, qkv, attended, probs, hidden
    )
    y_ref[...] = (middle[...] + second_half(plan, hidden, vec, held2, act, slope)).astype(BF16)
    branch = cot_ref[...]
    grad_hidden = None
    for part in range(QUART):
        grad_act = mm_nt(branch, block_of(plan, held2, QUART + part))
        grad_pre = (slope[:, columns_of(plan, part)] * grad_act).astype(BF16)
        term = mm_nt(grad_pre, block_of(plan, held2, part))
        grad_hidden = term if grad_hidden is None else grad_hidden + term
    xhat, rstd = normalised(middle[...])
    grad_middle = branch.astype(F32) + norm_back(grad_hidden, xhat, rstd, vec[5:6, :])
    grad_attended[...] = mm_nt(grad_middle.astype(BF16), block_of(plan, held1, OUT)).astype(BF16)
    attention_back(plan, probs, qkv, grad_attended, grad_rows)
    grad_normed = None
    for part in range(OUT):
        term = mm_nt(grad_rows[:, columns_of(plan, part)], block_of(plan, held1, part))
        grad_normed = term if grad_normed is None else grad_normed + term
    xhat, rstd = normalised(xin_ref[...].astype(F32))
    dx_ref[...] = (grad_middle + norm_back(grad_normed, xhat, rstd, vec[0:1, :])).astype(BF16)


class Stage:
    def __init__(self, plan, stage, sems):
        self.plan, self.stage, self.sems, self.sent = plan, stage, sems, 0

    def put(self, value, copies_of):
        slot = self.sent % 2
        if self.sent >= 2:
            wait_bytes(self.stage.at[slot], self.sems.at[slot])
        self.sent += 1
        plan = self.plan
        self.stage[slot] = value.astype(BF16).reshape(plan.shards, plan.rows, plan.width)
        start_all(copies_of(self.stage.at[slot], self.sems.at[slot]))

    def drain(self):
        for slot in range(min(2, self.sent)):
            wait_bytes(self.stage.at[slot], self.sems.at[slot])


def backward_kernel(
    plan, flag, arr_ref, cot_ref, xin_ref, vec, held1, held2,
    normed, qkv, attended, middle_ref, hidden, probs, act, slope,
    dx_ref, small_ref, grads, grad_pre_ref, grad_middle_ref, grad_attended, grad_rows, stage, stage_sems,
):
    length = plan.length
    branch = jnp.where(flag[0] == 0, arr_ref[...], cot_ref[...])
    small_ref[...] = jnp.zeros_like(small_ref)
    small_ref[7:8, :] = column_sum(branch)
    out = Stage(plan, stage, stage_sems)

    def copies_of(block):
        def copies(source, sem):
            return [
                pltpu.make_async_copy(source.at[device], grads.at[place, block], sem)
                for place, device in enumerate(plan.order)
            ]

        return copies

    def copies_of_down(part):
        def copies(source, sem):
            return [
                pltpu.make_async_copy(
                    source.at[pl.ds(row, count)],
                    grads.at[place, pl.ds(FIRST + QUART + first, count)],
                    sem,
                )
                for place, device in enumerate(plan.order)
                for first, count, block, row in down_rows(plan, device)
                if block == part
            ]

        return copies

    grad_hidden = None
    for part in range(QUART):
        columns = columns_of(plan, part)
        grad_act = mm_nt(branch, block_of(plan, held2, QUART + part))
        grad_pre = (slope[:, columns] * grad_act).astype(BF16)
        grad_pre_ref[:, columns] = grad_pre
        small_ref[8 + part : 9 + part, :] = column_sum(grad_pre)
        term = mm_nt(grad_pre, block_of(plan, held2, part))
        grad_hidden = term if grad_hidden is None else grad_hidden + term
        out.put(mm_tn(act[:, columns], branch), copies_of_down(part))
    for part in range(QUART):
        out.put(
            mm_tn(hidden[...], grad_pre_ref[:, columns_of(plan, part)]), copies_of(FIRST + part)
        )
    xhat, rstd = normalised(middle_ref[...])
    small_ref[5:6, :] = column_sum(grad_hidden * xhat)
    small_ref[6:7, :] = column_sum(grad_hidden)
    grad_middle = branch.astype(F32) + norm_back(grad_hidden, xhat, rstd, vec[5:6, :])
    grad_middle_ref[...] = grad_middle
    attn_grad = grad_middle.astype(BF16)
    small_ref[4:5, :] = column_sum(attn_grad)
    grad_attended[...] = mm_nt(attn_grad, block_of(plan, held1, OUT)).astype(BF16)
    out.put(mm_tn(attended[...], attn_grad), copies_of(OUT))
    attention_back(plan, probs, qkv, grad_attended, grad_rows)
    grad_normed = None
    for part in range(OUT):
        rows = grad_rows[:, columns_of(plan, part)]
        out.put(mm_tn(normed[...], rows), copies_of(part))
        term = mm_nt(rows, block_of(plan, held1, part))
        grad_normed = term if grad_normed is None else grad_normed + term
        if part != 1:
            small_ref[2 + part // 2 : 3 + part // 2, :] = column_sum(rows)
    xhat, rstd = normalised(xin_ref[...].astype(F32))
    small_ref[0:1, :] = column_sum(grad_normed * xhat)
    small_ref[1:2, :] = column_sum(grad_normed)
    for item in range(plan.items):
        small_ref[12 + item : 13 + item, :] = column_sum(
            grad_normed[item * length : (item + 1) * length]
        )
    dx_ref[...] = grad_middle_ref[...] + norm_back(grad_normed, xhat, rstd, vec[0:1, :])
    out.drain()


def pack_kernel(qkv_ref, out_ref, up_ref, down_ref, first_ref, second_ref):
    rows, width = out_ref.shape
    for part in range(OUT):
        first_ref[part] = qkv_ref[:, part * width : (part + 1) * width].astype(BF16)
    first_ref[OUT] = out_ref[...].astype(BF16)
    for part in range(QUART):
        second_ref[part] = up_ref[:, part * width : (part + 1) * width].astype(BF16)
        second_ref[QUART + part] = down_ref[part * rows : (part + 1) * rows, :].astype(BF16)


def unpack_kernel(grads_ref, qkv_ref, out_ref, up_ref, down_ref):
    _, rows, width = grads_ref.shape
    for part in range(OUT):
        qkv_ref[:, part * width : (part + 1) * width] = grads_ref[part].astype(F32)
    out_ref[...] = grads_ref[OUT].astype(F32)
    for part in range(QUART):
        up_ref[:, part * width : (part + 1) * width] = grads_ref[FIRST + part].astype(F32)
        down_ref[part * rows : (part + 1) * rows, :] = grads_ref[FIRST + QUART + part].astype(F32)


SMEM = pl.BlockSpec(memory_space=pltpu.SMEM)
VMEM = pl.BlockSpec(memory_space=pltpu.VMEM)
HBM = pl.BlockSpec(memory_space=pltpu.HBM)


def kept_shapes(plan):
    tokens, width = plan.tokens, plan.width
    return [
        ((tokens, width), BF16),
        ((tokens, 3 * width), BF16),
        ((tokens, width), BF16),
        ((tokens, width), F32),
        ((tokens, width), BF16),
        ((plan.items * plan.pairs, 2 * plan.length, plan.length), F32),
        ((tokens, 4 * width), BF16),
        ((tokens, 4 * width), F32),
    ]


def held_blocks(plan, blocks):
    return pltpu.VMEM((blocks, plan.shards, plan.rows, plan.width), BF16)


def call(kernel, outs, in_specs, out_specs, scratch, name, work, limit, args):
    args = [
        pltpu.with_memory_space_constraint(arg, pltpu.HBM) if spec is HBM else arg
        for arg, spec in zip(args, in_specs)
    ]
    return pl.pallas_call(
        kernel,
        out_shape=outs,
        in_specs=in_specs,
        out_specs=out_specs,
        scratch_shapes=scratch,
        compiler_params=pltpu.CompilerParams(vmem_limit_bytes=limit * 1024 * 1024),
        cost_estimate=pl.CostEstimate(flops=2 * work[0], bytes_accessed=work[1], transcendentals=0),
        name=name,
    )(*args)


def of(shape):
    return jax.ShapeDtypeStruct(*shape)


def inside(shape):
    return pltpu.VMEM(*shape)


def run_attend(plan, lengths, flag, devs, x, vec, pieces):
    kept = kept_shapes(plan)
    block = plan.width * plan.width
    return call(
        functools.partial(attend_kernel, plan),
        [of(kept[3]), of(kept[4])],
        [SMEM, SMEM, SMEM, VMEM, VMEM] + [HBM] * len(pieces),
        [VMEM, VMEM],
        [held_blocks(plan, FIRST)] + [inside(shape) for shape in kept[:3]] + [pltpu.SemaphoreType.DMA((2,))],
        "attend",
        (FIRST * block * plan.tokens, FIRST * block * 2),
        14,
        (lengths, flag, devs, x, vec, *pieces),
    )


def run_mlp(plan, middle, hidden, vec, gathered):
    block = plan.width * plan.width
    return call(
        functools.partial(mlp_kernel, plan),
        jax.ShapeDtypeStruct(hidden.shape, BF16),
        [VMEM, VMEM, VMEM, HBM],
        VMEM,
        [held_blocks(plan, SECOND), pltpu.SemaphoreType.DMA((SECOND,))],
        "mlp",
        (SECOND * block * plan.tokens, SECOND * block * 2),
        16,
        (middle, hidden, vec, gathered),
    )


def run_load(plan, devs, after, gathered, pieces):
    block = plan.width * plan.width
    return call(
        functools.partial(load_kernel, plan),
        [held_blocks(plan, FIRST), held_blocks(plan, SECOND)],
        [SMEM, pl.BlockSpec(memory_space=pl.ANY)] + [HBM] * (1 + len(pieces)),
        [VMEM, VMEM],
        [pltpu.SemaphoreType.DMA((2,))],
        "load",
        (0, (FIRST + SECOND) * block * 4),
        2,
        (devs, after, gathered, *pieces),
    )


def run_chain(plan, lengths, flag, x, recv, cot, vec, held1, held2):
    shapes = kept_shapes(plan)
    block = plan.width * plan.width
    return call(
        functools.partial(chain_kernel, plan),
        [of(shapes[0]), inside(shapes[0]), of(shapes[0])] + [inside(shape) for shape in shapes],
        [SMEM] * 2 + [VMEM] * 6,
        [VMEM] * (3 + len(shapes)),
        [inside(shapes[0]), inside(shapes[1])],
        "chain",
        (24 * block * plan.tokens, 12 * block),
        10,
        (lengths, flag, x, recv, cot, vec, held1, held2),
    )


def run_backward(plan, flag, arriving, cot, xin, vec, held1, held2, kept):
    shapes = kept_shapes(plan)
    block = plan.width * plan.width
    stage = (2, plan.shards, plan.rows, plan.width)
    return call(
        functools.partial(backward_kernel, plan),
        [
            of(shapes[3]),
            jax.ShapeDtypeStruct((16, plan.width), F32),
            pltpu.HBM((plan.shards, FIRST + SECOND, plan.rows, plan.width), BF16),
        ],
        [SMEM] + [VMEM] * (6 + len(kept)),
        [VMEM, VMEM, HBM],
        [inside(shapes[index]) for index in (6, 3, 0, 1)]
        + [pltpu.VMEM(stage, BF16), pltpu.SemaphoreType.DMA((2,))],
        "backward",
        (24 * block * plan.tokens, 12 * block * 2),
        12,
        (flag, arriving, cot, xin, vec, held1, held2, *kept),
    )


def shifted(value, axis, steps):
    count = lax.axis_size(axis)
    first, last = (max(0, -steps), min(count, count - steps))
    return lax.ppermute(value, axis, [(source, source + steps) for source in range(first, last)])


def small_gather(value, count):
    value = value[None]
    if count & (count - 1):
        return lax.all_gather(value, "dp", axis=0, tiled=True)
    index = lax.axis_index("dp")
    step = 1
    while step < count:
        other = lax.ppermute(value, "dp", [(i, i ^ step) for i in range(count)])
        value = jnp.where(
            (index & step) == 0,
            jnp.concatenate([value, other], 0),
            jnp.concatenate([other, value], 0),
        )
        step *= 2
    return value


def small_scatter(value, count):
    if count & (count - 1):
        return lax.psum_scatter(value, "dp", scatter_dimension=0, tiled=True)[0]
    index = lax.axis_index("dp")
    step = count // 2
    while step:
        upper = (index & step) != 0
        keep = jnp.where(upper, value[step:], value[:step])
        send = jnp.where(upper, value[:step], value[step:])
        value = keep + lax.ppermute(send, "dp", [(i, i ^ step) for i in range(count)])
        step //= 2
    return value[0]


class Ring:
    def __init__(self, count):
        self.chips = count // 2
        self.walk = list(range(0, self.chips, 2)) + list(range(self.chips - 1, 0, -2))
        self.order = [2 * chip + core for chip in self.walk for core in range(2)]
        after = self.walk[1:] + self.walk[:1]
        self.onward = [
            (2 * here + core, 2 * there + core)
            for here, there in zip(self.walk, after)
            for core in range(2)
        ]
        self.back = [(there, here) for here, there in self.onward]
        self.sibling = [(index, index ^ 1) for index in range(count)]

    def slots(self):
        index = lax.axis_index("dp")
        chip, core = index // 2, index % 2
        place = jnp.where(chip % 2 == 0, chip // 2, self.chips - 1 - chip // 2)
        ahead = (place + jnp.arange(self.chips, dtype=jnp.int32)) % self.chips
        chips = jnp.where(ahead < (self.chips + 1) // 2, 2 * ahead, 2 * (self.chips - 1 - ahead) + 1)
        return jnp.concatenate([2 * chips + core, 2 * chips + 1 - core]).astype(jnp.int32)

    def gather(self, shard, beside):
        half = self.chips // 2
        own = [None] * self.chips
        own[0] = shard
        ahead = behind = shard
        for step in range(1, half + 1):
            if step == 3:
                ahead, beside = lax.optimization_barrier((ahead, beside))
            ahead = lax.ppermute(ahead, "dp", self.onward)
            own[self.chips - step] = ahead
            if step < self.chips - half:
                behind = lax.ppermute(behind, "dp", self.back)
                own[step] = behind
        return own + [lax.ppermute(piece, "dp", self.sibling) for piece in own], beside


def body(
    block_input, cotangent, lengths, leads,
    norm_gain1, norm_bias1, lead_table, qkv_weight, query_bias, value_bias, out_weight, out_bias,
    norm_gain2, norm_bias2, up_weight, up_bias, down_weight, down_bias,
):
    count = lax.axis_size("dp")
    micro, local, length, width = block_input.shape
    items = micro * local
    rows = width // count
    leads_count = lead_table.shape[2]
    flag = lax.axis_index("section").astype(jnp.int32).reshape(1)
    flat = lambda value: value.reshape(items * length, width)
    x, cot = flat(block_input), flat(cotangent)
    lens, lead = lengths.reshape(items), leads.reshape(items)

    small = jnp.concatenate(
        [
            norm_gain1, norm_bias1, query_bias, value_bias, out_bias, norm_gain2, norm_bias2, down_bias,
            up_bias.reshape(4, rows), lead_table[0].T,
        ],
        0,
    ).astype(BF16)
    small = small_gather(small, count)
    wide = small.transpose(1, 0, 2).reshape(12 + leads_count, width).astype(F32)
    vec = jnp.concatenate(
        [wide[:8], small[:, 8:12].reshape(4, width).astype(F32)]
        + [lax.dynamic_slice_in_dim(wide, 12 + lead[item], 1, 0) for item in range(items)]
        + [jnp.zeros((4 - items, width), F32)],
        0,
    )

    aligned = rows % 16 == 0 and count % 4 == 0
    if aligned:
        ring = Ring(count)
        first, second = pl.pallas_call(
            pack_kernel,
            out_shape=[
                jax.ShapeDtypeStruct((FIRST, rows, width), BF16),
                jax.ShapeDtypeStruct((SECOND, rows, width), BF16),
            ],
            name="pack",
        )(qkv_weight[0], out_weight[0], up_weight[0], down_weight[0])
        gathered = lax.all_gather(second, "dp", axis=0, tiled=True, axis_index_groups=[ring.order])
        gathered = gathered.reshape(count, SECOND, rows, width)
        pieces, vec = ring.gather(first, vec)
        devs = ring.slots()
        plan = Plan(count, rows, ring.order, items, length, width)
    else:
        wide_blocks = lambda value: value[0].reshape(rows, -1, width).transpose(1, 0, 2)
        packed = jnp.concatenate(
            [wide_blocks(qkv_weight), out_weight, wide_blocks(up_weight), down_weight.reshape(QUART, rows, width)], 0
        )
        everything = lax.all_gather(packed.astype(BF16), "dp", axis=0)
        across_blocks = lambda value: value.transpose(1, 0, 2, 3).reshape(-1, width, width)
        pieces = [across_blocks(everything[:, :FIRST])]
        gathered = jnp.concatenate(
            [
                across_blocks(everything[:, FIRST : FIRST + QUART]),
                everything[:, FIRST + QUART :].reshape(QUART, width, width),
            ],
            0,
        )[None]
        devs = jnp.zeros((1,), jnp.int32)
        plan = Plan(1, width, [0], items, length, width)

    middle, hidden = run_attend(plan, lens, flag, devs, x, vec, pieces)
    first_out = run_mlp(plan, middle, hidden, vec, gathered)
    recv = shifted(first_out, "section", 1)
    held1, held2 = run_load(plan, devs, first_out, gathered, pieces)
    output, xin, first_grad, *kept = run_chain(plan, lens, flag, x, recv, cot, vec, held1, held2)
    arriving = shifted(first_grad, "section", -1)
    input_grad, sums, grads = run_backward(
        plan, flag, arriving, cot, xin, vec, held1, held2, kept
    )
    blocks = FIRST + SECOND
    if aligned:
        grads = lax.psum_scatter(
            grads.reshape(count * blocks, rows, width),
            "dp", scatter_dimension=0, tiled=True, axis_index_groups=[ring.order],
        )
        shapes = [(rows, OUT * width), (rows, width), (rows, QUART * width), (QUART * rows, width)]
        grads = pl.pallas_call(
            unpack_kernel,
            out_shape=[jax.ShapeDtypeStruct(shape, F32) for shape in shapes],
            name="unpack",
        )(grads)
    else:
        head, tail = grads[0, : FIRST + QUART], grads[0, FIRST + QUART :]
        grads = jnp.concatenate(
            [
                head.reshape(-1, count, rows, width).transpose(1, 0, 2, 3),
                tail.reshape(count, QUART, rows, width),
            ],
            1,
        )
        grads = lax.psum_scatter(grads, "dp", scatter_dimension=0, tiled=False).astype(F32)
        across = lambda value: value.transpose(1, 0, 2).reshape(rows, -1)
        grads = (
            across(grads[:OUT]),
            grads[OUT],
            across(grads[FIRST : FIRST + QUART]),
            grads[FIRST + QUART :].reshape(QUART * rows, width),
        )
    hot = (jnp.arange(leads_count)[:, None] == lead[None, :]).astype(F32)
    table = sum(hot[:, item : item + 1] * sums[12 + item : 13 + item] for item in range(items))
    spread = jnp.concatenate(
        [
            sums[:8].reshape(8, count, rows).transpose(1, 0, 2),
            sums[8:12].reshape(count, 4, rows),
            table.reshape(leads_count, count, rows).transpose(1, 0, 2),
        ],
        1,
    )
    spread = small_scatter(spread, count)

    vector = lambda index: spread[index : index + 1]
    shape = (1, micro, local, length, width)
    return (
        output.reshape(shape),
        input_grad.reshape(shape),
        vector(0),
        vector(1),
        spread[12:].T[None],
        grads[0][None],
        vector(2),
        vector(3),
        grads[1][None],
        vector(4),
        vector(5),
        vector(6),
        grads[2][None],
        spread[8:12].reshape(1, 4 * rows),
        grads[3][None],
        vector(7),
    )


def solution(mesh):
    weights = (
        P("section", "dp"),
        P("section", "dp"),
        P("section", "dp", None),
        P("section", "dp", None),
        P("section", "dp"),
        P("section", "dp"),
        P("section", "dp", None),
        P("section", "dp"),
        P("section", "dp"),
        P("section", "dp"),
        P("section", "dp", None),
        P("section", "dp"),
        P("section", "dp", None),
        P("section", "dp"),
    )
    rows = P(None, "dp", None, None)
    layers = P("section", None, "dp", None, None)
    return jax.shard_map(
        body,
        mesh=mesh,
        in_specs=(rows, rows, P(None, "dp"), P(None, "dp")) + weights,
        out_specs=(layers, layers) + weights,
        check_vma=False,
    )
```

time: 267 us -> 249 us (0.933)
  waiting for transfers between devices: 156 us -> 140 us
  local copies, waits for them, and re-layouts: 13.1 us -> 4.9 us
  starting transfers between devices: 18.6 us -> 24.7 us
    all_gather x1, waiting for transfers between devices: 60.7 us -> 0.02 us  [body(): lax.all_gather(second, 'dp', axis=0, tiled=True, axis_index_groups=[ring....]
    ppermute x0 -> x15, waiting for transfers between devices: none -> 38.7 us  [the longest x4 36.3 us: gather(): ahead = lax.ppermute(ahead, 'dp', self.onward)]
    ppermute x4, waiting for transfers between devices: 6.39 us -> 16.5 us  [small_gather(): other = lax.ppermute(value, 'dp', [(i, i ^ step) for i in range(count)])]
    ppermute x0 -> x15, starting transfers between devices: none -> 8.31 us  [the longest x3 5.6 us: gather(): behind = lax.ppermute(behind, 'dp', self.back)]
    ppermute x2, waiting for transfers between devices: 15.8 us -> 9.46 us  [shifted(): lax.ppermute(value, axis, [(source, source + steps) for source in range(f...]
    concatenate x5, other arithmetic: 0.02 us -> 3.41 us  [body(): jnp.concatenate([norm_gain1, norm_bias1, query_bias, value_bias, out_bias...]
    ppermute x4, starting transfers between devices: 4.76 us -> 1.95 us  [small_scatter(): lax.ppermute(send, 'dp', [(i, i ^ step) for i in range(count)])]
    pallas_call x3 -> x7, Pallas kernels: 56.3 us -> 54.9 us  [the longest x5 50.1 us: call(): pl.pallas_call(kernel, out_shape=outs, in_specs=in_specs, out_specs=out_s...]
  transfers between devices with their start and end apart: 12 -> 27, of which waited for: 12 -> 16; matrix products, arithmetic and copies ran while one was open for 2% -> 4% of each run, Pallas kernels for 0% -> 4%
where the time goes in v2:
time: 249 us; the launch traced here: 246 us
  waiting for transfers between devices  140 us (56%)
  Pallas kernels  54.9 us (22%)
  starting transfers between devices  24.7 us (10%)
  between operations  17.1 us (7%)
  local copies, waits for them, and re-layouts  4.9 us (2%)
  other arithmetic  4.63 us (2%)
    reduce_scatter x1, waiting for transfers between devices, body(): lax.psum_scatter(grads.reshape(count * blocks, rows, width), 'dp', scatte...  55.5 us
    pallas_call x5, Pallas kernels, call(): pl.pallas_call(kernel, out_shape=outs, in_specs=in_specs, out_specs=out_s...  50.1 us
    ppermute x4, waiting for transfers between devices, gather(): ahead = lax.ppermute(ahead, 'dp', self.onward)  36.3 us
    ppermute x4, waiting for transfers between devices, small_scatter(): lax.ppermute(send, 'dp', [(i, i ^ step) for i in range(count)])  19.8 us
    ppermute x4, waiting for transfers between devices, small_gather(): other = lax.ppermute(value, 'dp', [(i, i ^ step) for i in range(count)])  16.5 us
    ppermute x2, waiting for transfers between devices, shifted(): lax.ppermute(value, axis, [(source, source + steps) for source in range(f...  9.46 us
    ppermute x4, starting transfers between devices, small_gather(): other = lax.ppermute(value, 'dp', [(i, i ^ step) for i in range(count)])  9.06 us
    ppermute x3, starting transfers between devices, gather(): behind = lax.ppermute(behind, 'dp', self.back)  5.6 us
  transfers between devices with their start and end apart: 27, of which 16 were waited for; matrix products, arithmetic and copies ran while one was open for 4% of the time, Pallas kernels for 4%

profile of v2, /device:TPU:0, one launch (start us, length us, event | category | flops | bytes accessed | tf_op | source)
XLA Modules:
  0.0 246.2 jit_solution(5568155139290175713)
XLA Ops:
  7.2 2.4 pack.1
  9.8 0.7 convert_reduce_fusion
  10.5 0.7 convert_bitcast_fusion.8
  11.2 0.7 convert_bitcast_fusion.6
  11.9 0.7 convert_bitcast_fusion.4
  12.6 0.7 convert_bitcast_fusion.2
  13.2 0.7 convert_bitcast_fusion.1
  14.1 0.5 collective-permute-start.2
  14.6 0.8 collective-permute-done.2
  15.5 2.9 %collective-permute-start.3 = (bf16[2,36,48]{2,1,0:T(8,128)(2,1)S(1)}, bf16[2,36,48]{2,1,0:T(8,128)(2,1)S(1)}, u32[]{:S(2)}, u32[]{:S(2)}) collective-permute-start(bf16[2,36,48]{2,1,0:T(8,128)(2,1)S(1)} %maximum_select_fusion.3), channel_id=1, source_target_pairs={{0,2},{1,3},{2,0},{3,1},{4,6},{5,7},{6,4},{7,5},{8,10},{9,11},{10,... | collective-permute-start | bytes 20744 | tf_op jit(solution)/shard_map/ppermute | solution.py:551
  18.4 1.8 collective-permute-done.3
  20.2 2.1 collective-permute-start.4
  22.4 2.0 collective-permute-start.6
  24.4 0.9 collective-permute-done.4
  25.2 3.5 %collective-permute-start.5 = (bf16[8,36,48]{2,1,0:T(8,128)(2,1)S(1)}, bf16[8,36,48]{2,1,0:T(8,128)(2,1)S(1)}, u32[]{:S(2)}, u32[]{:S(2)}) collective-permute-start(bf16[8,36,48]{2,1,0:T(8,128)(2,1)S(1)} %maximum_select_fusion.1), channel_id=1, source_target_pairs={{0,8},{1,9},{2,10},{3,11},{4,12},{5,13},{6,14},{7,15},{8,0},{9,1},... | collective-permute-start | bytes 82952 | tf_op jit(solution)/shard_map/ppermute | solution.py:551
  28.7 1.3 fusion.2
  32.6 13.1 %collective-permute-done.5 = bf16[8,36,48]{2,1,0:T(8,128)(2,1)S(1)} collective-permute-done((bf16[8,36,48]{2,1,0:T(8,128)(2,1)S(1)}, bf16[8,36,48]{2,1,0:T(8,128)(2,1)S(1)}, u32[]{:S(2)}, u32[]{:S(2)}) %collective-permute-start.5) | collective-permute-done | bytes 27680 | tf_op jit(solution)/shard_map/ppermute | solution.py:551
  46.4 2.1 collective-permute-start.7
  48.5 12.3 %collective-permute-done.1.refs_6_ = bf16[4,48,768]{2,1,0:T(8,128)(2,1)S(1)} collective-permute-done((bf16[4,48,768]{2,1,0:T(8,128)(2,1)S(1)}, bf16[4,48,768]{2,1,0:T(8,128)(2,1)S(1)}, u32[]{:S(2)}, u32[]{:S(2)}) %collective-permute-start.1) | collective-permute-done | bytes 294944 | tf_op jit(solution)/shard_map/ppermute | solution.py:605
  60.8 0.5 collective-permute-start.9
  61.3 0.5 collective-permute-start.12
  61.8 1.6 collective-permute-start.8
  63.4 12.1 %collective-permute-done.9.refs_5_ = bf16[4,48,768]{2,1,0:T(8,128)(2,1)S(1)} collective-permute-done((bf16[4,48,768]{2,1,0:T(8,128)(2,1)S(1)}, bf16[4,48,768]{2,1,0:T(8,128)(2,1)S(1)}, u32[]{:S(2)}, u32[]{:S(2)}) %collective-permute-start.9) | collective-permute-done | bytes 294944 | tf_op jit(solution)/shard_map/ppermute | solution.py:605
  75.5 1.0 collective-permute-start.10
  77.2 0.7 collective-permute-done.8.refs_3_
  77.9 11.9 %collective-permute-done.10.refs_4_ = bf16[4,48,768]{2,1,0:T(8,128)(2,1)S(1)} collective-permute-done((bf16[4,48,768]{2,1,0:T(8,128)(2,1)S(1)}, bf16[4,48,768]{2,1,0:T(8,128)(2,1)S(1)}, u32[]{:S(2)}, u32[]{:S(2)}) %collective-permute-start.10) | collective-permute-done | bytes 294944 | tf_op jit(solution)/shard_map/ppermute | solution.py:605
  89.9 1.6 collective-permute-done.15.refs_12_
  91.6 5.5 %attend.1 = (f32[192,768]{1,0:T(8,128)S(1)}, bf16[192,768]{1,0:T(8,128)(2,1)S(1)}) custom-call(s32[2]{0:T(128)S(1)} %bitcast.82, s32[1]{0:T(128)} %bitcast.1.flag, s32[16]{0:T(128)S(1)} %pad_add_fusion.devs, bf16[192,768]{1,0:T(8,128)(2,1)S(1)} %bitcast.78, f32[16,768]{1,0:T(8,128)S(1)} %concatenate.84.vec, bf16[4,48,768]{2,1,0:T(8,128)(2,1)} %get-tuple-element.42.refs_0_, ...), custom_call_target="tpu_custom_call" | custom-call | flops 905969664 | bytes 4718592 | tf_op jit(solution)/shard_map/attend/pallas_call | solution.py:434
  97.1 5.1 %mlp.1.after = bf16[192,768]{1,0:T(8,128)(2,1)S(1)} custom-call(f32[192,768]{1,0:T(8,128)S(1)} %get-tuple-element.45.middle_ref, bf16[192,768]{1,0:T(8,128)(2,1)S(1)} %get-tuple-element.46.hidden_ref, f32[16,768]{1,0:T(8,128)S(1)} %concatenate.84.vec, bf16[16,8,48,768]{3,2,1,0:T(8,128)(2,1)} %bitcast.84), custom_call_target="tpu_custom_call" | custom-call | flops 1811939328 | bytes 9437184 | tf_op jit(solution)/shard_map/mlp/pallas_call | solution.py:434
  102.2 3.8 %collective-permute-start.19 = (bf16[192,768]{1,0:T(8,128)(2,1)S(1)}, bf16[192,768]{1,0:T(8,128)(2,1)S(1)}, u32[]{:S(2)}, u32[]{:S(2)}) collective-permute-start(bf16[192,768]{1,0:T(8,128)(2,1)S(1)} %mlp.1.after), channel_id=1, source_target_pairs={{0,16},{1,17},{2,18},{3,19},{4,20},{5,21},{6,22},{7,23},{8,24},{9,... | collective-permute-start | bytes 884744 | tf_op jit(solution)/shard_map/ppermute | solution.py:541
  106.0 5.6 %load.1 = (bf16[4,16,48,768]{3,2,1,0:T(8,128)(2,1)S(1)}, bf16[8,16,48,768]{3,2,1,0:T(8,128)(2,1)S(1)}) custom-call(s32[16]{0:T(128)S(1)} %pad_add_fusion.devs, bf16[192,768]{1,0:T(8,128)(2,1)S(1)} %mlp.1.after, bf16[16,8,48,768]{3,2,1,0:T(8,128)(2,1)} %bitcast.85, bf16[4,48,768]{2,1,0:T(8,128)(2,1)} %get-tuple-element.42.refs_0_, ...), custom_call_target="tpu_custom_call" | custom-call | bytes 28311552 | tf_op jit(solution)/shard_map/load/pallas_call | solution.py:434
  111.6 0.8 collective-permute-done.19.recv_ref
  112.3 15.3 %chain.1 = (bf16[192,768]{1,0:T(8,128)(2,1)}, bf16[192,768]{1,0:T(8,128)(2,1)S(1)}, bf16[192,768]{1,0:T(8,128)(2,1)S(1)}, bf16[192,768]{1,0:T(8,128)(2,1)S(1)}, ...) custom-call(s32[2]{0:T(128)S(1)} %bitcast.83, ...), custom_call_target="tpu_custom_call" | custom-call | flops 5435817984 | bytes 7077888 | tf_op jit(solution)/shard_map/chain/pallas_call | solution.py:434
  127.6 1.5 collective-permute-start.20
  129.1 8.7 %collective-permute-done.20.arr_ref = bf16[192,768]{1,0:T(8,128)(2,1)S(1)} collective-permute-done((bf16[192,768]{1,0:T(8,128)(2,1)S(1)}, bf16[192,768]{1,0:T(8,128)(2,1)S(1)}, u32[]{:S(2)}, u32[]{:S(2)}) %collective-permute-start.20) | collective-permute-done | bytes 294944 | tf_op jit(solution)/shard_map/ppermute | solution.py:541
  137.8 18.7 %backward.1 = (f32[192,768]{1,0:T(8,128)}, f32[16,768]{1,0:T(8,128)S(1)}, bf16[16,12,48,768]{3,2,1,0:T(8,128)(2,1)}) custom-call(s32[1]{0:T(128)} %bitcast.1.flag, bf16[192,768]{1,0:T(8,128)(2,1)S(1)} %collective-permute-done.20.arr_ref, bf16[192,768]{1,0:T(8,128)(2,1)S(1)} %bitcast.81, bf16[192,768]{1,0:T(8,128)(2,1)S(1)} %get-tuple-element.52.xin_ref, ...), custom_call_target="tpu_custom_call" | custom-call | flops 5435817984 | bytes 14155776 | tf_op jit(solution)/shard_map/backward/pallas_call | solution.py:434
  156.6 0.6 copy-done.13
  157.8 0.8 collective-permute-start.21
  158.7 9.6 %collective-permute-done.21 = f32[8,36,48]{2,1,0:T(8,128)S(1)} collective-permute-done((f32[8,36,48]{2,1,0:T(8,128)S(1)}, f32[8,36,48]{2,1,0:T(8,128)S(1)}, u32[]{:S(2)}, u32[]{:S(2)}) %collective-permute-start.21) | collective-permute-done | bytes 55328 | tf_op jit(solution)/shard_map/ppermute | solution.py:570
  168.4 5.4 %collective-permute-done.22 = f32[4,36,48]{2,1,0:T(8,128)S(1)} collective-permute-done((f32[4,36,48]{2,1,0:T(8,128)S(1)}, f32[4,36,48]{2,1,0:T(8,128)S(1)}, u32[]{:S(2)}, u32[]{:S(2)}) %collective-permute-start.22) | collective-permute-done | bytes 27680 | tf_op jit(solution)/shard_map/ppermute | solution.py:570
  173.8 1.0 collective-permute-start.23
  174.8 3.6 %collective-permute-done.23 = f32[2,36,48]{2,1,0:T(8,128)S(1)} collective-permute-done((f32[2,36,48]{2,1,0:T(8,128)S(1)}, f32[2,36,48]{2,1,0:T(8,128)S(1)}, u32[]{:S(2)}, u32[]{:S(2)}) %collective-permute-start.23) | collective-permute-done | bytes 13856 | tf_op jit(solution)/shard_map/ppermute | solution.py:570
  178.5 1.2 collective-permute-done.24
  179.7 0.6 reshape.272
  180.3 0.5 slice_bitcast_fusion.1
  180.9 0.6 slice_bitcast_fusion
  181.5 55.5 %reduce-scatter.2.cloned.1.call-done.grads_ref = bf16[12,48,768]{2,1,0:T(8,128)(2,1)} async-done(((bf16[192,48,768]{2,1,0:T(8,128)(2,1)}), bf16[12,48,768]{2,1,0:T(8,128)(2,1)}) %reduce-scatter.2.cloned.1.call-update) | async-done | bytes 884752 | tf_op jit(solution)/shard_map/reduce_scatter | solution.py:689
  237.0 2.4 unpack.1
  (92 shorter events, 2.7 us)
Async XLA Ops:
  7.2 84.4 %copy-start.2 = (s32[2,1]{0,1:T(1,128)S(1)}, s32[2,1]{0,1:T(1,128)}, u32[]{:S(2)}) copy-start(s32[2,1]{0,1:T(1,128)} %param.20) | copy-start | bytes 28
  7.2 84.4 %copy-start = (bf16[2,1,96,768]{3,2,1,0:T(8,128)(2,1)S(1)}, bf16[2,1,96,768]{3,2,1,0:T(8,128)(2,1)}, u32[]{:S(2)}) copy-start(bf16[2,1,96,768]{3,2,1,0:T(8,128)(2,1)} %param.18) | copy-start | bytes 884740
  7.2 89.9 %all-gather.2.cloned.1.call-start = ((), (), s32[]{:S(2)}) async-start(), calls=%async_computation.1 | async-start | bytes 10027008 | tf_op jit(solution)/shard_map/all_gather | solution.py:655
  9.7 227.3 %reduce-scatter.2.cloned.1.call-start = ((), (), s32[]{:S(2)}) async-start(), calls=%async_computation.2 | async-start | bytes 15040512 | tf_op jit(solution)/shard_map/reduce_scatter | solution.py:689
  14.1 1.3 collective-permute-start.2
  15.5 4.7 %collective-permute-start.3 = (bf16[2,36,48]{2,1,0:T(8,128)(2,1)S(1)}, bf16[2,36,48]{2,1,0:T(8,128)(2,1)S(1)}, u32[]{:S(2)}, u32[]{:S(2)}) collective-permute-start(bf16[2,36,48]{2,1,0:T(8,128)(2,1)S(1)} %maximum_select_fusion.3), channel_id=1, source_target_pairs={{0,2},{1,3},{2,0},{3,1},{4,6},{5,7},{6,4},{7,5},{8,10},{9,11},{10,... | collective-permute-start | bytes 20744 | tf_op jit(solution)/shard_map/ppermute | solution.py:551
  20.2 5.0 %collective-permute-start.4 = (bf16[4,36,48]{2,1,0:T(8,128)(2,1)S(1)}, bf16[4,36,48]{2,1,0:T(8,128)(2,1)S(1)}, u32[]{:S(2)}, u32[]{:S(2)}) collective-permute-start(bf16[4,36,48]{2,1,0:T(8,128)(2,1)S(1)} %maximum_select_fusion.2), channel_id=1, source_target_pairs={{0,4},{1,5},{2,6},{3,7},{4,0},{5,1},{6,2},{7,3},{8,12},{9,13},{10,... | collective-permute-start | bytes 41480 | tf_op jit(solution)/shard_map/ppermute | solution.py:551
  22.3 23.7 %collective-permute-start = (bf16[4,48,768]{2,1,0:T(8,128)(2,1)}, bf16[4,48,768]{2,1,0:T(8,128)(2,1)S(1)}, u32[]{:S(2)}, u32[]{:S(2)}) collective-permute-start(bf16[4,48,768]{2,1,0:T(8,128)(2,1)} %get-tuple-element.42.refs_0_), channel_id=1, source_target_pairs={{0,4},{1,5},{4,8},{5,9},{8,12},{9,13},{12,14},{13,15},{14,10},{15,... | collective-permute-start | bytes 884744 | tf_op jit(solution)/shard_map/ppermute | solution.py:605
  22.4 24.0 %collective-permute-start.6 = (bf16[4,48,768]{2,1,0:T(8,128)(2,1)}, bf16[4,48,768]{2,1,0:T(8,128)(2,1)S(1)}, u32[]{:S(2)}, u32[]{:S(2)}) collective-permute-start(bf16[4,48,768]{2,1,0:T(8,128)(2,1)} %get-tuple-element.42.refs_0_), channel_id=1, source_target_pairs={{4,0},{5,1},{8,4},{9,5},{12,8},{13,9},{14,12},{15,13},{10,14},{11,... | collective-permute-start | bytes 884744 | tf_op jit(solution)/shard_map/ppermute | solution.py:608
  25.2 20.5 %collective-permute-start.5 = (bf16[8,36,48]{2,1,0:T(8,128)(2,1)S(1)}, bf16[8,36,48]{2,1,0:T(8,128)(2,1)S(1)}, u32[]{:S(2)}, u32[]{:S(2)}) collective-permute-start(bf16[8,36,48]{2,1,0:T(8,128)(2,1)S(1)} %maximum_select_fusion.1), channel_id=1, source_target_pairs={{0,8},{1,9},{2,10},{3,11},{4,12},{5,13},{6,14},{7,15},{8,0},{9,1},... | collective-permute-start | bytes 82952 | tf_op jit(solution)/shard_map/ppermute | solution.py:551
  46.0 45.5 %copy-start.3 = (bf16[4,48,768]{2,1,0:T(8,128)(2,1)}, bf16[4,48,768]{2,1,0:T(8,128)(2,1)S(1)}, u32[]{:S(2)}) copy-start(bf16[4,48,768]{2,1,0:T(8,128)(2,1)S(1)} %collective-permute-done.refs_7_) | copy-start | bytes 884740
  46.0 14.8 %collective-permute-start.1 = (bf16[4,48,768]{2,1,0:T(8,128)(2,1)S(1)}, bf16[4,48,768]{2,1,0:T(8,128)(2,1)S(1)}, u32[]{:S(2)}, u32[]{:S(2)}) collective-permute-start(bf16[4,48,768]{2,1,0:T(8,128)(2,1)S(1)} %collective-permute-done.refs_7_), channel_id=1, source_target_pairs={{0,4},{1,5},{4,8},{5,9},{8,12},{9,13},{12,14},{13,15},{14,10},{15,... | collective-permute-start | bytes 884744 | tf_op jit(solution)/shard_map/ppermute | solution.py:605
  46.4 45.1 %copy-start.4 = (bf16[4,48,768]{2,1,0:T(8,128)(2,1)}, bf16[4,48,768]{2,1,0:T(8,128)(2,1)S(1)}, u32[]{:S(2)}) copy-start(bf16[4,48,768]{2,1,0:T(8,128)(2,1)S(1)} %collective-permute-done.6.refs_1_) | copy-start | bytes 884740
  46.4 15.4 %collective-permute-start.7 = (bf16[4,48,768]{2,1,0:T(8,128)(2,1)S(1)}, bf16[4,48,768]{2,1,0:T(8,128)(2,1)S(1)}, u32[]{:S(2)}, u32[]{:S(2)}) collective-permute-start(bf16[4,48,768]{2,1,0:T(8,128)(2,1)S(1)} %collective-permute-done.6.refs_1_), channel_id=1, source_target_pairs={{4,0},{5,1},{8,4},{9,5},{12,8},{13,9},{14,12},{15,13},{10,14},{11,... | collective-permute-start | bytes 884744 | tf_op jit(solution)/shard_map/ppermute | solution.py:608
  60.8 30.7 %copy-start.5 = (bf16[4,48,768]{2,1,0:T(8,128)(2,1)}, bf16[4,48,768]{2,1,0:T(8,128)(2,1)S(1)}, u32[]{:S(2)}) copy-start(bf16[4,48,768]{2,1,0:T(8,128)(2,1)S(1)} %collective-permute-done.1.refs_6_) | copy-start | bytes 884740
  60.8 14.7 %collective-permute-start.9 = (bf16[4,48,768]{2,1,0:T(8,128)(2,1)S(1)}, bf16[4,48,768]{2,1,0:T(8,128)(2,1)S(1)}, u32[]{:S(2)}, u32[]{:S(2)}) collective-permute-start(bf16[4,48,768]{2,1,0:T(8,128)(2,1)S(1)} %collective-permute-done.1.refs_6_), channel_id=1, source_target_pairs={{0,4},{1,5},{4,8},{5,9},{8,12},{9,13},{12,14},{13,15},{14,10},{15,... | collective-permute-start | bytes 884744 | tf_op jit(solution)/shard_map/ppermute | solution.py:605
  61.3 15.2 %collective-permute-start.11 = (bf16[4,48,768]{2,1,0:T(8,128)(2,1)}, bf16[4,48,768]{2,1,0:T(8,128)(2,1)S(1)}, u32[]{:S(2)}, u32[]{:S(2)}) collective-permute-start(bf16[4,48,768]{2,1,0:T(8,128)(2,1)} %get-tuple-element.42.refs_0_), channel_id=1, source_target_pairs={{0,1},{1,0},{2,3},{3,2},{4,5},{5,4},{6,7},{7,6},{8,9},{9,8},{10,11... | collective-permute-start | bytes 884744 | tf_op jit(solution)/shard_map/ppermute | solution.py:610
  61.3 15.3 %collective-permute-start.12 = (bf16[4,48,768]{2,1,0:T(8,128)(2,1)S(1)}, bf16[4,48,768]{2,1,0:T(8,128)(2,1)S(1)}, u32[]{:S(2)}, u32[]{:S(2)}) collective-permute-start(bf16[4,48,768]{2,1,0:T(8,128)(2,1)S(1)} %collective-permute-done.6.refs_1_), channel_id=1, source_target_pairs={{0,1},{1,0},{2,3},{3,2},{4,5},{5,4},{6,7},{7,6},{8,9},{9,8},{10,11... | collective-permute-start | bytes 884744 | tf_op jit(solution)/shard_map/ppermute | solution.py:610
  61.8 15.3 %collective-permute-start.18 = (bf16[4,48,768]{2,1,0:T(8,128)(2,1)S(1)}, bf16[4,48,768]{2,1,0:T(8,128)(2,1)S(1)}, u32[]{:S(2)}, u32[]{:S(2)}) collective-permute-start(bf16[4,48,768]{2,1,0:T(8,128)(2,1)S(1)} %collective-permute-done.refs_7_), channel_id=1, source_target_pairs={{0,1},{1,0},{2,3},{3,2},{4,5},{5,4},{6,7},{7,6},{8,9},{9,8},{10,11... | collective-permute-start | bytes 884744 | tf_op jit(solution)/shard_map/ppermute | solution.py:610
  61.8 29.7 %copy-start.6 = (bf16[4,48,768]{2,1,0:T(8,128)(2,1)}, bf16[4,48,768]{2,1,0:T(8,128)(2,1)S(1)}, u32[]{:S(2)}) copy-start(bf16[4,48,768]{2,1,0:T(8,128)(2,1)S(1)} %collective-permute-done.7.refs_2_) | copy-start | bytes 884740
  61.8 16.0 %collective-permute-start.8 = (bf16[4,48,768]{2,1,0:T(8,128)(2,1)S(1)}, bf16[4,48,768]{2,1,0:T(8,128)(2,1)S(1)}, u32[]{:S(2)}, u32[]{:S(2)}) collective-permute-start(bf16[4,48,768]{2,1,0:T(8,128)(2,1)S(1)} %collective-permute-done.7.refs_2_), channel_id=1, source_target_pairs={{4,0},{5,1},{8,4},{9,5},{12,8},{13,9},{14,12},{15,13},{10,14},{11,... | collective-permute-start | bytes 884744 | tf_op jit(solution)/shard_map/ppermute | solution.py:608
  75.5 16.0 %copy-start.7 = (bf16[4,48,768]{2,1,0:T(8,128)(2,1)}, bf16[4,48,768]{2,1,0:T(8,128)(2,1)S(1)}, u32[]{:S(2)}) copy-start(bf16[4,48,768]{2,1,0:T(8,128)(2,1)S(1)} %collective-permute-done.9.refs_5_) | copy-start | bytes 884740
  75.5 14.2 %collective-permute-start.10 = (bf16[4,48,768]{2,1,0:T(8,128)(2,1)S(1)}, bf16[4,48,768]{2,1,0:T(8,128)(2,1)S(1)}, u32[]{:S(2)}, u32[]{:S(2)}) collective-permute-start(bf16[4,48,768]{2,1,0:T(8,128)(2,1)S(1)} %collective-permute-done.9.refs_5_), channel_id=1, source_target_pairs={{0,4},{1,5},{4,8},{5,9},{8,12},{9,13},{12,14},{13,15},{14,10},{15,... | collective-permute-start | bytes 884744 | tf_op jit(solution)/shard_map/ppermute | solution.py:605
  76.5 15.0 %copy-start.8 = (bf16[4,48,768]{2,1,0:T(8,128)(2,1)}, bf16[4,48,768]{2,1,0:T(8,128)(2,1)S(1)}, u32[]{:S(2)}) copy-start(bf16[4,48,768]{2,1,0:T(8,128)(2,1)S(1)} %collective-permute-done.11.refs_8_) | copy-start | bytes 884740
  76.5 13.3 %collective-permute-start.13 = (bf16[4,48,768]{2,1,0:T(8,128)(2,1)S(1)}, bf16[4,48,768]{2,1,0:T(8,128)(2,1)}, u32[]{:S(2)}, u32[]{:S(2)}) collective-permute-start(bf16[4,48,768]{2,1,0:T(8,128)(2,1)S(1)} %collective-permute-done.7.refs_2_), channel_id=1, source_target_pairs={{0,1},{1,0},{2,3},{3,2},{4,5},{5,4},{6,7},{7,6},{8,9},{9,8},{10,11... | collective-permute-start | bytes 884744 | tf_op jit(solution)/shard_map/ppermute | solution.py:610
  76.6 15.0 %copy-start.9 = (bf16[4,48,768]{2,1,0:T(8,128)(2,1)}, bf16[4,48,768]{2,1,0:T(8,128)(2,1)S(1)}, u32[]{:S(2)}) copy-start(bf16[4,48,768]{2,1,0:T(8,128)(2,1)S(1)} %collective-permute-done.12.refs_9_) | copy-start | bytes 884740
  76.6 13.3 %collective-permute-start.17 = (bf16[4,48,768]{2,1,0:T(8,128)(2,1)S(1)}, bf16[4,48,768]{2,1,0:T(8,128)(2,1)}, u32[]{:S(2)}, u32[]{:S(2)}) collective-permute-start(bf16[4,48,768]{2,1,0:T(8,128)(2,1)S(1)} %collective-permute-done.1.refs_6_), channel_id=1, source_target_pairs={{0,1},{1,0},{2,3},{3,2},{4,5},{5,4},{6,7},{7,6},{8,9},{9,8},{10,11... | collective-permute-start | bytes 884744 | tf_op jit(solution)/shard_map/ppermute | solution.py:610
  77.1 14.4 %copy-start.10 = (bf16[4,48,768]{2,1,0:T(8,128)(2,1)}, bf16[4,48,768]{2,1,0:T(8,128)(2,1)S(1)}, u32[]{:S(2)}) copy-start(bf16[4,48,768]{2,1,0:T(8,128)(2,1)S(1)} %collective-permute-done.18.refs_15_) | copy-start | bytes 884740
  77.1 12.8 %collective-permute-start.16 = (bf16[4,48,768]{2,1,0:T(8,128)(2,1)S(1)}, bf16[4,48,768]{2,1,0:T(8,128)(2,1)}, u32[]{:S(2)}, u32[]{:S(2)}) collective-permute-start(bf16[4,48,768]{2,1,0:T(8,128)(2,1)S(1)} %collective-permute-done.9.refs_5_), channel_id=1, source_target_pairs={{0,1},{1,0},{2,3},{3,2},{4,5},{5,4},{6,7},{7,6},{8,9},{9,8},{10,11... | collective-permute-start | bytes 884744 | tf_op jit(solution)/shard_map/ppermute | solution.py:610
  77.9 13.6 %copy-start.11 = (bf16[4,48,768]{2,1,0:T(8,128)(2,1)}, bf16[4,48,768]{2,1,0:T(8,128)(2,1)S(1)}, u32[]{:S(2)}) copy-start(bf16[4,48,768]{2,1,0:T(8,128)(2,1)S(1)} %collective-permute-done.8.refs_3_) | copy-start | bytes 884740
  77.9 12.0 %collective-permute-start.14 = (bf16[4,48,768]{2,1,0:T(8,128)(2,1)S(1)}, bf16[4,48,768]{2,1,0:T(8,128)(2,1)}, u32[]{:S(2)}, u32[]{:S(2)}) collective-permute-start(bf16[4,48,768]{2,1,0:T(8,128)(2,1)S(1)} %collective-permute-done.8.refs_3_), channel_id=1, source_target_pairs={{0,1},{1,0},{2,3},{3,2},{4,5},{5,4},{6,7},{7,6},{8,9},{9,8},{10,11... | collective-permute-start | bytes 884744 | tf_op jit(solution)/shard_map/ppermute | solution.py:610
  89.8 1.7 copy-start.12
  89.8 1.7 collective-permute-start.15
  102.2 10.1 %copy-start.1 = (bf16[2,1,96,768]{3,2,1,0:T(8,128)(2,1)S(1)}, bf16[2,1,96,768]{3,2,1,0:T(8,128)(2,1)}, u32[]{:S(2)}) copy-start(bf16[2,1,96,768]{3,2,1,0:T(8,128)(2,1)} %param.19) | copy-start | bytes 884740
  102.2 10.1 %collective-permute-start.19 = (bf16[192,768]{1,0:T(8,128)(2,1)S(1)}, bf16[192,768]{1,0:T(8,128)(2,1)S(1)}, u32[]{:S(2)}, u32[]{:S(2)}) collective-permute-start(bf16[192,768]{1,0:T(8,128)(2,1)S(1)} %mlp.1.after), channel_id=1, source_target_pairs={{0,16},{1,17},{2,18},{3,19},{4,20},{5,21},{6,22},{7,23},{8,24},{9,... | collective-permute-start | bytes 884744 | tf_op jit(solution)/shard_map/ppermute | solution.py:541
  127.6 10.2 %collective-permute-start.20 = (bf16[192,768]{1,0:T(8,128)(2,1)S(1)}, bf16[192,768]{1,0:T(8,128)(2,1)S(1)}, u32[]{:S(2)}, u32[]{:S(2)}) collective-permute-start(bf16[192,768]{1,0:T(8,128)(2,1)S(1)} %get-tuple-element.51), channel_id=1, source_target_pairs={{16,0},{17,1},{18,2},{19,3},{20,4},{21,5},{22,6},{23,7},{24,8},{25... | collective-permute-start | bytes 884744 | tf_op jit(solution)/shard_map/ppermute | solution.py:541
  156.5 0.7 copy-start.13
  157.8 10.4 %collective-permute-start.21 = (f32[8,36,48]{2,1,0:T(8,128)S(1)}, f32[8,36,48]{2,1,0:T(8,128)S(1)}, u32[]{:S(2)}, u32[]{:S(2)}) collective-permute-start(f32[8,36,48]{2,1,0:T(8,128)S(1)} %slice_select_fusion), channel_id=1, source_target_pairs={{0,8},{1,9},{2,10},{3,11},{4,12},{5,13},{6,14},{7,15},{8,0},{9,1},... | collective-permute-start | bytes 165896 | tf_op jit(solution)/shard_map/ppermute | solution.py:570
  168.3 5.5 %collective-permute-start.22 = (f32[4,36,48]{2,1,0:T(8,128)S(1)}, f32[4,36,48]{2,1,0:T(8,128)S(1)}, u32[]{:S(2)}, u32[]{:S(2)}) collective-permute-start(f32[4,36,48]{2,1,0:T(8,128)S(1)} %slice_select_fusion.1), channel_id=1, source_target_pairs={{0,4},{1,5},{2,6},{3,7},{4,0},{5,1},{6,2},{7,3},{8,12},{9,13},{10,... | collective-permute-start | bytes 82952 | tf_op jit(solution)/shard_map/ppermute | solution.py:570
  173.8 4.6 %collective-permute-start.23 = (f32[2,36,48]{2,1,0:T(8,128)S(1)}, f32[2,36,48]{2,1,0:T(8,128)S(1)}, u32[]{:S(2)}, u32[]{:S(2)}) collective-permute-start(f32[2,36,48]{2,1,0:T(8,128)S(1)} %slice_select_fusion.2), channel_id=1, source_target_pairs={{0,2},{1,3},{2,0},{3,1},{4,6},{5,7},{6,4},{7,5},{8,10},{9,11},{10,... | collective-permute-start | bytes 41480 | tf_op jit(solution)/shard_map/ppermute | solution.py:570
  178.4 1.3 collective-permute-start.24
Sparse Core Ops, SparseCore 0:
  10.2 82.5 all-gather.1
  156.7 80.2 reduce-scatter.1

commit v3 on v2

--- a/solution.py
+++ b/solution.py
@@ -19,6 +19,7 @@
 FIRST = 4
 SECOND = 8
 QUART = 4
+EXTRA = 16
 
 
 def mm(left, right):
@@ -71,46 +72,57 @@
 
 
 class Plan:
-    def __init__(self, shards, rows, order, items, length, width):
-        self.shards, self.rows, self.order = shards, rows, order
+    def __init__(self, order, rows, items, length, width):
+        self.order, self.shards, self.rows = order, len(order), rows
         self.items, self.length, self.width = items, length, width
         self.tokens = items * length
         self.pairs = width // PAIR
-
-
-def first_copies(pieces, devs, held, sem, blocks):
+        whole = self.shards % QUART == 0
+        self.runs = [(0, QUART)] if whole else [(block, 1) for block in range(QUART)]
+        self.parts = 2 if self.shards > 1 else 1
+
+
+def first_copies(plan, pieces, devs, held, sem, blocks):
+    if plan.shards == 1:
+        return block_copies(pieces, devs, held, sem, blocks)
     return [
-        pltpu.make_async_copy(piece.at[blocks], held.at[blocks, devs[slot]], sem)
+        pltpu.make_async_copy(
+            piece.at[pl.ds(block * plan.rows, plan.rows)], held.at[block, devs[slot]], sem
+        )
+        for slot, piece in enumerate(pieces)
+        for block in range(blocks.start, blocks.start + blocks.size)
+    ]
+
+
+def block_copies(pieces, devs, held, sem, blocks, at=0):
+    return [
+        pltpu.make_async_copy(
+            piece.at[blocks], held.at[pl.ds(at + blocks.start, blocks.size), devs[slot]], sem
+        )
         for slot, piece in enumerate(pieces)
     ]
 
 
-def down_rows(plan, device):
-    whole = plan.shards % QUART == 0
-    parts = [(0, QUART)] if whole else [(block, 1) for block in range(QUART)]
-    return [
-        (first, count, *divmod(QUART * device + first, plan.shards)) for first, count in parts
-    ]
-
-
-def up_copies(plan, gathered, held, sem, part):
-    return [
-        pltpu.make_async_copy(gathered.at[place, part], held.at[part, device], sem)
-        for place, device in enumerate(plan.order)
-    ]
-
-
-def down_copies(plan, gathered, held, sem, part):
-    return [
-        pltpu.make_async_copy(
-            gathered.at[place, pl.ds(QUART + first, count)],
-            held.at[QUART + block, pl.ds(row, count)],
-            sem,
-        )
-        for place, device in enumerate(plan.order)
-        for first, count, block, row in down_rows(plan, device)
-        if block == part
-    ]
+def down_copies(plan, pieces, devs, held, sems):
+    copies = []
+    for slot, piece in enumerate(pieces):
+        for first, count in plan.runs:
+            row = QUART * devs[slot] + first
+            block = row // plan.shards
+            copies.append(
+                pltpu.make_async_copy(
+                    piece.at[pl.ds(first, count)],
+                    held.at[QUART + block, pl.ds(row % plan.shards, count)],
+                    sems.at[block],
+                )
+            )
+    return copies
+
+
+def second_pieces(plan, gathered):
+    ups = [gathered.at[place, pl.ds(0, QUART)] for place in range(plan.shards)]
+    downs = [gathered.at[place, pl.ds(QUART, QUART)] for place in range(plan.shards)]
+    return ups, downs
 
 
 def start_all(copies):
@@ -217,56 +229,62 @@
     return jnp.sum(values.astype(F32), 0, keepdims=True)
 
 
-def load_first(held, pieces, devs, sems):
-    start_all(first_copies(pieces, devs, held, sems.at[0], pl.ds(0, OUT)))
-    start_all(first_copies(pieces, devs, held, sems.at[1], pl.ds(OUT, 1)))
+def attend_kernel(plan, lengths, flag, devs, x_ref, vec, *refs):
+    pieces, (middle_ref, hidden_ref, held, normed, qkv, attended, sems) = refs[:-7], refs[-7:]
+    start_all(first_copies(plan, pieces, devs, held, sems.at[0], pl.ds(0, OUT)))
+    start_all(first_copies(plan, pieces, devs, held, sems.at[1], pl.ds(OUT, 1)))
 
     def wait(group):
         blocks = pl.ds(OUT, 1) if group else pl.ds(0, OUT)
         wait_bytes(held.at[blocks], sems.at[group])
 
-    return wait
-
-
-def attend_kernel(plan, lengths, flag, devs, x_ref, vec, *refs):
-    pieces, (middle_ref, hidden_ref, held, normed, qkv, attended, sems) = refs[:-7], refs[-7:]
-    wait = load_first(held, pieces, devs, sems)
     middle_ref[...] = first_half(
         plan, x_ref[...], lengths, vec, held, wait, normed, qkv, attended, None, hidden_ref
     )
 
 
-def mlp_kernel(plan, middle_ref, hidden_ref, vec, gathered, y_ref, held, sems):
-    for part in range(QUART):
-        start_all(up_copies(plan, gathered, held, sems.at[part], part))
-        start_all(down_copies(plan, gathered, held, sems.at[QUART + part], part))
+def mlp_kernel(plan, middle_ref, hidden_ref, vec, gathered, y_ref, held, sems, down_sems):
+    (ups, downs), devs = second_pieces(plan, gathered), plan.order
+    start_all(block_copies(ups, devs, held, sems.at[0], pl.ds(0, 1)))
+    start_all(down_copies(plan, downs, devs, held, down_sems))
+    for part in range(1, QUART):
+        start_all(block_copies(ups, devs, held, sems.at[part], pl.ds(part, 1)))
 
     def wait(block):
-        wait_bytes(held.at[block], sems.at[block])
+        sem = sems.at[block] if block < QUART else down_sems.at[block - QUART]
+        wait_bytes(held.at[block], sem)
 
     total = second_half(plan, hidden_ref, vec, held, wait=wait)
     y_ref[...] = (middle_ref[...] + total).astype(BF16)
 
 
 def load_kernel(plan, devs, after, gathered, *refs):
-    pieces, (held1, held2, sems) = refs[:-3], refs[-3:]
-    copies = first_copies(pieces, devs, held1, sems.at[0], pl.ds(0, FIRST))
+    firsts, (held1, held2, sems, down_sems) = refs[:-4], refs[-4:]
+    ups, downs = second_pieces(plan, gathered)
+    start_all(first_copies(plan, firsts, devs, held1, sems.at[0], pl.ds(0, FIRST)))
+    start_all(block_copies(ups, plan.order, held2, sems.at[1], pl.ds(0, QUART)))
+    start_all(down_copies(plan, downs, plan.order, held2, down_sems))
+    wait_bytes(held1, sems.at[0])
+    wait_bytes(held2.at[pl.ds(0, QUART)], sems.at[1])
     for part in range(QUART):
-        copies += up_copies(plan, gathered, held2, sems.at[1], part)
-        copies += down_copies(plan, gathered, held2, sems.at[1], part)
-    start_all(copies)
-    wait_bytes(held1, sems.at[0])
-    wait_bytes(held2, sems.at[1])
+        wait_bytes(held2.at[QUART + part], down_sems.at[part])
 
 
 def chain_kernel(
     plan, lengths, flag, x_ref, recv_ref, cot_ref, vec, held1, held2,
-    y_ref, xin_ref, dx_ref, normed, qkv, attended, middle, hidden, probs, act, slope, grad_attended, grad_rows,
+    y_ref, dx_ref, hidden, act, slope, *refs,
 ):
+    outs, (xin_ref, normed, qkv, attended, middle, probs, grad_attended, grad_rows, sems) = refs[:6], refs[6:]
+    kept = (xin_ref, normed, qkv, attended, middle, probs)
+    copies = [
+        pltpu.make_async_copy(source, target, sems.at[index])
+        for index, (source, target) in enumerate(zip(kept, outs))
+    ]
     xin_ref[...] = jnp.where(flag[0] == 0, x_ref[...], recv_ref[...])
     middle[...] = first_half(
         plan, xin_ref[...], lengths, vec, held1, lambda group: None, normed, qkv, attended, probs, hidden
     )
+    start_all(copies)
     y_ref[...] = (middle[...] + second_half(plan, hidden, vec, held2, act, slope)).astype(BF16)
     branch = cot_ref[...]
     grad_hidden = None
@@ -285,6 +303,8 @@
         grad_normed = term if grad_normed is None else grad_normed + term
     xhat, rstd = normalised(xin_ref[...].astype(F32))
     dx_ref[...] = (grad_middle + norm_back(grad_normed, xhat, rstd, vec[0:1, :])).astype(BF16)
+    for copy in copies:
+        copy.wait()
 
 
 class Stage:
@@ -305,21 +325,19 @@
             wait_bytes(self.stage.at[slot], self.sems.at[slot])
 
 
-def backward_kernel(
-    plan, flag, arr_ref, cot_ref, xin_ref, vec, held1, held2,
-    normed, qkv, attended, middle_ref, hidden, probs, act, slope,
-    dx_ref, small_ref, grads, grad_pre_ref, grad_middle_ref, grad_attended, grad_rows, stage, stage_sems,
+def mlp_back_kernel(
+    plan, flag, arr_ref, cot_ref, held2, hidden, act, slope,
+    grad_hidden_ref, small_ref, grads, grad_pre_ref, stage, stage_sems,
 ):
-    length = plan.length
     branch = jnp.where(flag[0] == 0, arr_ref[...], cot_ref[...])
     small_ref[...] = jnp.zeros_like(small_ref)
     small_ref[7:8, :] = column_sum(branch)
     out = Stage(plan, stage, stage_sems)
 
-    def copies_of(block):
+    def copies_of_up(part):
         def copies(source, sem):
             return [
-                pltpu.make_async_copy(source.at[device], grads.at[place, block], sem)
+                pltpu.make_async_copy(source.at[device], grads.at[place, part], sem)
                 for place, device in enumerate(plan.order)
             ]
 
@@ -327,16 +345,19 @@
 
     def copies_of_down(part):
         def copies(source, sem):
-            return [
-                pltpu.make_async_copy(
-                    source.at[pl.ds(row, count)],
-                    grads.at[place, pl.ds(FIRST + QUART + first, count)],
-                    sem,
-                )
-                for place, device in enumerate(plan.order)
-                for first, count, block, row in down_rows(plan, device)
-                if block == part
-            ]
+            made = []
+            for place, device in enumerate(plan.order):
+                for first, count in plan.runs:
+                    block, row = divmod(QUART * device + first, plan.shards)
+                    if block == part:
+                        made.append(
+                            pltpu.make_async_copy(
+                                source.at[pl.ds(row, count)],
+                                grads.at[place, pl.ds(QUART + first, count)],
+                                sem,
+                            )
+                        )
+            return made
 
         return copies
 
@@ -350,10 +371,85 @@
         term = mm_nt(grad_pre, block_of(plan, held2, part))
         grad_hidden = term if grad_hidden is None else grad_hidden + term
         out.put(mm_tn(act[:, columns], branch), copies_of_down(part))
+    grad_hidden_ref[...] = grad_hidden
     for part in range(QUART):
-        out.put(
-            mm_tn(hidden[...], grad_pre_ref[:, columns_of(plan, part)]), copies_of(FIRST + part)
-        )
+        out.put(mm_tn(hidden[...], grad_pre_ref[:, columns_of(plan, part)]), copies_of_up(part))
+    out.drain()
+
+
+def slot_copies(plan, devs, grads, block):
+    each = plan.shards // plan.parts
+
+    def copies(source, sem):
+        return [
+            pltpu.make_async_copy(
+                source.at[devs[slot]],
+                grads[slot // each].at[slot % each, pl.ds(block * plan.rows, plan.rows)],
+                sem,
+            )
+            for slot in range(plan.shards)
+        ]
+
+    return copies
+
+
+def pack_sums(plan, lead, many, sums, stack, lines):
+    rows, width = plan.rows, plan.width
+    across = width // rows
+    groups = pl.cdiv(many, across)
+    high = groups * across
+    leads = many - 12
+    entry = lax.broadcasted_iota(jnp.int32, (high - 12, width), 0)
+    table = jnp.zeros((high - 12, width), F32)
+    for item in range(plan.items):
+        table = table + jnp.where(entry == lead[item], sums[12 + item : 13 + item], 0.0)
+    top, ups = sums[:8], sums[8:12]
+    for device in range(plan.shards):
+        columns = slice(device * rows, (device + 1) * rows)
+        line, place = divmod(QUART * device * rows, width)
+        parts = [
+            ups[line : line + 1, place + part * rows : place + (part + 1) * rows]
+            for part in range(QUART)
+        ]
+        share = jnp.concatenate([top[:, columns], *parts, table[:, columns]], 0)
+        stack[device * high : (device + 1) * high, :] = share.astype(BF16)
+    entry = lax.broadcasted_iota(jnp.int32, (rows, width), 0)
+    column = lax.broadcasted_iota(jnp.int32, (rows, width), 1)
+    tile = jnp.where(lax.rem(column, rows) == entry, 1.0, 0.0).astype(BF16)
+    line = lax.broadcasted_iota(jnp.int32, (high, width), 0)
+    lane = lax.broadcasted_iota(jnp.int32, (high, width), 1)
+    place = lax.rem(line, across) * rows
+    chosen = (lane >= place) & (lane < place + rows)
+    lines[...] = jnp.zeros_like(lines)
+    for device in range(plan.shards):
+        spread = mm(stack[device * high : (device + 1) * high, :], tile)
+        spread = jnp.where(chosen, spread, 0.0).reshape(groups, across, width)
+        lines[device, 0:groups, :] = jnp.sum(spread, 1)
+
+
+def rest_kernel(
+    plan, many, flag, devs, lead, arr_ref, cot_ref, grad_hidden_ref, small_in, vec, *refs,
+):
+    kept_in, pieces, refs = refs[:6], refs[6 : 6 + plan.shards], refs[6 + plan.shards :]
+    dx_ref, small_ref = refs[:2]
+    grads, refs = refs[2 : 2 + plan.parts], refs[2 + plan.parts :]
+    kept, refs = refs[:6], refs[6:]
+    held, grad_middle_ref, grad_attended, grad_rows, sems, kept_sems, stage, stage_sems, out_sem, stack, lines, packed = refs
+    xin_ref, normed, qkv, attended, middle_ref, probs = kept
+    start_all(first_copies(plan, pieces, devs, held, sems.at[1], pl.ds(OUT, 1)))
+    copies = [
+        pltpu.make_async_copy(source, target, kept_sems.at[index])
+        for index, (source, target) in enumerate(zip(kept_in, kept))
+    ]
+    for index in (4, 3, 2, 5, 1, 0):
+        copies[index].start()
+    start_all(first_copies(plan, pieces, devs, held, sems.at[0], pl.ds(0, OUT)))
+    length = plan.length
+    branch = jnp.where(flag[0] == 0, arr_ref[...], cot_ref[...])
+    out = Stage(plan, stage, stage_sems)
+    small_ref[...] = small_in[...]
+    grad_hidden = grad_hidden_ref[...]
+    copies[4].wait()
     xhat, rstd = normalised(middle_ref[...])
     small_ref[5:6, :] = column_sum(grad_hidden * xhat)
     small_ref[6:7, :] = column_sum(grad_hidden)
@@ -361,17 +457,24 @@
     grad_middle_ref[...] = grad_middle
     attn_grad = grad_middle.astype(BF16)
     small_ref[4:5, :] = column_sum(attn_grad)
-    grad_attended[...] = mm_nt(attn_grad, block_of(plan, held1, OUT)).astype(BF16)
-    out.put(mm_tn(attended[...], attn_grad), copies_of(OUT))
+    wait_bytes(held.at[pl.ds(OUT, 1)], sems.at[1])
+    grad_attended[...] = mm_nt(attn_grad, block_of(plan, held, OUT)).astype(BF16)
+    copies[3].wait()
+    out.put(mm_tn(attended[...], attn_grad), slot_copies(plan, devs, grads, OUT))
+    copies[2].wait()
+    copies[5].wait()
     attention_back(plan, probs, qkv, grad_attended, grad_rows)
+    copies[1].wait()
+    copies[0].wait()
+    wait_bytes(held.at[pl.ds(0, OUT)], sems.at[0])
     grad_normed = None
     for part in range(OUT):
         rows = grad_rows[:, columns_of(plan, part)]
-        out.put(mm_tn(normed[...], rows), copies_of(part))
-        term = mm_nt(rows, block_of(plan, held1, part))
+        term = mm_nt(rows, block_of(plan, held, part))
         grad_normed = term if grad_normed is None else grad_normed + term
         if part != 1:
             small_ref[2 + part // 2 : 3 + part // 2, :] = column_sum(rows)
+        out.put(mm_tn(normed[...], rows), slot_copies(plan, devs, grads, part))
     xhat, rstd = normalised(xin_ref[...].astype(F32))
     small_ref[0:1, :] = column_sum(grad_normed * xhat)
     small_ref[1:2, :] = column_sum(grad_normed)
@@ -380,32 +483,141 @@
             grad_normed[item * length : (item + 1) * length]
         )
     dx_ref[...] = grad_middle_ref[...] + norm_back(grad_normed, xhat, rstd, vec[0:1, :])
+    if plan.parts == 2:
+        pack_sums(plan, lead, many, small_ref[...], stack, lines)
+        packed[...] = lines[...].astype(BF16)
+        each = plan.shards // plan.parts
+        start_all(
+            [
+                pltpu.make_async_copy(
+                    packed.at[devs[slot]],
+                    grads[slot // each].at[slot % each, pl.ds(FIRST * plan.rows, EXTRA)],
+                    out_sem.at[0],
+                )
+                for slot in range(plan.shards)
+            ]
+        )
+        wait_bytes(packed, out_sem.at[0])
     out.drain()
 
 
-def pack_kernel(qkv_ref, out_ref, up_ref, down_ref, first_ref, second_ref):
+def pack_kernel(qkv_ref, out_ref, up_ref, down_ref, *refs):
     rows, width = out_ref.shape
+    vectors, (up_bias, table, first_ref, second_ref, small, wide) = refs[:8], refs[8:]
+    for index, vector in enumerate(vectors):
+        small[index : index + 1, :] = vector[...]
+    for part in range(QUART):
+        small[8 + part : 9 + part, :] = up_bias[:, part * rows : (part + 1) * rows]
+    many = 12 + table.shape[0]
+    small[12:many, :] = table[...]
+    across = width // rows
+    wide[...] = jnp.zeros_like(wide)
+    for index in range(many):
+        line, place = divmod(index, across)
+        wide[line : line + 1, place * rows : (place + 1) * rows] = small[index : index + 1, :]
     for part in range(OUT):
-        first_ref[part] = qkv_ref[:, part * width : (part + 1) * width].astype(BF16)
-    first_ref[OUT] = out_ref[...].astype(BF16)
+        first_ref[part * rows : (part + 1) * rows, :] = qkv_ref[:, part * width : (part + 1) * width].astype(BF16)
+    first_ref[OUT * rows : FIRST * rows, :] = out_ref[...].astype(BF16)
+    first_ref[FIRST * rows :, :] = wide[...].astype(BF16)
     for part in range(QUART):
         second_ref[part] = up_ref[:, part * width : (part + 1) * width].astype(BF16)
         second_ref[QUART + part] = down_ref[part * rows : (part + 1) * rows, :].astype(BF16)
 
 
-def unpack_kernel(grads_ref, qkv_ref, out_ref, up_ref, down_ref):
+def vectors_kernel(plan, many, devs, *refs):
+    pieces, (out_ref, lines, spread, sem) = refs[: plan.shards], refs[plan.shards :]
+    rows, width = plan.rows, plan.width
+    across = width // rows
+    groups = pl.cdiv(many, across)
+    start_all(
+        [
+            pltpu.make_async_copy(piece.at[pl.ds(FIRST * rows, EXTRA)], lines.at[slot], sem.at[0])
+            for slot, piece in enumerate(pieces)
+        ]
+    )
+    wait_bytes(lines, sem.at[0])
+    line = lax.broadcasted_iota(jnp.int32, (across, width), 0)
+    lane = lax.broadcasted_iota(jnp.int32, (across, width), 1)
+    chosen = (lane >= line * rows) & (lane < (line + 1) * rows)
+    for slot in range(plan.shards):
+        values = lines[slot].astype(F32)
+        for group in range(groups):
+            at = (slot * groups + group) * across
+            picked = jnp.where(chosen, jnp.broadcast_to(values[group : group + 1], chosen.shape), 0.0)
+            spread[at : at + across, :] = picked.astype(BF16)
+    source = lax.broadcasted_iota(jnp.int32, (width, rows), 0)
+    target = lax.broadcasted_iota(jnp.int32, (width, rows), 1)
+    fold = sum(jnp.where(source == target + place * rows, 1.0, 0.0) for place in range(across))
+    narrow = mm(spread[...], fold.astype(BF16)).astype(BF16)
+    entry = lax.broadcasted_iota(jnp.int32, (rows, width), 0)
+    column = lax.broadcasted_iota(jnp.int32, (rows, width), 1)
+    total = None
+    for slot in range(plan.shards):
+        at = slot * groups * across
+        place = jnp.where(column == entry + devs[slot] * rows, 1.0, 0.0).astype(BF16)
+        term = mm(narrow[at : at + groups * across], place)
+        total = term if total is None else total + term
+    out_ref[...] = total
+
+
+def unpack_kernel(grads_ref, up_ref, down_ref):
     _, rows, width = grads_ref.shape
-    for part in range(OUT):
-        qkv_ref[:, part * width : (part + 1) * width] = grads_ref[part].astype(F32)
-    out_ref[...] = grads_ref[OUT].astype(F32)
     for part in range(QUART):
-        up_ref[:, part * width : (part + 1) * width] = grads_ref[FIRST + part].astype(F32)
-        down_ref[part * rows : (part + 1) * rows, :] = grads_ref[FIRST + QUART + part].astype(F32)
+        up_ref[:, part * width : (part + 1) * width] = grads_ref[part].astype(F32)
+        down_ref[part * rows : (part + 1) * rows, :] = grads_ref[QUART + part].astype(F32)
+
+
+def add_kernel(work, *refs):
+    outs, at = refs[len(refs) - len(work) :], 0
+    for (terms, first), out in zip(work, outs):
+        rows = out.shape[0] // terms
+        came = refs[at + 2 * terms] if first is not None else None
+        for term in range(terms):
+            low = term * rows
+            value = refs[at][0].astype(F32) + refs[at + 1][0].astype(F32)
+            if came is not None and first <= low < first + came.shape[0]:
+                value = value + came[low - first : low - first + rows, :].astype(F32)
+            out[low : low + rows, :] = value.astype(BF16)
+            at += 2
+        at += came is not None
+
+
+def total_kernel(terms, many, *refs):
+    pairs, (ahead, behind) = refs[: 2 * terms], refs[2 * terms : 2 * terms + 2]
+    outs = refs[2 * terms + 2 :]
+    high, width = pairs[0].shape[1:]
+
+    def rows_of(low, count):
+        term, first = divmod(low, high)
+        value = pairs[2 * term][0, first : first + count, :].astype(F32)
+        value = value + pairs[2 * term + 1][0, first : first + count, :].astype(F32)
+        came = ahead[low : low + count, :].astype(F32) + behind[low : low + count, :].astype(F32)
+        return value + came
+
+    rows = (high - (EXTRA if many else 0)) // FIRST
+    low = 0
+    for out in outs[:2]:
+        for row in range(out.shape[0] // rows):
+            for column in range(out.shape[1] // width):
+                out[row * rows : (row + 1) * rows, column * width : (column + 1) * width] = rows_of(low, rows)
+                low += rows
+    if many:
+        vectors, (up_bias, table, small) = outs[2:10], outs[10:]
+        lines = rows_of(low, EXTRA)
+        for index in range(many):
+            line, place = divmod(index, width // rows)
+            small[index : index + 1, :] = lines[line : line + 1, place * rows : (place + 1) * rows]
+        for index, vector in enumerate(vectors):
+            vector[...] = small[index : index + 1, :]
+        for part in range(QUART):
+            up_bias[:, part * rows : (part + 1) * rows] = small[8 + part : 9 + part, :]
+        table[...] = small[12:many, :]
 
 
 SMEM = pl.BlockSpec(memory_space=pltpu.SMEM)
 VMEM = pl.BlockSpec(memory_space=pltpu.VMEM)
 HBM = pl.BlockSpec(memory_space=pltpu.HBM)
+ANY = pl.BlockSpec(memory_space=pl.ANY)
 
 
 def kept_shapes(plan):
@@ -467,6 +679,25 @@
     )
 
 
+def run_vectors(plan, many, devs, pieces):
+    groups = pl.cdiv(many, plan.width // plan.rows) * (plan.width // plan.rows)
+    return call(
+        functools.partial(vectors_kernel, plan, many),
+        jax.ShapeDtypeStruct((groups, plan.width), F32),
+        [SMEM] + [HBM] * len(pieces),
+        VMEM,
+        [
+            pltpu.VMEM((plan.shards, EXTRA, plan.width), BF16),
+            pltpu.VMEM((plan.shards * groups, plan.width), BF16),
+            pltpu.SemaphoreType.DMA((1,)),
+        ],
+        "vectors",
+        (plan.width * plan.width * plan.rows, plan.width * plan.width * 4),
+        12,
+        (devs, *pieces),
+    )
+
+
 def run_mlp(plan, middle, hidden, vec, gathered):
     block = plan.width * plan.width
     return call(
@@ -474,7 +705,7 @@
         jax.ShapeDtypeStruct(hidden.shape, BF16),
         [VMEM, VMEM, VMEM, HBM],
         VMEM,
-        [held_blocks(plan, SECOND), pltpu.SemaphoreType.DMA((SECOND,))],
+        [held_blocks(plan, SECOND), pltpu.SemaphoreType.DMA((QUART,)), pltpu.SemaphoreType.DMA((QUART,))],
         "mlp",
         (SECOND * block * plan.tokens, SECOND * block * 2),
         16,
@@ -482,57 +713,149 @@
     )
 
 
-def run_load(plan, devs, after, gathered, pieces):
+def run_load(plan, devs, after, firsts, gathered):
     block = plan.width * plan.width
     return call(
         functools.partial(load_kernel, plan),
         [held_blocks(plan, FIRST), held_blocks(plan, SECOND)],
-        [SMEM, pl.BlockSpec(memory_space=pl.ANY)] + [HBM] * (1 + len(pieces)),
+        [SMEM, ANY] + [HBM] * (1 + len(firsts)),
         [VMEM, VMEM],
-        [pltpu.SemaphoreType.DMA((2,))],
+        [pltpu.SemaphoreType.DMA((2,)), pltpu.SemaphoreType.DMA((QUART,))],
         "load",
         (0, (FIRST + SECOND) * block * 4),
         2,
-        (devs, after, gathered, *pieces),
+        (devs, after, gathered, *firsts),
     )
 
 
 def run_chain(plan, lengths, flag, x, recv, cot, vec, held1, held2):
     shapes = kept_shapes(plan)
     block = plan.width * plan.width
+    rest = [shapes[index] for index in (0, 0, 1, 2, 3, 5)]
     return call(
         functools.partial(chain_kernel, plan),
-        [of(shapes[0]), inside(shapes[0]), of(shapes[0])] + [inside(shape) for shape in shapes],
+        [of(shapes[0]), of(shapes[0])]
+        + [inside(shapes[index]) for index in (4, 6, 7)]
+        + [pltpu.HBM(*shape) for shape in rest],
         [SMEM] * 2 + [VMEM] * 6,
-        [VMEM] * (3 + len(shapes)),
-        [inside(shapes[0]), inside(shapes[1])],
+        [VMEM] * 5 + [HBM] * len(rest),
+        [inside(shape) for shape in rest]
+        + [inside(shapes[0]), inside(shapes[1]), pltpu.SemaphoreType.DMA((len(rest),))],
         "chain",
         (24 * block * plan.tokens, 12 * block),
-        10,
+        14,
         (lengths, flag, x, recv, cot, vec, held1, held2),
     )
 
 
-def run_backward(plan, flag, arriving, cot, xin, vec, held1, held2, kept):
+def grad_shapes(plan, extra=0):
+    rows = FIRST * plan.rows + (extra if plan.parts == 2 else 0)
+    return [pltpu.HBM((plan.shards // plan.parts, rows, plan.width), BF16)] * plan.parts
+
+
+def stage_scratch(plan):
+    return [
+        pltpu.VMEM((2, plan.shards, plan.rows, plan.width), BF16),
+        pltpu.SemaphoreType.DMA((2,)),
+    ]
+
+
+def run_mlp_back(plan, flag, arriving, cot, held2, hidden, act, slope):
     shapes = kept_shapes(plan)
     block = plan.width * plan.width
-    stage = (2, plan.shards, plan.rows, plan.width)
     return call(
-        functools.partial(backward_kernel, plan),
+        functools.partial(mlp_back_kernel, plan),
         [
             of(shapes[3]),
             jax.ShapeDtypeStruct((16, plan.width), F32),
-            pltpu.HBM((plan.shards, FIRST + SECOND, plan.rows, plan.width), BF16),
+            pltpu.HBM((plan.shards, SECOND, plan.rows, plan.width), BF16),
         ],
-        [SMEM] + [VMEM] * (6 + len(kept)),
+        [SMEM] + [VMEM] * 6,
         [VMEM, VMEM, HBM],
-        [inside(shapes[index]) for index in (6, 3, 0, 1)]
-        + [pltpu.VMEM(stage, BF16), pltpu.SemaphoreType.DMA((2,))],
-        "backward",
-        (24 * block * plan.tokens, 12 * block * 2),
-        12,
-        (flag, arriving, cot, xin, vec, held1, held2, *kept),
-    )
+        [inside(shapes[6])] + stage_scratch(plan),
+        "mlp_back",
+        (2 * SECOND * block * plan.tokens, SECOND * block * 2),
+        10,
+        (flag, arriving, cot, held2, hidden, act, slope),
+    )
+
+
+def run_rest(plan, many, flag, devs, lead, arriving, cot, grad_hidden, small, vec, kept, pieces):
+    shapes = kept_shapes(plan)
+    block = plan.width * plan.width
+    across = plan.width // plan.rows
+    high = pl.cdiv(many, across) * across
+    lines = (plan.shards, EXTRA, plan.width)
+    rest = [shapes[index] for index in (0, 0, 1, 2, 3, 5)]
+    input_grad, small, *grads = call(
+        functools.partial(rest_kernel, plan, many),
+        [of(shapes[3]), jax.ShapeDtypeStruct((16, plan.width), F32)] + grad_shapes(plan, EXTRA),
+        [SMEM] * 3 + [VMEM] * 5 + [HBM] * (len(rest) + len(pieces)),
+        [VMEM] * 2 + [HBM] * plan.parts,
+        [inside(shape) for shape in rest]
+        + [held_blocks(plan, FIRST)]
+        + [inside(shapes[index]) for index in (3, 0, 1)]
+        + [pltpu.SemaphoreType.DMA((2,)), pltpu.SemaphoreType.DMA((len(rest),))]
+        + stage_scratch(plan)
+        + [pltpu.SemaphoreType.DMA((1,)), pltpu.VMEM((plan.shards * high, plan.rows), BF16)]
+        + [pltpu.VMEM(lines, F32), pltpu.VMEM(lines, BF16)],
+        "rest",
+        (2 * FIRST * block * plan.tokens, 2 * FIRST * block * 2),
+        26,
+        (flag, devs, lead, arriving, cot, grad_hidden, small, vec, *kept, *pieces),
+    )
+    return input_grad, small, grads
+
+
+def run_add(work, beside):
+    specs, args, plans, outs = [], [], [], []
+    for slot, terms, came in work:
+        _, rows, width = terms[0][0].shape
+        for pair in terms:
+            one = pl.BlockSpec((1, rows, width), lambda index, slot=slot: (slot, 0, 0))
+            specs += [one, one]
+            args += [pltpu.with_memory_space_constraint(array, pltpu.HBM) for array in pair]
+        first = None
+        if came is not None:
+            specs.append(pl.BlockSpec(came.shape, lambda index: (0, 0)))
+            args.append(came)
+            alone = came.shape[0] == len(terms) * rows
+            first = 0 if alone or not outs else rows
+        plans.append((len(terms), first))
+        outs.append((len(terms) * rows, width))
+    kernel = functools.partial(add_kernel, plans)
+    return pl.pallas_call(
+        lambda *refs: kernel(*refs[len(beside) :]),
+        out_shape=[jax.ShapeDtypeStruct(shape, BF16) for shape in outs],
+        grid=(1,),
+        in_specs=[ANY] * len(beside) + specs,
+        out_specs=[pl.BlockSpec(shape, lambda index: (0, 0)) for shape in outs],
+        compiler_params=pltpu.CompilerParams(vmem_limit_bytes=14 * 1024 * 1024),
+        name="add",
+    )(*beside, *args)
+
+
+def run_total(one, many, shapes):
+    args = [
+        pltpu.with_memory_space_constraint(array, pltpu.HBM) for pair in one.terms for array in pair
+    ]
+    _, rows, width = args[0].shape
+    first = pl.BlockSpec((1, rows, width), lambda index: (0, 0, 0))
+    whole = pl.BlockSpec((len(one.terms) * rows, width), lambda index: (0, 0))
+    return pl.pallas_call(
+        functools.partial(total_kernel, len(one.terms), many),
+        out_shape=[jax.ShapeDtypeStruct(shape, F32) for shape in shapes],
+        grid=(1,),
+        in_specs=[first] * len(args) + [whole] * 2,
+        out_specs=[pl.BlockSpec(shape, lambda index: (0, 0)) for shape in shapes],
+        scratch_shapes=[pltpu.VMEM((many, shapes[2][1]), F32)] if many else [],
+        compiler_params=pltpu.CompilerParams(vmem_limit_bytes=14 * 1024 * 1024),
+        name="total",
+    )(*args, *one.carried)
+
+
+def after(value, *others):
+    return lax.optimization_barrier((value, *others))[0]
 
 
 def shifted(value, axis, steps):
@@ -541,40 +864,9 @@
     return lax.ppermute(value, axis, [(source, source + steps) for source in range(first, last)])
 
 
-def small_gather(value, count):
-    value = value[None]
-    if count & (count - 1):
-        return lax.all_gather(value, "dp", axis=0, tiled=True)
-    index = lax.axis_index("dp")
-    step = 1
-    while step < count:
-        other = lax.ppermute(value, "dp", [(i, i ^ step) for i in range(count)])
-        value = jnp.where(
-            (index & step) == 0,
-            jnp.concatenate([value, other], 0),
-            jnp.concatenate([other, value], 0),
-        )
-        step *= 2
-    return value
-
-
-def small_scatter(value, count):
-    if count & (count - 1):
-        return lax.psum_scatter(value, "dp", scatter_dimension=0, tiled=True)[0]
-    index = lax.axis_index("dp")
-    step = count // 2
-    while step:
-        upper = (index & step) != 0
-        keep = jnp.where(upper, value[step:], value[:step])
-        send = jnp.where(upper, value[:step], value[step:])
-        value = keep + lax.ppermute(send, "dp", [(i, i ^ step) for i in range(count)])
-        step //= 2
-    return value[0]
-
-
 class Ring:
     def __init__(self, count):
-        self.chips = count // 2
+        self.count, self.chips = count, count // 2
         self.walk = list(range(0, self.chips, 2)) + list(range(self.chips - 1, 0, -2))
         self.order = [2 * chip + core for chip in self.walk for core in range(2)]
         after = self.walk[1:] + self.walk[:1]
@@ -589,25 +881,57 @@
     def slots(self):
         index = lax.axis_index("dp")
         chip, core = index // 2, index % 2
-        place = jnp.where(chip % 2 == 0, chip // 2, self.chips - 1 - chip // 2)
-        ahead = (place + jnp.arange(self.chips, dtype=jnp.int32)) % self.chips
+        place_of = lambda chip: jnp.where(chip % 2 == 0, chip // 2, self.chips - 1 - chip // 2)
+        steps = jnp.arange(self.chips, dtype=jnp.int32)
+        ahead = (place_of(chip) + steps) % self.chips
         chips = jnp.where(ahead < (self.chips + 1) // 2, 2 * ahead, 2 * (self.chips - 1 - ahead) + 1)
-        return jnp.concatenate([2 * chips + core, 2 * chips + 1 - core]).astype(jnp.int32)
-
-    def gather(self, shard, beside):
+        devs = jnp.concatenate([2 * chips + core, 2 * chips + 1 - core]).astype(jnp.int32)
+        return devs
+
+    def step(self, ahead, behind):
+        return lax.ppermute(ahead, "dp", self.onward), lax.ppermute(behind, "dp", self.back)
+
+    def gather(self, shard):
         half = self.chips // 2
-        own = [None] * self.chips
-        own[0] = shard
+        own = [shard] + [None] * (self.chips - 1)
         ahead = behind = shard
-        for step in range(1, half + 1):
-            if step == 3:
-                ahead, beside = lax.optimization_barrier((ahead, beside))
-            ahead = lax.ppermute(ahead, "dp", self.onward)
-            own[self.chips - step] = ahead
-            if step < self.chips - half:
-                behind = lax.ppermute(behind, "dp", self.back)
-                own[step] = behind
-        return own + [lax.ppermute(piece, "dp", self.sibling) for piece in own], beside
+        for step in range(1, half):
+            ahead, behind = self.step(ahead, behind)
+            own[self.chips - step], own[step] = ahead, behind
+            ahead, behind = lax.optimization_barrier((ahead, behind))
+        own[half] = lax.ppermute(ahead, "dp", self.onward)
+        return own
+
+    def siblings(self, pieces):
+        return [lax.ppermute(piece, "dp", self.sibling) for piece in pieces]
+
+
+class RingSum:
+    def __init__(self, ring, terms):
+        self.ring, self.terms = ring, terms
+        self.time = ring.chips // 2
+        self.carried = [None, None]
+
+    def add(self, *beside):
+        opposite = self.time == self.ring.chips // 2
+        work = []
+        for way in range(2):
+            slot = self.time if way == 0 else self.ring.chips - self.time
+            terms = self.terms
+            if opposite:
+                terms = self.terms[way : way + 1]
+            if terms:
+                work.append((way, slot, terms, self.carried[way]))
+        sums = run_add([entry[1:] for entry in work], beside)
+        for entry, value in zip(work, sums):
+            self.carried[entry[0]] = value
+        return sums[0]
+
+    def send(self):
+        for way, route in enumerate((self.ring.onward, self.ring.back)):
+            if self.carried[way] is not None:
+                self.carried[way] = lax.ppermute(self.carried[way], "dp", route)
+        self.time -= 1
 
 
 def body(
@@ -625,38 +949,27 @@
     x, cot = flat(block_input), flat(cotangent)
     lens, lead = lengths.reshape(items), leads.reshape(items)
 
-    small = jnp.concatenate(
-        [
-            norm_gain1, norm_bias1, query_bias, value_bias, out_bias, norm_gain2, norm_bias2, down_bias,
-            up_bias.reshape(4, rows), lead_table[0].T,
-        ],
-        0,
-    ).astype(BF16)
-    small = small_gather(small, count)
-    wide = small.transpose(1, 0, 2).reshape(12 + leads_count, width).astype(F32)
-    vec = jnp.concatenate(
-        [wide[:8], small[:, 8:12].reshape(4, width).astype(F32)]
-        + [lax.dynamic_slice_in_dim(wide, 12 + lead[item], 1, 0) for item in range(items)]
-        + [jnp.zeros((4 - items, width), F32)],
-        0,
-    )
-
-    aligned = rows % 16 == 0 and count % 4 == 0
+    vectors = (
+        norm_gain1, norm_bias1, query_bias, value_bias, out_bias, norm_gain2, norm_bias2, down_bias
+    )
+    many = 12 + leads_count
+    aligned = rows % 16 == 0 and count % 4 == 0 and pl.cdiv(many, width // rows) <= EXTRA
     if aligned:
         ring = Ring(count)
         first, second = pl.pallas_call(
             pack_kernel,
-            out_shape=[
-                jax.ShapeDtypeStruct((FIRST, rows, width), BF16),
-                jax.ShapeDtypeStruct((SECOND, rows, width), BF16),
-            ],
+            out_shape=[jax.ShapeDtypeStruct((FIRST * rows + EXTRA, width), BF16)]
+            + [jax.ShapeDtypeStruct((SECOND, rows, width), BF16)],
+            scratch_shapes=[pltpu.VMEM((many, rows), F32), pltpu.VMEM((EXTRA, width), F32)],
             name="pack",
-        )(qkv_weight[0], out_weight[0], up_weight[0], down_weight[0])
+        )(qkv_weight[0], out_weight[0], up_weight[0], down_weight[0], *vectors, up_bias, lead_table[0].T)
         gathered = lax.all_gather(second, "dp", axis=0, tiled=True, axis_index_groups=[ring.order])
         gathered = gathered.reshape(count, SECOND, rows, width)
-        pieces, vec = ring.gather(first, vec)
+        firsts = ring.gather(first)
+        firsts = firsts + ring.siblings(firsts)
         devs = ring.slots()
-        plan = Plan(count, rows, ring.order, items, length, width)
+        plan = Plan(ring.order, rows, items, length, width)
+        wide = run_vectors(plan, many, devs, firsts)
     else:
         wide_blocks = lambda value: value[0].reshape(rows, -1, width).transpose(1, 0, 2)
         packed = jnp.concatenate(
@@ -664,7 +977,7 @@
         )
         everything = lax.all_gather(packed.astype(BF16), "dp", axis=0)
         across_blocks = lambda value: value.transpose(1, 0, 2, 3).reshape(-1, width, width)
-        pieces = [across_blocks(everything[:, :FIRST])]
+        firsts = [across_blocks(everything[:, :FIRST])]
         gathered = jnp.concatenate(
             [
                 across_blocks(everything[:, FIRST : FIRST + QUART]),
@@ -673,77 +986,92 @@
             0,
         )[None]
         devs = jnp.zeros((1,), jnp.int32)
-        plan = Plan(1, width, [0], items, length, width)
-
-    middle, hidden = run_attend(plan, lens, flag, devs, x, vec, pieces)
+        plan = Plan([0], width, items, length, width)
+        small = jnp.concatenate([*vectors, up_bias.reshape(4, rows), lead_table[0].T], 0).astype(BF16)
+        wide = lax.all_gather(small, "dp", axis=1, tiled=True).astype(F32)
+
+    vec = jnp.concatenate(
+        [wide[:8], wide[8:12].reshape(4, count, rows).transpose(1, 0, 2).reshape(4, width)]
+        + [lax.dynamic_slice_in_dim(wide, 12 + lead[item], 1, 0) for item in range(items)]
+        + [jnp.zeros((4 - items, width), F32)],
+        0,
+    )
+
+    middle, hidden = run_attend(plan, lens, flag, devs, x, vec, firsts)
     first_out = run_mlp(plan, middle, hidden, vec, gathered)
     recv = shifted(first_out, "section", 1)
-    held1, held2 = run_load(plan, devs, first_out, gathered, pieces)
-    output, xin, first_grad, *kept = run_chain(plan, lens, flag, x, recv, cot, vec, held1, held2)
+    held1, held2 = run_load(plan, devs, first_out, firsts, gathered)
+    output, first_grad, hidden, act, slope, *kept = run_chain(
+        plan, lens, flag, x, recv, cot, vec, held1, held2
+    )
     arriving = shifted(first_grad, "section", -1)
-    input_grad, sums, grads = run_backward(
-        plan, flag, arriving, cot, xin, vec, held1, held2, kept
-    )
-    blocks = FIRST + SECOND
+    grad_hidden, sums, grads2 = run_mlp_back(plan, flag, arriving, cot, held2, hidden, act, slope)
+    input_grad, sums, grads1 = run_rest(
+        plan, many, flag, devs, lead, arriving, cot, grad_hidden, sums, vec, kept, firsts
+    )
     if aligned:
-        grads = lax.psum_scatter(
-            grads.reshape(count * blocks, rows, width),
+        first_sum = RingSum(ring, [(grads1[0], *ring.siblings(grads1[1:]))])
+        while first_sum.time:
+            first_sum.add()
+            first_sum.send()
+        grads2 = lax.psum_scatter(
+            grads2.reshape(count * SECOND, rows, width),
             "dp", scatter_dimension=0, tiled=True, axis_index_groups=[ring.order],
         )
-        shapes = [(rows, OUT * width), (rows, width), (rows, QUART * width), (QUART * rows, width)]
-        grads = pl.pallas_call(
+        grad_up, grad_down = pl.pallas_call(
             unpack_kernel,
-            out_shape=[jax.ShapeDtypeStruct(shape, F32) for shape in shapes],
+            out_shape=[
+                jax.ShapeDtypeStruct((rows, QUART * width), F32),
+                jax.ShapeDtypeStruct((QUART * rows, width), F32),
+            ],
             name="unpack",
-        )(grads)
+        )(grads2)
+        grad_qkv, grad_out, *small_grads = run_total(
+            first_sum, many,
+            [(rows, OUT * width), (rows, width)] + [(1, rows)] * 8 + [(1, QUART * rows), (leads_count, rows)],
+        )
     else:
-        head, tail = grads[0, : FIRST + QUART], grads[0, FIRST + QUART :]
+        split = lambda value: value[0].reshape(-1, count, rows, width).transpose(1, 0, 2, 3)
         grads = jnp.concatenate(
             [
-                head.reshape(-1, count, rows, width).transpose(1, 0, 2, 3),
-                tail.reshape(count, QUART, rows, width),
+                split(grads1[0]),
+                split(grads2[0, :QUART].reshape(1, QUART * width, width)),
+                grads2[0, QUART:].reshape(count, QUART, rows, width),
             ],
             1,
         )
         grads = lax.psum_scatter(grads, "dp", scatter_dimension=0, tiled=False).astype(F32)
         across = lambda value: value.transpose(1, 0, 2).reshape(rows, -1)
-        grads = (
-            across(grads[:OUT]),
-            grads[OUT],
-            across(grads[FIRST : FIRST + QUART]),
-            grads[FIRST + QUART :].reshape(QUART * rows, width),
+        grad_qkv, grad_out = across(grads[:OUT]), grads[OUT]
+        grad_up = across(grads[FIRST : FIRST + QUART])
+        grad_down = grads[FIRST + QUART :].reshape(QUART * rows, width)
+        hot = (jnp.arange(leads_count)[:, None] == lead[None, :]).astype(F32)
+        table = sum(hot[:, item : item + 1] * sums[12 + item : 13 + item] for item in range(items))
+        up_sums = sums[8:12].reshape(count, 4, rows).transpose(1, 0, 2).reshape(4, width)
+        spread = lax.psum_scatter(
+            jnp.concatenate([sums[:8], up_sums, table], 0), "dp", scatter_dimension=1, tiled=True
         )
-    hot = (jnp.arange(leads_count)[:, None] == lead[None, :]).astype(F32)
-    table = sum(hot[:, item : item + 1] * sums[12 + item : 13 + item] for item in range(items))
-    spread = jnp.concatenate(
-        [
-            sums[:8].reshape(8, count, rows).transpose(1, 0, 2),
-            sums[8:12].reshape(count, 4, rows),
-            table.reshape(leads_count, count, rows).transpose(1, 0, 2),
-        ],
-        1,
-    )
-    spread = small_scatter(spread, count)
-
-    vector = lambda index: spread[index : index + 1]
+        small_grads = [spread[index : index + 1] for index in range(8)]
+        small_grads += [spread[8:12].reshape(1, 4 * rows), spread[12:]]
+    vector = small_grads
     shape = (1, micro, local, length, width)
     return (
         output.reshape(shape),
         input_grad.reshape(shape),
-        vector(0),
-        vector(1),
-        spread[12:].T[None],
-        grads[0][None],
-        vector(2),
-        vector(3),
-        grads[1][None],
-        vector(4),
-        vector(5),
-        vector(6),
-        grads[2][None],
-        spread[8:12].reshape(1, 4 * rows),
-        grads[3][None],
-        vector(7),
+        vector[0],
+        vector[1],
+        vector[9].T[None],
+        grad_qkv[None],
+        vector[2],
+        vector[3],
+        grad_out[None],
+        vector[4],
+        vector[5],
+        vector[6],
+        grad_up[None],
+        vector[8],
+        grad_down[None],
+        vector[7],
     )
 
 

time: 249 us -> 237 us (0.952)
  waiting for transfers between devices: 140 us -> 120 us
  Pallas kernels: 54.9 us -> 73.8 us
  other arithmetic: 4.63 us -> 0.09 us
  starting transfers between devices: 24.7 us -> 21.7 us
    reduce_scatter x1, waiting for transfers between devices: 55.5 us -> 1.98 us  [body(): lax.psum_scatter(grads2.reshape(count * SECOND, rows, width), 'dp', scatt...]
    ppermute x23, waiting for transfers between devices: 75 us -> 107 us  [the longest x7 47.6 us: send(): self.carried[way] = lax.ppermute(self.carried[way], 'dp', route)]
    pallas_call x5 -> x7, Pallas kernels: 50.1 us -> 61.3 us  [call(): pl.pallas_call(kernel, out_shape=outs, in_specs=in_specs, out_specs=out_s...]
    pallas_call x2 -> x7, Pallas kernels: 4.81 us -> 12.5 us  [the longest x4 5.66 us: run_add(): pl.pallas_call(lambda *refs: kernel(*refs[len(beside):]), out_shape=[jax....]
    concatenate x6 -> x0, other arithmetic: 3.45 us -> none  [the longest x5 3.41 us: body(): jnp.concatenate([norm_gain1, norm_bias1, query_bias, value_bias, out_bias...]
    ppermute x23, starting transfers between devices: 19.3 us -> 16.4 us  [the longest x7 7.18 us: send(): self.carried[way] = lax.ppermute(self.carried[way], 'dp', route)]
  transfers between devices with their start and end apart: 27 -> 27, of which waited for: 16 -> 19; matrix products, arithmetic and copies ran while one was open for 4% -> 1% of each run, Pallas kernels for 4% -> 16%
where the time goes in v3:
time: 237 us; the launch traced here: 236 us
  waiting for transfers between devices  120 us (51%)
  Pallas kernels  73.8 us (31%)
  starting transfers between devices  21.7 us (9%)
  between operations  17 us (7%)
  local copies, waits for them, and re-layouts  3.69 us (2%)
    pallas_call x7, Pallas kernels, call(): pl.pallas_call(kernel, out_shape=outs, in_specs=in_specs, out_specs=out_s...  61.3 us
    ppermute x7, waiting for transfers between devices, send(): self.carried[way] = lax.ppermute(self.carried[way], 'dp', route)  47.6 us
    ppermute x3, waiting for transfers between devices, step(): lax.ppermute(behind, 'dp', self.back)  29.6 us
    ppermute x1, waiting for transfers between devices, gather(): own[half] = lax.ppermute(ahead, 'dp', self.onward)  14 us
    ppermute x3, waiting for transfers between devices, step(): lax.ppermute(ahead, 'dp', self.onward)  10.5 us
    ppermute x2, waiting for transfers between devices, shifted(): lax.ppermute(value, axis, [(source, source + steps) for source in range(f...  9.39 us
    ppermute x7, starting transfers between devices, send(): self.carried[way] = lax.ppermute(self.carried[way], 'dp', route)  7.18 us
    pallas_call x4, Pallas kernels, run_add(): pl.pallas_call(lambda *refs: kernel(*refs[len(beside):]), out_shape=[jax....  5.66 us
  transfers between devices with their start and end apart: 27, of which 19 were waited for; matrix products, arithmetic and copies ran while one was open for 1% of the time, Pallas kernels for 16%

profile of v3, /device:TPU:0, one launch (start us, length us, event | category | flops | bytes accessed | tf_op | source)
XLA Modules:
  0.0 236.4 jit_solution(6534501459817585051)
XLA Ops:
  7.2 2.6 %pack.1 = (bf16[208,768]{1,0:T(8,128)(2,1)}, bf16[8,48,768]{2,1,0:T(8,128)(2,1)}) custom-call(f32[48,2304]{1,0:T(8,128)} %bitcast.47, f32[48,768]{1,0:T(8,128)} %bitcast.48, f32[48,3072]{1,0:T(8,128)} %bitcast.45, f32[192,768]{1,0:T(8,128)} %bitcast.46, f32[1,48]{1,0:T(1,128)} %refs_0_.1, f32[1,48]{1,0:T(1,128)} %refs_1_.1, f32[1,48]{1,0:T(1,128)} %refs_2_.1, ...), custom_call_target="tpu_custom_call" | custom-call | tf_op jit(solution)/shard_map/pack/pallas_call | solution.py:959
  9.9 3.1 %collective-permute-start.1 = (bf16[208,768]{1,0:T(8,128)(2,1)}, bf16[208,768]{1,0:T(8,128)(2,1)S(1)}, u32[]{:S(2)}, u32[]{:S(2)}) collective-permute-start(bf16[208,768]{1,0:T(8,128)(2,1)} %get-tuple-element.64.refs_0_.refs_6_), channel_id=1, source_target_pairs={{0,4},{1,5},{4,8},{5,9},{8,12},{9,13},{12,14},{13,15},{14,10},{15,... | collective-permute-start | bytes 958472 | tf_op jit(solution)/shard_map/ppermute | solution.py:892
  13.0 8.4 %collective-permute-done.1.refs_7_.refs_13_ = bf16[208,768]{1,0:T(8,128)(2,1)S(1)} collective-permute-done((bf16[208,768]{1,0:T(8,128)(2,1)}, bf16[208,768]{1,0:T(8,128)(2,1)S(1)}, u32[]{:S(2)}, u32[]{:S(2)}) %collective-permute-start.1) | collective-permute-done | bytes 319520 | tf_op jit(solution)/shard_map/ppermute | solution.py:892
  21.4 2.2 collective-permute-done.refs_1_.refs_7_
  23.9 1.7 collective-permute-start.3
  25.7 14.1 %collective-permute-done.2.refs_2_.refs_8_ = bf16[208,768]{1,0:T(8,128)(2,1)S(1)} collective-permute-done((bf16[208,768]{1,0:T(8,128)(2,1)S(1)}, bf16[208,768]{1,0:T(8,128)(2,1)S(1)}, u32[]{:S(2)}, u32[]{:S(2)}) %collective-permute-start.2) | collective-permute-done | bytes 319520 | tf_op jit(solution)/shard_map/ppermute | solution.py:892
  39.9 1.5 collective-permute-start.4
  41.9 0.5 collective-permute-start.14
  42.4 13.3 %collective-permute-done.4.refs_3_.refs_9_ = bf16[208,768]{1,0:T(8,128)(2,1)S(1)} collective-permute-done((bf16[208,768]{1,0:T(8,128)(2,1)S(1)}, bf16[208,768]{1,0:T(8,128)(2,1)S(1)}, u32[]{:S(2)}, u32[]{:S(2)}) %collective-permute-start.4) | collective-permute-done | bytes 319520 | tf_op jit(solution)/shard_map/ppermute | solution.py:892
  55.7 2.0 collective-permute-done.5.refs_5_.refs_11_
  58.2 0.5 collective-permute-start.13
  59.2 14.0 %collective-permute-done.6.refs_4_.refs_10_ = bf16[208,768]{1,0:T(8,128)(2,1)} collective-permute-done((bf16[208,768]{1,0:T(8,128)(2,1)S(1)}, bf16[208,768]{1,0:T(8,128)(2,1)}, u32[]{:S(2)}, u32[]{:S(2)}) %collective-permute-start.6) | collective-permute-done | bytes 319520 | tf_op jit(solution)/shard_map/ppermute | solution.py:902
  73.2 1.3 fusion.2
  77.4 2.8 %vectors.1 = f32[48,768]{1,0:T(8,128)S(1)} custom-call(s32[16]{0:T(128)S(1)} %pad_add_fusion.devs, bf16[208,768]{1,0:T(8,128)(2,1)} %get-tuple-element.64.refs_0_.refs_6_, bf16[208,768]{1,0:T(8,128)(2,1)} %copy-done.6, bf16[208,768]{1,0:T(8,128)(2,1)} %copy-done.7, bf16[208,768]{1,0:T(8,128)(2,1)} %copy-done.9, ...), custom_call_target="tpu_custom_call" | custom-call | flops 56623104 | bytes 2359296 | tf_op jit(solution)/shard_map/vectors/pallas_call | solution.py:646
  80.6 5.5 %attend.1 = (f32[192,768]{1,0:T(8,128)S(1)}, bf16[192,768]{1,0:T(8,128)(2,1)S(1)}) custom-call(s32[2]{0:T(128)S(1)} %bitcast.40, s32[1]{0:T(128)} %bitcast.1.flag, s32[16]{0:T(128)S(1)} %pad_add_fusion.devs, bf16[192,768]{1,0:T(8,128)(2,1)S(1)} %bitcast.37, f32[16,768]{1,0:T(8,128)S(1)} %concatenate.7.vec, ...), custom_call_target="tpu_custom_call" | custom-call | flops 905969664 | bytes 4718592 | tf_op jit(solution)/shard_map/attend/pallas_call | solution.py:646
  86.1 1.8 all-gather.2.cloned.1.call-done
  87.9 6.1 %mlp.1.after = bf16[192,768]{1,0:T(8,128)(2,1)S(1)} custom-call(f32[192,768]{1,0:T(8,128)S(1)} %get-tuple-element.70.middle_ref, bf16[192,768]{1,0:T(8,128)(2,1)S(1)} %get-tuple-element.71.hidden_ref, f32[16,768]{1,0:T(8,128)S(1)} %concatenate.7.vec, bf16[16,8,48,768]{3,2,1,0:T(8,128)(2,1)} %bitcast.42), custom_call_target="tpu_custom_call" | custom-call | flops 1811939328 | bytes 9437184 | tf_op jit(solution)/shard_map/mlp/pallas_call | solution.py:646
  94.0 3.7 %collective-permute-start.15 = (bf16[192,768]{1,0:T(8,128)(2,1)S(1)}, bf16[192,768]{1,0:T(8,128)(2,1)S(1)}, u32[]{:S(2)}, u32[]{:S(2)}) collective-permute-start(bf16[192,768]{1,0:T(8,128)(2,1)S(1)} %mlp.1.after), channel_id=1, source_target_pairs={{0,16},{1,17},{2,18},{3,19},{4,20},{5,21},{6,22},{7,23},{8,24},{9,... | collective-permute-start | bytes 884744 | tf_op jit(solution)/shard_map/ppermute | solution.py:864
  97.7 5.9 %load.1 = (bf16[4,16,48,768]{3,2,1,0:T(8,128)(2,1)S(1)}, bf16[8,16,48,768]{3,2,1,0:T(8,128)(2,1)S(1)}) custom-call(s32[16]{0:T(128)S(1)} %pad_add_fusion.devs, bf16[192,768]{1,0:T(8,128)(2,1)S(1)} %mlp.1.after, bf16[16,8,48,768]{3,2,1,0:T(8,128)(2,1)} %bitcast.43, bf16[208,768]{1,0:T(8,128)(2,1)} %get-tuple-element.64.refs_0_.refs_6_, ...), custom_call_target="tpu_custom_call" | custom-call | bytes 28311552 | tf_op jit(solution)/shard_map/load/pallas_call | solution.py:646
  103.6 0.6 collective-permute-done.15.recv_ref
  104.2 16.8 %chain.1 = (bf16[192,768]{1,0:T(8,128)(2,1)}, bf16[192,768]{1,0:T(8,128)(2,1)S(1)}, bf16[192,768]{1,0:T(8,128)(2,1)S(1)}, bf16[192,3072]{1,0:T(8,128)(2,1)S(1)},...) custom-call(s32[2]{0:T(128)S(1)} %bitcast.41, ...), custom_call_target="tpu_custom_call" | custom-call | flops 5435817984 | bytes 7077888 | tf_op jit(solution)/shard_map/chain/pallas_call | solution.py:646
  121.0 1.5 collective-permute-start.16
  122.5 8.8 %collective-permute-done.16.arr_ref = bf16[192,768]{1,0:T(8,128)(2,1)S(1)} collective-permute-done((bf16[192,768]{1,0:T(8,128)(2,1)S(1)}, bf16[192,768]{1,0:T(8,128)(2,1)S(1)}, u32[]{:S(2)}, u32[]{:S(2)}) %collective-permute-start.16) | collective-permute-done | bytes 294944 | tf_op jit(solution)/shard_map/ppermute | solution.py:864
  131.4 9.2 %mlp_back.1 = (f32[192,768]{1,0:T(8,128)S(1)}, f32[16,768]{1,0:T(8,128)S(1)}, bf16[16,8,48,768]{3,2,1,0:T(8,128)(2,1)}) custom-call(s32[1]{0:T(128)} %bitcast.1.flag, bf16[192,768]{1,0:T(8,128)(2,1)S(1)} %collective-permute-done.16.arr_ref, bf16[192,768]{1,0:T(8,128)(2,1)S(1)} %bitcast.35, bf16[8,16,48,768]{3,2,1,0:T(8,128)(2,1)S(1)} %get-tuple-element.74.held2, ...), custom_call_target="tpu_custom_call" | custom-call | flops 3623878656 | bytes 9437184 | tf_op jit(solution)/shard_map/mlp_back/pallas_call | solution.py:646
  140.7 0.6 copy-done.2
  141.3 14.8 %rest.1 = (f32[192,768]{1,0:T(8,128)}, f32[16,768]{1,0:T(8,128)}, bf16[8,208,768]{2,1,0:T(8,128)(2,1)}, bf16[8,208,768]{2,1,0:T(8,128)(2,1)}) custom-call(s32[1]{0:T(128)} %bitcast.1.flag, s32[16]{0:T(128)S(1)} %pad_add_fusion.devs, s32[2]{0:T(128)S(1)} %bitcast.39, bf16[192,768]{1,0:T(8,128)(2,1)S(1)} %collective-permute-done.16.arr_ref, ...), custom_call_target="tpu_custom_call" | custom-call | flops 1811939328 | bytes 9437184 | tf_op jit(solution)/shard_map/rest/pallas_call | solution.py:646
  156.2 5.2 %collective-permute-done.17.refs_1_.refs_4_ = bf16[8,208,768]{2,1,0:T(8,128)(2,1)S(1)} collective-permute-done((bf16[8,208,768]{2,1,0:T(8,128)(2,1)}, bf16[8,208,768]{2,1,0:T(8,128)(2,1)S(1)}, u32[]{:S(2)}, u32[]{:S(2)}) %collective-permute-start.17) | collective-permute-done | bytes 2555936 | tf_op jit(solution)/shard_map/ppermute | solution.py:906
  161.4 1.5 copy-done.4
  162.9 1.2 add.113
  164.0 0.9 collective-permute-start.18
  165.0 12.4 %collective-permute-done.18.refs_2_ = bf16[208,768]{1,0:T(8,128)(2,1)S(1)} collective-permute-done((bf16[208,768]{1,0:T(8,128)(2,1)S(1)}, bf16[208,768]{1,0:T(8,128)(2,1)S(1)}, u32[]{:S(2)}, u32[]{:S(2)}) %collective-permute-start.18) | collective-permute-done | bytes 319520 | tf_op jit(solution)/shard_map/ppermute | solution.py:933
  177.4 1.5 add.114
  178.8 1.0 collective-permute-start.19
  179.8 1.1 collective-permute-start.20
  180.9 11.2 %collective-permute-done.19.refs_2_ = bf16[208,768]{1,0:T(8,128)(2,1)S(1)} collective-permute-done((bf16[208,768]{1,0:T(8,128)(2,1)S(1)}, bf16[208,768]{1,0:T(8,128)(2,1)S(1)}, u32[]{:S(2)}, u32[]{:S(2)}) %collective-permute-start.19) | collective-permute-done | bytes 319520 | tf_op jit(solution)/shard_map/ppermute | solution.py:933
  192.1 0.7 collective-permute-done.20.refs_5_
  192.9 1.5 add.115
  194.4 1.3 collective-permute-start.21
  195.7 0.7 collective-permute-start.22
  196.5 10.5 %collective-permute-done.21.refs_2_ = bf16[208,768]{1,0:T(8,128)(2,1)S(1)} collective-permute-done((bf16[208,768]{1,0:T(8,128)(2,1)S(1)}, bf16[208,768]{1,0:T(8,128)(2,1)S(1)}, u32[]{:S(2)}, u32[]{:S(2)}) %collective-permute-start.21) | collective-permute-done | bytes 319520 | tf_op jit(solution)/shard_map/ppermute | solution.py:933
  207.0 1.2 collective-permute-done.22.refs_5_
  208.1 1.5 add.116
  209.6 1.8 collective-permute-start.23
  211.7 10.0 %collective-permute-done.23.refs_2_ = bf16[208,768]{1,0:T(8,128)(2,1)S(1)} collective-permute-done((bf16[208,768]{1,0:T(8,128)(2,1)S(1)}, bf16[208,768]{1,0:T(8,128)(2,1)S(1)}, u32[]{:S(2)}, u32[]{:S(2)}) %collective-permute-start.23) | collective-permute-done | bytes 319520 | tf_op jit(solution)/shard_map/ppermute | solution.py:933
  221.7 1.7 collective-permute-done.24.refs_3_
  223.4 2.1 total.1
  225.5 2.0 reduce-scatter.2.cloned.1.call-done.grads_ref
  227.4 2.1 unpack.1
  (61 shorter events, 2.7 us)
Async XLA Ops:
  7.2 80.7 %all-gather.2.cloned.1.call-start = ((), (), s32[]{:S(2)}) async-start(), calls=%async_computation.1 | async-start | bytes 10027008 | tf_op jit(solution)/shard_map/all_gather | solution.py:966
  9.9 217.6 %reduce-scatter.2.cloned.1.call-start = ((), (), s32[]{:S(2)}) async-start(), calls=%async_computation.2 | async-start | bytes 10027008 | tf_op jit(solution)/shard_map/reduce_scatter | solution.py:1017
  9.9 11.5 %collective-permute-start.1 = (bf16[208,768]{1,0:T(8,128)(2,1)}, bf16[208,768]{1,0:T(8,128)(2,1)S(1)}, u32[]{:S(2)}, u32[]{:S(2)}) collective-permute-start(bf16[208,768]{1,0:T(8,128)(2,1)} %get-tuple-element.64.refs_0_.refs_6_), channel_id=1, source_target_pairs={{0,4},{1,5},{4,8},{5,9},{8,12},{9,13},{12,14},{13,15},{14,10},{15,... | collective-permute-start | bytes 958472 | tf_op jit(solution)/shard_map/ppermute | solution.py:892
  13.0 10.6 %collective-permute-start = (bf16[208,768]{1,0:T(8,128)(2,1)}, bf16[208,768]{1,0:T(8,128)(2,1)S(1)}, u32[]{:S(2)}, u32[]{:S(2)}) collective-permute-start(bf16[208,768]{1,0:T(8,128)(2,1)} %get-tuple-element.64.refs_0_.refs_6_), channel_id=1, source_target_pairs={{4,0},{5,1},{8,4},{9,5},{12,8},{13,9},{14,12},{15,13},{10,14},{11,... | collective-permute-start | bytes 958472 | tf_op jit(solution)/shard_map/ppermute | solution.py:892
  21.4 56.0 %copy-start.5 = (bf16[208,768]{1,0:T(8,128)(2,1)}, bf16[208,768]{1,0:T(8,128)(2,1)S(1)}, u32[]{:S(2)}) copy-start(bf16[208,768]{1,0:T(8,128)(2,1)S(1)} %collective-permute-done.1.refs_7_.refs_13_) | copy-start | bytes 958468
  23.6 53.7 %copy-start.6 = (bf16[208,768]{1,0:T(8,128)(2,1)}, bf16[208,768]{1,0:T(8,128)(2,1)S(1)}, u32[]{:S(2)}) copy-start(bf16[208,768]{1,0:T(8,128)(2,1)S(1)} %collective-permute-done.refs_1_.refs_7_) | copy-start | bytes 958468
  23.6 16.2 %collective-permute-start.2 = (bf16[208,768]{1,0:T(8,128)(2,1)S(1)}, bf16[208,768]{1,0:T(8,128)(2,1)S(1)}, u32[]{:S(2)}, u32[]{:S(2)}) collective-permute-start(bf16[208,768]{1,0:T(8,128)(2,1)S(1)} %collective-permute-done.refs_1_.refs_7_), channel_id=1, source_target_pairs={{4,0},{5,1},{8,4},{9,5},{12,8},{13,9},{14,12},{15,13},{10,14},{11,... | collective-permute-start | bytes 958472 | tf_op jit(solution)/shard_map/ppermute | solution.py:892
  23.9 16.0 %collective-permute-start.3 = (bf16[208,768]{1,0:T(8,128)(2,1)S(1)}, bf16[208,768]{1,0:T(8,128)(2,1)S(1)}, u32[]{:S(2)}, u32[]{:S(2)}) collective-permute-start(bf16[208,768]{1,0:T(8,128)(2,1)S(1)} %collective-permute-done.1.refs_7_.refs_13_), channel_id=1, source_target_pairs={{0,4},{1,5},{4,8},{5,9},{8,12},{9,13},{12,14},{13,15},{14,10},{15,... | collective-permute-start | bytes 958472 | tf_op jit(solution)/shard_map/ppermute | solution.py:892
  39.8 37.6 %copy-start.7 = (bf16[208,768]{1,0:T(8,128)(2,1)}, bf16[208,768]{1,0:T(8,128)(2,1)S(1)}, u32[]{:S(2)}) copy-start(bf16[208,768]{1,0:T(8,128)(2,1)S(1)} %collective-permute-done.2.refs_2_.refs_8_) | copy-start | bytes 958468
  39.9 37.5 %copy-start.8 = (bf16[208,768]{1,0:T(8,128)(2,1)}, bf16[208,768]{1,0:T(8,128)(2,1)S(1)}, u32[]{:S(2)}) copy-start(bf16[208,768]{1,0:T(8,128)(2,1)S(1)} %collective-permute-done.3.refs_6_.refs_12_) | copy-start | bytes 958468
  39.9 15.8 %collective-permute-start.4 = (bf16[208,768]{1,0:T(8,128)(2,1)S(1)}, bf16[208,768]{1,0:T(8,128)(2,1)S(1)}, u32[]{:S(2)}, u32[]{:S(2)}) collective-permute-start(bf16[208,768]{1,0:T(8,128)(2,1)S(1)} %collective-permute-done.2.refs_2_.refs_8_), channel_id=1, source_target_pairs={{4,0},{5,1},{8,4},{9,5},{12,8},{13,9},{14,12},{15,13},{10,14},{11,... | collective-permute-start | bytes 958472 | tf_op jit(solution)/shard_map/ppermute | solution.py:892
  41.4 16.3 %collective-permute-start.5 = (bf16[208,768]{1,0:T(8,128)(2,1)S(1)}, bf16[208,768]{1,0:T(8,128)(2,1)S(1)}, u32[]{:S(2)}, u32[]{:S(2)}) collective-permute-start(bf16[208,768]{1,0:T(8,128)(2,1)S(1)} %collective-permute-done.3.refs_6_.refs_12_), channel_id=1, source_target_pairs={{0,4},{1,5},{4,8},{5,9},{8,12},{9,13},{12,14},{13,15},{14,10},{15,... | collective-permute-start | bytes 958472 | tf_op jit(solution)/shard_map/ppermute | solution.py:892
  41.9 16.3 %collective-permute-start.7 = (bf16[208,768]{1,0:T(8,128)(2,1)}, bf16[208,768]{1,0:T(8,128)(2,1)S(1)}, u32[]{:S(2)}, u32[]{:S(2)}) collective-permute-start(bf16[208,768]{1,0:T(8,128)(2,1)} %get-tuple-element.64.refs_0_.refs_6_), channel_id=1, source_target_pairs={{0,1},{1,0},{2,3},{3,2},{4,5},{5,4},{6,7},{7,6},{8,9},{9,8},{10,11... | collective-permute-start | bytes 958472 | tf_op jit(solution)/shard_map/ppermute | solution.py:906
  41.9 16.8 %collective-permute-start.14 = (bf16[208,768]{1,0:T(8,128)(2,1)S(1)}, bf16[208,768]{1,0:T(8,128)(2,1)S(1)}, u32[]{:S(2)}, u32[]{:S(2)}) collective-permute-start(bf16[208,768]{1,0:T(8,128)(2,1)S(1)} %collective-permute-done.1.refs_7_.refs_13_), channel_id=1, source_target_pairs={{0,1},{1,0},{2,3},{3,2},{4,5},{5,4},{6,7},{7,6},{8,9},{9,8},{10,11... | collective-permute-start | bytes 958472 | tf_op jit(solution)/shard_map/ppermute | solution.py:906
  42.4 16.4 %collective-permute-start.8 = (bf16[208,768]{1,0:T(8,128)(2,1)S(1)}, bf16[208,768]{1,0:T(8,128)(2,1)S(1)}, u32[]{:S(2)}, u32[]{:S(2)}) collective-permute-start(bf16[208,768]{1,0:T(8,128)(2,1)S(1)} %collective-permute-done.refs_1_.refs_7_), channel_id=1, source_target_pairs={{0,1},{1,0},{2,3},{3,2},{4,5},{5,4},{6,7},{7,6},{8,9},{9,8},{10,11... | collective-permute-start | bytes 958472 | tf_op jit(solution)/shard_map/ppermute | solution.py:906
  55.7 21.7 %copy-start.9 = (bf16[208,768]{1,0:T(8,128)(2,1)}, bf16[208,768]{1,0:T(8,128)(2,1)S(1)}, u32[]{:S(2)}) copy-start(bf16[208,768]{1,0:T(8,128)(2,1)S(1)} %collective-permute-done.4.refs_3_.refs_9_) | copy-start | bytes 958468
  57.7 19.7 %copy-start.10 = (bf16[208,768]{1,0:T(8,128)(2,1)}, bf16[208,768]{1,0:T(8,128)(2,1)S(1)}, u32[]{:S(2)}) copy-start(bf16[208,768]{1,0:T(8,128)(2,1)S(1)} %collective-permute-done.5.refs_5_.refs_11_) | copy-start | bytes 958468
  57.7 15.5 %collective-permute-start.6 = (bf16[208,768]{1,0:T(8,128)(2,1)S(1)}, bf16[208,768]{1,0:T(8,128)(2,1)}, u32[]{:S(2)}, u32[]{:S(2)}) collective-permute-start(bf16[208,768]{1,0:T(8,128)(2,1)S(1)} %collective-permute-done.5.refs_5_.refs_11_), channel_id=1, source_target_pairs={{0,4},{1,5},{4,8},{5,9},{8,12},{9,13},{12,14},{13,15},{14,10},{15,... | collective-permute-start | bytes 958472 | tf_op jit(solution)/shard_map/ppermute | solution.py:902
  58.2 19.1 %collective-permute-start.9 = (bf16[208,768]{1,0:T(8,128)(2,1)S(1)}, bf16[208,768]{1,0:T(8,128)(2,1)}, u32[]{:S(2)}, u32[]{:S(2)}) collective-permute-start(bf16[208,768]{1,0:T(8,128)(2,1)S(1)} %collective-permute-done.2.refs_2_.refs_8_), channel_id=1, source_target_pairs={{0,1},{1,0},{2,3},{3,2},{4,5},{5,4},{6,7},{7,6},{8,9},{9,8},{10,11... | collective-permute-start | bytes 958472 | tf_op jit(solution)/shard_map/ppermute | solution.py:906
  58.2 19.2 %copy-start.11 = (bf16[208,768]{1,0:T(8,128)(2,1)}, bf16[208,768]{1,0:T(8,128)(2,1)S(1)}, u32[]{:S(2)}) copy-start(bf16[208,768]{1,0:T(8,128)(2,1)S(1)} %collective-permute-done.7.refs_8_.refs_14_) | copy-start | bytes 958468
  58.2 19.1 %collective-permute-start.13 = (bf16[208,768]{1,0:T(8,128)(2,1)S(1)}, bf16[208,768]{1,0:T(8,128)(2,1)}, u32[]{:S(2)}, u32[]{:S(2)}) collective-permute-start(bf16[208,768]{1,0:T(8,128)(2,1)S(1)} %collective-permute-done.3.refs_6_.refs_12_), channel_id=1, source_target_pairs={{0,1},{1,0},{2,3},{3,2},{4,5},{5,4},{6,7},{7,6},{8,9},{9,8},{10,11... | collective-permute-start | bytes 958472 | tf_op jit(solution)/shard_map/ppermute | solution.py:906
  58.7 18.7 %copy-start.12 = (bf16[208,768]{1,0:T(8,128)(2,1)}, bf16[208,768]{1,0:T(8,128)(2,1)S(1)}, u32[]{:S(2)}) copy-start(bf16[208,768]{1,0:T(8,128)(2,1)S(1)} %collective-permute-done.14.refs_15_.refs_21_) | copy-start | bytes 958468
  58.7 18.6 %collective-permute-start.10 = (bf16[208,768]{1,0:T(8,128)(2,1)S(1)}, bf16[208,768]{1,0:T(8,128)(2,1)}, u32[]{:S(2)}, u32[]{:S(2)}) collective-permute-start(bf16[208,768]{1,0:T(8,128)(2,1)S(1)} %collective-permute-done.4.refs_3_.refs_9_), channel_id=1, source_target_pairs={{0,1},{1,0},{2,3},{3,2},{4,5},{5,4},{6,7},{7,6},{8,9},{9,8},{10,11... | collective-permute-start | bytes 958472 | tf_op jit(solution)/shard_map/ppermute | solution.py:906
  58.8 18.4 %copy-start.13 = (bf16[208,768]{1,0:T(8,128)(2,1)}, bf16[208,768]{1,0:T(8,128)(2,1)S(1)}, u32[]{:S(2)}) copy-start(bf16[208,768]{1,0:T(8,128)(2,1)S(1)} %collective-permute-done.8.refs_9_.refs_15_) | copy-start | bytes 958468
  58.8 18.5 %collective-permute-start.12 = (bf16[208,768]{1,0:T(8,128)(2,1)S(1)}, bf16[208,768]{1,0:T(8,128)(2,1)}, u32[]{:S(2)}, u32[]{:S(2)}) collective-permute-start(bf16[208,768]{1,0:T(8,128)(2,1)S(1)} %collective-permute-done.5.refs_5_.refs_11_), channel_id=1, source_target_pairs={{0,1},{1,0},{2,3},{3,2},{4,5},{5,4},{6,7},{7,6},{8,9},{9,8},{10,11... | collective-permute-start | bytes 958472 | tf_op jit(solution)/shard_map/ppermute | solution.py:906
  73.2 4.1 %collective-permute-start.11 = (bf16[208,768]{1,0:T(8,128)(2,1)}, bf16[208,768]{1,0:T(8,128)(2,1)}, u32[]{:S(2)}, u32[]{:S(2)}) collective-permute-start(bf16[208,768]{1,0:T(8,128)(2,1)} %collective-permute-done.6.refs_4_.refs_10_), channel_id=1, source_target_pairs={{0,1},{1,0},{2,3},{3,2},{4,5},{5,4},{6,7},{7,6},{8,9},{9,8},{10,11... | collective-permute-start | bytes 958472 | tf_op jit(solution)/shard_map/ppermute | solution.py:906
  77.3 3.3 %copy-start.1 = (bf16[2,1,96,768]{3,2,1,0:T(8,128)(2,1)S(1)}, bf16[2,1,96,768]{3,2,1,0:T(8,128)(2,1)}, u32[]{:S(2)}) copy-start(bf16[2,1,96,768]{3,2,1,0:T(8,128)(2,1)} %param.18) | copy-start | bytes 884740
  77.3 3.3 %copy-start.3 = (s32[2,1]{0,1:T(1,128)S(1)}, s32[2,1]{0,1:T(1,128)}, u32[]{:S(2)}) copy-start(s32[2,1]{0,1:T(1,128)} %param.20) | copy-start | bytes 28
  94.0 10.2 %copy-start = (bf16[2,1,96,768]{3,2,1,0:T(8,128)(2,1)S(1)}, bf16[2,1,96,768]{3,2,1,0:T(8,128)(2,1)}, u32[]{:S(2)}) copy-start(bf16[2,1,96,768]{3,2,1,0:T(8,128)(2,1)} %param.19) | copy-start | bytes 884740
  94.0 10.2 %collective-permute-start.15 = (bf16[192,768]{1,0:T(8,128)(2,1)S(1)}, bf16[192,768]{1,0:T(8,128)(2,1)S(1)}, u32[]{:S(2)}, u32[]{:S(2)}) collective-permute-start(bf16[192,768]{1,0:T(8,128)(2,1)S(1)} %mlp.1.after), channel_id=1, source_target_pairs={{0,16},{1,17},{2,18},{3,19},{4,20},{5,21},{6,22},{7,23},{8,24},{9,... | collective-permute-start | bytes 884744 | tf_op jit(solution)/shard_map/ppermute | solution.py:864
  121.0 10.4 %collective-permute-start.16 = (bf16[192,768]{1,0:T(8,128)(2,1)S(1)}, bf16[192,768]{1,0:T(8,128)(2,1)S(1)}, u32[]{:S(2)}, u32[]{:S(2)}) collective-permute-start(bf16[192,768]{1,0:T(8,128)(2,1)S(1)} %get-tuple-element.76), channel_id=1, source_target_pairs={{16,0},{17,1},{18,2},{19,3},{20,4},{21,5},{22,6},{23,7},{24,8},{25... | collective-permute-start | bytes 884744 | tf_op jit(solution)/shard_map/ppermute | solution.py:864
  140.6 0.7 copy-start.2
  156.1 5.3 %collective-permute-start.17 = (bf16[8,208,768]{2,1,0:T(8,128)(2,1)}, bf16[8,208,768]{2,1,0:T(8,128)(2,1)S(1)}, u32[]{:S(2)}, u32[]{:S(2)}) collective-permute-start(bf16[8,208,768]{2,1,0:T(8,128)(2,1)} %get-tuple-element.90), channel_id=1, source_target_pairs={{0,1},{1,0},{2,3},{3,2},{4,5},{5,4},{6,7},{7,6},{8,9},{9,8},{10,11... | collective-permute-start | bytes 7667720 | tf_op jit(solution)/shard_map/ppermute | solution.py:906
  161.4 1.5 copy-start.4
  164.0 13.3 %collective-permute-start.18 = (bf16[208,768]{1,0:T(8,128)(2,1)S(1)}, bf16[208,768]{1,0:T(8,128)(2,1)S(1)}, u32[]{:S(2)}, u32[]{:S(2)}) collective-permute-start(bf16[208,768]{1,0:T(8,128)(2,1)S(1)} %add.113), channel_id=1, source_target_pairs={{0,4},{1,5},{4,8},{5,9},{8,12},{9,13},{12,14},{13,15},{14,10},{15,... | collective-permute-start | bytes 958472 | tf_op jit(solution)/shard_map/ppermute | solution.py:933
  178.8 13.3 %collective-permute-start.19 = (bf16[208,768]{1,0:T(8,128)(2,1)S(1)}, bf16[208,768]{1,0:T(8,128)(2,1)S(1)}, u32[]{:S(2)}, u32[]{:S(2)}) collective-permute-start(bf16[208,768]{1,0:T(8,128)(2,1)S(1)} %get-tuple-element.91), channel_id=1, source_target_pairs={{0,4},{1,5},{4,8},{5,9},{8,12},{9,13},{12,14},{13,15},{14,10},{15,... | collective-permute-start | bytes 958472 | tf_op jit(solution)/shard_map/ppermute | solution.py:933
  179.8 13.0 %collective-permute-start.20 = (bf16[208,768]{1,0:T(8,128)(2,1)S(1)}, bf16[208,768]{1,0:T(8,128)(2,1)S(1)}, u32[]{:S(2)}, u32[]{:S(2)}) collective-permute-start(bf16[208,768]{1,0:T(8,128)(2,1)S(1)} %get-tuple-element.92), channel_id=1, source_target_pairs={{4,0},{5,1},{8,4},{9,5},{12,8},{13,9},{14,12},{15,13},{10,14},{11,... | collective-permute-start | bytes 958472 | tf_op jit(solution)/shard_map/ppermute | solution.py:933
  194.4 12.6 %collective-permute-start.21 = (bf16[208,768]{1,0:T(8,128)(2,1)S(1)}, bf16[208,768]{1,0:T(8,128)(2,1)S(1)}, u32[]{:S(2)}, u32[]{:S(2)}) collective-permute-start(bf16[208,768]{1,0:T(8,128)(2,1)S(1)} %get-tuple-element.93), channel_id=1, source_target_pairs={{0,4},{1,5},{4,8},{5,9},{8,12},{9,13},{12,14},{13,15},{14,10},{15,... | collective-permute-start | bytes 958472 | tf_op jit(solution)/shard_map/ppermute | solution.py:933
  195.7 12.4 %collective-permute-start.22 = (bf16[208,768]{1,0:T(8,128)(2,1)S(1)}, bf16[208,768]{1,0:T(8,128)(2,1)S(1)}, u32[]{:S(2)}, u32[]{:S(2)}) collective-permute-start(bf16[208,768]{1,0:T(8,128)(2,1)S(1)} %get-tuple-element.94), channel_id=1, source_target_pairs={{4,0},{5,1},{8,4},{9,5},{12,8},{13,9},{14,12},{15,13},{10,14},{11,... | collective-permute-start | bytes 958472 | tf_op jit(solution)/shard_map/ppermute | solution.py:933
  209.6 12.1 %collective-permute-start.23 = (bf16[208,768]{1,0:T(8,128)(2,1)S(1)}, bf16[208,768]{1,0:T(8,128)(2,1)S(1)}, u32[]{:S(2)}, u32[]{:S(2)}) collective-permute-start(bf16[208,768]{1,0:T(8,128)(2,1)S(1)} %get-tuple-element.95), channel_id=1, source_target_pairs={{0,4},{1,5},{4,8},{5,9},{8,12},{9,13},{12,14},{13,15},{14,10},{15,... | collective-permute-start | bytes 958472 | tf_op jit(solution)/shard_map/ppermute | solution.py:933
  211.4 11.9 %collective-permute-start.24 = (bf16[208,768]{1,0:T(8,128)(2,1)S(1)}, bf16[208,768]{1,0:T(8,128)(2,1)S(1)}, u32[]{:S(2)}, u32[]{:S(2)}) collective-permute-start(bf16[208,768]{1,0:T(8,128)(2,1)S(1)} %get-tuple-element.96), channel_id=1, source_target_pairs={{4,0},{5,1},{8,4},{9,5},{12,8},{13,9},{14,12},{15,13},{10,14},{11,... | collective-permute-start | bytes 958472 | tf_op jit(solution)/shard_map/ppermute | solution.py:933
Sparse Core Ops, SparseCore 0:
  10.2 77.6 all-gather.1
  140.8 86.6 reduce-scatter.1

commit v4 on v3

--- a/solution.py
+++ b/solution.py
@@ -20,6 +20,7 @@
 SECOND = 8
 QUART = 4
 EXTRA = 16
+LOW = 2
 
 
 def mm(left, right):
@@ -76,20 +77,38 @@
         self.order, self.shards, self.rows = order, len(order), rows
         self.items, self.length, self.width = items, length, width
         self.tokens = items * length
+        self.low = LOW * rows
         self.pairs = width // PAIR
         whole = self.shards % QUART == 0
         self.runs = [(0, QUART)] if whole else [(block, 1) for block in range(QUART)]
         self.parts = 2 if self.shards > 1 else 1
 
 
-def first_copies(plan, pieces, devs, held, sem, blocks):
+def slot_pieces(plan, refs):
     if plan.shards == 1:
-        return block_copies(pieces, devs, held, sem, blocks)
+        return [[(0, refs[0])]]
+    refs, slots, half = list(refs), [], plan.shards // 4
+    for slot in range(plan.shards):
+        parts = [(0, refs.pop(0))]
+        if slot % (plan.shards // 2) == half:
+            parts.append((plan.low, refs.pop(0)))
+        slots.append(parts)
+    return slots
+
+
+def piece_rows(parts, row, count):
+    start, ref = [part for part in parts if part[0] <= row][-1]
+    return ref.at[pl.ds(row - start, count)]
+
+
+def first_copies(plan, refs, devs, held, sem, blocks):
+    if plan.shards == 1:
+        return block_copies(refs, devs, held, sem, blocks)
     return [
         pltpu.make_async_copy(
-            piece.at[pl.ds(block * plan.rows, plan.rows)], held.at[block, devs[slot]], sem
+            piece_rows(parts, block * plan.rows, plan.rows), held.at[block, devs[slot]], sem
         )
-        for slot, piece in enumerate(pieces)
+        for slot, parts in enumerate(slot_pieces(plan, refs))
         for block in range(blocks.start, blocks.start + blocks.size)
     ]
 
@@ -107,15 +126,13 @@
     copies = []
     for slot, piece in enumerate(pieces):
         for first, count in plan.runs:
-            row = QUART * devs[slot] + first
-            block = row // plan.shards
-            copies.append(
-                pltpu.make_async_copy(
-                    piece.at[pl.ds(first, count)],
-                    held.at[QUART + block, pl.ds(row % plan.shards, count)],
-                    sems.at[block],
-                )
+            block, row = divmod(QUART * devs[slot] + first, plan.shards)
+            copy = pltpu.make_async_copy(
+                piece.at[pl.ds(first, count)],
+                held.at[QUART + block, pl.ds(row, count)],
+                sems.at[block],
             )
+            copies.append((block, copy))
     return copies
 
 
@@ -245,10 +262,10 @@
 
 def mlp_kernel(plan, middle_ref, hidden_ref, vec, gathered, y_ref, held, sems, down_sems):
     (ups, downs), devs = second_pieces(plan, gathered), plan.order
-    start_all(block_copies(ups, devs, held, sems.at[0], pl.ds(0, 1)))
-    start_all(down_copies(plan, downs, devs, held, down_sems))
-    for part in range(1, QUART):
+    down = down_copies(plan, downs, devs, held, down_sems)
+    for part in range(QUART):
         start_all(block_copies(ups, devs, held, sems.at[part], pl.ds(part, 1)))
+        start_all([copy for block, copy in down if block == part])
 
     def wait(block):
         sem = sems.at[block] if block < QUART else down_sems.at[block - QUART]
@@ -263,7 +280,7 @@
     ups, downs = second_pieces(plan, gathered)
     start_all(first_copies(plan, firsts, devs, held1, sems.at[0], pl.ds(0, FIRST)))
     start_all(block_copies(ups, plan.order, held2, sems.at[1], pl.ds(0, QUART)))
-    start_all(down_copies(plan, downs, plan.order, held2, down_sems))
+    start_all([copy for _, copy in down_copies(plan, downs, plan.order, held2, down_sems)])
     wait_bytes(held1, sems.at[0])
     wait_bytes(held2.at[pl.ds(0, QUART)], sems.at[1])
     for part in range(QUART):
@@ -430,7 +447,8 @@
 def rest_kernel(
     plan, many, flag, devs, lead, arr_ref, cot_ref, grad_hidden_ref, small_in, vec, *refs,
 ):
-    kept_in, pieces, refs = refs[:6], refs[6 : 6 + plan.shards], refs[6 + plan.shards :]
+    count = plan.shards + plan.parts * (plan.parts - 1)
+    kept_in, pieces, refs = refs[:6], refs[6 : 6 + count], refs[6 + count :]
     dx_ref, small_ref = refs[:2]
     grads, refs = refs[2 : 2 + plan.parts], refs[2 + plan.parts :]
     kept, refs = refs[:6], refs[6:]
@@ -524,27 +542,36 @@
         second_ref[QUART + part] = down_ref[part * rows : (part + 1) * rows, :].astype(BF16)
 
 
-def vectors_kernel(plan, many, devs, *refs):
-    pieces, (out_ref, lines, spread, sem) = refs[: plan.shards], refs[plan.shards :]
+def vectors_kernel(plan, many, devs, lead, *refs):
+    pieces, (out_ref, lines, spread, sem) = slot_pieces(plan, refs[:-4]), refs[-4:]
     rows, width = plan.rows, plan.width
     across = width // rows
     groups = pl.cdiv(many, across)
     start_all(
         [
-            pltpu.make_async_copy(piece.at[pl.ds(FIRST * rows, EXTRA)], lines.at[slot], sem.at[0])
-            for slot, piece in enumerate(pieces)
+            pltpu.make_async_copy(piece_rows(parts, FIRST * rows, EXTRA), lines.at[slot], sem.at[0])
+            for slot, parts in enumerate(pieces)
         ]
     )
     wait_bytes(lines, sem.at[0])
     line = lax.broadcasted_iota(jnp.int32, (across, width), 0)
     lane = lax.broadcasted_iota(jnp.int32, (across, width), 1)
     chosen = (lane >= line * rows) & (lane < (line + 1) * rows)
+    up_line = lax.broadcasted_iota(jnp.int32, (QUART, width), 0)
+    up_lane = lax.broadcasted_iota(jnp.int32, (QUART, width), 1)
+    ups = jnp.zeros((QUART, width), F32)
     for slot in range(plan.shards):
         values = lines[slot].astype(F32)
         for group in range(groups):
             at = (slot * groups + group) * across
             picked = jnp.where(chosen, jnp.broadcast_to(values[group : group + 1], chosen.shape), 0.0)
             spread[at : at + across, :] = picked.astype(BF16)
+        first = QUART * rows * devs[slot]
+        there = lax.rem(first, width)
+        moved = jnp.broadcast_to(values[8 // across : 8 // across + 1], (8, width))
+        moved = pltpu.roll(moved, lax.rem(there + width - 8 % across * rows, width), 1)[:QUART]
+        here = (up_line == first // width) & (up_lane >= there) & (up_lane < there + QUART * rows)
+        ups = jnp.where(here, moved, ups)
     source = lax.broadcasted_iota(jnp.int32, (width, rows), 0)
     target = lax.broadcasted_iota(jnp.int32, (width, rows), 1)
     fold = sum(jnp.where(source == target + place * rows, 1.0, 0.0) for place in range(across))
@@ -557,7 +584,13 @@
         place = jnp.where(column == entry + devs[slot] * rows, 1.0, 0.0).astype(BF16)
         term = mm(narrow[at : at + groups * across], place)
         total = term if total is None else total + term
-    out_ref[...] = total
+    out_ref[...] = jnp.zeros_like(out_ref)
+    out_ref[:8, :] = total[:8]
+    out_ref[8 : 8 + QUART, :] = ups
+    entry = lax.broadcasted_iota(jnp.int32, total.shape, 0)
+    for item in range(plan.items):
+        picked = jnp.where(entry == 12 + lead[item], total, 0.0)
+        out_ref[12 + item : 13 + item, :] = jnp.sum(picked, 0, keepdims=True)
 
 
 def unpack_kernel(grads_ref, up_ref, down_ref):
@@ -569,49 +602,43 @@
 
 def add_kernel(work, *refs):
     outs, at = refs[len(refs) - len(work) :], 0
-    for (terms, first), out in zip(work, outs):
-        rows = out.shape[0] // terms
-        came = refs[at + 2 * terms] if first is not None else None
-        for term in range(terms):
-            low = term * rows
-            value = refs[at][0].astype(F32) + refs[at + 1][0].astype(F32)
-            if came is not None and first <= low < first + came.shape[0]:
-                value = value + came[low - first : low - first + rows, :].astype(F32)
-            out[low : low + rows, :] = value.astype(BF16)
-            at += 2
-        at += came is not None
-
-
-def total_kernel(terms, many, *refs):
-    pairs, (ahead, behind) = refs[: 2 * terms], refs[2 * terms : 2 * terms + 2]
-    outs = refs[2 * terms + 2 :]
-    high, width = pairs[0].shape[1:]
+    for (low, high, first), out in zip(work, outs):
+        mine, other = refs[at], refs[at + 1]
+        at += 2
+        cuts, came = [low, high], None
+        if first is not None:
+            came = refs[at]
+            at += 1
+            cuts = sorted({low, first, first + came.shape[0], high})
+        for start, end in zip(cuts, cuts[1:]):
+            value = mine[0, start:end, :].astype(F32) + other[0, start:end, :].astype(F32)
+            if came is not None and first <= start < first + came.shape[0]:
+                value = value + came[start - first : end - first, :].astype(F32)
+            out[start - low : end - low, :] = value.astype(BF16)
+
+
+def total_kernel(many, mine, other, ahead, behind, qkv, out, *refs):
+    width = mine.shape[2]
+    rows = out.shape[0]
 
     def rows_of(low, count):
-        term, first = divmod(low, high)
-        value = pairs[2 * term][0, first : first + count, :].astype(F32)
-        value = value + pairs[2 * term + 1][0, first : first + count, :].astype(F32)
-        came = ahead[low : low + count, :].astype(F32) + behind[low : low + count, :].astype(F32)
-        return value + came
-
-    rows = (high - (EXTRA if many else 0)) // FIRST
-    low = 0
-    for out in outs[:2]:
-        for row in range(out.shape[0] // rows):
-            for column in range(out.shape[1] // width):
-                out[row * rows : (row + 1) * rows, column * width : (column + 1) * width] = rows_of(low, rows)
-                low += rows
-    if many:
-        vectors, (up_bias, table, small) = outs[2:10], outs[10:]
-        lines = rows_of(low, EXTRA)
-        for index in range(many):
-            line, place = divmod(index, width // rows)
-            small[index : index + 1, :] = lines[line : line + 1, place * rows : (place + 1) * rows]
-        for index, vector in enumerate(vectors):
-            vector[...] = small[index : index + 1, :]
-        for part in range(QUART):
-            up_bias[:, part * rows : (part + 1) * rows] = small[8 + part : 9 + part, :]
-        table[...] = small[12:many, :]
+        here = slice(low, low + count)
+        value = mine[0, here, :].astype(F32) + other[0, here, :].astype(F32)
+        return value + (ahead[here, :].astype(F32) + behind[here, :].astype(F32))
+
+    for part in range(OUT):
+        qkv[:, part * width : (part + 1) * width] = rows_of(part * rows, rows)
+    out[...] = rows_of(OUT * rows, rows)
+    vectors, (up_bias, table, small) = refs[:8], refs[8:]
+    lines = rows_of(FIRST * rows, EXTRA)
+    for index in range(many):
+        line, place = divmod(index, width // rows)
+        small[index : index + 1, :] = lines[line : line + 1, place * rows : (place + 1) * rows]
+    for index, vector in enumerate(vectors):
+        vector[...] = small[index : index + 1, :]
+    for part in range(QUART):
+        up_bias[:, part * rows : (part + 1) * rows] = small[8 + part : 9 + part, :]
+    table[...] = small[12:many, :]
 
 
 SMEM = pl.BlockSpec(memory_space=pltpu.SMEM)
@@ -679,12 +706,12 @@
     )
 
 
-def run_vectors(plan, many, devs, pieces):
+def run_vectors(plan, many, devs, lead, pieces):
     groups = pl.cdiv(many, plan.width // plan.rows) * (plan.width // plan.rows)
     return call(
         functools.partial(vectors_kernel, plan, many),
-        jax.ShapeDtypeStruct((groups, plan.width), F32),
-        [SMEM] + [HBM] * len(pieces),
+        jax.ShapeDtypeStruct((16, plan.width), F32),
+        [SMEM, SMEM] + [HBM] * len(pieces),
         VMEM,
         [
             pltpu.VMEM((plan.shards, EXTRA, plan.width), BF16),
@@ -694,7 +721,7 @@
         "vectors",
         (plan.width * plan.width * plan.rows, plan.width * plan.width * 4),
         12,
-        (devs, *pieces),
+        (devs, lead, *pieces),
     )
 
 
@@ -807,48 +834,44 @@
     return input_grad, small, grads
 
 
-def run_add(work, beside):
+def run_add(mine, other, work):
+    _, rows, width = mine.shape
+    mine, other = (pltpu.with_memory_space_constraint(array, pltpu.HBM) for array in (mine, other))
     specs, args, plans, outs = [], [], [], []
-    for slot, terms, came in work:
-        _, rows, width = terms[0][0].shape
-        for pair in terms:
-            one = pl.BlockSpec((1, rows, width), lambda index, slot=slot: (slot, 0, 0))
-            specs += [one, one]
-            args += [pltpu.with_memory_space_constraint(array, pltpu.HBM) for array in pair]
+    for way, (slot, low, high, came) in enumerate(work):
+        one = pl.BlockSpec((1, rows, width), lambda index, slot=slot: (slot, 0, 0))
+        specs += [one, one]
+        args += [mine, other]
         first = None
         if came is not None:
             specs.append(pl.BlockSpec(came.shape, lambda index: (0, 0)))
             args.append(came)
-            alone = came.shape[0] == len(terms) * rows
-            first = 0 if alone or not outs else rows
-        plans.append((len(terms), first))
-        outs.append((len(terms) * rows, width))
-    kernel = functools.partial(add_kernel, plans)
+            first = rows - came.shape[0] if way else 0
+        plans.append((low, high, first))
+        outs.append((high - low, width))
     return pl.pallas_call(
-        lambda *refs: kernel(*refs[len(beside) :]),
+        functools.partial(add_kernel, plans),
         out_shape=[jax.ShapeDtypeStruct(shape, BF16) for shape in outs],
         grid=(1,),
-        in_specs=[ANY] * len(beside) + specs,
+        in_specs=specs,
         out_specs=[pl.BlockSpec(shape, lambda index: (0, 0)) for shape in outs],
         compiler_params=pltpu.CompilerParams(vmem_limit_bytes=14 * 1024 * 1024),
         name="add",
-    )(*beside, *args)
+    )(*args)
 
 
 def run_total(one, many, shapes):
-    args = [
-        pltpu.with_memory_space_constraint(array, pltpu.HBM) for pair in one.terms for array in pair
-    ]
-    _, rows, width = args[0].shape
+    args = [pltpu.with_memory_space_constraint(array, pltpu.HBM) for array in (one.mine, one.other)]
+    _, rows, width = one.mine.shape
     first = pl.BlockSpec((1, rows, width), lambda index: (0, 0, 0))
-    whole = pl.BlockSpec((len(one.terms) * rows, width), lambda index: (0, 0))
+    whole = pl.BlockSpec((rows, width), lambda index: (0, 0))
     return pl.pallas_call(
-        functools.partial(total_kernel, len(one.terms), many),
+        functools.partial(total_kernel, many),
         out_shape=[jax.ShapeDtypeStruct(shape, F32) for shape in shapes],
         grid=(1,),
-        in_specs=[first] * len(args) + [whole] * 2,
+        in_specs=[first, first, whole, whole],
         out_specs=[pl.BlockSpec(shape, lambda index: (0, 0)) for shape in shapes],
-        scratch_shapes=[pltpu.VMEM((many, shapes[2][1]), F32)] if many else [],
+        scratch_shapes=[pltpu.VMEM((many, shapes[2][1]), F32)],
         compiler_params=pltpu.CompilerParams(vmem_limit_bytes=14 * 1024 * 1024),
         name="total",
     )(*args, *one.carried)
@@ -891,46 +914,40 @@
     def step(self, ahead, behind):
         return lax.ppermute(ahead, "dp", self.onward), lax.ppermute(behind, "dp", self.back)
 
-    def gather(self, shard):
+    def gather(self, shard, low):
         half = self.chips // 2
-        own = [shard] + [None] * (self.chips - 1)
+        own = [[shard]] + [None] * (self.chips - 1)
         ahead = behind = shard
         for step in range(1, half):
             ahead, behind = self.step(ahead, behind)
-            own[self.chips - step], own[step] = ahead, behind
+            own[self.chips - step], own[step] = [ahead], [behind]
             ahead, behind = lax.optimization_barrier((ahead, behind))
-        own[half] = lax.ppermute(ahead, "dp", self.onward)
-        return own
+        own[half] = list(self.step(ahead[:low], behind[low:]))
+        return [piece for pieces in own for piece in pieces]
 
     def siblings(self, pieces):
         return [lax.ppermute(piece, "dp", self.sibling) for piece in pieces]
 
 
 class RingSum:
-    def __init__(self, ring, terms):
-        self.ring, self.terms = ring, terms
+    def __init__(self, ring, mine, other, low):
+        self.ring, self.mine, self.other, self.low = ring, mine, other, low
         self.time = ring.chips // 2
         self.carried = [None, None]
 
-    def add(self, *beside):
-        opposite = self.time == self.ring.chips // 2
-        work = []
-        for way in range(2):
-            slot = self.time if way == 0 else self.ring.chips - self.time
-            terms = self.terms
-            if opposite:
-                terms = self.terms[way : way + 1]
-            if terms:
-                work.append((way, slot, terms, self.carried[way]))
-        sums = run_add([entry[1:] for entry in work], beside)
-        for entry, value in zip(work, sums):
-            self.carried[entry[0]] = value
-        return sums[0]
+    def add(self):
+        rows = self.mine.shape[1]
+        if self.carried[0] is None:
+            work = [(self.time, 0, self.low, None), (self.time, self.low, rows, None)]
+        else:
+            work = [
+                (self.time, 0, rows, self.carried[0]),
+                (self.ring.chips - self.time, 0, rows, self.carried[1]),
+            ]
+        self.carried = run_add(self.mine, self.other, work)
 
     def send(self):
-        for way, route in enumerate((self.ring.onward, self.ring.back)):
-            if self.carried[way] is not None:
-                self.carried[way] = lax.ppermute(self.carried[way], "dp", route)
+        self.carried = self.ring.step(*self.carried)
         self.time -= 1
 
 
@@ -965,11 +982,11 @@
         )(qkv_weight[0], out_weight[0], up_weight[0], down_weight[0], *vectors, up_bias, lead_table[0].T)
         gathered = lax.all_gather(second, "dp", axis=0, tiled=True, axis_index_groups=[ring.order])
         gathered = gathered.reshape(count, SECOND, rows, width)
-        firsts = ring.gather(first)
+        firsts = ring.gather(first, LOW * rows)
         firsts = firsts + ring.siblings(firsts)
         devs = ring.slots()
         plan = Plan(ring.order, rows, items, length, width)
-        wide = run_vectors(plan, many, devs, firsts)
+        vec = run_vectors(plan, many, devs, lead, firsts)
     else:
         wide_blocks = lambda value: value[0].reshape(rows, -1, width).transpose(1, 0, 2)
         packed = jnp.concatenate(
@@ -989,13 +1006,12 @@
         plan = Plan([0], width, items, length, width)
         small = jnp.concatenate([*vectors, up_bias.reshape(4, rows), lead_table[0].T], 0).astype(BF16)
         wide = lax.all_gather(small, "dp", axis=1, tiled=True).astype(F32)
-
-    vec = jnp.concatenate(
-        [wide[:8], wide[8:12].reshape(4, count, rows).transpose(1, 0, 2).reshape(4, width)]
-        + [lax.dynamic_slice_in_dim(wide, 12 + lead[item], 1, 0) for item in range(items)]
-        + [jnp.zeros((4 - items, width), F32)],
-        0,
-    )
+        vec = jnp.concatenate(
+            [wide[:8], wide[8:12].reshape(4, count, rows).transpose(1, 0, 2).reshape(4, width)]
+            + [lax.dynamic_slice_in_dim(wide, 12 + lead[item], 1, 0) for item in range(items)]
+            + [jnp.zeros((4 - items, width), F32)],
+            0,
+        )
 
     middle, hidden = run_attend(plan, lens, flag, devs, x, vec, firsts)
     first_out = run_mlp(plan, middle, hidden, vec, gathered)
@@ -1010,7 +1026,7 @@
         plan, many, flag, devs, lead, arriving, cot, grad_hidden, sums, vec, kept, firsts
     )
     if aligned:
-        first_sum = RingSum(ring, [(grads1[0], *ring.siblings(grads1[1:]))])
+        first_sum = RingSum(ring, grads1[0], *ring.siblings(grads1[1:]), LOW * rows)
         while first_sum.time:
             first_sum.add()
             first_sum.send()

time: 237 us -> 230 us (0.970)
  waiting for transfers between devices: 120 us -> 115 us
  starting transfers between devices: 21.7 us -> 24.5 us
  between operations: 17 us -> 14.3 us
    ppermute x8 -> x0, waiting for transfers between devices: 61.6 us -> none  [the longest x7 47.6 us: send(): self.carried[way] = lax.ppermute(self.carried[way], 'dp', route)]
    ppermute x3 -> x8, waiting for transfers between devices: 10.5 us -> 55.9 us  [step(): lax.ppermute(ahead, 'dp', self.onward)]
    ppermute x8 -> x0, starting transfers between devices: 7.66 us -> none  [the longest x7 7.18 us: send(): self.carried[way] = lax.ppermute(self.carried[way], 'dp', route)]
    ppermute x3 -> x8, starting transfers between devices: 5.3 us -> 12.6 us  [step(): lax.ppermute(ahead, 'dp', self.onward)]
    ppermute x3 -> x8, waiting for transfers between devices: 29.6 us -> 34.9 us  [step(): lax.ppermute(behind, 'dp', self.back)]
    all_gather x1, waiting for transfers between devices: 1.76 us -> 5.26 us  [body(): lax.all_gather(second, 'dp', axis=0, tiled=True, axis_index_groups=[ring....]
    ppermute x3 -> x8, starting transfers between devices: 1.83 us -> 4.89 us  [step(): lax.ppermute(behind, 'dp', self.back)]
    ppermute x9 -> x10, waiting for transfers between devices: 5.21 us -> 6.61 us  [siblings(): return [lax.ppermute(piece, 'dp', self.sibling) for piece in pieces]]
  transfers between devices with their start and end apart: 27 -> 30, of which waited for: 19 -> 22; matrix products, arithmetic and copies ran while one was open for 1% -> 1% of each run, Pallas kernels for 16% -> 16%
where the time goes in v4:
time: 230 us
  waiting for transfers between devices  115 us (50%)
  Pallas kernels  73.2 us (32%)
  starting transfers between devices  24.5 us (11%)
  between operations  14.3 us (6%)
  local copies, waits for them, and re-layouts  2.94 us (1%)
    pallas_call x7, Pallas kernels, call(): pl.pallas_call(kernel, out_shape=outs, in_specs=in_specs, out_specs=out_s...  60.4 us
    ppermute x8, waiting for transfers between devices, step(): lax.ppermute(ahead, 'dp', self.onward)  55.9 us
    ppermute x8, waiting for transfers between devices, step(): lax.ppermute(behind, 'dp', self.back)  34.9 us
    ppermute x8, starting transfers between devices, step(): lax.ppermute(ahead, 'dp', self.onward)  12.6 us
    ppermute x2, waiting for transfers between devices, shifted(): lax.ppermute(value, axis, [(source, source + steps) for source in range(f...  9.49 us
    ppermute x10, waiting for transfers between devices, siblings(): return [lax.ppermute(piece, 'dp', self.sibling) for piece in pieces]  6.61 us
    pallas_call x4, Pallas kernels, run_add(): pl.pallas_call(functools.partial(add_kernel, plans), out_shape=[jax.Shape...  5.86 us
    all_gather x1, waiting for transfers between devices, body(): lax.all_gather(second, 'dp', axis=0, tiled=True, axis_index_groups=[ring....  5.26 us
  transfers between devices with their start and end apart: 30, of which 22 were waited for; matrix products, arithmetic and copies ran while one was open for 1% of the time, Pallas kernels for 16%

profile of v4, /device:TPU:0, one launch (start us, length us, event | category | flops | bytes accessed | tf_op | source)
XLA Modules:
  0.0 229.7 jit_solution(10326143938997437116)
XLA Ops:
  7.2 2.6 %pack.1 = (bf16[208,768]{1,0:T(8,128)(2,1)}, bf16[8,48,768]{2,1,0:T(8,128)(2,1)}) custom-call(f32[48,2304]{1,0:T(8,128)} %bitcast.41, f32[48,768]{1,0:T(8,128)} %bitcast.42, f32[48,3072]{1,0:T(8,128)} %bitcast.39, f32[192,768]{1,0:T(8,128)} %bitcast.40, f32[1,48]{1,0:T(1,128)} %refs_0_.1, f32[1,48]{1,0:T(1,128)} %refs_1_.1, f32[1,48]{1,0:T(1,128)} %refs_2_.1, ...), custom_call_target="tpu_custom_call" | custom-call | tf_op jit(solution)/shard_map/pack/pallas_call | solution.py:976
  9.9 3.1 %collective-permute-start.1 = (bf16[208,768]{1,0:T(8,128)(2,1)}, bf16[208,768]{1,0:T(8,128)(2,1)S(1)}, u32[]{:S(2)}, u32[]{:S(2)}) collective-permute-start(bf16[208,768]{1,0:T(8,128)(2,1)} %get-tuple-element.67.refs_0_.refs_6_), channel_id=1, source_target_pairs={{0,4},{1,5},{4,8},{5,9},{8,12},{9,13},{12,14},{13,15},{14,10},{15,... | collective-permute-start | bytes 958472 | tf_op jit(solution)/shard_map/ppermute | solution.py:915
  13.0 8.4 %collective-permute-done.1.refs_8_.refs_14_ = bf16[208,768]{1,0:T(8,128)(2,1)S(1)} collective-permute-done((bf16[208,768]{1,0:T(8,128)(2,1)}, bf16[208,768]{1,0:T(8,128)(2,1)S(1)}, u32[]{:S(2)}, u32[]{:S(2)}) %collective-permute-start.1) | collective-permute-done | bytes 319520 | tf_op jit(solution)/shard_map/ppermute | solution.py:915
  21.4 2.2 collective-permute-done.refs_1_.refs_7_
  23.9 1.7 collective-permute-start.3
  25.7 14.1 %collective-permute-done.2.refs_2_.refs_8_ = bf16[208,768]{1,0:T(8,128)(2,1)S(1)} collective-permute-done((bf16[208,768]{1,0:T(8,128)(2,1)S(1)}, bf16[208,768]{1,0:T(8,128)(2,1)S(1)}, u32[]{:S(2)}, u32[]{:S(2)}) %collective-permute-start.2) | collective-permute-done | bytes 319520 | tf_op jit(solution)/shard_map/ppermute | solution.py:915
  39.9 1.5 collective-permute-start.4
  41.9 0.5 collective-permute-start.16
  42.5 13.3 %collective-permute-done.4.refs_3_.refs_9_ = bf16[208,768]{1,0:T(8,128)(2,1)S(1)} collective-permute-done((bf16[208,768]{1,0:T(8,128)(2,1)S(1)}, bf16[208,768]{1,0:T(8,128)(2,1)S(1)}, u32[]{:S(2)}, u32[]{:S(2)}) %collective-permute-start.4) | collective-permute-done | bytes 319520 | tf_op jit(solution)/shard_map/ppermute | solution.py:915
  55.7 1.4 collective-permute-done.5.refs_6_.refs_12_
  57.1 0.7 slice.7
  57.9 1.6 collective-permute-start.7
  59.5 0.7 slice.6
  61.2 8.4 %collective-permute-done.6.refs_4_.refs_10_ = bf16[96,768]{1,0:T(8,128)(2,1)} collective-permute-done((bf16[96,768]{1,0:T(8,128)(2,1)}, bf16[96,768]{1,0:T(8,128)(2,1)}, u32[]{:S(2)}, u32[]{:S(2)}) %collective-permute-start.6) | collective-permute-done | bytes 147488 | tf_op jit(solution)/shard_map/ppermute | solution.py:915
  70.2 1.1 collective-permute-done.12.refs_13_.refs_19_
  71.9 2.9 %vectors.1.vec = f32[16,768]{1,0:T(8,128)S(1)} custom-call(s32[16]{0:T(128)S(1)} %pad_add_fusion.devs, s32[2]{0:T(128)S(1)} %bitcast.32, bf16[208,768]{1,0:T(8,128)(2,1)} %get-tuple-element.67.refs_0_.refs_6_, bf16[208,768]{1,0:T(8,128)(2,1)} %copy-done.8, bf16[208,768]{1,0:T(8,128)(2,1)} %copy-done.9, bf16[208,768]{1,0:T(8,128)(2,1)} %copy-done.5, ...), custom_call_target="tpu_custom_call" | custom-call | flops 56623104 | bytes 2359296 | tf_op jit(solution)/shard_map/vectors/pallas_call | solution.py:673
  74.8 5.5 %attend.1 = (f32[192,768]{1,0:T(8,128)S(1)}, bf16[192,768]{1,0:T(8,128)(2,1)S(1)}) custom-call(s32[2]{0:T(128)S(1)} %bitcast.34, s32[1]{0:T(128)} %bitcast.1.flag, s32[16]{0:T(128)S(1)} %pad_add_fusion.devs, bf16[192,768]{1,0:T(8,128)(2,1)S(1)} %bitcast.30, f32[16,768]{1,0:T(8,128)S(1)} %vectors.1.vec, bf16[208,768]{1,0:T(8,128)(2,1)} %get-tuple-element.67.refs_0_.refs_6_, ...), custom_call_target="tpu_custom_call" | custom-call | flops 905969664 | bytes 4718592 | tf_op jit(solution)/shard_map/attend/pallas_call | solution.py:673
  80.3 5.3 %all-gather.2.cloned.1.call-done = bf16[128,48,768]{2,1,0:T(8,128)(2,1)} async-done(((bf16[8,48,768]{2,1,0:T(8,128)(2,1)}), bf16[128,48,768]{2,1,0:T(8,128)(2,1)}) %all-gather.2.cloned.1.call-update) | async-done | bytes 9437200 | tf_op jit(solution)/shard_map/all_gather | solution.py:983
  85.6 5.1 %mlp.1.after = bf16[192,768]{1,0:T(8,128)(2,1)S(1)} custom-call(f32[192,768]{1,0:T(8,128)S(1)} %get-tuple-element.74.middle_ref, bf16[192,768]{1,0:T(8,128)(2,1)S(1)} %get-tuple-element.75.hidden_ref, f32[16,768]{1,0:T(8,128)S(1)} %vectors.1.vec, bf16[16,8,48,768]{3,2,1,0:T(8,128)(2,1)} %bitcast.36), custom_call_target="tpu_custom_call" | custom-call | flops 1811939328 | bytes 9437184 | tf_op jit(solution)/shard_map/mlp/pallas_call | solution.py:673
  90.7 3.7 %collective-permute-start.17 = (bf16[192,768]{1,0:T(8,128)(2,1)S(1)}, bf16[192,768]{1,0:T(8,128)(2,1)S(1)}, u32[]{:S(2)}, u32[]{:S(2)}) collective-permute-start(bf16[192,768]{1,0:T(8,128)(2,1)S(1)} %mlp.1.after), channel_id=1, source_target_pairs={{0,16},{1,17},{2,18},{3,19},{4,20},{5,21},{6,22},{7,23},{8,24},{9,... | collective-permute-start | bytes 884744 | tf_op jit(solution)/shard_map/ppermute | solution.py:887
  94.4 5.8 %load.1 = (bf16[4,16,48,768]{3,2,1,0:T(8,128)(2,1)S(1)}, bf16[8,16,48,768]{3,2,1,0:T(8,128)(2,1)S(1)}) custom-call(s32[16]{0:T(128)S(1)} %pad_add_fusion.devs, bf16[192,768]{1,0:T(8,128)(2,1)S(1)} %mlp.1.after, bf16[16,8,48,768]{3,2,1,0:T(8,128)(2,1)} %bitcast.37, bf16[208,768]{1,0:T(8,128)(2,1)} %get-tuple-element.67.refs_0_.refs_6_, ...), custom_call_target="tpu_custom_call" | custom-call | bytes 28311552 | tf_op jit(solution)/shard_map/load/pallas_call | solution.py:673
  100.2 0.6 collective-permute-done.17.recv_ref
  100.9 16.9 %chain.1 = (bf16[192,768]{1,0:T(8,128)(2,1)}, bf16[192,768]{1,0:T(8,128)(2,1)S(1)}, bf16[192,768]{1,0:T(8,128)(2,1)S(1)}, bf16[192,3072]{1,0:T(8,128)(2,1)S(1)},...) custom-call(s32[2]{0:T(128)S(1)} %bitcast.35, ...), custom_call_target="tpu_custom_call" | custom-call | flops 5435817984 | bytes 7077888 | tf_op jit(solution)/shard_map/chain/pallas_call | solution.py:673
  117.7 1.5 collective-permute-start.18
  119.3 8.8 %collective-permute-done.18.arr_ref = bf16[192,768]{1,0:T(8,128)(2,1)S(1)} collective-permute-done((bf16[192,768]{1,0:T(8,128)(2,1)S(1)}, bf16[192,768]{1,0:T(8,128)(2,1)S(1)}, u32[]{:S(2)}, u32[]{:S(2)}) %collective-permute-start.18) | collective-permute-done | bytes 294944 | tf_op jit(solution)/shard_map/ppermute | solution.py:887
  128.1 9.4 %mlp_back.1 = (f32[192,768]{1,0:T(8,128)S(1)}, f32[16,768]{1,0:T(8,128)S(1)}, bf16[16,8,48,768]{3,2,1,0:T(8,128)(2,1)}) custom-call(s32[1]{0:T(128)} %bitcast.1.flag, bf16[192,768]{1,0:T(8,128)(2,1)S(1)} %collective-permute-done.18.arr_ref, bf16[192,768]{1,0:T(8,128)(2,1)S(1)} %bitcast.28, bf16[8,16,48,768]{3,2,1,0:T(8,128)(2,1)S(1)} %get-tuple-element.78.held2, ...), custom_call_target="tpu_custom_call" | custom-call | flops 3623878656 | bytes 9437184 | tf_op jit(solution)/shard_map/mlp_back/pallas_call | solution.py:673
  137.5 14.9 %rest.1 = (f32[192,768]{1,0:T(8,128)}, f32[16,768]{1,0:T(8,128)}, bf16[8,208,768]{2,1,0:T(8,128)(2,1)}, bf16[8,208,768]{2,1,0:T(8,128)(2,1)}) custom-call(s32[1]{0:T(128)} %bitcast.1.flag, s32[16]{0:T(128)S(1)} %pad_add_fusion.devs, s32[2]{0:T(128)S(1)} %bitcast.33, bf16[192,768]{1,0:T(8,128)(2,1)S(1)} %collective-permute-done.18.arr_ref, ...), custom_call_target="tpu_custom_call" | custom-call | flops 1811939328 | bytes 9437184 | tf_op jit(solution)/shard_map/rest/pallas_call | solution.py:673
  152.5 5.0 %collective-permute-done.19.refs_1_.refs_3_.refs_4_.other = bf16[8,208,768]{2,1,0:T(8,128)(2,1)S(1)} collective-permute-done((bf16[8,208,768]{2,1,0:T(8,128)(2,1)}, bf16[8,208,768]{2,1,0:T(8,128)(2,1)S(1)}, u32[]{:S(2)}, u32[]{:S(2)}) %collective-permute-start.19) | collective-permute-done | bytes 2555936 | tf_op jit(solution)/shard_map/ppermute | solution.py:929
  157.5 1.5 copy-done.4
  159.0 1.4 add.77
  160.9 1.6 collective-permute-start.20
  162.5 6.2 %collective-permute-done.20.refs_2_ = bf16[96,768]{1,0:T(8,128)(2,1)S(1)} collective-permute-done((bf16[96,768]{1,0:T(8,128)(2,1)S(1)}, bf16[96,768]{1,0:T(8,128)(2,1)S(1)}, u32[]{:S(2)}, u32[]{:S(2)}) %collective-permute-start.20) | collective-permute-done | bytes 147488 | tf_op jit(solution)/shard_map/ppermute | solution.py:915
  168.9 1.5 add.78
  170.4 2.1 collective-permute-start.22
  172.5 11.0 %collective-permute-done.22.refs_2_ = bf16[208,768]{1,0:T(8,128)(2,1)S(1)} collective-permute-done((bf16[208,768]{1,0:T(8,128)(2,1)S(1)}, bf16[208,768]{1,0:T(8,128)(2,1)S(1)}, u32[]{:S(2)}, u32[]{:S(2)}) %collective-permute-start.22) | collective-permute-done | bytes 319520 | tf_op jit(solution)/shard_map/ppermute | solution.py:915
  183.5 1.9 collective-permute-done.23.refs_5_
  185.5 1.5 add.79
  187.0 1.5 collective-permute-start.24
  188.5 0.5 collective-permute-start.25
  189.1 10.5 %collective-permute-done.24.refs_2_ = bf16[208,768]{1,0:T(8,128)(2,1)S(1)} collective-permute-done((bf16[208,768]{1,0:T(8,128)(2,1)S(1)}, bf16[208,768]{1,0:T(8,128)(2,1)S(1)}, u32[]{:S(2)}, u32[]{:S(2)}) %collective-permute-start.24) | collective-permute-done | bytes 319520 | tf_op jit(solution)/shard_map/ppermute | solution.py:915
  199.6 1.4 collective-permute-done.25.refs_5_
  201.0 1.5 add.80
  202.5 1.7 collective-permute-start.26
  204.6 9.9 %collective-permute-done.26.ahead = bf16[208,768]{1,0:T(8,128)(2,1)S(1)} collective-permute-done((bf16[208,768]{1,0:T(8,128)(2,1)S(1)}, bf16[208,768]{1,0:T(8,128)(2,1)S(1)}, u32[]{:S(2)}, u32[]{:S(2)}) %collective-permute-start.26) | collective-permute-done | bytes 319520 | tf_op jit(solution)/shard_map/ppermute | solution.py:915
  214.5 1.6 collective-permute-done.27.behind
  216.1 2.1 total.1
  218.3 2.5 %reduce-scatter.2.cloned.1.call-done.grads_ref = bf16[8,48,768]{2,1,0:T(8,128)(2,1)} async-done(((bf16[128,48,768]{2,1,0:T(8,128)(2,1)}), bf16[8,48,768]{2,1,0:T(8,128)(2,1)}) %reduce-scatter.2.cloned.1.call-update) | async-done | bytes 589840 | tf_op jit(solution)/shard_map/reduce_scatter | solution.py:1033
  220.7 2.1 unpack.1
  (64 shorter events, 4.4 us)
Async XLA Ops:
  7.2 64.6 %copy-start.2 = (s32[2,1]{0,1:T(1,128)S(1)}, s32[2,1]{0,1:T(1,128)}, u32[]{:S(2)}) copy-start(s32[2,1]{0,1:T(1,128)} %param.21) | copy-start | bytes 28
  7.2 78.4 %all-gather.2.cloned.1.call-start = ((), (), s32[]{:S(2)}) async-start(), calls=%async_computation.1 | async-start | bytes 10027008 | tf_op jit(solution)/shard_map/all_gather | solution.py:983
  9.9 210.8 %reduce-scatter.2.cloned.1.call-start = ((), (), s32[]{:S(2)}) async-start(), calls=%async_computation.2 | async-start | bytes 10027008 | tf_op jit(solution)/shard_map/reduce_scatter | solution.py:1033
  9.9 11.5 %collective-permute-start.1 = (bf16[208,768]{1,0:T(8,128)(2,1)}, bf16[208,768]{1,0:T(8,128)(2,1)S(1)}, u32[]{:S(2)}, u32[]{:S(2)}) collective-permute-start(bf16[208,768]{1,0:T(8,128)(2,1)} %get-tuple-element.67.refs_0_.refs_6_), channel_id=1, source_target_pairs={{0,4},{1,5},{4,8},{5,9},{8,12},{9,13},{12,14},{13,15},{14,10},{15,... | collective-permute-start | bytes 958472 | tf_op jit(solution)/shard_map/ppermute | solution.py:915
  13.0 10.6 %collective-permute-start = (bf16[208,768]{1,0:T(8,128)(2,1)}, bf16[208,768]{1,0:T(8,128)(2,1)S(1)}, u32[]{:S(2)}, u32[]{:S(2)}) collective-permute-start(bf16[208,768]{1,0:T(8,128)(2,1)} %get-tuple-element.67.refs_0_.refs_6_), channel_id=1, source_target_pairs={{4,0},{5,1},{8,4},{9,5},{12,8},{13,9},{14,12},{15,13},{10,14},{11,... | collective-permute-start | bytes 958472 | tf_op jit(solution)/shard_map/ppermute | solution.py:915
  21.4 50.3 %copy-start.7 = (bf16[208,768]{1,0:T(8,128)(2,1)}, bf16[208,768]{1,0:T(8,128)(2,1)S(1)}, u32[]{:S(2)}) copy-start(bf16[208,768]{1,0:T(8,128)(2,1)S(1)} %collective-permute-done.1.refs_8_.refs_14_) | copy-start | bytes 958468
  23.6 48.1 %copy-start.8 = (bf16[208,768]{1,0:T(8,128)(2,1)}, bf16[208,768]{1,0:T(8,128)(2,1)S(1)}, u32[]{:S(2)}) copy-start(bf16[208,768]{1,0:T(8,128)(2,1)S(1)} %collective-permute-done.refs_1_.refs_7_) | copy-start | bytes 958468
  23.6 16.2 %collective-permute-start.2 = (bf16[208,768]{1,0:T(8,128)(2,1)S(1)}, bf16[208,768]{1,0:T(8,128)(2,1)S(1)}, u32[]{:S(2)}, u32[]{:S(2)}) collective-permute-start(bf16[208,768]{1,0:T(8,128)(2,1)S(1)} %collective-permute-done.refs_1_.refs_7_), channel_id=1, source_target_pairs={{4,0},{5,1},{8,4},{9,5},{12,8},{13,9},{14,12},{15,13},{10,14},{11,... | collective-permute-start | bytes 958472 | tf_op jit(solution)/shard_map/ppermute | solution.py:915
  23.9 16.0 %collective-permute-start.3 = (bf16[208,768]{1,0:T(8,128)(2,1)S(1)}, bf16[208,768]{1,0:T(8,128)(2,1)S(1)}, u32[]{:S(2)}, u32[]{:S(2)}) collective-permute-start(bf16[208,768]{1,0:T(8,128)(2,1)S(1)} %collective-permute-done.1.refs_8_.refs_14_), channel_id=1, source_target_pairs={{0,4},{1,5},{4,8},{5,9},{8,12},{9,13},{12,14},{13,15},{14,10},{15,... | collective-permute-start | bytes 958472 | tf_op jit(solution)/shard_map/ppermute | solution.py:915
  39.8 32.0 %copy-start.9 = (bf16[208,768]{1,0:T(8,128)(2,1)}, bf16[208,768]{1,0:T(8,128)(2,1)S(1)}, u32[]{:S(2)}) copy-start(bf16[208,768]{1,0:T(8,128)(2,1)S(1)} %collective-permute-done.2.refs_2_.refs_8_) | copy-start | bytes 958468
  39.9 31.9 %copy-start.10 = (bf16[208,768]{1,0:T(8,128)(2,1)}, bf16[208,768]{1,0:T(8,128)(2,1)S(1)}, u32[]{:S(2)}) copy-start(bf16[208,768]{1,0:T(8,128)(2,1)S(1)} %collective-permute-done.3.refs_7_.refs_13_) | copy-start | bytes 958468
  39.9 15.8 %collective-permute-start.4 = (bf16[208,768]{1,0:T(8,128)(2,1)S(1)}, bf16[208,768]{1,0:T(8,128)(2,1)S(1)}, u32[]{:S(2)}, u32[]{:S(2)}) collective-permute-start(bf16[208,768]{1,0:T(8,128)(2,1)S(1)} %collective-permute-done.2.refs_2_.refs_8_), channel_id=1, source_target_pairs={{4,0},{5,1},{8,4},{9,5},{12,8},{13,9},{14,12},{15,13},{10,14},{11,... | collective-permute-start | bytes 958472 | tf_op jit(solution)/shard_map/ppermute | solution.py:915
  41.5 15.6 %collective-permute-start.5 = (bf16[208,768]{1,0:T(8,128)(2,1)S(1)}, bf16[208,768]{1,0:T(8,128)(2,1)S(1)}, u32[]{:S(2)}, u32[]{:S(2)}) collective-permute-start(bf16[208,768]{1,0:T(8,128)(2,1)S(1)} %collective-permute-done.3.refs_7_.refs_13_), channel_id=1, source_target_pairs={{0,4},{1,5},{4,8},{5,9},{8,12},{9,13},{12,14},{13,15},{14,10},{15,... | collective-permute-start | bytes 958472 | tf_op jit(solution)/shard_map/ppermute | solution.py:915
  41.9 18.2 %collective-permute-start.8 = (bf16[208,768]{1,0:T(8,128)(2,1)}, bf16[208,768]{1,0:T(8,128)(2,1)S(1)}, u32[]{:S(2)}, u32[]{:S(2)}) collective-permute-start(bf16[208,768]{1,0:T(8,128)(2,1)} %get-tuple-element.67.refs_0_.refs_6_), channel_id=1, source_target_pairs={{0,1},{1,0},{2,3},{3,2},{4,5},{5,4},{6,7},{7,6},{8,9},{9,8},{10,11... | collective-permute-start | bytes 958472 | tf_op jit(solution)/shard_map/ppermute | solution.py:929
  41.9 18.6 %collective-permute-start.16 = (bf16[208,768]{1,0:T(8,128)(2,1)S(1)}, bf16[208,768]{1,0:T(8,128)(2,1)S(1)}, u32[]{:S(2)}, u32[]{:S(2)}) collective-permute-start(bf16[208,768]{1,0:T(8,128)(2,1)S(1)} %collective-permute-done.1.refs_8_.refs_14_), channel_id=1, source_target_pairs={{0,1},{1,0},{2,3},{3,2},{4,5},{5,4},{6,7},{7,6},{8,9},{9,8},{10,11... | collective-permute-start | bytes 958472 | tf_op jit(solution)/shard_map/ppermute | solution.py:929
  42.4 18.1 %collective-permute-start.9 = (bf16[208,768]{1,0:T(8,128)(2,1)S(1)}, bf16[208,768]{1,0:T(8,128)(2,1)S(1)}, u32[]{:S(2)}, u32[]{:S(2)}) collective-permute-start(bf16[208,768]{1,0:T(8,128)(2,1)S(1)} %collective-permute-done.refs_1_.refs_7_), channel_id=1, source_target_pairs={{0,1},{1,0},{2,3},{3,2},{4,5},{5,4},{6,7},{7,6},{8,9},{9,8},{10,11... | collective-permute-start | bytes 958472 | tf_op jit(solution)/shard_map/ppermute | solution.py:929
  55.7 16.1 %copy-start.5 = (bf16[208,768]{1,0:T(8,128)(2,1)}, bf16[208,768]{1,0:T(8,128)(2,1)S(1)}, u32[]{:S(2)}) copy-start(bf16[208,768]{1,0:T(8,128)(2,1)S(1)} %collective-permute-done.4.refs_3_.refs_9_) | copy-start | bytes 958468
  55.7 5.4 %collective-permute-start.10 = (bf16[208,768]{1,0:T(8,128)(2,1)S(1)}, bf16[208,768]{1,0:T(8,128)(2,1)S(1)}, u32[]{:S(2)}, u32[]{:S(2)}) collective-permute-start(bf16[208,768]{1,0:T(8,128)(2,1)S(1)} %collective-permute-done.2.refs_2_.refs_8_), channel_id=1, source_target_pairs={{0,1},{1,0},{2,3},{3,2},{4,5},{5,4},{6,7},{7,6},{8,9},{9,8},{10,11... | collective-permute-start | bytes 958472 | tf_op jit(solution)/shard_map/ppermute | solution.py:929
  57.1 14.7 %copy-start.6 = (bf16[208,768]{1,0:T(8,128)(2,1)}, bf16[208,768]{1,0:T(8,128)(2,1)S(1)}, u32[]{:S(2)}) copy-start(bf16[208,768]{1,0:T(8,128)(2,1)S(1)} %collective-permute-done.5.refs_6_.refs_12_) | copy-start | bytes 958468
  57.9 11.7 %collective-permute-start.7 = (bf16[112,768]{1,0:T(8,128)(2,1)}, bf16[112,768]{1,0:T(8,128)(2,1)}, u32[]{:S(2)}, u32[]{:S(2)}) collective-permute-start(bf16[112,768]{1,0:T(8,128)(2,1)} %slice.7), channel_id=1, source_target_pairs={{4,0},{5,1},{8,4},{9,5},{12,8},{13,9},{14,12},{15,13},{10,14},{11,... | collective-permute-start | bytes 516104 | tf_op jit(solution)/shard_map/ppermute | solution.py:915
  60.2 11.6 %copy-start.11 = (bf16[208,768]{1,0:T(8,128)(2,1)}, bf16[208,768]{1,0:T(8,128)(2,1)S(1)}, u32[]{:S(2)}) copy-start(bf16[208,768]{1,0:T(8,128)(2,1)S(1)} %collective-permute-done.8.refs_9_.refs_15_) | copy-start | bytes 958468
  60.2 9.4 %collective-permute-start.6 = (bf16[96,768]{1,0:T(8,128)(2,1)}, bf16[96,768]{1,0:T(8,128)(2,1)}, u32[]{:S(2)}, u32[]{:S(2)}) collective-permute-start(bf16[96,768]{1,0:T(8,128)(2,1)} %slice.6), channel_id=1, source_target_pairs={{0,4},{1,5},{4,8},{5,9},{8,12},{9,13},{12,14},{13,15},{14,10},{15,... | collective-permute-start | bytes 442376 | tf_op jit(solution)/shard_map/ppermute | solution.py:915
  60.6 11.3 %copy-start.12 = (bf16[208,768]{1,0:T(8,128)(2,1)}, bf16[208,768]{1,0:T(8,128)(2,1)S(1)}, u32[]{:S(2)}) copy-start(bf16[208,768]{1,0:T(8,128)(2,1)S(1)} %collective-permute-done.16.refs_17_.refs_23_) | copy-start | bytes 958468
  60.6 9.6 %collective-permute-start.15 = (bf16[208,768]{1,0:T(8,128)(2,1)S(1)}, bf16[208,768]{1,0:T(8,128)(2,1)S(1)}, u32[]{:S(2)}, u32[]{:S(2)}) collective-permute-start(bf16[208,768]{1,0:T(8,128)(2,1)S(1)} %collective-permute-done.3.refs_7_.refs_13_), channel_id=1, source_target_pairs={{0,1},{1,0},{2,3},{3,2},{4,5},{5,4},{6,7},{7,6},{8,9},{9,8},{10,11... | collective-permute-start | bytes 958472 | tf_op jit(solution)/shard_map/ppermute | solution.py:929
  60.6 11.2 %copy-start.13 = (bf16[208,768]{1,0:T(8,128)(2,1)}, bf16[208,768]{1,0:T(8,128)(2,1)S(1)}, u32[]{:S(2)}) copy-start(bf16[208,768]{1,0:T(8,128)(2,1)S(1)} %collective-permute-done.9.refs_10_.refs_16_) | copy-start | bytes 958468
  60.6 10.7 %collective-permute-start.11 = (bf16[208,768]{1,0:T(8,128)(2,1)S(1)}, bf16[208,768]{1,0:T(8,128)(2,1)}, u32[]{:S(2)}, u32[]{:S(2)}) collective-permute-start(bf16[208,768]{1,0:T(8,128)(2,1)S(1)} %collective-permute-done.4.refs_3_.refs_9_), channel_id=1, source_target_pairs={{0,1},{1,0},{2,3},{3,2},{4,5},{5,4},{6,7},{7,6},{8,9},{9,8},{10,11... | collective-permute-start | bytes 958472 | tf_op jit(solution)/shard_map/ppermute | solution.py:929
  61.1 10.7 %copy-start.14 = (bf16[208,768]{1,0:T(8,128)(2,1)}, bf16[208,768]{1,0:T(8,128)(2,1)S(1)}, u32[]{:S(2)}) copy-start(bf16[208,768]{1,0:T(8,128)(2,1)S(1)} %collective-permute-done.10.refs_11_.refs_17_) | copy-start | bytes 958468
  61.1 10.2 %collective-permute-start.14 = (bf16[208,768]{1,0:T(8,128)(2,1)S(1)}, bf16[208,768]{1,0:T(8,128)(2,1)}, u32[]{:S(2)}, u32[]{:S(2)}) collective-permute-start(bf16[208,768]{1,0:T(8,128)(2,1)S(1)} %collective-permute-done.5.refs_6_.refs_12_), channel_id=1, source_target_pairs={{0,1},{1,0},{2,3},{3,2},{4,5},{5,4},{6,7},{7,6},{8,9},{9,8},{10,11... | collective-permute-start | bytes 958472 | tf_op jit(solution)/shard_map/ppermute | solution.py:929
  69.6 1.7 collective-permute-start.12
  69.6 2.2 collective-permute-start.13
  70.2 1.6 copy-start.15
  71.8 2.9 %copy-start.1 = (bf16[2,1,96,768]{3,2,1,0:T(8,128)(2,1)S(1)}, bf16[2,1,96,768]{3,2,1,0:T(8,128)(2,1)}, u32[]{:S(2)}) copy-start(bf16[2,1,96,768]{3,2,1,0:T(8,128)(2,1)} %param.18) | copy-start | bytes 884740
  71.8 2.9 %copy-start.3 = (s32[2,1]{0,1:T(1,128)S(1)}, s32[2,1]{0,1:T(1,128)}, u32[]{:S(2)}) copy-start(s32[2,1]{0,1:T(1,128)} %param.20) | copy-start | bytes 28
  90.7 10.2 %copy-start = (bf16[2,1,96,768]{3,2,1,0:T(8,128)(2,1)S(1)}, bf16[2,1,96,768]{3,2,1,0:T(8,128)(2,1)}, u32[]{:S(2)}) copy-start(bf16[2,1,96,768]{3,2,1,0:T(8,128)(2,1)} %param.19) | copy-start | bytes 884740
  90.7 10.2 %collective-permute-start.17 = (bf16[192,768]{1,0:T(8,128)(2,1)S(1)}, bf16[192,768]{1,0:T(8,128)(2,1)S(1)}, u32[]{:S(2)}, u32[]{:S(2)}) collective-permute-start(bf16[192,768]{1,0:T(8,128)(2,1)S(1)} %mlp.1.after), channel_id=1, source_target_pairs={{0,16},{1,17},{2,18},{3,19},{4,20},{5,21},{6,22},{7,23},{8,24},{9,... | collective-permute-start | bytes 884744 | tf_op jit(solution)/shard_map/ppermute | solution.py:887
  117.7 10.4 %collective-permute-start.18 = (bf16[192,768]{1,0:T(8,128)(2,1)S(1)}, bf16[192,768]{1,0:T(8,128)(2,1)S(1)}, u32[]{:S(2)}, u32[]{:S(2)}) collective-permute-start(bf16[192,768]{1,0:T(8,128)(2,1)S(1)} %get-tuple-element.80), channel_id=1, source_target_pairs={{16,0},{17,1},{18,2},{19,3},{20,4},{21,5},{22,6},{23,7},{24,8},{25... | collective-permute-start | bytes 884744 | tf_op jit(solution)/shard_map/ppermute | solution.py:887
  152.4 5.1 %collective-permute-start.19 = (bf16[8,208,768]{2,1,0:T(8,128)(2,1)}, bf16[8,208,768]{2,1,0:T(8,128)(2,1)S(1)}, u32[]{:S(2)}, u32[]{:S(2)}) collective-permute-start(bf16[8,208,768]{2,1,0:T(8,128)(2,1)} %get-tuple-element.94), channel_id=1, source_target_pairs={{0,1},{1,0},{2,3},{3,2},{4,5},{5,4},{6,7},{7,6},{8,9},{9,8},{10,11... | collective-permute-start | bytes 7667720 | tf_op jit(solution)/shard_map/ppermute | solution.py:929
  157.5 1.5 copy-start.4
  160.4 8.6 %collective-permute-start.21 = (bf16[112,768]{1,0:T(8,128)(2,1)S(1)}, bf16[112,768]{1,0:T(8,128)(2,1)S(1)}, u32[]{:S(2)}, u32[]{:S(2)}) collective-permute-start(bf16[112,768]{1,0:T(8,128)(2,1)S(1)} %get-tuple-element.96), channel_id=1, source_target_pairs={{4,0},{5,1},{8,4},{9,5},{12,8},{13,9},{14,12},{15,13},{10,14},{11,... | collective-permute-start | bytes 516104 | tf_op jit(solution)/shard_map/ppermute | solution.py:915
  160.9 7.7 %collective-permute-start.20 = (bf16[96,768]{1,0:T(8,128)(2,1)S(1)}, bf16[96,768]{1,0:T(8,128)(2,1)S(1)}, u32[]{:S(2)}, u32[]{:S(2)}) collective-permute-start(bf16[96,768]{1,0:T(8,128)(2,1)S(1)} %get-tuple-element.95), channel_id=1, source_target_pairs={{0,4},{1,5},{4,8},{5,9},{8,12},{9,13},{12,14},{13,15},{14,10},{15,... | collective-permute-start | bytes 442376 | tf_op jit(solution)/shard_map/ppermute | solution.py:915
  170.4 13.1 %collective-permute-start.22 = (bf16[208,768]{1,0:T(8,128)(2,1)S(1)}, bf16[208,768]{1,0:T(8,128)(2,1)S(1)}, u32[]{:S(2)}, u32[]{:S(2)}) collective-permute-start(bf16[208,768]{1,0:T(8,128)(2,1)S(1)} %get-tuple-element.97), channel_id=1, source_target_pairs={{0,4},{1,5},{4,8},{5,9},{8,12},{9,13},{12,14},{13,15},{14,10},{15,... | collective-permute-start | bytes 958472 | tf_op jit(solution)/shard_map/ppermute | solution.py:915
  172.5 13.0 %collective-permute-start.23 = (bf16[208,768]{1,0:T(8,128)(2,1)S(1)}, bf16[208,768]{1,0:T(8,128)(2,1)S(1)}, u32[]{:S(2)}, u32[]{:S(2)}) collective-permute-start(bf16[208,768]{1,0:T(8,128)(2,1)S(1)} %get-tuple-element.98), channel_id=1, source_target_pairs={{4,0},{5,1},{8,4},{9,5},{12,8},{13,9},{14,12},{15,13},{10,14},{11,... | collective-permute-start | bytes 958472 | tf_op jit(solution)/shard_map/ppermute | solution.py:915
  187.0 12.6 %collective-permute-start.24 = (bf16[208,768]{1,0:T(8,128)(2,1)S(1)}, bf16[208,768]{1,0:T(8,128)(2,1)S(1)}, u32[]{:S(2)}, u32[]{:S(2)}) collective-permute-start(bf16[208,768]{1,0:T(8,128)(2,1)S(1)} %get-tuple-element.99), channel_id=1, source_target_pairs={{0,4},{1,5},{4,8},{5,9},{8,12},{9,13},{12,14},{13,15},{14,10},{15,... | collective-permute-start | bytes 958472 | tf_op jit(solution)/shard_map/ppermute | solution.py:915
  188.5 12.5 %collective-permute-start.25 = (bf16[208,768]{1,0:T(8,128)(2,1)S(1)}, bf16[208,768]{1,0:T(8,128)(2,1)S(1)}, u32[]{:S(2)}, u32[]{:S(2)}) collective-permute-start(bf16[208,768]{1,0:T(8,128)(2,1)S(1)} %get-tuple-element.100), channel_id=1, source_target_pairs={{4,0},{5,1},{8,4},{9,5},{12,8},{13,9},{14,12},{15,13},{10,14},{11,... | collective-permute-start | bytes 958472 | tf_op jit(solution)/shard_map/ppermute | solution.py:915
  202.5 12.0 %collective-permute-start.26 = (bf16[208,768]{1,0:T(8,128)(2,1)S(1)}, bf16[208,768]{1,0:T(8,128)(2,1)S(1)}, u32[]{:S(2)}, u32[]{:S(2)}) collective-permute-start(bf16[208,768]{1,0:T(8,128)(2,1)S(1)} %get-tuple-element.101), channel_id=1, source_target_pairs={{0,4},{1,5},{4,8},{5,9},{8,12},{9,13},{12,14},{13,15},{14,10},{15,... | collective-permute-start | bytes 958472 | tf_op jit(solution)/shard_map/ppermute | solution.py:915
  204.2 11.9 %collective-permute-start.27 = (bf16[208,768]{1,0:T(8,128)(2,1)S(1)}, bf16[208,768]{1,0:T(8,128)(2,1)S(1)}, u32[]{:S(2)}, u32[]{:S(2)}) collective-permute-start(bf16[208,768]{1,0:T(8,128)(2,1)S(1)} %get-tuple-element.102), channel_id=1, source_target_pairs={{4,0},{5,1},{8,4},{9,5},{12,8},{13,9},{14,12},{15,13},{10,14},{11,... | collective-permute-start | bytes 958472 | tf_op jit(solution)/shard_map/ppermute | solution.py:915
Sparse Core Ops, SparseCore 0:
  10.2 75.3 all-gather.1
  137.6 83.0 reduce-scatter.1

commit v5 on v4

--- a/solution.py
+++ b/solution.py
@@ -21,6 +21,7 @@
 QUART = 4
 EXTRA = 16
 LOW = 2
+SLOTS = 4
 
 
 def mm(left, right):
@@ -70,6 +71,12 @@
     count = stacked.shape[0] // 2
     lane = lax.broadcasted_iota(jnp.int32, (count, PAIR), 1)
     return jnp.where(lane < HEAD, stacked[:count], stacked[count:])
+
+
+def runs_of(order):
+    if all(order[at + 1] == order[at] + 1 for at in range(0, len(order) - 1, 2)) and len(order) > 1:
+        return [(at, order[at], 2) for at in range(0, len(order), 2)]
+    return [(at, device, 1) for at, device in enumerate(order)]
 
 
 class Plan:
@@ -81,7 +88,7 @@
         self.pairs = width // PAIR
         whole = self.shards % QUART == 0
         self.runs = [(0, QUART)] if whole else [(block, 1) for block in range(QUART)]
-        self.parts = 2 if self.shards > 1 else 1
+        self.parts = 3 if self.shards > 1 else 1
 
 
 def slot_pieces(plan, refs):
@@ -119,6 +126,15 @@
             piece.at[blocks], held.at[pl.ds(at + blocks.start, blocks.size), devs[slot]], sem
         )
         for slot, piece in enumerate(pieces)
+    ]
+
+
+def up_copies(plan, gathered, held, sem, part):
+    return [
+        pltpu.make_async_copy(
+            gathered.at[pl.ds(place, count), part], held.at[part, pl.ds(device, count)], sem
+        )
+        for place, device, count in runs_of(plan.order)
     ]
 
 
@@ -261,10 +277,10 @@
 
 
 def mlp_kernel(plan, middle_ref, hidden_ref, vec, gathered, y_ref, held, sems, down_sems):
-    (ups, downs), devs = second_pieces(plan, gathered), plan.order
-    down = down_copies(plan, downs, devs, held, down_sems)
+    _, downs = second_pieces(plan, gathered)
+    down = down_copies(plan, downs, plan.order, held, down_sems)
     for part in range(QUART):
-        start_all(block_copies(ups, devs, held, sems.at[part], pl.ds(part, 1)))
+        start_all(up_copies(plan, gathered, held, sems.at[part], part))
         start_all([copy for block, copy in down if block == part])
 
     def wait(block):
@@ -275,23 +291,26 @@
     y_ref[...] = (middle_ref[...] + total).astype(BF16)
 
 
-def load_kernel(plan, devs, after, gathered, *refs):
-    firsts, (held1, held2, sems, down_sems) = refs[:-4], refs[-4:]
+def load_kernel(plan, devs, after, cot_ref, gathered, *refs):
+    firsts, (held1, held2, grad_act, sems, down_sems) = refs[:-5], refs[-5:]
     ups, downs = second_pieces(plan, gathered)
+    start_all([copy for _, copy in down_copies(plan, downs, plan.order, held2, down_sems)])
+    start_all(block_copies(ups, plan.order, held2, sems.at[1], pl.ds(0, QUART)))
     start_all(first_copies(plan, firsts, devs, held1, sems.at[0], pl.ds(0, FIRST)))
-    start_all(block_copies(ups, plan.order, held2, sems.at[1], pl.ds(0, QUART)))
-    start_all([copy for _, copy in down_copies(plan, downs, plan.order, held2, down_sems)])
-    wait_bytes(held1, sems.at[0])
-    wait_bytes(held2.at[pl.ds(0, QUART)], sems.at[1])
     for part in range(QUART):
         wait_bytes(held2.at[QUART + part], down_sems.at[part])
+        grad_act[:, columns_of(plan, part)] = mm_nt(
+            cot_ref[...], block_of(plan, held2, QUART + part)
+        )
+    wait_bytes(held2.at[pl.ds(0, QUART)], sems.at[1])
+    wait_bytes(held1, sems.at[0])
 
 
 def chain_kernel(
-    plan, lengths, flag, x_ref, recv_ref, cot_ref, vec, held1, held2,
-    y_ref, dx_ref, hidden, act, slope, *refs,
+    plan, lengths, flag, x_ref, recv_ref, cot_ref, vec, held1, held2, grad_act,
+    y_out, dx_ref, hidden, act, slope, *refs,
 ):
-    outs, (xin_ref, normed, qkv, attended, middle, probs, grad_attended, grad_rows, sems) = refs[:6], refs[6:]
+    outs, (xin_ref, normed, qkv, attended, middle, probs, y_ref, grad_attended, grad_rows, sems) = refs[:6], refs[6:]
     kept = (xin_ref, normed, qkv, attended, middle, probs)
     copies = [
         pltpu.make_async_copy(source, target, sems.at[index])
@@ -303,11 +322,12 @@
     )
     start_all(copies)
     y_ref[...] = (middle[...] + second_half(plan, hidden, vec, held2, act, slope)).astype(BF16)
+    copies.append(pltpu.make_async_copy(y_ref, y_out, sems.at[len(copies)]))
+    copies[-1].start()
     branch = cot_ref[...]
     grad_hidden = None
     for part in range(QUART):
-        grad_act = mm_nt(branch, block_of(plan, held2, QUART + part))
-        grad_pre = (slope[:, columns_of(plan, part)] * grad_act).astype(BF16)
+        grad_pre = (slope[:, columns_of(plan, part)] * grad_act[:, columns_of(plan, part)]).astype(BF16)
         term = mm_nt(grad_pre, block_of(plan, held2, part))
         grad_hidden = term if grad_hidden is None else grad_hidden + term
     xhat, rstd = normalised(middle[...])
@@ -329,8 +349,8 @@
         self.plan, self.stage, self.sems, self.sent = plan, stage, sems, 0
 
     def put(self, value, copies_of):
-        slot = self.sent % 2
-        if self.sent >= 2:
+        slot = self.sent % SLOTS
+        if self.sent >= SLOTS:
             wait_bytes(self.stage.at[slot], self.sems.at[slot])
         self.sent += 1
         plan = self.plan
@@ -338,7 +358,7 @@
         start_all(copies_of(self.stage.at[slot], self.sems.at[slot]))
 
     def drain(self):
-        for slot in range(min(2, self.sent)):
+        for slot in range(min(SLOTS, self.sent)):
             wait_bytes(self.stage.at[slot], self.sems.at[slot])
 
 
@@ -354,8 +374,10 @@
     def copies_of_up(part):
         def copies(source, sem):
             return [
-                pltpu.make_async_copy(source.at[device], grads.at[place, part], sem)
-                for place, device in enumerate(plan.order)
+                pltpu.make_async_copy(
+                    source.at[pl.ds(device, count)], grads.at[pl.ds(place, count), part], sem
+                )
+                for place, device, count in runs_of(plan.order)
             ]
 
         return copies
@@ -394,14 +416,21 @@
     out.drain()
 
 
+def slot_target(plan, grads, slot):
+    if plan.parts == 1:
+        return grads[0].at[0]
+    half = plan.shards // 2
+    if slot == half + half // 2:
+        return grads[2].at[0]
+    return grads[slot // half].at[slot % half]
+
+
 def slot_copies(plan, devs, grads, block):
-    each = plan.shards // plan.parts
-
     def copies(source, sem):
         return [
             pltpu.make_async_copy(
                 source.at[devs[slot]],
-                grads[slot // each].at[slot % each, pl.ds(block * plan.rows, plan.rows)],
+                slot_target(plan, grads, slot).at[pl.ds(block * plan.rows, plan.rows)],
                 sem,
             )
             for slot in range(plan.shards)
@@ -447,7 +476,7 @@
 def rest_kernel(
     plan, many, flag, devs, lead, arr_ref, cot_ref, grad_hidden_ref, small_in, vec, *refs,
 ):
-    count = plan.shards + plan.parts * (plan.parts - 1)
+    count = plan.shards + (2 if plan.parts > 1 else 0)
     kept_in, pieces, refs = refs[:6], refs[6 : 6 + count], refs[6 + count :]
     dx_ref, small_ref = refs[:2]
     grads, refs = refs[2 : 2 + plan.parts], refs[2 + plan.parts :]
@@ -501,15 +530,14 @@
             grad_normed[item * length : (item + 1) * length]
         )
     dx_ref[...] = grad_middle_ref[...] + norm_back(grad_normed, xhat, rstd, vec[0:1, :])
-    if plan.parts == 2:
+    if plan.parts > 1:
         pack_sums(plan, lead, many, small_ref[...], stack, lines)
         packed[...] = lines[...].astype(BF16)
-        each = plan.shards // plan.parts
         start_all(
             [
                 pltpu.make_async_copy(
                     packed.at[devs[slot]],
-                    grads[slot // each].at[slot % each, pl.ds(FIRST * plan.rows, EXTRA)],
+                    slot_target(plan, grads, slot).at[pl.ds(FIRST * plan.rows, EXTRA)],
                     out_sem.at[0],
                 )
                 for slot in range(plan.shards)
@@ -740,50 +768,56 @@
     )
 
 
-def run_load(plan, devs, after, firsts, gathered):
+def run_load(plan, devs, after, cot, firsts, gathered):
     block = plan.width * plan.width
     return call(
         functools.partial(load_kernel, plan),
-        [held_blocks(plan, FIRST), held_blocks(plan, SECOND)],
-        [SMEM, ANY] + [HBM] * (1 + len(firsts)),
-        [VMEM, VMEM],
+        [held_blocks(plan, FIRST), held_blocks(plan, SECOND), inside(kept_shapes(plan)[7])],
+        [SMEM, ANY, VMEM] + [HBM] * (1 + len(firsts)),
+        [VMEM] * 3,
         [pltpu.SemaphoreType.DMA((2,)), pltpu.SemaphoreType.DMA((QUART,))],
         "load",
-        (0, (FIRST + SECOND) * block * 4),
-        2,
-        (devs, after, gathered, *firsts),
-    )
-
-
-def run_chain(plan, lengths, flag, x, recv, cot, vec, held1, held2):
+        (QUART * block * plan.tokens, (FIRST + SECOND) * block * 4),
+        4,
+        (devs, after, cot, gathered, *firsts),
+    )
+
+
+def run_chain(plan, lengths, flag, x, recv, cot, vec, held1, held2, grad_act):
     shapes = kept_shapes(plan)
     block = plan.width * plan.width
     rest = [shapes[index] for index in (0, 0, 1, 2, 3, 5)]
     return call(
         functools.partial(chain_kernel, plan),
-        [of(shapes[0]), of(shapes[0])]
+        [pltpu.HBM(*shapes[0]), of(shapes[0])]
         + [inside(shapes[index]) for index in (4, 6, 7)]
         + [pltpu.HBM(*shape) for shape in rest],
-        [SMEM] * 2 + [VMEM] * 6,
-        [VMEM] * 5 + [HBM] * len(rest),
+        [SMEM] * 2 + [VMEM] * 7,
+        [HBM] + [VMEM] * 4 + [HBM] * len(rest),
         [inside(shape) for shape in rest]
-        + [inside(shapes[0]), inside(shapes[1]), pltpu.SemaphoreType.DMA((len(rest),))],
+        + [inside(shapes[0]), inside(shapes[0]), inside(shapes[1])]
+        + [pltpu.SemaphoreType.DMA((len(rest) + 1,))],
         "chain",
         (24 * block * plan.tokens, 12 * block),
         14,
-        (lengths, flag, x, recv, cot, vec, held1, held2),
-    )
-
-
-def grad_shapes(plan, extra=0):
-    rows = FIRST * plan.rows + (extra if plan.parts == 2 else 0)
-    return [pltpu.HBM((plan.shards // plan.parts, rows, plan.width), BF16)] * plan.parts
+        (lengths, flag, x, recv, cot, vec, held1, held2, grad_act),
+    )
+
+
+def grad_shapes(plan):
+    if plan.parts == 1:
+        return [pltpu.HBM((1, FIRST * plan.rows, plan.width), BF16)]
+    rows = FIRST * plan.rows + EXTRA
+    return [
+        pltpu.HBM((count, rows, plan.width), BF16)
+        for count in (plan.shards // 2, plan.shards // 2, 1)
+    ]
 
 
 def stage_scratch(plan):
     return [
-        pltpu.VMEM((2, plan.shards, plan.rows, plan.width), BF16),
-        pltpu.SemaphoreType.DMA((2,)),
+        pltpu.VMEM((SLOTS, plan.shards, plan.rows, plan.width), BF16),
+        pltpu.SemaphoreType.DMA((SLOTS,)),
     ]
 
 
@@ -816,7 +850,7 @@
     rest = [shapes[index] for index in (0, 0, 1, 2, 3, 5)]
     input_grad, small, *grads = call(
         functools.partial(rest_kernel, plan, many),
-        [of(shapes[3]), jax.ShapeDtypeStruct((16, plan.width), F32)] + grad_shapes(plan, EXTRA),
+        [of(shapes[3]), jax.ShapeDtypeStruct((16, plan.width), F32)] + grad_shapes(plan),
         [SMEM] * 3 + [VMEM] * 5 + [HBM] * (len(rest) + len(pieces)),
         [VMEM] * 2 + [HBM] * plan.parts,
         [inside(shape) for shape in rest]
@@ -836,11 +870,14 @@
 
 def run_add(mine, other, work):
     _, rows, width = mine.shape
-    mine, other = (pltpu.with_memory_space_constraint(array, pltpu.HBM) for array in (mine, other))
+    mine = pltpu.with_memory_space_constraint(mine, pltpu.HBM)
     specs, args, plans, outs = [], [], [], []
     for way, (slot, low, high, came) in enumerate(work):
-        one = pl.BlockSpec((1, rows, width), lambda index, slot=slot: (slot, 0, 0))
-        specs += [one, one]
+        there = slot if other.shape[0] > 1 else 0
+        specs += [
+            pl.BlockSpec((1, rows, width), lambda index, slot=slot: (slot, 0, 0))
+            for slot in (slot, there)
+        ]
         args += [mine, other]
         first = None
         if came is not None:
@@ -861,7 +898,7 @@
 
 
 def run_total(one, many, shapes):
-    args = [pltpu.with_memory_space_constraint(array, pltpu.HBM) for array in (one.mine, one.other)]
+    args = [pltpu.with_memory_space_constraint(one.mine, pltpu.HBM), one.other]
     _, rows, width = one.mine.shape
     first = pl.BlockSpec((1, rows, width), lambda index: (0, 0, 0))
     whole = pl.BlockSpec((rows, width), lambda index: (0, 0))
@@ -930,21 +967,24 @@
 
 
 class RingSum:
-    def __init__(self, ring, mine, other, low):
-        self.ring, self.mine, self.other, self.low = ring, mine, other, low
+    def __init__(self, ring, mine, other, opposite, low):
+        self.ring, self.mine, self.low = ring, mine, low
+        self.other, self.opposite = other, opposite
         self.time = ring.chips // 2
         self.carried = [None, None]
 
     def add(self):
         rows = self.mine.shape[1]
+        other = self.other
         if self.carried[0] is None:
+            other = self.opposite
             work = [(self.time, 0, self.low, None), (self.time, self.low, rows, None)]
         else:
             work = [
                 (self.time, 0, rows, self.carried[0]),
                 (self.ring.chips - self.time, 0, rows, self.carried[1]),
             ]
-        self.carried = run_add(self.mine, self.other, work)
+        self.carried = run_add(self.mine, other, work)
 
     def send(self):
         self.carried = self.ring.step(*self.carried)
@@ -975,8 +1015,10 @@
         ring = Ring(count)
         first, second = pl.pallas_call(
             pack_kernel,
-            out_shape=[jax.ShapeDtypeStruct((FIRST * rows + EXTRA, width), BF16)]
-            + [jax.ShapeDtypeStruct((SECOND, rows, width), BF16)],
+            out_shape=[
+                jax.ShapeDtypeStruct((FIRST * rows + EXTRA, width), BF16),
+                jax.ShapeDtypeStruct((SECOND, rows, width), BF16),
+            ],
             scratch_shapes=[pltpu.VMEM((many, rows), F32), pltpu.VMEM((EXTRA, width), F32)],
             name="pack",
         )(qkv_weight[0], out_weight[0], up_weight[0], down_weight[0], *vectors, up_bias, lead_table[0].T)
@@ -1016,9 +1058,9 @@
     middle, hidden = run_attend(plan, lens, flag, devs, x, vec, firsts)
     first_out = run_mlp(plan, middle, hidden, vec, gathered)
     recv = shifted(first_out, "section", 1)
-    held1, held2 = run_load(plan, devs, first_out, firsts, gathered)
+    held1, held2, grad_act = run_load(plan, devs, first_out, cot, firsts, gathered)
     output, first_grad, hidden, act, slope, *kept = run_chain(
-        plan, lens, flag, x, recv, cot, vec, held1, held2
+        plan, lens, flag, x, recv, cot, vec, held1, held2, grad_act
     )
     arriving = shifted(first_grad, "section", -1)
     grad_hidden, sums, grads2 = run_mlp_back(plan, flag, arriving, cot, held2, hidden, act, slope)
@@ -1026,7 +1068,9 @@
         plan, many, flag, devs, lead, arriving, cot, grad_hidden, sums, vec, kept, firsts
     )
     if aligned:
-        first_sum = RingSum(ring, grads1[0], *ring.siblings(grads1[1:]), LOW * rows)
+        (opposite,) = ring.siblings(grads1[2:])
+        (other,) = ring.siblings([after(grads1[1], opposite)])
+        first_sum = RingSum(ring, grads1[0], other, opposite, LOW * rows)
         while first_sum.time:
             first_sum.add()
             first_sum.send()

time: 230 us -> 225 us (0.978)
  Pallas kernels: 73.2 us -> 67.2 us
    reduce_scatter x1, waiting for transfers between devices: 2.47 us -> 7.92 us  [body(): lax.psum_scatter(grads2.reshape(count * SECOND, rows, width), 'dp', scatt...]
    pallas_call x7, Pallas kernels: 60.4 us -> 55.3 us  [call(): pl.pallas_call(kernel, out_shape=outs, in_specs=in_specs, out_specs=out_s...]
    ppermute x10 -> x11, waiting for transfers between devices: 6.61 us -> 3.17 us  [siblings(): return [lax.ppermute(piece, 'dp', self.sibling) for piece in pieces]]
  transfers between devices with their start and end apart: 30 -> 31, of which waited for: 22 -> 22; matrix products, arithmetic and copies ran while one was open for 1% -> 1% of each run, Pallas kernels for 16% -> 15%
where the time goes in v5:
time: 225 us
  waiting for transfers between devices  116 us (52%)
  Pallas kernels  67.2 us (30%)
  starting transfers between devices  24.9 us (11%)
  between operations  14.3 us (6%)
  local copies, waits for them, and re-layouts  2.45 us (1%)
    pallas_call x7, Pallas kernels, call(): pl.pallas_call(kernel, out_shape=outs, in_specs=in_specs, out_specs=out_s...  55.3 us
    ppermute x8, waiting for transfers between devices, step(): lax.ppermute(ahead, 'dp', self.onward)  55.2 us
    ppermute x8, waiting for transfers between devices, step(): lax.ppermute(behind, 'dp', self.back)  34.7 us
    ppermute x8, starting transfers between devices, step(): lax.ppermute(ahead, 'dp', self.onward)  12 us
    ppermute x2, waiting for transfers between devices, shifted(): lax.ppermute(value, axis, [(source, source + steps) for source in range(f...  9.7 us
    reduce_scatter x1, waiting for transfers between devices, body(): lax.psum_scatter(grads2.reshape(count * SECOND, rows, width), 'dp', scatt...  7.92 us
    ppermute x8, starting transfers between devices, step(): lax.ppermute(behind, 'dp', self.back)  5.5 us
    ppermute x2, starting transfers between devices, shifted(): lax.ppermute(value, axis, [(source, source + steps) for source in range(f...  5.11 us
  transfers between devices with their start and end apart: 31, of which 22 were waited for; matrix products, arithmetic and copies ran while one was open for 1% of the time, Pallas kernels for 15%

profile of v5, /device:TPU:0, one launch (start us, length us, event | category | flops | bytes accessed | tf_op | source)
XLA Modules:
  0.0 224.6 jit_solution(18403576604706108420)
XLA Ops:
  7.2 2.6 %pack.1 = (bf16[208,768]{1,0:T(8,128)(2,1)}, bf16[8,48,768]{2,1,0:T(8,128)(2,1)}) custom-call(f32[48,2304]{1,0:T(8,128)} %bitcast.42, f32[48,768]{1,0:T(8,128)} %bitcast.43, f32[48,3072]{1,0:T(8,128)} %bitcast.40, f32[192,768]{1,0:T(8,128)} %bitcast.41, f32[1,48]{1,0:T(1,128)} %refs_0_.1, f32[1,48]{1,0:T(1,128)} %refs_1_.1, f32[1,48]{1,0:T(1,128)} %refs_2_.1, ...), custom_call_target="tpu_custom_call" | custom-call | tf_op jit(solution)/shard_map/pack/pallas_call | solution.py:1016
  9.9 3.1 %collective-permute-start.1 = (bf16[208,768]{1,0:T(8,128)(2,1)}, bf16[208,768]{1,0:T(8,128)(2,1)S(1)}, u32[]{:S(2)}, u32[]{:S(2)}) collective-permute-start(bf16[208,768]{1,0:T(8,128)(2,1)} %get-tuple-element.70.refs_0_.refs_6_), channel_id=1, source_target_pairs={{0,4},{1,5},{4,8},{5,9},{8,12},{9,13},{12,14},{13,15},{14,10},{15,... | collective-permute-start | bytes 958472 | tf_op jit(solution)/shard_map/ppermute | solution.py:952
  13.0 8.4 %collective-permute-done.1.refs_8_.refs_14_ = bf16[208,768]{1,0:T(8,128)(2,1)S(1)} collective-permute-done((bf16[208,768]{1,0:T(8,128)(2,1)}, bf16[208,768]{1,0:T(8,128)(2,1)S(1)}, u32[]{:S(2)}, u32[]{:S(2)}) %collective-permute-start.1) | collective-permute-done | bytes 319520 | tf_op jit(solution)/shard_map/ppermute | solution.py:952
  21.4 2.2 collective-permute-done.refs_1_.refs_7_
  23.9 1.7 collective-permute-start.3
  25.7 14.1 %collective-permute-done.2.refs_2_.refs_8_ = bf16[208,768]{1,0:T(8,128)(2,1)S(1)} collective-permute-done((bf16[208,768]{1,0:T(8,128)(2,1)S(1)}, bf16[208,768]{1,0:T(8,128)(2,1)S(1)}, u32[]{:S(2)}, u32[]{:S(2)}) %collective-permute-start.2) | collective-permute-done | bytes 319520 | tf_op jit(solution)/shard_map/ppermute | solution.py:952
  39.9 1.5 collective-permute-start.4
  42.5 13.3 %collective-permute-done.4.refs_3_.refs_9_ = bf16[208,768]{1,0:T(8,128)(2,1)S(1)} collective-permute-done((bf16[208,768]{1,0:T(8,128)(2,1)S(1)}, bf16[208,768]{1,0:T(8,128)(2,1)S(1)}, u32[]{:S(2)}, u32[]{:S(2)}) %collective-permute-start.4) | collective-permute-done | bytes 319520 | tf_op jit(solution)/shard_map/ppermute | solution.py:952
  55.7 1.4 collective-permute-done.5.refs_6_.refs_12_
  57.1 0.7 slice.7
  57.8 1.6 collective-permute-start.7
  59.5 0.7 slice.6
  62.1 7.5 %collective-permute-done.6.refs_4_.refs_10_ = bf16[96,768]{1,0:T(8,128)(2,1)} collective-permute-done((bf16[96,768]{1,0:T(8,128)(2,1)}, bf16[96,768]{1,0:T(8,128)(2,1)}, u32[]{:S(2)}, u32[]{:S(2)}) %collective-permute-start.6) | collective-permute-done | bytes 147488 | tf_op jit(solution)/shard_map/ppermute | solution.py:952
  70.2 1.1 collective-permute-done.12.refs_13_.refs_19_
  72.1 2.9 %vectors.1.vec = f32[16,768]{1,0:T(8,128)S(1)} custom-call(s32[16]{0:T(128)S(1)} %pad_add_fusion.devs, s32[2]{0:T(128)S(1)} %bitcast.33, bf16[208,768]{1,0:T(8,128)(2,1)} %get-tuple-element.70.refs_0_.refs_6_, bf16[208,768]{1,0:T(8,128)(2,1)} %copy-done.7, bf16[208,768]{1,0:T(8,128)(2,1)} %copy-done.8, bf16[208,768]{1,0:T(8,128)(2,1)} %copy-done.4, ...), custom_call_target="tpu_custom_call" | custom-call | flops 56623104 | bytes 2359296 | tf_op jit(solution)/shard_map/vectors/pallas_call | solution.py:701
  75.0 5.5 %attend.1 = (f32[192,768]{1,0:T(8,128)S(1)}, bf16[192,768]{1,0:T(8,128)(2,1)S(1)}) custom-call(s32[2]{0:T(128)S(1)} %bitcast.35, s32[1]{0:T(128)} %bitcast.1.flag, s32[16]{0:T(128)S(1)} %pad_add_fusion.devs, bf16[192,768]{1,0:T(8,128)(2,1)S(1)} %bitcast.31, f32[16,768]{1,0:T(8,128)S(1)} %vectors.1.vec, bf16[208,768]{1,0:T(8,128)(2,1)} %get-tuple-element.70.refs_0_.refs_6_, ...), custom_call_target="tpu_custom_call" | custom-call | flops 905969664 | bytes 4718592 | tf_op jit(solution)/shard_map/attend/pallas_call | solution.py:701
  80.5 5.0 %all-gather.2.cloned.1.call-done = bf16[128,48,768]{2,1,0:T(8,128)(2,1)} async-done(((bf16[8,48,768]{2,1,0:T(8,128)(2,1)}), bf16[128,48,768]{2,1,0:T(8,128)(2,1)}) %all-gather.2.cloned.1.call-update) | async-done | bytes 9437200 | tf_op jit(solution)/shard_map/all_gather | solution.py:1025
  85.6 5.1 %mlp.1.after = bf16[192,768]{1,0:T(8,128)(2,1)S(1)} custom-call(f32[192,768]{1,0:T(8,128)S(1)} %get-tuple-element.77.middle_ref, bf16[192,768]{1,0:T(8,128)(2,1)S(1)} %get-tuple-element.78.hidden_ref, f32[16,768]{1,0:T(8,128)S(1)} %vectors.1.vec, bf16[16,8,48,768]{3,2,1,0:T(8,128)(2,1)} %bitcast.37), custom_call_target="tpu_custom_call" | custom-call | flops 1811939328 | bytes 9437184 | tf_op jit(solution)/shard_map/mlp/pallas_call | solution.py:701
  90.7 3.6 %collective-permute-start.17 = (bf16[192,768]{1,0:T(8,128)(2,1)S(1)}, bf16[192,768]{1,0:T(8,128)(2,1)S(1)}, u32[]{:S(2)}, u32[]{:S(2)}) collective-permute-start(bf16[192,768]{1,0:T(8,128)(2,1)S(1)} %mlp.1.after), channel_id=1, source_target_pairs={{0,16},{1,17},{2,18},{3,19},{4,20},{5,21},{6,22},{7,23},{8,24},{9,... | collective-permute-start | bytes 884744 | tf_op jit(solution)/shard_map/ppermute | solution.py:924
  94.3 5.6 %load.1 = (bf16[4,16,48,768]{3,2,1,0:T(8,128)(2,1)S(1)}, bf16[8,16,48,768]{3,2,1,0:T(8,128)(2,1)S(1)}, f32[192,3072]{1,0:T(8,128)S(1)}) custom-call(s32[16]{0:T(128)S(1)} %pad_add_fusion.devs, bf16[192,768]{1,0:T(8,128)(2,1)S(1)} %mlp.1.after, bf16[192,768]{1,0:T(8,128)(2,1)S(1)} %bitcast.27, bf16[16,8,48,768]{3,2,1,0:T(8,128)(2,1)} %bitcast.38, ...), custom_call_target="tpu_custom_call" | custom-call | flops 905969664 | bytes 28311552 | tf_op jit(solution)/shard_map/load/pallas_call | solution.py:701
  99.9 0.9 collective-permute-done.17.recv_ref
  100.8 14.8 %chain.1 = (bf16[192,768]{1,0:T(8,128)(2,1)}, bf16[192,768]{1,0:T(8,128)(2,1)S(1)}, bf16[192,768]{1,0:T(8,128)(2,1)S(1)}, bf16[192,3072]{1,0:T(8,128)(2,1)S(1)},...) custom-call(s32[2]{0:T(128)S(1)} %bitcast.36, ...), custom_call_target="tpu_custom_call" | custom-call | flops 5435817984 | bytes 7077888 | tf_op jit(solution)/shard_map/chain/pallas_call | solution.py:701
  115.5 1.5 collective-permute-start.18
  117.1 8.8 %collective-permute-done.18.arr_ref = bf16[192,768]{1,0:T(8,128)(2,1)S(1)} collective-permute-done((bf16[192,768]{1,0:T(8,128)(2,1)S(1)}, bf16[192,768]{1,0:T(8,128)(2,1)S(1)}, u32[]{:S(2)}, u32[]{:S(2)}) %collective-permute-start.18) | collective-permute-done | bytes 294944 | tf_op jit(solution)/shard_map/ppermute | solution.py:924
  125.9 8.0 %mlp_back.1 = (f32[192,768]{1,0:T(8,128)S(1)}, f32[16,768]{1,0:T(8,128)S(1)}, bf16[16,8,48,768]{3,2,1,0:T(8,128)(2,1)}) custom-call(s32[1]{0:T(128)} %bitcast.1.flag, bf16[192,768]{1,0:T(8,128)(2,1)S(1)} %collective-permute-done.18.arr_ref, bf16[192,768]{1,0:T(8,128)(2,1)S(1)} %bitcast.29, bf16[8,16,48,768]{3,2,1,0:T(8,128)(2,1)S(1)} %get-tuple-element.81.held2, ...), custom_call_target="tpu_custom_call" | custom-call | flops 3623878656 | bytes 9437184 | tf_op jit(solution)/shard_map/mlp_back/pallas_call | solution.py:701
  133.9 13.5 %rest.1 = (f32[192,768]{1,0:T(8,128)}, f32[16,768]{1,0:T(8,128)}, bf16[8,208,768]{2,1,0:T(8,128)(2,1)}, bf16[8,208,768]{2,1,0:T(8,128)(2,1)}, bf16[1,208,768]{2,1,0:T(8,128)(2,1)}) custom-call(s32[1]{0:T(128)} %bitcast.1.flag, s32[16]{0:T(128)S(1)} %pad_add_fusion.devs, s32[2]{0:T(128)S(1)} %bitcast.34, ...), custom_call_target="tpu_custom_call" | custom-call | flops 1811939328 | bytes 9437184 | tf_op jit(solution)/shard_map/rest/pallas_call | solution.py:701
  147.5 1.8 collective-permute-done.19.refs_1_.refs_3_
  149.4 1.2 add.77
  151.1 1.6 collective-permute-start.21
  152.7 5.9 %collective-permute-done.21.refs_2_ = bf16[96,768]{1,0:T(8,128)(2,1)S(1)} collective-permute-done((bf16[96,768]{1,0:T(8,128)(2,1)S(1)}, bf16[96,768]{1,0:T(8,128)(2,1)S(1)}, u32[]{:S(2)}, u32[]{:S(2)}) %collective-permute-start.21) | collective-permute-done | bytes 147488 | tf_op jit(solution)/shard_map/ppermute | solution.py:952
  158.6 0.8 collective-permute-done.22.refs_5_
  159.5 1.3 add.78
  160.7 1.5 collective-permute-start.23
  162.3 0.5 collective-permute-start.24
  162.8 11.1 %collective-permute-done.23.refs_2_ = bf16[208,768]{1,0:T(8,128)(2,1)S(1)} collective-permute-done((bf16[208,768]{1,0:T(8,128)(2,1)S(1)}, bf16[208,768]{1,0:T(8,128)(2,1)S(1)}, u32[]{:S(2)}, u32[]{:S(2)}) %collective-permute-start.23) | collective-permute-done | bytes 319520 | tf_op jit(solution)/shard_map/ppermute | solution.py:952
  174.0 1.4 collective-permute-done.24.refs_5_
  175.4 1.3 add.79
  176.7 1.7 collective-permute-start.25
  178.8 10.7 %collective-permute-done.25.refs_2_ = bf16[208,768]{1,0:T(8,128)(2,1)S(1)} collective-permute-done((bf16[208,768]{1,0:T(8,128)(2,1)S(1)}, bf16[208,768]{1,0:T(8,128)(2,1)S(1)}, u32[]{:S(2)}, u32[]{:S(2)}) %collective-permute-start.25) | collective-permute-done | bytes 319520 | tf_op jit(solution)/shard_map/ppermute | solution.py:952
  189.5 1.4 collective-permute-done.26.refs_5_
  190.9 1.3 add.80
  192.2 1.5 collective-permute-start.27
  193.7 0.5 collective-permute-start.28
  194.3 10.0 %collective-permute-done.27.ahead = bf16[208,768]{1,0:T(8,128)(2,1)S(1)} collective-permute-done((bf16[208,768]{1,0:T(8,128)(2,1)S(1)}, bf16[208,768]{1,0:T(8,128)(2,1)S(1)}, u32[]{:S(2)}, u32[]{:S(2)}) %collective-permute-start.27) | collective-permute-done | bytes 319520 | tf_op jit(solution)/shard_map/ppermute | solution.py:952
  204.3 1.4 collective-permute-done.28.behind
  205.7 2.0 total.1
  207.7 7.9 %reduce-scatter.2.cloned.1.call-done.grads_ref = bf16[8,48,768]{2,1,0:T(8,128)(2,1)} async-done(((bf16[128,48,768]{2,1,0:T(8,128)(2,1)}), bf16[8,48,768]{2,1,0:T(8,128)(2,1)}) %reduce-scatter.2.cloned.1.call-update) | async-done | bytes 589840 | tf_op jit(solution)/shard_map/reduce_scatter | solution.py:1077
  215.6 2.1 unpack.1
  (68 shorter events, 5.9 us)
Async XLA Ops:
  7.2 64.9 %copy-start.2 = (s32[2,1]{0,1:T(1,128)S(1)}, s32[2,1]{0,1:T(1,128)}, u32[]{:S(2)}) copy-start(s32[2,1]{0,1:T(1,128)} %param.21) | copy-start | bytes 28
  7.2 78.4 %all-gather.2.cloned.1.call-start = ((), (), s32[]{:S(2)}) async-start(), calls=%async_computation.1 | async-start | bytes 10027008 | tf_op jit(solution)/shard_map/all_gather | solution.py:1025
  9.9 205.7 %reduce-scatter.2.cloned.1.call-start = ((), (), s32[]{:S(2)}) async-start(), calls=%async_computation.2 | async-start | bytes 10027008 | tf_op jit(solution)/shard_map/reduce_scatter | solution.py:1077
  9.9 11.5 %collective-permute-start.1 = (bf16[208,768]{1,0:T(8,128)(2,1)}, bf16[208,768]{1,0:T(8,128)(2,1)S(1)}, u32[]{:S(2)}, u32[]{:S(2)}) collective-permute-start(bf16[208,768]{1,0:T(8,128)(2,1)} %get-tuple-element.70.refs_0_.refs_6_), channel_id=1, source_target_pairs={{0,4},{1,5},{4,8},{5,9},{8,12},{9,13},{12,14},{13,15},{14,10},{15,... | collective-permute-start | bytes 958472 | tf_op jit(solution)/shard_map/ppermute | solution.py:952
  13.0 10.6 %collective-permute-start = (bf16[208,768]{1,0:T(8,128)(2,1)}, bf16[208,768]{1,0:T(8,128)(2,1)S(1)}, u32[]{:S(2)}, u32[]{:S(2)}) collective-permute-start(bf16[208,768]{1,0:T(8,128)(2,1)} %get-tuple-element.70.refs_0_.refs_6_), channel_id=1, source_target_pairs={{4,0},{5,1},{8,4},{9,5},{12,8},{13,9},{14,12},{15,13},{10,14},{11,... | collective-permute-start | bytes 958472 | tf_op jit(solution)/shard_map/ppermute | solution.py:952
  21.4 50.6 %copy-start.6 = (bf16[208,768]{1,0:T(8,128)(2,1)}, bf16[208,768]{1,0:T(8,128)(2,1)S(1)}, u32[]{:S(2)}) copy-start(bf16[208,768]{1,0:T(8,128)(2,1)S(1)} %collective-permute-done.1.refs_8_.refs_14_) | copy-start | bytes 958468
  23.6 48.4 %copy-start.7 = (bf16[208,768]{1,0:T(8,128)(2,1)}, bf16[208,768]{1,0:T(8,128)(2,1)S(1)}, u32[]{:S(2)}) copy-start(bf16[208,768]{1,0:T(8,128)(2,1)S(1)} %collective-permute-done.refs_1_.refs_7_) | copy-start | bytes 958468
  23.6 16.2 %collective-permute-start.2 = (bf16[208,768]{1,0:T(8,128)(2,1)S(1)}, bf16[208,768]{1,0:T(8,128)(2,1)S(1)}, u32[]{:S(2)}, u32[]{:S(2)}) collective-permute-start(bf16[208,768]{1,0:T(8,128)(2,1)S(1)} %collective-permute-done.refs_1_.refs_7_), channel_id=1, source_target_pairs={{4,0},{5,1},{8,4},{9,5},{12,8},{13,9},{14,12},{15,13},{10,14},{11,... | collective-permute-start | bytes 958472 | tf_op jit(solution)/shard_map/ppermute | solution.py:952
  23.9 16.0 %collective-permute-start.3 = (bf16[208,768]{1,0:T(8,128)(2,1)S(1)}, bf16[208,768]{1,0:T(8,128)(2,1)S(1)}, u32[]{:S(2)}, u32[]{:S(2)}) collective-permute-start(bf16[208,768]{1,0:T(8,128)(2,1)S(1)} %collective-permute-done.1.refs_8_.refs_14_), channel_id=1, source_target_pairs={{0,4},{1,5},{4,8},{5,9},{8,12},{9,13},{12,14},{13,15},{14,10},{15,... | collective-permute-start | bytes 958472 | tf_op jit(solution)/shard_map/ppermute | solution.py:952
  39.8 32.2 %copy-start.8 = (bf16[208,768]{1,0:T(8,128)(2,1)}, bf16[208,768]{1,0:T(8,128)(2,1)S(1)}, u32[]{:S(2)}) copy-start(bf16[208,768]{1,0:T(8,128)(2,1)S(1)} %collective-permute-done.2.refs_2_.refs_8_) | copy-start | bytes 958468
  39.9 32.1 %copy-start.9 = (bf16[208,768]{1,0:T(8,128)(2,1)}, bf16[208,768]{1,0:T(8,128)(2,1)S(1)}, u32[]{:S(2)}) copy-start(bf16[208,768]{1,0:T(8,128)(2,1)S(1)} %collective-permute-done.3.refs_7_.refs_13_) | copy-start | bytes 958468
  39.9 15.8 %collective-permute-start.4 = (bf16[208,768]{1,0:T(8,128)(2,1)S(1)}, bf16[208,768]{1,0:T(8,128)(2,1)S(1)}, u32[]{:S(2)}, u32[]{:S(2)}) collective-permute-start(bf16[208,768]{1,0:T(8,128)(2,1)S(1)} %collective-permute-done.2.refs_2_.refs_8_), channel_id=1, source_target_pairs={{4,0},{5,1},{8,4},{9,5},{12,8},{13,9},{14,12},{15,13},{10,14},{11,... | collective-permute-start | bytes 958472 | tf_op jit(solution)/shard_map/ppermute | solution.py:952
  41.5 15.6 %collective-permute-start.5 = (bf16[208,768]{1,0:T(8,128)(2,1)S(1)}, bf16[208,768]{1,0:T(8,128)(2,1)S(1)}, u32[]{:S(2)}, u32[]{:S(2)}) collective-permute-start(bf16[208,768]{1,0:T(8,128)(2,1)S(1)} %collective-permute-done.3.refs_7_.refs_13_), channel_id=1, source_target_pairs={{0,4},{1,5},{4,8},{5,9},{8,12},{9,13},{12,14},{13,15},{14,10},{15,... | collective-permute-start | bytes 958472 | tf_op jit(solution)/shard_map/ppermute | solution.py:952
  41.9 18.2 %collective-permute-start.8 = (bf16[208,768]{1,0:T(8,128)(2,1)}, bf16[208,768]{1,0:T(8,128)(2,1)S(1)}, u32[]{:S(2)}, u32[]{:S(2)}) collective-permute-start(bf16[208,768]{1,0:T(8,128)(2,1)} %get-tuple-element.70.refs_0_.refs_6_), channel_id=1, source_target_pairs={{0,1},{1,0},{2,3},{3,2},{4,5},{5,4},{6,7},{7,6},{8,9},{9,8},{10,11... | collective-permute-start | bytes 958472 | tf_op jit(solution)/shard_map/ppermute | solution.py:966
  41.9 18.6 %collective-permute-start.16 = (bf16[208,768]{1,0:T(8,128)(2,1)S(1)}, bf16[208,768]{1,0:T(8,128)(2,1)S(1)}, u32[]{:S(2)}, u32[]{:S(2)}) collective-permute-start(bf16[208,768]{1,0:T(8,128)(2,1)S(1)} %collective-permute-done.1.refs_8_.refs_14_), channel_id=1, source_target_pairs={{0,1},{1,0},{2,3},{3,2},{4,5},{5,4},{6,7},{7,6},{8,9},{9,8},{10,11... | collective-permute-start | bytes 958472 | tf_op jit(solution)/shard_map/ppermute | solution.py:966
  42.4 18.1 %collective-permute-start.9 = (bf16[208,768]{1,0:T(8,128)(2,1)S(1)}, bf16[208,768]{1,0:T(8,128)(2,1)S(1)}, u32[]{:S(2)}, u32[]{:S(2)}) collective-permute-start(bf16[208,768]{1,0:T(8,128)(2,1)S(1)} %collective-permute-done.refs_1_.refs_7_), channel_id=1, source_target_pairs={{0,1},{1,0},{2,3},{3,2},{4,5},{5,4},{6,7},{7,6},{8,9},{9,8},{10,11... | collective-permute-start | bytes 958472 | tf_op jit(solution)/shard_map/ppermute | solution.py:966
  55.7 16.3 %copy-start.4 = (bf16[208,768]{1,0:T(8,128)(2,1)}, bf16[208,768]{1,0:T(8,128)(2,1)S(1)}, u32[]{:S(2)}) copy-start(bf16[208,768]{1,0:T(8,128)(2,1)S(1)} %collective-permute-done.4.refs_3_.refs_9_) | copy-start | bytes 958468
  55.7 5.3 %collective-permute-start.10 = (bf16[208,768]{1,0:T(8,128)(2,1)S(1)}, bf16[208,768]{1,0:T(8,128)(2,1)S(1)}, u32[]{:S(2)}, u32[]{:S(2)}) collective-permute-start(bf16[208,768]{1,0:T(8,128)(2,1)S(1)} %collective-permute-done.2.refs_2_.refs_8_), channel_id=1, source_target_pairs={{0,1},{1,0},{2,3},{3,2},{4,5},{5,4},{6,7},{7,6},{8,9},{9,8},{10,11... | collective-permute-start | bytes 958472 | tf_op jit(solution)/shard_map/ppermute | solution.py:966
  57.1 14.9 %copy-start.5 = (bf16[208,768]{1,0:T(8,128)(2,1)}, bf16[208,768]{1,0:T(8,128)(2,1)S(1)}, u32[]{:S(2)}) copy-start(bf16[208,768]{1,0:T(8,128)(2,1)S(1)} %collective-permute-done.5.refs_6_.refs_12_) | copy-start | bytes 958468
  57.8 11.7 %collective-permute-start.7 = (bf16[112,768]{1,0:T(8,128)(2,1)}, bf16[112,768]{1,0:T(8,128)(2,1)S(1)}, u32[]{:S(2)}, u32[]{:S(2)}) collective-permute-start(bf16[112,768]{1,0:T(8,128)(2,1)} %slice.7), channel_id=1, source_target_pairs={{4,0},{5,1},{8,4},{9,5},{12,8},{13,9},{14,12},{15,13},{10,14},{11,... | collective-permute-start | bytes 516104 | tf_op jit(solution)/shard_map/ppermute | solution.py:952
  60.1 11.9 %copy-start.10 = (bf16[208,768]{1,0:T(8,128)(2,1)}, bf16[208,768]{1,0:T(8,128)(2,1)S(1)}, u32[]{:S(2)}) copy-start(bf16[208,768]{1,0:T(8,128)(2,1)S(1)} %collective-permute-done.8.refs_9_.refs_15_) | copy-start | bytes 958468
  60.1 9.4 %collective-permute-start.6 = (bf16[96,768]{1,0:T(8,128)(2,1)}, bf16[96,768]{1,0:T(8,128)(2,1)}, u32[]{:S(2)}, u32[]{:S(2)}) collective-permute-start(bf16[96,768]{1,0:T(8,128)(2,1)} %slice.6), channel_id=1, source_target_pairs={{0,4},{1,5},{4,8},{5,9},{8,12},{9,13},{12,14},{13,15},{14,10},{15,... | collective-permute-start | bytes 442376 | tf_op jit(solution)/shard_map/ppermute | solution.py:952
  60.5 11.5 %copy-start.11 = (bf16[208,768]{1,0:T(8,128)(2,1)}, bf16[208,768]{1,0:T(8,128)(2,1)S(1)}, u32[]{:S(2)}) copy-start(bf16[208,768]{1,0:T(8,128)(2,1)S(1)} %collective-permute-done.16.refs_17_.refs_23_) | copy-start | bytes 958468
  60.5 9.6 %collective-permute-start.15 = (bf16[208,768]{1,0:T(8,128)(2,1)S(1)}, bf16[208,768]{1,0:T(8,128)(2,1)S(1)}, u32[]{:S(2)}, u32[]{:S(2)}) collective-permute-start(bf16[208,768]{1,0:T(8,128)(2,1)S(1)} %collective-permute-done.3.refs_7_.refs_13_), channel_id=1, source_target_pairs={{0,1},{1,0},{2,3},{3,2},{4,5},{5,4},{6,7},{7,6},{8,9},{9,8},{10,11... | collective-permute-start | bytes 958472 | tf_op jit(solution)/shard_map/ppermute | solution.py:966
  60.6 0.8 copy-start.12
  60.6 10.7 %collective-permute-start.11 = (bf16[208,768]{1,0:T(8,128)(2,1)S(1)}, bf16[208,768]{1,0:T(8,128)(2,1)S(1)}, u32[]{:S(2)}, u32[]{:S(2)}) collective-permute-start(bf16[208,768]{1,0:T(8,128)(2,1)S(1)} %collective-permute-done.4.refs_3_.refs_9_), channel_id=1, source_target_pairs={{0,1},{1,0},{2,3},{3,2},{4,5},{5,4},{6,7},{7,6},{8,9},{9,8},{10,11... | collective-permute-start | bytes 958472 | tf_op jit(solution)/shard_map/ppermute | solution.py:966
  61.3 0.7 copy-start.13
  61.3 9.9 %collective-permute-start.14 = (bf16[208,768]{1,0:T(8,128)(2,1)S(1)}, bf16[208,768]{1,0:T(8,128)(2,1)}, u32[]{:S(2)}, u32[]{:S(2)}) collective-permute-start(bf16[208,768]{1,0:T(8,128)(2,1)S(1)} %collective-permute-done.5.refs_6_.refs_12_), channel_id=1, source_target_pairs={{0,1},{1,0},{2,3},{3,2},{4,5},{5,4},{6,7},{7,6},{8,9},{9,8},{10,11... | collective-permute-start | bytes 958472 | tf_op jit(solution)/shard_map/ppermute | solution.py:966
  69.5 1.7 collective-permute-start.12
  69.6 2.5 %copy-start.16 = (bf16[112,768]{1,0:T(8,128)(2,1)}, bf16[112,768]{1,0:T(8,128)(2,1)S(1)}, u32[]{:S(2)}) copy-start(bf16[112,768]{1,0:T(8,128)(2,1)S(1)} %collective-permute-done.7.refs_5_.refs_11_) | copy-start | bytes 516100
  69.6 1.9 collective-permute-start.13
  70.2 1.3 copy-start.14
  71.3 0.7 copy-start.15
  72.1 2.9 %copy-start.1 = (bf16[2,1,96,768]{3,2,1,0:T(8,128)(2,1)S(1)}, bf16[2,1,96,768]{3,2,1,0:T(8,128)(2,1)}, u32[]{:S(2)}) copy-start(bf16[2,1,96,768]{3,2,1,0:T(8,128)(2,1)} %param.18) | copy-start | bytes 884740
  72.1 2.9 %copy-start.3 = (s32[2,1]{0,1:T(1,128)S(1)}, s32[2,1]{0,1:T(1,128)}, u32[]{:S(2)}) copy-start(s32[2,1]{0,1:T(1,128)} %param.20) | copy-start | bytes 28
  85.6 8.7 %copy-start = (bf16[2,1,96,768]{3,2,1,0:T(8,128)(2,1)S(1)}, bf16[2,1,96,768]{3,2,1,0:T(8,128)(2,1)}, u32[]{:S(2)}) copy-start(bf16[2,1,96,768]{3,2,1,0:T(8,128)(2,1)} %param.19) | copy-start | bytes 884740
  90.7 10.1 %collective-permute-start.17 = (bf16[192,768]{1,0:T(8,128)(2,1)S(1)}, bf16[192,768]{1,0:T(8,128)(2,1)S(1)}, u32[]{:S(2)}, u32[]{:S(2)}) collective-permute-start(bf16[192,768]{1,0:T(8,128)(2,1)S(1)} %mlp.1.after), channel_id=1, source_target_pairs={{0,16},{1,17},{2,18},{3,19},{4,20},{5,21},{6,22},{7,23},{8,24},{9,... | collective-permute-start | bytes 884744 | tf_op jit(solution)/shard_map/ppermute | solution.py:924
  115.5 10.4 %collective-permute-start.18 = (bf16[192,768]{1,0:T(8,128)(2,1)S(1)}, bf16[192,768]{1,0:T(8,128)(2,1)S(1)}, u32[]{:S(2)}, u32[]{:S(2)}) collective-permute-start(bf16[192,768]{1,0:T(8,128)(2,1)S(1)} %get-tuple-element.84), channel_id=1, source_target_pairs={{16,0},{17,1},{18,2},{19,3},{20,4},{21,5},{22,6},{23,7},{24,8},{25... | collective-permute-start | bytes 884744 | tf_op jit(solution)/shard_map/ppermute | solution.py:924
  147.4 1.9 collective-permute-start.19
  149.3 10.2 %collective-permute-start.20 = (bf16[8,208,768]{2,1,0:T(8,128)(2,1)}, bf16[8,208,768]{2,1,0:T(8,128)(2,1)S(1)}, u32[]{:S(2)}, u32[]{:S(2)}) collective-permute-start(bf16[8,208,768]{2,1,0:T(8,128)(2,1)} %get-tuple-element.100), channel_id=1, source_target_pairs={{0,1},{1,0},{2,3},{3,2},{4,5},{5,4},{6,7},{7,6},{8,9},{9,8},{10,11... | collective-permute-start | bytes 7667720 | tf_op jit(solution)/shard_map/ppermute | solution.py:966
  150.6 8.9 %collective-permute-start.22 = (bf16[112,768]{1,0:T(8,128)(2,1)S(1)}, bf16[112,768]{1,0:T(8,128)(2,1)S(1)}, u32[]{:S(2)}, u32[]{:S(2)}) collective-permute-start(bf16[112,768]{1,0:T(8,128)(2,1)S(1)} %get-tuple-element.102), channel_id=1, source_target_pairs={{4,0},{5,1},{8,4},{9,5},{12,8},{13,9},{14,12},{15,13},{10,14},{11,... | collective-permute-start | bytes 516104 | tf_op jit(solution)/shard_map/ppermute | solution.py:952
  151.1 7.5 %collective-permute-start.21 = (bf16[96,768]{1,0:T(8,128)(2,1)S(1)}, bf16[96,768]{1,0:T(8,128)(2,1)S(1)}, u32[]{:S(2)}, u32[]{:S(2)}) collective-permute-start(bf16[96,768]{1,0:T(8,128)(2,1)S(1)} %get-tuple-element.101), channel_id=1, source_target_pairs={{0,4},{1,5},{4,8},{5,9},{8,12},{9,13},{12,14},{13,15},{14,10},{15,... | collective-permute-start | bytes 442376 | tf_op jit(solution)/shard_map/ppermute | solution.py:952
  160.7 13.2 %collective-permute-start.23 = (bf16[208,768]{1,0:T(8,128)(2,1)S(1)}, bf16[208,768]{1,0:T(8,128)(2,1)S(1)}, u32[]{:S(2)}, u32[]{:S(2)}) collective-permute-start(bf16[208,768]{1,0:T(8,128)(2,1)S(1)} %get-tuple-element.103), channel_id=1, source_target_pairs={{0,4},{1,5},{4,8},{5,9},{8,12},{9,13},{12,14},{13,15},{14,10},{15,... | collective-permute-start | bytes 958472 | tf_op jit(solution)/shard_map/ppermute | solution.py:952
  162.3 13.1 %collective-permute-start.24 = (bf16[208,768]{1,0:T(8,128)(2,1)S(1)}, bf16[208,768]{1,0:T(8,128)(2,1)S(1)}, u32[]{:S(2)}, u32[]{:S(2)}) collective-permute-start(bf16[208,768]{1,0:T(8,128)(2,1)S(1)} %get-tuple-element.104), channel_id=1, source_target_pairs={{4,0},{5,1},{8,4},{9,5},{12,8},{13,9},{14,12},{15,13},{10,14},{11,... | collective-permute-start | bytes 958472 | tf_op jit(solution)/shard_map/ppermute | solution.py:952
  176.7 12.8 %collective-permute-start.25 = (bf16[208,768]{1,0:T(8,128)(2,1)S(1)}, bf16[208,768]{1,0:T(8,128)(2,1)S(1)}, u32[]{:S(2)}, u32[]{:S(2)}) collective-permute-start(bf16[208,768]{1,0:T(8,128)(2,1)S(1)} %get-tuple-element.105), channel_id=1, source_target_pairs={{0,4},{1,5},{4,8},{5,9},{8,12},{9,13},{12,14},{13,15},{14,10},{15,... | collective-permute-start | bytes 958472 | tf_op jit(solution)/shard_map/ppermute | solution.py:952
  178.4 12.5 %collective-permute-start.26 = (bf16[208,768]{1,0:T(8,128)(2,1)S(1)}, bf16[208,768]{1,0:T(8,128)(2,1)S(1)}, u32[]{:S(2)}, u32[]{:S(2)}) collective-permute-start(bf16[208,768]{1,0:T(8,128)(2,1)S(1)} %get-tuple-element.106), channel_id=1, source_target_pairs={{4,0},{5,1},{8,4},{9,5},{12,8},{13,9},{14,12},{15,13},{10,14},{11,... | collective-permute-start | bytes 958472 | tf_op jit(solution)/shard_map/ppermute | solution.py:952
  192.2 12.1 %collective-permute-start.27 = (bf16[208,768]{1,0:T(8,128)(2,1)S(1)}, bf16[208,768]{1,0:T(8,128)(2,1)S(1)}, u32[]{:S(2)}, u32[]{:S(2)}) collective-permute-start(bf16[208,768]{1,0:T(8,128)(2,1)S(1)} %get-tuple-element.107), channel_id=1, source_target_pairs={{0,4},{1,5},{4,8},{5,9},{8,12},{9,13},{12,14},{13,15},{14,10},{15,... | collective-permute-start | bytes 958472 | tf_op jit(solution)/shard_map/ppermute | solution.py:952
  193.7 11.9 %collective-permute-start.28 = (bf16[208,768]{1,0:T(8,128)(2,1)S(1)}, bf16[208,768]{1,0:T(8,128)(2,1)S(1)}, u32[]{:S(2)}, u32[]{:S(2)}) collective-permute-start(bf16[208,768]{1,0:T(8,128)(2,1)S(1)} %get-tuple-element.108), channel_id=1, source_target_pairs={{4,0},{5,1},{8,4},{9,5},{12,8},{13,9},{14,12},{15,13},{10,14},{11,... | collective-permute-start | bytes 958472 | tf_op jit(solution)/shard_map/ppermute | solution.py:952
Sparse Core Ops, SparseCore 0:
  10.2 75.3 all-gather.1
  134.0 81.5 reduce-scatter.1

commit v6 on v5

--- a/solution.py
+++ b/solution.py
@@ -21,7 +21,6 @@
 QUART = 4
 EXTRA = 16
 LOW = 2
-SLOTS = 4
 
 
 def mm(left, right):
@@ -236,9 +235,9 @@
     return total + vec[7:8, :]
 
 
-def attention_back(plan, probs_ref, qkv_ref, grad_attended_ref, rows_ref):
+def attention_back(plan, probs_ref, qkv_ref, grad_attended_ref, rows_ref, items=None):
     width, length = plan.width, plan.length
-    for item in range(plan.items):
+    for item in range(plan.items) if items is None else items:
         rows = slice(item * length, (item + 1) * length)
         for pair in range(plan.pairs):
             at = pair * PAIR
@@ -276,19 +275,21 @@
     )
 
 
-def mlp_kernel(plan, middle_ref, hidden_ref, vec, gathered, y_ref, held, sems, down_sems):
-    _, downs = second_pieces(plan, gathered)
-    down = down_copies(plan, downs, plan.order, held, down_sems)
-    for part in range(QUART):
-        start_all(up_copies(plan, gathered, held, sems.at[part], part))
-        start_all([copy for block, copy in down if block == part])
-
-    def wait(block):
-        sem = sems.at[block] if block < QUART else down_sems.at[block - QUART]
-        wait_bytes(held.at[block], sem)
-
-    total = second_half(plan, hidden_ref, vec, held, wait=wait)
-    y_ref[...] = (middle_ref[...] + total).astype(BF16)
+def mlp_kernel(plan, flag, middle_ref, hidden_ref, vec, gathered, y_ref, held, sems, down_sems):
+    @pl.when(flag[0] == 0)
+    def _():
+        _, downs = second_pieces(plan, gathered)
+        down = down_copies(plan, downs, plan.order, held, down_sems)
+        for part in range(QUART):
+            start_all(up_copies(plan, gathered, held, sems.at[part], part))
+            start_all([copy for block, copy in down if block == part])
+
+        def wait(block):
+            sem = sems.at[block] if block < QUART else down_sems.at[block - QUART]
+            wait_bytes(held.at[block], sem)
+
+        total = second_half(plan, hidden_ref, vec, held, wait=wait)
+        y_ref[...] = (middle_ref[...] + total).astype(BF16)
 
 
 def load_kernel(plan, devs, after, cot_ref, gathered, *refs):
@@ -306,11 +307,22 @@
     wait_bytes(held1, sems.at[0])
 
 
+def input_grad(plan, items, vec, held1, xin_ref, qkv, probs, grad_middle, grad_attended, grad_rows, dx_ref):
+    attention_back(plan, probs, qkv, grad_attended, grad_rows, items)
+    rows = slice(items.start * plan.length, items.stop * plan.length)
+    grad_normed = None
+    for part in range(OUT):
+        term = mm_nt(grad_rows[rows, columns_of(plan, part)], block_of(plan, held1, part))
+        grad_normed = term if grad_normed is None else grad_normed + term
+    xhat, rstd = normalised(xin_ref[rows, :].astype(F32))
+    dx_ref[...] = (grad_middle[rows, :] + norm_back(grad_normed, xhat, rstd, vec[0:1, :])).astype(BF16)
+
+
 def chain_kernel(
     plan, lengths, flag, x_ref, recv_ref, cot_ref, vec, held1, held2, grad_act,
-    y_out, dx_ref, hidden, act, slope, *refs,
+    y_out, dx_ref, hidden, act, slope, xin_ref, qkv, probs, grad_middle, grad_attended, *refs,
 ):
-    outs, (xin_ref, normed, qkv, attended, middle, probs, y_ref, grad_attended, grad_rows, sems) = refs[:6], refs[6:]
+    outs, (normed, attended, middle, y_ref, grad_rows, sems) = refs[:6], refs[6:]
     kept = (xin_ref, normed, qkv, attended, middle, probs)
     copies = [
         pltpu.make_async_copy(source, target, sems.at[index])
@@ -324,24 +336,33 @@
     y_ref[...] = (middle[...] + second_half(plan, hidden, vec, held2, act, slope)).astype(BF16)
     copies.append(pltpu.make_async_copy(y_ref, y_out, sems.at[len(copies)]))
     copies[-1].start()
-    branch = cot_ref[...]
-    grad_hidden = None
-    for part in range(QUART):
-        grad_pre = (slope[:, columns_of(plan, part)] * grad_act[:, columns_of(plan, part)]).astype(BF16)
-        term = mm_nt(grad_pre, block_of(plan, held2, part))
-        grad_hidden = term if grad_hidden is None else grad_hidden + term
-    xhat, rstd = normalised(middle[...])
-    grad_middle = branch.astype(F32) + norm_back(grad_hidden, xhat, rstd, vec[5:6, :])
-    grad_attended[...] = mm_nt(grad_middle.astype(BF16), block_of(plan, held1, OUT)).astype(BF16)
-    attention_back(plan, probs, qkv, grad_attended, grad_rows)
-    grad_normed = None
-    for part in range(OUT):
-        term = mm_nt(grad_rows[:, columns_of(plan, part)], block_of(plan, held1, part))
-        grad_normed = term if grad_normed is None else grad_normed + term
-    xhat, rstd = normalised(xin_ref[...].astype(F32))
-    dx_ref[...] = (grad_middle + norm_back(grad_normed, xhat, rstd, vec[0:1, :])).astype(BF16)
+
+    @pl.when(flag[0] == 1)
+    def _():
+        branch = cot_ref[...]
+        grad_hidden = None
+        for part in range(QUART):
+            grad_pre = (slope[:, columns_of(plan, part)] * grad_act[:, columns_of(plan, part)]).astype(BF16)
+            term = mm_nt(grad_pre, block_of(plan, held2, part))
+            grad_hidden = term if grad_hidden is None else grad_hidden + term
+        xhat, rstd = normalised(middle[...])
+        grad_middle[...] = branch.astype(F32) + norm_back(grad_hidden, xhat, rstd, vec[5:6, :])
+        grad_attended[...] = mm_nt(grad_middle[...].astype(BF16), block_of(plan, held1, OUT)).astype(BF16)
+        input_grad(
+            plan, range(plan.items // 2), vec, held1, xin_ref, qkv, probs, grad_middle, grad_attended, grad_rows, dx_ref
+        )
+
     for copy in copies:
         copy.wait()
+
+
+def chain_end_kernel(plan, flag, vec, held1, xin_ref, qkv, probs, grad_middle, grad_attended, dx_ref, grad_rows):
+    @pl.when(flag[0] == 1)
+    def _():
+        input_grad(
+            plan, range(plan.items // 2, plan.items), vec, held1, xin_ref, qkv, probs, grad_middle, grad_attended,
+            grad_rows, dx_ref,
+        )
 
 
 class Stage:
@@ -349,8 +370,9 @@
         self.plan, self.stage, self.sems, self.sent = plan, stage, sems, 0
 
     def put(self, value, copies_of):
-        slot = self.sent % SLOTS
-        if self.sent >= SLOTS:
+        slots = self.stage.shape[0]
+        slot = self.sent % slots
+        if self.sent >= slots:
             wait_bytes(self.stage.at[slot], self.sems.at[slot])
         self.sent += 1
         plan = self.plan
@@ -358,17 +380,16 @@
         start_all(copies_of(self.stage.at[slot], self.sems.at[slot]))
 
     def drain(self):
-        for slot in range(min(SLOTS, self.sent)):
+        for slot in range(min(self.stage.shape[0], self.sent)):
             wait_bytes(self.stage.at[slot], self.sems.at[slot])
 
 
 def mlp_back_kernel(
-    plan, flag, arr_ref, cot_ref, held2, hidden, act, slope,
-    grad_hidden_ref, small_ref, grads, grad_pre_ref, stage, stage_sems,
+    plan, flag, some_ref, other_ref, cot_ref, held2, hidden, act, slope,
+    grad_pre_out, small_ref, grads, grad_pre_ref, stage, stage_sems, pre_sem,
 ):
-    branch = jnp.where(flag[0] == 0, arr_ref[...], cot_ref[...])
-    small_ref[...] = jnp.zeros_like(small_ref)
-    small_ref[7:8, :] = column_sum(branch)
+    arrived = jnp.concatenate([some_ref[...], other_ref[...]], 0)
+    branch = jnp.where(flag[0] == 0, arrived, cot_ref[...])
     out = Stage(plan, stage, stage_sems)
 
     def copies_of_up(part):
@@ -400,20 +421,21 @@
 
         return copies
 
-    grad_hidden = None
     for part in range(QUART):
         columns = columns_of(plan, part)
         grad_act = mm_nt(branch, block_of(plan, held2, QUART + part))
         grad_pre = (slope[:, columns] * grad_act).astype(BF16)
         grad_pre_ref[:, columns] = grad_pre
-        small_ref[8 + part : 9 + part, :] = column_sum(grad_pre)
-        term = mm_nt(grad_pre, block_of(plan, held2, part))
-        grad_hidden = term if grad_hidden is None else grad_hidden + term
         out.put(mm_tn(act[:, columns], branch), copies_of_down(part))
-    grad_hidden_ref[...] = grad_hidden
+        out.put(mm_tn(hidden[...], grad_pre), copies_of_up(part))
+    copy = pltpu.make_async_copy(grad_pre_ref, grad_pre_out, pre_sem.at[0])
+    copy.start()
+    small_ref[...] = jnp.zeros_like(small_ref)
+    small_ref[7:8, :] = column_sum(branch)
     for part in range(QUART):
-        out.put(mm_tn(hidden[...], grad_pre_ref[:, columns_of(plan, part)]), copies_of_up(part))
+        small_ref[8 + part : 9 + part, :] = column_sum(grad_pre_ref[:, columns_of(plan, part)])
     out.drain()
+    copy.wait()
 
 
 def slot_target(plan, grads, slot):
@@ -474,15 +496,19 @@
 
 
 def rest_kernel(
-    plan, many, flag, devs, lead, arr_ref, cot_ref, grad_hidden_ref, small_in, vec, *refs,
+    plan, many, flag, devs, lead, some_ref, other_ref, cot_ref, small_in, vec, gathered, grad_pre_in, *refs,
 ):
     count = plan.shards + (2 if plan.parts > 1 else 0)
     kept_in, pieces, refs = refs[:6], refs[6 : 6 + count], refs[6 + count :]
     dx_ref, small_ref = refs[:2]
     grads, refs = refs[2 : 2 + plan.parts], refs[2 + plan.parts :]
-    kept, refs = refs[:6], refs[6:]
+    kept, (held2, grad_pre, up_sems, pre_sem), refs = refs[:6], refs[6:10], refs[10:]
     held, grad_middle_ref, grad_attended, grad_rows, sems, kept_sems, stage, stage_sems, out_sem, stack, lines, packed = refs
     xin_ref, normed, qkv, attended, middle_ref, probs = kept
+    pre_copy = pltpu.make_async_copy(grad_pre_in, grad_pre, pre_sem.at[0])
+    pre_copy.start()
+    for part in range(QUART):
+        start_all(up_copies(plan, gathered, held2, up_sems.at[part], part))
     start_all(first_copies(plan, pieces, devs, held, sems.at[1], pl.ds(OUT, 1)))
     copies = [
         pltpu.make_async_copy(source, target, kept_sems.at[index])
@@ -492,10 +518,16 @@
         copies[index].start()
     start_all(first_copies(plan, pieces, devs, held, sems.at[0], pl.ds(0, OUT)))
     length = plan.length
-    branch = jnp.where(flag[0] == 0, arr_ref[...], cot_ref[...])
+    arrived = jnp.concatenate([some_ref[...], other_ref[...]], 0)
+    branch = jnp.where(flag[0] == 0, arrived, cot_ref[...])
     out = Stage(plan, stage, stage_sems)
     small_ref[...] = small_in[...]
-    grad_hidden = grad_hidden_ref[...]
+    pre_copy.wait()
+    grad_hidden = None
+    for part in range(QUART):
+        wait_bytes(held2.at[part], up_sems.at[part])
+        term = mm_nt(grad_pre[:, columns_of(plan, part)], block_of(plan, held2, part))
+        grad_hidden = term if grad_hidden is None else grad_hidden + term
     copies[4].wait()
     xhat, rstd = normalised(middle_ref[...])
     small_ref[5:6, :] = column_sum(grad_hidden * xhat)
@@ -753,18 +785,18 @@
     )
 
 
-def run_mlp(plan, middle, hidden, vec, gathered):
+def run_mlp(plan, flag, middle, hidden, vec, gathered):
     block = plan.width * plan.width
     return call(
         functools.partial(mlp_kernel, plan),
         jax.ShapeDtypeStruct(hidden.shape, BF16),
-        [VMEM, VMEM, VMEM, HBM],
+        [SMEM, VMEM, VMEM, VMEM, HBM],
         VMEM,
         [held_blocks(plan, SECOND), pltpu.SemaphoreType.DMA((QUART,)), pltpu.SemaphoreType.DMA((QUART,))],
         "mlp",
         (SECOND * block * plan.tokens, SECOND * block * 2),
         16,
-        (middle, hidden, vec, gathered),
+        (flag, middle, hidden, vec, gathered),
     )
 
 
@@ -787,20 +819,38 @@
     shapes = kept_shapes(plan)
     block = plan.width * plan.width
     rest = [shapes[index] for index in (0, 0, 1, 2, 3, 5)]
-    return call(
+    some = ((plan.items // 2 * plan.length, plan.width), BF16)
+    results = call(
         functools.partial(chain_kernel, plan),
-        [pltpu.HBM(*shapes[0]), of(shapes[0])]
-        + [inside(shapes[index]) for index in (4, 6, 7)]
+        [pltpu.HBM(*shapes[0]), of(some)]
+        + [inside(shapes[index]) for index in (4, 6, 7, 0, 1, 5, 3, 0)]
         + [pltpu.HBM(*shape) for shape in rest],
         [SMEM] * 2 + [VMEM] * 7,
-        [HBM] + [VMEM] * 4 + [HBM] * len(rest),
-        [inside(shape) for shape in rest]
-        + [inside(shapes[0]), inside(shapes[0]), inside(shapes[1])]
+        [HBM] + [VMEM] * 9 + [HBM] * len(rest),
+        [inside(shapes[index]) for index in (0, 2, 3, 0, 1)]
         + [pltpu.SemaphoreType.DMA((len(rest) + 1,))],
         "chain",
-        (24 * block * plan.tokens, 12 * block),
-        14,
+        (20 * block * plan.tokens, 12 * block),
+        12,
         (lengths, flag, x, recv, cot, vec, held1, held2, grad_act),
+    )
+    return results[0], results[1], results[2:5], results[5:10], results[10:]
+
+
+def run_chain_end(plan, flag, vec, held1, end):
+    shapes = kept_shapes(plan)
+    block = plan.width * plan.width
+    left = plan.items - plan.items // 2
+    return call(
+        functools.partial(chain_end_kernel, plan),
+        of(((left * plan.length, plan.width), BF16)),
+        [SMEM] + [VMEM] * 7,
+        VMEM,
+        [inside(shapes[1])],
+        "chain_end",
+        (2 * block * plan.tokens, 3 * block),
+        6,
+        (flag, vec, held1, *end),
     )
 
 
@@ -814,10 +864,10 @@
     ]
 
 
-def stage_scratch(plan):
+def stage_scratch(plan, slots):
     return [
-        pltpu.VMEM((SLOTS, plan.shards, plan.rows, plan.width), BF16),
-        pltpu.SemaphoreType.DMA((SLOTS,)),
+        pltpu.VMEM((slots, plan.shards, plan.rows, plan.width), BF16),
+        pltpu.SemaphoreType.DMA((slots,)),
     ]
 
 
@@ -827,21 +877,21 @@
     return call(
         functools.partial(mlp_back_kernel, plan),
         [
-            of(shapes[3]),
+            pltpu.HBM(*shapes[6]),
             jax.ShapeDtypeStruct((16, plan.width), F32),
             pltpu.HBM((plan.shards, SECOND, plan.rows, plan.width), BF16),
         ],
-        [SMEM] + [VMEM] * 6,
-        [VMEM, VMEM, HBM],
-        [inside(shapes[6])] + stage_scratch(plan),
+        [SMEM] + [VMEM] * 7,
+        [HBM, VMEM, HBM],
+        [inside(shapes[6])] + stage_scratch(plan, SECOND) + [pltpu.SemaphoreType.DMA((1,))],
         "mlp_back",
         (2 * SECOND * block * plan.tokens, SECOND * block * 2),
-        10,
-        (flag, arriving, cot, held2, hidden, act, slope),
-    )
-
-
-def run_rest(plan, many, flag, devs, lead, arriving, cot, grad_hidden, small, vec, kept, pieces):
+        16,
+        (flag, *arriving, cot, held2, hidden, act, slope),
+    )
+
+
+def run_rest(plan, many, flag, devs, lead, arriving, cot, small, vec, gathered, grad_pre, kept, pieces):
     shapes = kept_shapes(plan)
     block = plan.width * plan.width
     across = plan.width // plan.rows
@@ -851,19 +901,21 @@
     input_grad, small, *grads = call(
         functools.partial(rest_kernel, plan, many),
         [of(shapes[3]), jax.ShapeDtypeStruct((16, plan.width), F32)] + grad_shapes(plan),
-        [SMEM] * 3 + [VMEM] * 5 + [HBM] * (len(rest) + len(pieces)),
+        [SMEM] * 3 + [VMEM] * 5 + [HBM] * (2 + len(rest) + len(pieces)),
         [VMEM] * 2 + [HBM] * plan.parts,
         [inside(shape) for shape in rest]
+        + [held_blocks(plan, QUART), inside(shapes[6])]
+        + [pltpu.SemaphoreType.DMA((QUART,)), pltpu.SemaphoreType.DMA((1,))]
         + [held_blocks(plan, FIRST)]
         + [inside(shapes[index]) for index in (3, 0, 1)]
         + [pltpu.SemaphoreType.DMA((2,)), pltpu.SemaphoreType.DMA((len(rest),))]
-        + stage_scratch(plan)
+        + stage_scratch(plan, FIRST)
         + [pltpu.SemaphoreType.DMA((1,)), pltpu.VMEM((plan.shards * high, plan.rows), BF16)]
         + [pltpu.VMEM(lines, F32), pltpu.VMEM(lines, BF16)],
         "rest",
-        (2 * FIRST * block * plan.tokens, 2 * FIRST * block * 2),
-        26,
-        (flag, devs, lead, arriving, cot, grad_hidden, small, vec, *kept, *pieces),
+        (3 * FIRST * block * plan.tokens, 3 * FIRST * block * 2),
+        34,
+        (flag, devs, lead, *arriving, cot, small, vec, gathered, grad_pre, *kept, *pieces),
     )
     return input_grad, small, grads
 
@@ -1056,16 +1108,17 @@
         )
 
     middle, hidden = run_attend(plan, lens, flag, devs, x, vec, firsts)
-    first_out = run_mlp(plan, middle, hidden, vec, gathered)
+    first_out = run_mlp(plan, flag, middle, hidden, vec, gathered)
     recv = shifted(first_out, "section", 1)
     held1, held2, grad_act = run_load(plan, devs, first_out, cot, firsts, gathered)
-    output, first_grad, hidden, act, slope, *kept = run_chain(
+    output, some_grad, (hidden, act, slope), end, kept = run_chain(
         plan, lens, flag, x, recv, cot, vec, held1, held2, grad_act
     )
-    arriving = shifted(first_grad, "section", -1)
-    grad_hidden, sums, grads2 = run_mlp_back(plan, flag, arriving, cot, held2, hidden, act, slope)
+    other_grad = run_chain_end(plan, flag, vec, held1, end)
+    arriving = [shifted(grad, "section", -1) for grad in (some_grad, other_grad)]
+    grad_pre, sums, grads2 = run_mlp_back(plan, flag, arriving, cot, held2, hidden, act, slope)
     input_grad, sums, grads1 = run_rest(
-        plan, many, flag, devs, lead, arriving, cot, grad_hidden, sums, vec, kept, firsts
+        plan, many, flag, devs, lead, arriving, cot, sums, vec, gathered, grad_pre, kept, firsts
     )
     if aligned:
         (opposite,) = ring.siblings(grads1[2:])

time: 225 us -> 220 us (0.978)
  Pallas kernels: 67.2 us -> 63.4 us
    reduce_scatter x1, waiting for transfers between devices: 7.92 us -> 2.4 us  [body(): lax.psum_scatter(grads2.reshape(count * SECOND, rows, width), 'dp', scatt...]
    ppermute x2 -> x3, waiting for transfers between devices: 9.7 us -> 14.7 us  [shifted(): lax.ppermute(value, axis, [(source, source + steps) for source in range(f...]
    pallas_call x7 -> x8, Pallas kernels: 55.3 us -> 51.6 us  [call(): pl.pallas_call(kernel, out_shape=outs, in_specs=in_specs, out_specs=out_s...]
    ppermute x2 -> x3, starting transfers between devices: 5.11 us -> 4.29 us  [shifted(): lax.ppermute(value, axis, [(source, source + steps) for source in range(f...]
  transfers between devices with their start and end apart: 31 -> 32, of which waited for: 22 -> 23; matrix products, arithmetic and copies ran while one was open for 1% -> 1% of each run, Pallas kernels for 15% -> 18%
where the time goes in v6:
time: 220 us
  waiting for transfers between devices  115 us (52%)
  Pallas kernels  63.4 us (29%)
  starting transfers between devices  24 us (11%)
  between operations  14.3 us (6%)
  local copies, waits for them, and re-layouts  2.56 us (1%)
    ppermute x8, waiting for transfers between devices, step(): lax.ppermute(ahead, 'dp', self.onward)  55.4 us
    pallas_call x8, Pallas kernels, call(): pl.pallas_call(kernel, out_shape=outs, in_specs=in_specs, out_specs=out_s...  51.6 us
    ppermute x8, waiting for transfers between devices, step(): lax.ppermute(behind, 'dp', self.back)  34.6 us
    ppermute x3, waiting for transfers between devices, shifted(): lax.ppermute(value, axis, [(source, source + steps) for source in range(f...  14.7 us
    ppermute x8, starting transfers between devices, step(): lax.ppermute(ahead, 'dp', self.onward)  12.2 us
    ppermute x8, starting transfers between devices, step(): lax.ppermute(behind, 'dp', self.back)  5.25 us
    pallas_call x4, Pallas kernels, run_add(): pl.pallas_call(functools.partial(add_kernel, plans), out_shape=[jax.Shape...  5.07 us
    all_gather x1, waiting for transfers between devices, body(): lax.all_gather(second, 'dp', axis=0, tiled=True, axis_index_groups=[ring....  5.01 us
  transfers between devices with their start and end apart: 32, of which 23 were waited for; matrix products, arithmetic and copies ran while one was open for 1% of the time, Pallas kernels for 18%

profile of v6, /device:TPU:0, one launch (start us, length us, event | category | flops | bytes accessed | tf_op | source)
XLA Modules:
  0.0 219.7 jit_solution(12854012960549442385)
XLA Ops:
  7.2 2.6 %pack.1 = (bf16[208,768]{1,0:T(8,128)(2,1)}, bf16[8,48,768]{2,1,0:T(8,128)(2,1)}) custom-call(f32[48,2304]{1,0:T(8,128)} %bitcast.43, f32[48,768]{1,0:T(8,128)} %bitcast.44, f32[48,3072]{1,0:T(8,128)} %bitcast.41, f32[192,768]{1,0:T(8,128)} %bitcast.42, f32[1,48]{1,0:T(1,128)} %refs_0_.1, f32[1,48]{1,0:T(1,128)} %refs_1_.1, f32[1,48]{1,0:T(1,128)} %refs_2_.1, ...), custom_call_target="tpu_custom_call" | custom-call | tf_op jit(solution)/shard_map/pack/pallas_call | solution.py:1068
  9.9 3.1 %collective-permute-start.1 = (bf16[208,768]{1,0:T(8,128)(2,1)}, bf16[208,768]{1,0:T(8,128)(2,1)S(1)}, u32[]{:S(2)}, u32[]{:S(2)}) collective-permute-start(bf16[208,768]{1,0:T(8,128)(2,1)} %get-tuple-element.75.refs_0_.refs_6_), channel_id=1, source_target_pairs={{0,4},{1,5},{4,8},{5,9},{8,12},{9,13},{12,14},{13,15},{14,10},{15,... | collective-permute-start | bytes 958472 | tf_op jit(solution)/shard_map/ppermute | solution.py:1004
  13.0 8.4 %collective-permute-done.1.refs_8_.refs_14_ = bf16[208,768]{1,0:T(8,128)(2,1)S(1)} collective-permute-done((bf16[208,768]{1,0:T(8,128)(2,1)}, bf16[208,768]{1,0:T(8,128)(2,1)S(1)}, u32[]{:S(2)}, u32[]{:S(2)}) %collective-permute-start.1) | collective-permute-done | bytes 319520 | tf_op jit(solution)/shard_map/ppermute | solution.py:1004
  21.4 2.2 %collective-permute-done.refs_1_.refs_7_ = bf16[208,768]{1,0:T(8,128)(2,1)S(1)} collective-permute-done((bf16[208,768]{1,0:T(8,128)(2,1)}, bf16[208,768]{1,0:T(8,128)(2,1)S(1)}, u32[]{:S(2)}, u32[]{:S(2)}) %collective-permute-start) | collective-permute-done | bytes 319520 | tf_op jit(solution)/shard_map/ppermute | solution.py:1004
  23.9 1.7 collective-permute-start.3
  25.7 14.1 %collective-permute-done.2.refs_2_.refs_8_ = bf16[208,768]{1,0:T(8,128)(2,1)S(1)} collective-permute-done((bf16[208,768]{1,0:T(8,128)(2,1)S(1)}, bf16[208,768]{1,0:T(8,128)(2,1)S(1)}, u32[]{:S(2)}, u32[]{:S(2)}) %collective-permute-start.2) | collective-permute-done | bytes 319520 | tf_op jit(solution)/shard_map/ppermute | solution.py:1004
  39.9 1.5 collective-permute-start.4
  42.5 13.3 %collective-permute-done.4.refs_3_.refs_9_ = bf16[208,768]{1,0:T(8,128)(2,1)S(1)} collective-permute-done((bf16[208,768]{1,0:T(8,128)(2,1)S(1)}, bf16[208,768]{1,0:T(8,128)(2,1)S(1)}, u32[]{:S(2)}, u32[]{:S(2)}) %collective-permute-start.4) | collective-permute-done | bytes 319520 | tf_op jit(solution)/shard_map/ppermute | solution.py:1004
  55.7 1.4 collective-permute-done.5.refs_6_.refs_12_
  57.1 0.7 slice.7
  57.8 1.6 collective-permute-start.7
  62.1 7.4 %collective-permute-done.6.refs_4_.refs_10_ = bf16[96,768]{1,0:T(8,128)(2,1)} collective-permute-done((bf16[96,768]{1,0:T(8,128)(2,1)}, bf16[96,768]{1,0:T(8,128)(2,1)}, u32[]{:S(2)}, u32[]{:S(2)}) %collective-permute-start.6) | collective-permute-done | bytes 147488 | tf_op jit(solution)/shard_map/ppermute | solution.py:1004
  70.2 1.1 collective-permute-done.12.refs_13_.refs_19_
  72.1 2.9 %vectors.1.vec = f32[16,768]{1,0:T(8,128)S(1)} custom-call(s32[16]{0:T(128)S(1)} %pad_add_fusion.devs, s32[2]{0:T(128)S(1)} %bitcast.35, bf16[208,768]{1,0:T(8,128)(2,1)} %get-tuple-element.75.refs_0_.refs_6_, bf16[208,768]{1,0:T(8,128)(2,1)} %copy-done.7, bf16[208,768]{1,0:T(8,128)(2,1)} %copy-done.8, bf16[208,768]{1,0:T(8,128)(2,1)} %copy-done.4, ...), custom_call_target="tpu_custom_call" | custom-call | flops 56623104 | bytes 2359296 | tf_op jit(solution)/shard_map/vectors/pallas_call | solution.py:733
  75.0 5.5 %attend.1 = (f32[192,768]{1,0:T(8,128)S(1)}, bf16[192,768]{1,0:T(8,128)(2,1)S(1)}) custom-call(s32[2]{0:T(128)S(1)} %bitcast.33, s32[1]{0:T(128)} %bitcast.1.flag, s32[16]{0:T(128)S(1)} %pad_add_fusion.devs, bf16[192,768]{1,0:T(8,128)(2,1)S(1)} %bitcast.31, f32[16,768]{1,0:T(8,128)S(1)} %vectors.1.vec, bf16[208,768]{1,0:T(8,128)(2,1)} %get-tuple-element.75.refs_0_.refs_6_, ...), custom_call_target="tpu_custom_call" | custom-call | flops 905969664 | bytes 4718592 | tf_op jit(solution)/shard_map/attend/pallas_call | solution.py:733
  80.6 5.0 %all-gather.2.cloned.1.call-done = bf16[128,48,768]{2,1,0:T(8,128)(2,1)} async-done(((bf16[8,48,768]{2,1,0:T(8,128)(2,1)}), bf16[128,48,768]{2,1,0:T(8,128)(2,1)}) %all-gather.2.cloned.1.call-update) | async-done | bytes 9437200 | tf_op jit(solution)/shard_map/all_gather | solution.py:1077
  85.6 5.1 %mlp.1.after = bf16[192,768]{1,0:T(8,128)(2,1)S(1)} custom-call(s32[1]{0:T(128)} %bitcast.1.flag, f32[192,768]{1,0:T(8,128)S(1)} %get-tuple-element.82.middle_ref, bf16[192,768]{1,0:T(8,128)(2,1)S(1)} %get-tuple-element.83.hidden_ref, f32[16,768]{1,0:T(8,128)S(1)} %vectors.1.vec, bf16[16,8,48,768]{3,2,1,0:T(8,128)(2,1)} %bitcast.37), custom_call_target="tpu_custom_call" | custom-call | flops 1811939328 | bytes 9437184 | tf_op jit(solution)/shard_map/mlp/pallas_call | solution.py:733
  90.7 1.5 collective-permute-start.17
  92.2 5.6 %load.1 = (bf16[4,16,48,768]{3,2,1,0:T(8,128)(2,1)S(1)}, bf16[8,16,48,768]{3,2,1,0:T(8,128)(2,1)S(1)}, f32[192,3072]{1,0:T(8,128)S(1)}) custom-call(s32[16]{0:T(128)S(1)} %pad_add_fusion.devs, bf16[192,768]{1,0:T(8,128)(2,1)S(1)} %mlp.1.after, bf16[192,768]{1,0:T(8,128)(2,1)S(1)} %bitcast.27, bf16[16,8,48,768]{3,2,1,0:T(8,128)(2,1)} %bitcast.38, ...), custom_call_target="tpu_custom_call" | custom-call | flops 905969664 | bytes 28311552 | tf_op jit(solution)/shard_map/load/pallas_call | solution.py:733
  97.8 1.1 collective-permute-done.17.recv_ref
  99.0 8.0 %chain.1 = (bf16[192,768]{1,0:T(8,128)(2,1)}, bf16[96,768]{1,0:T(8,128)(2,1)S(1)}, bf16[192,768]{1,0:T(8,128)(2,1)S(1)}, bf16[192,3072]{1,0:T(8,128)(2,1)S(1)}, ...) custom-call(s32[2]{0:T(128)S(1)} %bitcast.34, ...), custom_call_target="tpu_custom_call" | custom-call | flops 4529848320 | bytes 7077888 | tf_op jit(solution)/shard_map/chain/pallas_call | solution.py:733
  107.0 1.3 collective-permute-start.18
  108.3 1.5 collective-permute-start.19
  109.8 9.1 %collective-permute-done.18.some_ref = bf16[96,768]{1,0:T(8,128)(2,1)S(1)} collective-permute-done((bf16[96,768]{1,0:T(8,128)(2,1)S(1)}, bf16[96,768]{1,0:T(8,128)(2,1)S(1)}, u32[]{:S(2)}, u32[]{:S(2)}) %collective-permute-start.18) | collective-permute-done | bytes 147488 | tf_op jit(solution)/shard_map/ppermute | solution.py:976
  119.0 4.4 %collective-permute-done.19.other_ref = bf16[96,768]{1,0:T(8,128)(2,1)S(1)} collective-permute-done((bf16[96,768]{1,0:T(8,128)(2,1)S(1)}, bf16[96,768]{1,0:T(8,128)(2,1)S(1)}, u32[]{:S(2)}, u32[]{:S(2)}) %collective-permute-start.19) | collective-permute-done | bytes 147488 | tf_op jit(solution)/shard_map/ppermute | solution.py:976
  123.4 5.7 %mlp_back.1 = (bf16[192,3072]{1,0:T(8,128)(2,1)}, f32[16,768]{1,0:T(8,128)S(1)}, bf16[16,8,48,768]{3,2,1,0:T(8,128)(2,1)}) custom-call(s32[1]{0:T(128)} %bitcast.1.flag, bf16[96,768]{1,0:T(8,128)(2,1)S(1)} %collective-permute-done.18.some_ref, bf16[96,768]{1,0:T(8,128)(2,1)S(1)} %collective-permute-done.19.other_ref, bf16[192,768]{1,0:T(8,128)(2,1)S(1)} %bitcast.29, ...), custom_call_target="tpu_custom_call" | custom-call | flops 3623878656 | bytes 9437184 | tf_op jit(solution)/shard_map/mlp_back/pallas_call | solution.py:733
  129.2 18.7 %rest.1 = (f32[192,768]{1,0:T(8,128)}, f32[16,768]{1,0:T(8,128)}, bf16[8,208,768]{2,1,0:T(8,128)(2,1)}, bf16[8,208,768]{2,1,0:T(8,128)(2,1)}, bf16[1,208,768]{2,1,0:T(8,128)(2,1)}) custom-call(s32[1]{0:T(128)} %bitcast.1.flag, s32[16]{0:T(128)S(1)} %pad_add_fusion.devs, s32[2]{0:T(128)S(1)} %bitcast.36, ...), custom_call_target="tpu_custom_call" | custom-call | flops 2717908992 | bytes 14155776 | tf_op jit(solution)/shard_map/rest/pallas_call | solution.py:733
  147.9 1.8 collective-permute-done.20.refs_1_.refs_3_
  149.9 1.2 add.77
  151.2 1.9 collective-permute-start.22
  153.1 6.0 %collective-permute-done.22.refs_2_ = bf16[96,768]{1,0:T(8,128)(2,1)S(1)} collective-permute-done((bf16[96,768]{1,0:T(8,128)(2,1)S(1)}, bf16[96,768]{1,0:T(8,128)(2,1)S(1)}, u32[]{:S(2)}, u32[]{:S(2)}) %collective-permute-start.22) | collective-permute-done | bytes 147488 | tf_op jit(solution)/shard_map/ppermute | solution.py:1004
  159.1 0.8 collective-permute-done.23.refs_5_
  159.9 1.3 add.78
  161.2 1.3 collective-permute-start.24
  162.5 0.8 collective-permute-start.25
  163.3 11.2 %collective-permute-done.24.refs_2_ = bf16[208,768]{1,0:T(8,128)(2,1)S(1)} collective-permute-done((bf16[208,768]{1,0:T(8,128)(2,1)S(1)}, bf16[208,768]{1,0:T(8,128)(2,1)S(1)}, u32[]{:S(2)}, u32[]{:S(2)}) %collective-permute-start.24) | collective-permute-done | bytes 319520 | tf_op jit(solution)/shard_map/ppermute | solution.py:1004
  174.5 1.1 collective-permute-done.25.refs_5_
  175.6 1.3 add.79
  177.0 1.7 collective-permute-start.26
  179.0 10.7 %collective-permute-done.26.refs_2_ = bf16[208,768]{1,0:T(8,128)(2,1)S(1)} collective-permute-done((bf16[208,768]{1,0:T(8,128)(2,1)S(1)}, bf16[208,768]{1,0:T(8,128)(2,1)S(1)}, u32[]{:S(2)}, u32[]{:S(2)}) %collective-permute-start.26) | collective-permute-done | bytes 319520 | tf_op jit(solution)/shard_map/ppermute | solution.py:1004
  189.8 1.5 collective-permute-done.27.refs_5_
  191.3 1.3 add.80
  192.6 1.6 collective-permute-start.28
  194.7 10.0 %collective-permute-done.28.ahead = bf16[208,768]{1,0:T(8,128)(2,1)S(1)} collective-permute-done((bf16[208,768]{1,0:T(8,128)(2,1)S(1)}, bf16[208,768]{1,0:T(8,128)(2,1)S(1)}, u32[]{:S(2)}, u32[]{:S(2)}) %collective-permute-start.28) | collective-permute-done | bytes 319520 | tf_op jit(solution)/shard_map/ppermute | solution.py:1004
  204.7 1.5 collective-permute-done.29.behind
  206.3 2.0 total.1
  208.3 2.4 %reduce-scatter.2.cloned.1.call-done.grads_ref = bf16[8,48,768]{2,1,0:T(8,128)(2,1)} async-done(((bf16[128,48,768]{2,1,0:T(8,128)(2,1)}), bf16[8,48,768]{2,1,0:T(8,128)(2,1)}) %reduce-scatter.2.cloned.1.call-update) | async-done | bytes 589840 | tf_op jit(solution)/shard_map/reduce_scatter | solution.py:1130
  210.7 2.1 unpack.1
  (71 shorter events, 6.7 us)
Async XLA Ops:
  7.2 64.9 %copy-start.3 = (s32[2,1]{0,1:T(1,128)S(1)}, s32[2,1]{0,1:T(1,128)}, u32[]{:S(2)}) copy-start(s32[2,1]{0,1:T(1,128)} %param.21) | copy-start | bytes 28
  7.2 78.4 %all-gather.2.cloned.1.call-start = ((), (), s32[]{:S(2)}) async-start(), calls=%async_computation.1 | async-start | bytes 10027008 | tf_op jit(solution)/shard_map/all_gather | solution.py:1077
  9.9 200.8 %reduce-scatter.2.cloned.1.call-start = ((), (), s32[]{:S(2)}) async-start(), calls=%async_computation.2 | async-start | bytes 10027008 | tf_op jit(solution)/shard_map/reduce_scatter | solution.py:1130
  9.9 11.5 %collective-permute-start.1 = (bf16[208,768]{1,0:T(8,128)(2,1)}, bf16[208,768]{1,0:T(8,128)(2,1)S(1)}, u32[]{:S(2)}, u32[]{:S(2)}) collective-permute-start(bf16[208,768]{1,0:T(8,128)(2,1)} %get-tuple-element.75.refs_0_.refs_6_), channel_id=1, source_target_pairs={{0,4},{1,5},{4,8},{5,9},{8,12},{9,13},{12,14},{13,15},{14,10},{15,... | collective-permute-start | bytes 958472 | tf_op jit(solution)/shard_map/ppermute | solution.py:1004
  13.0 10.6 %collective-permute-start = (bf16[208,768]{1,0:T(8,128)(2,1)}, bf16[208,768]{1,0:T(8,128)(2,1)S(1)}, u32[]{:S(2)}, u32[]{:S(2)}) collective-permute-start(bf16[208,768]{1,0:T(8,128)(2,1)} %get-tuple-element.75.refs_0_.refs_6_), channel_id=1, source_target_pairs={{4,0},{5,1},{8,4},{9,5},{12,8},{13,9},{14,12},{15,13},{10,14},{11,... | collective-permute-start | bytes 958472 | tf_op jit(solution)/shard_map/ppermute | solution.py:1004
  21.4 50.6 %copy-start.6 = (bf16[208,768]{1,0:T(8,128)(2,1)}, bf16[208,768]{1,0:T(8,128)(2,1)S(1)}, u32[]{:S(2)}) copy-start(bf16[208,768]{1,0:T(8,128)(2,1)S(1)} %collective-permute-done.1.refs_8_.refs_14_) | copy-start | bytes 958468
  23.6 48.4 %copy-start.7 = (bf16[208,768]{1,0:T(8,128)(2,1)}, bf16[208,768]{1,0:T(8,128)(2,1)S(1)}, u32[]{:S(2)}) copy-start(bf16[208,768]{1,0:T(8,128)(2,1)S(1)} %collective-permute-done.refs_1_.refs_7_) | copy-start | bytes 958468
  23.6 16.2 %collective-permute-start.2 = (bf16[208,768]{1,0:T(8,128)(2,1)S(1)}, bf16[208,768]{1,0:T(8,128)(2,1)S(1)}, u32[]{:S(2)}, u32[]{:S(2)}) collective-permute-start(bf16[208,768]{1,0:T(8,128)(2,1)S(1)} %collective-permute-done.refs_1_.refs_7_), channel_id=1, source_target_pairs={{4,0},{5,1},{8,4},{9,5},{12,8},{13,9},{14,12},{15,13},{10,14},{11,... | collective-permute-start | bytes 958472 | tf_op jit(solution)/shard_map/ppermute | solution.py:1004
  23.9 16.0 %collective-permute-start.3 = (bf16[208,768]{1,0:T(8,128)(2,1)S(1)}, bf16[208,768]{1,0:T(8,128)(2,1)S(1)}, u32[]{:S(2)}, u32[]{:S(2)}) collective-permute-start(bf16[208,768]{1,0:T(8,128)(2,1)S(1)} %collective-permute-done.1.refs_8_.refs_14_), channel_id=1, source_target_pairs={{0,4},{1,5},{4,8},{5,9},{8,12},{9,13},{12,14},{13,15},{14,10},{15,... | collective-permute-start | bytes 958472 | tf_op jit(solution)/shard_map/ppermute | solution.py:1004
  39.8 32.2 %copy-start.8 = (bf16[208,768]{1,0:T(8,128)(2,1)}, bf16[208,768]{1,0:T(8,128)(2,1)S(1)}, u32[]{:S(2)}) copy-start(bf16[208,768]{1,0:T(8,128)(2,1)S(1)} %collective-permute-done.2.refs_2_.refs_8_) | copy-start | bytes 958468
  39.9 32.1 %copy-start.9 = (bf16[208,768]{1,0:T(8,128)(2,1)}, bf16[208,768]{1,0:T(8,128)(2,1)S(1)}, u32[]{:S(2)}) copy-start(bf16[208,768]{1,0:T(8,128)(2,1)S(1)} %collective-permute-done.3.refs_7_.refs_13_) | copy-start | bytes 958468
  39.9 15.8 %collective-permute-start.4 = (bf16[208,768]{1,0:T(8,128)(2,1)S(1)}, bf16[208,768]{1,0:T(8,128)(2,1)S(1)}, u32[]{:S(2)}, u32[]{:S(2)}) collective-permute-start(bf16[208,768]{1,0:T(8,128)(2,1)S(1)} %collective-permute-done.2.refs_2_.refs_8_), channel_id=1, source_target_pairs={{4,0},{5,1},{8,4},{9,5},{12,8},{13,9},{14,12},{15,13},{10,14},{11,... | collective-permute-start | bytes 958472 | tf_op jit(solution)/shard_map/ppermute | solution.py:1004
  41.5 15.6 %collective-permute-start.5 = (bf16[208,768]{1,0:T(8,128)(2,1)S(1)}, bf16[208,768]{1,0:T(8,128)(2,1)S(1)}, u32[]{:S(2)}, u32[]{:S(2)}) collective-permute-start(bf16[208,768]{1,0:T(8,128)(2,1)S(1)} %collective-permute-done.3.refs_7_.refs_13_), channel_id=1, source_target_pairs={{0,4},{1,5},{4,8},{5,9},{8,12},{9,13},{12,14},{13,15},{14,10},{15,... | collective-permute-start | bytes 958472 | tf_op jit(solution)/shard_map/ppermute | solution.py:1004
  41.9 18.2 %collective-permute-start.8 = (bf16[208,768]{1,0:T(8,128)(2,1)}, bf16[208,768]{1,0:T(8,128)(2,1)S(1)}, u32[]{:S(2)}, u32[]{:S(2)}) collective-permute-start(bf16[208,768]{1,0:T(8,128)(2,1)} %get-tuple-element.75.refs_0_.refs_6_), channel_id=1, source_target_pairs={{0,1},{1,0},{2,3},{3,2},{4,5},{5,4},{6,7},{7,6},{8,9},{9,8},{10,11... | collective-permute-start | bytes 958472 | tf_op jit(solution)/shard_map/ppermute | solution.py:1018
  41.9 18.6 %collective-permute-start.16 = (bf16[208,768]{1,0:T(8,128)(2,1)S(1)}, bf16[208,768]{1,0:T(8,128)(2,1)S(1)}, u32[]{:S(2)}, u32[]{:S(2)}) collective-permute-start(bf16[208,768]{1,0:T(8,128)(2,1)S(1)} %collective-permute-done.1.refs_8_.refs_14_), channel_id=1, source_target_pairs={{0,1},{1,0},{2,3},{3,2},{4,5},{5,4},{6,7},{7,6},{8,9},{9,8},{10,11... | collective-permute-start | bytes 958472 | tf_op jit(solution)/shard_map/ppermute | solution.py:1018
  42.4 18.1 %collective-permute-start.9 = (bf16[208,768]{1,0:T(8,128)(2,1)S(1)}, bf16[208,768]{1,0:T(8,128)(2,1)S(1)}, u32[]{:S(2)}, u32[]{:S(2)}) collective-permute-start(bf16[208,768]{1,0:T(8,128)(2,1)S(1)} %collective-permute-done.refs_1_.refs_7_), channel_id=1, source_target_pairs={{0,1},{1,0},{2,3},{3,2},{4,5},{5,4},{6,7},{7,6},{8,9},{9,8},{10,11... | collective-permute-start | bytes 958472 | tf_op jit(solution)/shard_map/ppermute | solution.py:1018
  55.7 16.3 %copy-start.4 = (bf16[208,768]{1,0:T(8,128)(2,1)}, bf16[208,768]{1,0:T(8,128)(2,1)S(1)}, u32[]{:S(2)}) copy-start(bf16[208,768]{1,0:T(8,128)(2,1)S(1)} %collective-permute-done.4.refs_3_.refs_9_) | copy-start | bytes 958468
  55.7 5.3 %collective-permute-start.10 = (bf16[208,768]{1,0:T(8,128)(2,1)S(1)}, bf16[208,768]{1,0:T(8,128)(2,1)S(1)}, u32[]{:S(2)}, u32[]{:S(2)}) collective-permute-start(bf16[208,768]{1,0:T(8,128)(2,1)S(1)} %collective-permute-done.2.refs_2_.refs_8_), channel_id=1, source_target_pairs={{0,1},{1,0},{2,3},{3,2},{4,5},{5,4},{6,7},{7,6},{8,9},{9,8},{10,11... | collective-permute-start | bytes 958472 | tf_op jit(solution)/shard_map/ppermute | solution.py:1018
  57.1 14.9 %copy-start.5 = (bf16[208,768]{1,0:T(8,128)(2,1)}, bf16[208,768]{1,0:T(8,128)(2,1)S(1)}, u32[]{:S(2)}) copy-start(bf16[208,768]{1,0:T(8,128)(2,1)S(1)} %collective-permute-done.5.refs_6_.refs_12_) | copy-start | bytes 958468
  57.8 11.7 %collective-permute-start.7 = (bf16[112,768]{1,0:T(8,128)(2,1)}, bf16[112,768]{1,0:T(8,128)(2,1)S(1)}, u32[]{:S(2)}, u32[]{:S(2)}) collective-permute-start(bf16[112,768]{1,0:T(8,128)(2,1)} %slice.7), channel_id=1, source_target_pairs={{4,0},{5,1},{8,4},{9,5},{12,8},{13,9},{14,12},{15,13},{10,14},{11,... | collective-permute-start | bytes 516104 | tf_op jit(solution)/shard_map/ppermute | solution.py:1004
  60.1 11.9 %copy-start.10 = (bf16[208,768]{1,0:T(8,128)(2,1)}, bf16[208,768]{1,0:T(8,128)(2,1)S(1)}, u32[]{:S(2)}) copy-start(bf16[208,768]{1,0:T(8,128)(2,1)S(1)} %collective-permute-done.8.refs_9_.refs_15_) | copy-start | bytes 958468
  60.1 9.4 %collective-permute-start.6 = (bf16[96,768]{1,0:T(8,128)(2,1)}, bf16[96,768]{1,0:T(8,128)(2,1)}, u32[]{:S(2)}, u32[]{:S(2)}) collective-permute-start(bf16[96,768]{1,0:T(8,128)(2,1)} %slice.6), channel_id=1, source_target_pairs={{0,4},{1,5},{4,8},{5,9},{8,12},{9,13},{12,14},{13,15},{14,10},{15,... | collective-permute-start | bytes 442376 | tf_op jit(solution)/shard_map/ppermute | solution.py:1004
  60.5 11.5 %copy-start.11 = (bf16[208,768]{1,0:T(8,128)(2,1)}, bf16[208,768]{1,0:T(8,128)(2,1)S(1)}, u32[]{:S(2)}) copy-start(bf16[208,768]{1,0:T(8,128)(2,1)S(1)} %collective-permute-done.16.refs_17_.refs_23_) | copy-start | bytes 958468
  60.5 9.6 %collective-permute-start.15 = (bf16[208,768]{1,0:T(8,128)(2,1)S(1)}, bf16[208,768]{1,0:T(8,128)(2,1)S(1)}, u32[]{:S(2)}, u32[]{:S(2)}) collective-permute-start(bf16[208,768]{1,0:T(8,128)(2,1)S(1)} %collective-permute-done.3.refs_7_.refs_13_), channel_id=1, source_target_pairs={{0,1},{1,0},{2,3},{3,2},{4,5},{5,4},{6,7},{7,6},{8,9},{9,8},{10,11... | collective-permute-start | bytes 958472 | tf_op jit(solution)/shard_map/ppermute | solution.py:1018
  60.6 0.8 copy-start.12
  60.6 10.7 %collective-permute-start.11 = (bf16[208,768]{1,0:T(8,128)(2,1)S(1)}, bf16[208,768]{1,0:T(8,128)(2,1)S(1)}, u32[]{:S(2)}, u32[]{:S(2)}) collective-permute-start(bf16[208,768]{1,0:T(8,128)(2,1)S(1)} %collective-permute-done.4.refs_3_.refs_9_), channel_id=1, source_target_pairs={{0,1},{1,0},{2,3},{3,2},{4,5},{5,4},{6,7},{7,6},{8,9},{9,8},{10,11... | collective-permute-start | bytes 958472 | tf_op jit(solution)/shard_map/ppermute | solution.py:1018
  61.4 0.7 copy-start.13
  61.4 9.9 %collective-permute-start.14 = (bf16[208,768]{1,0:T(8,128)(2,1)S(1)}, bf16[208,768]{1,0:T(8,128)(2,1)}, u32[]{:S(2)}, u32[]{:S(2)}) collective-permute-start(bf16[208,768]{1,0:T(8,128)(2,1)S(1)} %collective-permute-done.5.refs_6_.refs_12_), channel_id=1, source_target_pairs={{0,1},{1,0},{2,3},{3,2},{4,5},{5,4},{6,7},{7,6},{8,9},{9,8},{10,11... | collective-permute-start | bytes 958472 | tf_op jit(solution)/shard_map/ppermute | solution.py:1018
  69.6 1.7 collective-permute-start.12
  69.6 2.5 %copy-start.16 = (bf16[112,768]{1,0:T(8,128)(2,1)}, bf16[112,768]{1,0:T(8,128)(2,1)S(1)}, u32[]{:S(2)}) copy-start(bf16[112,768]{1,0:T(8,128)(2,1)S(1)} %collective-permute-done.7.refs_5_.refs_11_) | copy-start | bytes 516100
  69.6 1.9 collective-permute-start.13
  70.2 1.3 copy-start.14
  72.1 2.9 %copy-start.1 = (bf16[2,1,96,768]{3,2,1,0:T(8,128)(2,1)S(1)}, bf16[2,1,96,768]{3,2,1,0:T(8,128)(2,1)}, u32[]{:S(2)}) copy-start(bf16[2,1,96,768]{3,2,1,0:T(8,128)(2,1)} %param.18) | copy-start | bytes 884740
  72.1 2.9 %copy-start.2 = (s32[2,1]{0,1:T(1,128)S(1)}, s32[2,1]{0,1:T(1,128)}, u32[]{:S(2)}) copy-start(s32[2,1]{0,1:T(1,128)} %param.20) | copy-start | bytes 28
  85.6 6.6 %copy-start = (bf16[2,1,96,768]{3,2,1,0:T(8,128)(2,1)S(1)}, bf16[2,1,96,768]{3,2,1,0:T(8,128)(2,1)}, u32[]{:S(2)}) copy-start(bf16[2,1,96,768]{3,2,1,0:T(8,128)(2,1)} %param.19) | copy-start | bytes 884740
  90.7 8.2 %collective-permute-start.17 = (bf16[192,768]{1,0:T(8,128)(2,1)S(1)}, bf16[192,768]{1,0:T(8,128)(2,1)S(1)}, u32[]{:S(2)}, u32[]{:S(2)}) collective-permute-start(bf16[192,768]{1,0:T(8,128)(2,1)S(1)} %mlp.1.after), channel_id=1, source_target_pairs={{0,16},{1,17},{2,18},{3,19},{4,20},{5,21},{6,22},{7,23},{8,24},{9,... | collective-permute-start | bytes 884744 | tf_op jit(solution)/shard_map/ppermute | solution.py:976
  107.0 12.0 %collective-permute-start.18 = (bf16[96,768]{1,0:T(8,128)(2,1)S(1)}, bf16[96,768]{1,0:T(8,128)(2,1)S(1)}, u32[]{:S(2)}, u32[]{:S(2)}) collective-permute-start(bf16[96,768]{1,0:T(8,128)(2,1)S(1)} %get-tuple-element.89), channel_id=1, source_target_pairs={{16,0},{17,1},{18,2},{19,3},{20,4},{21,5},{22,6},{23,7},{24,8},{25... | collective-permute-start | bytes 442376 | tf_op jit(solution)/shard_map/ppermute | solution.py:976
  108.3 15.1 %collective-permute-start.19 = (bf16[96,768]{1,0:T(8,128)(2,1)S(1)}, bf16[96,768]{1,0:T(8,128)(2,1)S(1)}, u32[]{:S(2)}, u32[]{:S(2)}) collective-permute-start(bf16[96,768]{1,0:T(8,128)(2,1)S(1)} %chain_end.1), channel_id=1, source_target_pairs={{16,0},{17,1},{18,2},{19,3},{20,4},{21,5},{22,6},{23,7},{24,8},{25... | collective-permute-start | bytes 442376 | tf_op jit(solution)/shard_map/ppermute | solution.py:976
  147.8 1.9 collective-permute-start.20
  149.7 10.2 %collective-permute-start.21 = (bf16[8,208,768]{2,1,0:T(8,128)(2,1)}, bf16[8,208,768]{2,1,0:T(8,128)(2,1)S(1)}, u32[]{:S(2)}, u32[]{:S(2)}) collective-permute-start(bf16[8,208,768]{2,1,0:T(8,128)(2,1)} %get-tuple-element.110), channel_id=1, source_target_pairs={{0,1},{1,0},{2,3},{3,2},{4,5},{5,4},{6,7},{7,6},{8,9},{9,8},{10,11... | collective-permute-start | bytes 7667720 | tf_op jit(solution)/shard_map/ppermute | solution.py:1018
  151.0 8.9 %collective-permute-start.23 = (bf16[112,768]{1,0:T(8,128)(2,1)S(1)}, bf16[112,768]{1,0:T(8,128)(2,1)S(1)}, u32[]{:S(2)}, u32[]{:S(2)}) collective-permute-start(bf16[112,768]{1,0:T(8,128)(2,1)S(1)} %get-tuple-element.112), channel_id=1, source_target_pairs={{4,0},{5,1},{8,4},{9,5},{12,8},{13,9},{14,12},{15,13},{10,14},{11,... | collective-permute-start | bytes 516104 | tf_op jit(solution)/shard_map/ppermute | solution.py:1004
  151.2 8.0 %collective-permute-start.22 = (bf16[96,768]{1,0:T(8,128)(2,1)S(1)}, bf16[96,768]{1,0:T(8,128)(2,1)S(1)}, u32[]{:S(2)}, u32[]{:S(2)}) collective-permute-start(bf16[96,768]{1,0:T(8,128)(2,1)S(1)} %get-tuple-element.111), channel_id=1, source_target_pairs={{0,4},{1,5},{4,8},{5,9},{8,12},{9,13},{12,14},{13,15},{14,10},{15,... | collective-permute-start | bytes 442376 | tf_op jit(solution)/shard_map/ppermute | solution.py:1004
  161.2 13.3 %collective-permute-start.24 = (bf16[208,768]{1,0:T(8,128)(2,1)S(1)}, bf16[208,768]{1,0:T(8,128)(2,1)S(1)}, u32[]{:S(2)}, u32[]{:S(2)}) collective-permute-start(bf16[208,768]{1,0:T(8,128)(2,1)S(1)} %get-tuple-element.113), channel_id=1, source_target_pairs={{0,4},{1,5},{4,8},{5,9},{8,12},{9,13},{12,14},{13,15},{14,10},{15,... | collective-permute-start | bytes 958472 | tf_op jit(solution)/shard_map/ppermute | solution.py:1004
  162.5 13.2 %collective-permute-start.25 = (bf16[208,768]{1,0:T(8,128)(2,1)S(1)}, bf16[208,768]{1,0:T(8,128)(2,1)S(1)}, u32[]{:S(2)}, u32[]{:S(2)}) collective-permute-start(bf16[208,768]{1,0:T(8,128)(2,1)S(1)} %get-tuple-element.114), channel_id=1, source_target_pairs={{4,0},{5,1},{8,4},{9,5},{12,8},{13,9},{14,12},{15,13},{10,14},{11,... | collective-permute-start | bytes 958472 | tf_op jit(solution)/shard_map/ppermute | solution.py:1004
  177.0 12.8 %collective-permute-start.26 = (bf16[208,768]{1,0:T(8,128)(2,1)S(1)}, bf16[208,768]{1,0:T(8,128)(2,1)S(1)}, u32[]{:S(2)}, u32[]{:S(2)}) collective-permute-start(bf16[208,768]{1,0:T(8,128)(2,1)S(1)} %get-tuple-element.115), channel_id=1, source_target_pairs={{0,4},{1,5},{4,8},{5,9},{8,12},{9,13},{12,14},{13,15},{14,10},{15,... | collective-permute-start | bytes 958472 | tf_op jit(solution)/shard_map/ppermute | solution.py:1004
  178.7 12.6 %collective-permute-start.27 = (bf16[208,768]{1,0:T(8,128)(2,1)S(1)}, bf16[208,768]{1,0:T(8,128)(2,1)S(1)}, u32[]{:S(2)}, u32[]{:S(2)}) collective-permute-start(bf16[208,768]{1,0:T(8,128)(2,1)S(1)} %get-tuple-element.116), channel_id=1, source_target_pairs={{4,0},{5,1},{8,4},{9,5},{12,8},{13,9},{14,12},{15,13},{10,14},{11,... | collective-permute-start | bytes 958472 | tf_op jit(solution)/shard_map/ppermute | solution.py:1004
  192.6 12.1 %collective-permute-start.28 = (bf16[208,768]{1,0:T(8,128)(2,1)S(1)}, bf16[208,768]{1,0:T(8,128)(2,1)S(1)}, u32[]{:S(2)}, u32[]{:S(2)}) collective-permute-start(bf16[208,768]{1,0:T(8,128)(2,1)S(1)} %get-tuple-element.117), channel_id=1, source_target_pairs={{0,4},{1,5},{4,8},{5,9},{8,12},{9,13},{12,14},{13,15},{14,10},{15,... | collective-permute-start | bytes 958472 | tf_op jit(solution)/shard_map/ppermute | solution.py:1004
  194.2 12.0 %collective-permute-start.29 = (bf16[208,768]{1,0:T(8,128)(2,1)S(1)}, bf16[208,768]{1,0:T(8,128)(2,1)S(1)}, u32[]{:S(2)}, u32[]{:S(2)}) collective-permute-start(bf16[208,768]{1,0:T(8,128)(2,1)S(1)} %get-tuple-element.118), channel_id=1, source_target_pairs={{4,0},{5,1},{8,4},{9,5},{12,8},{13,9},{14,12},{15,13},{10,14},{11,... | collective-permute-start | bytes 958472 | tf_op jit(solution)/shard_map/ppermute | solution.py:1004
  (1 other events, 0.7 us)
Sparse Core Ops, SparseCore 0:
  10.2 75.3 all-gather.1
  129.3 81.3 reduce-scatter.1

commit v7 on v6

--- a/solution.py
+++ b/solution.py
@@ -217,19 +217,18 @@
     return middle
 
 
-def second_half(plan, hidden_ref, vec, held, act_ref=None, slope_ref=None, wait=None):
+def activate(plan, part, hidden_ref, vec, held):
+    pre_act = mm(hidden_ref[...], block_of(plan, held, part)) + vec[8 + part : 9 + part, :]
+    act, slope = gelu_both(pre_act)
+    return act.astype(BF16), slope
+
+
+def second_half(plan, hidden_ref, vec, held, wait):
     total = None
     for part in range(QUART):
-        if wait is not None:
-            wait(part)
-        pre_act = mm(hidden_ref[...], block_of(plan, held, part)) + vec[8 + part : 9 + part, :]
-        act, slope = gelu_both(pre_act)
-        act = act.astype(BF16)
-        if act_ref is not None:
-            act_ref[:, columns_of(plan, part)] = act
-            slope_ref[:, columns_of(plan, part)] = slope
-        if wait is not None:
-            wait(QUART + part)
+        wait(part)
+        act, _ = activate(plan, part, hidden_ref, vec, held)
+        wait(QUART + part)
         term = mm(act, block_of(plan, held, QUART + part))
         total = term if total is None else total + term
     return total + vec[7:8, :]
@@ -288,7 +287,7 @@
             sem = sems.at[block] if block < QUART else down_sems.at[block - QUART]
             wait_bytes(held.at[block], sem)
 
-        total = second_half(plan, hidden_ref, vec, held, wait=wait)
+        total = second_half(plan, hidden_ref, vec, held, wait)
         y_ref[...] = (middle_ref[...] + total).astype(BF16)
 
 
@@ -320,9 +319,9 @@
 
 def chain_kernel(
     plan, lengths, flag, x_ref, recv_ref, cot_ref, vec, held1, held2, grad_act,
-    y_out, dx_ref, hidden, act, slope, xin_ref, qkv, probs, grad_middle, grad_attended, *refs,
+    dx_ref, hidden, act, slope, xin_ref, qkv, probs, grad_middle, grad_attended, middle, *refs,
 ):
-    outs, (normed, attended, middle, y_ref, grad_rows, sems) = refs[:6], refs[6:]
+    outs, (normed, attended, grad_rows, sems) = refs[:6], refs[6:]
     kept = (xin_ref, normed, qkv, attended, middle, probs)
     copies = [
         pltpu.make_async_copy(source, target, sems.at[index])
@@ -333,9 +332,9 @@
         plan, xin_ref[...], lengths, vec, held1, lambda group: None, normed, qkv, attended, probs, hidden
     )
     start_all(copies)
-    y_ref[...] = (middle[...] + second_half(plan, hidden, vec, held2, act, slope)).astype(BF16)
-    copies.append(pltpu.make_async_copy(y_ref, y_out, sems.at[len(copies)]))
-    copies[-1].start()
+    for part in range(QUART):
+        columns = columns_of(plan, part)
+        act[:, columns], slope[:, columns] = activate(plan, part, hidden, vec, held2)
 
     @pl.when(flag[0] == 1)
     def _():
@@ -365,6 +364,14 @@
         )
 
 
+def output_kernel(plan, flag, act, middle_ref, vec, held2, y_ref):
+    total = None
+    for part in range(QUART):
+        term = mm(act[:, columns_of(plan, part)], block_of(plan, held2, QUART + part))
+        total = term if total is None else total + term
+    y_ref[...] = (middle_ref[...] + (total + vec[7:8, :])).astype(BF16)
+
+
 class Stage:
     def __init__(self, plan, stage, sems):
         self.plan, self.stage, self.sems, self.sent = plan, stage, sems, 0
@@ -385,7 +392,7 @@
 
 
 def mlp_back_kernel(
-    plan, flag, some_ref, other_ref, cot_ref, held2, hidden, act, slope,
+    plan, flag, beside, some_ref, other_ref, cot_ref, held2, hidden, act, slope,
     grad_pre_out, small_ref, grads, grad_pre_ref, stage, stage_sems, pre_sem,
 ):
     arrived = jnp.concatenate([some_ref[...], other_ref[...]], 0)
@@ -822,19 +829,34 @@
     some = ((plan.items // 2 * plan.length, plan.width), BF16)
     results = call(
         functools.partial(chain_kernel, plan),
-        [pltpu.HBM(*shapes[0]), of(some)]
-        + [inside(shapes[index]) for index in (4, 6, 7, 0, 1, 5, 3, 0)]
+        [of(some)]
+        + [inside(shapes[index]) for index in (4, 6, 7, 0, 1, 5, 3, 0, 3)]
         + [pltpu.HBM(*shape) for shape in rest],
         [SMEM] * 2 + [VMEM] * 7,
-        [HBM] + [VMEM] * 9 + [HBM] * len(rest),
-        [inside(shapes[index]) for index in (0, 2, 3, 0, 1)]
-        + [pltpu.SemaphoreType.DMA((len(rest) + 1,))],
+        [VMEM] * 10 + [HBM] * len(rest),
+        [inside(shapes[index]) for index in (0, 2, 1)]
+        + [pltpu.SemaphoreType.DMA((len(rest),))],
         "chain",
         (20 * block * plan.tokens, 12 * block),
         12,
         (lengths, flag, x, recv, cot, vec, held1, held2, grad_act),
     )
-    return results[0], results[1], results[2:5], results[5:10], results[10:]
+    return results[0], results[1:4], results[4:9], results[9], results[10:]
+
+
+def run_output(plan, flag, act, middle, vec, held2):
+    block = plan.width * plan.width
+    return call(
+        functools.partial(output_kernel, plan),
+        of(kept_shapes(plan)[0]),
+        [SMEM] + [VMEM] * 4,
+        VMEM,
+        [],
+        "output",
+        (QUART * block * plan.tokens, QUART * block),
+        4,
+        (flag, act, middle, vec, held2),
+    )
 
 
 def run_chain_end(plan, flag, vec, held1, end):
@@ -871,7 +893,7 @@
     ]
 
 
-def run_mlp_back(plan, flag, arriving, cot, held2, hidden, act, slope):
+def run_mlp_back(plan, flag, beside, arriving, cot, held2, hidden, act, slope):
     shapes = kept_shapes(plan)
     block = plan.width * plan.width
     return call(
@@ -881,13 +903,13 @@
             jax.ShapeDtypeStruct((16, plan.width), F32),
             pltpu.HBM((plan.shards, SECOND, plan.rows, plan.width), BF16),
         ],
-        [SMEM] + [VMEM] * 7,
+        [SMEM, HBM] + [VMEM] * 7,
         [HBM, VMEM, HBM],
         [inside(shapes[6])] + stage_scratch(plan, SECOND) + [pltpu.SemaphoreType.DMA((1,))],
         "mlp_back",
         (2 * SECOND * block * plan.tokens, SECOND * block * 2),
         16,
-        (flag, *arriving, cot, held2, hidden, act, slope),
+        (flag, beside, *arriving, cot, held2, hidden, act, slope),
     )
 
 
@@ -1111,12 +1133,15 @@
     first_out = run_mlp(plan, flag, middle, hidden, vec, gathered)
     recv = shifted(first_out, "section", 1)
     held1, held2, grad_act = run_load(plan, devs, first_out, cot, firsts, gathered)
-    output, some_grad, (hidden, act, slope), end, kept = run_chain(
+    some_grad, (hidden, act, slope), end, middle, kept = run_chain(
         plan, lens, flag, x, recv, cot, vec, held1, held2, grad_act
     )
     other_grad = run_chain_end(plan, flag, vec, held1, end)
     arriving = [shifted(grad, "section", -1) for grad in (some_grad, other_grad)]
-    grad_pre, sums, grads2 = run_mlp_back(plan, flag, arriving, cot, held2, hidden, act, slope)
+    output = run_output(plan, flag, act, middle, vec, held2)
+    grad_pre, sums, grads2 = run_mlp_back(
+        plan, flag, output, arriving, cot, held2, hidden, act, slope
+    )
     input_grad, sums, grads1 = run_rest(
         plan, many, flag, devs, lead, arriving, cot, sums, vec, gathered, grad_pre, kept, firsts
     )

time: 220 us -> 219 us (level)
    pallas_call x8 -> x9, Pallas kernels: 51.6 us -> 51.8 us  [call(): pl.pallas_call(kernel, out_shape=outs, in_specs=in_specs, out_specs=out_s...]
  transfers between devices with their start and end apart: 32 -> 32, of which waited for: 23 -> 23; matrix products, arithmetic and copies ran while one was open for 1% -> 1% of each run, Pallas kernels for 18% -> 19%
where the time goes in v7:
time: 219 us
  waiting for transfers between devices  114 us (52%)
  Pallas kernels  63.6 us (29%)
  starting transfers between devices  24 us (11%)
  between operations  14.3 us (7%)
  local copies, waits for them, and re-layouts  2.56 us (1%)
    ppermute x8, waiting for transfers between devices, step(): lax.ppermute(ahead, 'dp', self.onward)  55.3 us
    pallas_call x9, Pallas kernels, call(): pl.pallas_call(kernel, out_shape=outs, in_specs=in_specs, out_specs=out_s...  51.8 us
    ppermute x8, waiting for transfers between devices, step(): lax.ppermute(behind, 'dp', self.back)  34.6 us
    ppermute x3, waiting for transfers between devices, shifted(): lax.ppermute(value, axis, [(source, source + steps) for source in range(f...  13.4 us
    ppermute x8, starting transfers between devices, step(): lax.ppermute(ahead, 'dp', self.onward)  12.3 us
    ppermute x8, starting transfers between devices, step(): lax.ppermute(behind, 'dp', self.back)  5.19 us
    pallas_call x4, Pallas kernels, run_add(): pl.pallas_call(functools.partial(add_kernel, plans), out_shape=[jax.Shape...  5.07 us
    all_gather x1, waiting for transfers between devices, body(): lax.all_gather(second, 'dp', axis=0, tiled=True, axis_index_groups=[ring....  5.01 us
  transfers between devices with their start and end apart: 32, of which 23 were waited for; matrix products, arithmetic and copies ran while one was open for 1% of the time, Pallas kernels for 19%

profile of v7, /device:TPU:0, one launch (start us, length us, event | category | flops | bytes accessed | tf_op | source)
XLA Modules:
  0.0 218.6 jit_solution(691794470012883444)
XLA Ops:
  7.2 2.6 %pack.1 = (bf16[208,768]{1,0:T(8,128)(2,1)}, bf16[8,48,768]{2,1,0:T(8,128)(2,1)}) custom-call(f32[48,2304]{1,0:T(8,128)} %bitcast.44, f32[48,768]{1,0:T(8,128)} %bitcast.45, f32[48,3072]{1,0:T(8,128)} %bitcast.42, f32[192,768]{1,0:T(8,128)} %bitcast.43, f32[1,48]{1,0:T(1,128)} %refs_0_.1, f32[1,48]{1,0:T(1,128)} %refs_1_.1, f32[1,48]{1,0:T(1,128)} %refs_2_.1, ...), custom_call_target="tpu_custom_call" | custom-call | tf_op jit(solution)/shard_map/pack/pallas_call | solution.py:1090
  9.9 3.1 %collective-permute-start.1 = (bf16[208,768]{1,0:T(8,128)(2,1)}, bf16[208,768]{1,0:T(8,128)(2,1)S(1)}, u32[]{:S(2)}, u32[]{:S(2)}) collective-permute-start(bf16[208,768]{1,0:T(8,128)(2,1)} %get-tuple-element.75.refs_0_.refs_6_), channel_id=1, source_target_pairs={{0,4},{1,5},{4,8},{5,9},{8,12},{9,13},{12,14},{13,15},{14,10},{15,... | collective-permute-start | bytes 958472 | tf_op jit(solution)/shard_map/ppermute | solution.py:1026
  13.0 8.4 %collective-permute-done.1.refs_8_.refs_14_ = bf16[208,768]{1,0:T(8,128)(2,1)S(1)} collective-permute-done((bf16[208,768]{1,0:T(8,128)(2,1)}, bf16[208,768]{1,0:T(8,128)(2,1)S(1)}, u32[]{:S(2)}, u32[]{:S(2)}) %collective-permute-start.1) | collective-permute-done | bytes 319520 | tf_op jit(solution)/shard_map/ppermute | solution.py:1026
  21.4 2.2 %collective-permute-done.refs_1_.refs_7_ = bf16[208,768]{1,0:T(8,128)(2,1)S(1)} collective-permute-done((bf16[208,768]{1,0:T(8,128)(2,1)}, bf16[208,768]{1,0:T(8,128)(2,1)S(1)}, u32[]{:S(2)}, u32[]{:S(2)}) %collective-permute-start) | collective-permute-done | bytes 319520 | tf_op jit(solution)/shard_map/ppermute | solution.py:1026
  23.9 1.7 collective-permute-start.3
  25.7 14.1 %collective-permute-done.2.refs_2_.refs_8_ = bf16[208,768]{1,0:T(8,128)(2,1)S(1)} collective-permute-done((bf16[208,768]{1,0:T(8,128)(2,1)S(1)}, bf16[208,768]{1,0:T(8,128)(2,1)S(1)}, u32[]{:S(2)}, u32[]{:S(2)}) %collective-permute-start.2) | collective-permute-done | bytes 319520 | tf_op jit(solution)/shard_map/ppermute | solution.py:1026
  39.9 1.5 collective-permute-start.4
  42.5 13.3 %collective-permute-done.4.refs_3_.refs_9_ = bf16[208,768]{1,0:T(8,128)(2,1)S(1)} collective-permute-done((bf16[208,768]{1,0:T(8,128)(2,1)S(1)}, bf16[208,768]{1,0:T(8,128)(2,1)S(1)}, u32[]{:S(2)}, u32[]{:S(2)}) %collective-permute-start.4) | collective-permute-done | bytes 319520 | tf_op jit(solution)/shard_map/ppermute | solution.py:1026
  55.7 1.4 collective-permute-done.5.refs_6_.refs_12_
  57.1 0.7 slice.7
  57.8 1.6 collective-permute-start.7
  62.1 7.4 %collective-permute-done.6.refs_4_.refs_10_ = bf16[96,768]{1,0:T(8,128)(2,1)} collective-permute-done((bf16[96,768]{1,0:T(8,128)(2,1)}, bf16[96,768]{1,0:T(8,128)(2,1)}, u32[]{:S(2)}, u32[]{:S(2)}) %collective-permute-start.6) | collective-permute-done | bytes 147488 | tf_op jit(solution)/shard_map/ppermute | solution.py:1026
  70.2 1.1 collective-permute-done.12.refs_13_.refs_19_
  72.1 2.9 %vectors.1.vec = f32[16,768]{1,0:T(8,128)S(1)} custom-call(s32[16]{0:T(128)S(1)} %pad_add_fusion.devs, s32[2]{0:T(128)S(1)} %bitcast.35, bf16[208,768]{1,0:T(8,128)(2,1)} %get-tuple-element.75.refs_0_.refs_6_, bf16[208,768]{1,0:T(8,128)(2,1)} %copy-done.7, bf16[208,768]{1,0:T(8,128)(2,1)} %copy-done.8, bf16[208,768]{1,0:T(8,128)(2,1)} %copy-done.4, ...), custom_call_target="tpu_custom_call" | custom-call | flops 56623104 | bytes 2359296 | tf_op jit(solution)/shard_map/vectors/pallas_call | solution.py:740
  75.0 5.5 %attend.1 = (f32[192,768]{1,0:T(8,128)S(1)}, bf16[192,768]{1,0:T(8,128)(2,1)S(1)}) custom-call(s32[2]{0:T(128)S(1)} %bitcast.33, s32[1]{0:T(128)} %bitcast.flag, s32[16]{0:T(128)S(1)} %pad_add_fusion.devs, bf16[192,768]{1,0:T(8,128)(2,1)S(1)} %bitcast.31, f32[16,768]{1,0:T(8,128)S(1)} %vectors.1.vec, bf16[208,768]{1,0:T(8,128)(2,1)} %get-tuple-element.75.refs_0_.refs_6_, ...), custom_call_target="tpu_custom_call" | custom-call | flops 905969664 | bytes 4718592 | tf_op jit(solution)/shard_map/attend/pallas_call | solution.py:740
  80.6 5.0 %all-gather.2.cloned.1.call-done = bf16[128,48,768]{2,1,0:T(8,128)(2,1)} async-done(((bf16[8,48,768]{2,1,0:T(8,128)(2,1)}), bf16[128,48,768]{2,1,0:T(8,128)(2,1)}) %all-gather.2.cloned.1.call-update) | async-done | bytes 9437200 | tf_op jit(solution)/shard_map/all_gather | solution.py:1099
  85.6 5.1 %mlp.1.after = bf16[192,768]{1,0:T(8,128)(2,1)S(1)} custom-call(s32[1]{0:T(128)} %bitcast.flag, f32[192,768]{1,0:T(8,128)S(1)} %get-tuple-element.82.middle_ref, bf16[192,768]{1,0:T(8,128)(2,1)S(1)} %get-tuple-element.83.hidden_ref, f32[16,768]{1,0:T(8,128)S(1)} %vectors.1.vec, bf16[16,8,48,768]{3,2,1,0:T(8,128)(2,1)} %bitcast.37), custom_call_target="tpu_custom_call" | custom-call | flops 1811939328 | bytes 9437184 | tf_op jit(solution)/shard_map/mlp/pallas_call | solution.py:740
  90.7 1.5 collective-permute-start.17
  92.2 5.6 %load.1 = (bf16[4,16,48,768]{3,2,1,0:T(8,128)(2,1)S(1)}, bf16[8,16,48,768]{3,2,1,0:T(8,128)(2,1)S(1)}, f32[192,3072]{1,0:T(8,128)S(1)}) custom-call(s32[16]{0:T(128)S(1)} %pad_add_fusion.devs, bf16[192,768]{1,0:T(8,128)(2,1)S(1)} %mlp.1.after, bf16[192,768]{1,0:T(8,128)(2,1)S(1)} %bitcast.27, bf16[16,8,48,768]{3,2,1,0:T(8,128)(2,1)} %bitcast.38, ...), custom_call_target="tpu_custom_call" | custom-call | flops 905969664 | bytes 28311552 | tf_op jit(solution)/shard_map/load/pallas_call | solution.py:740
  97.8 1.1 collective-permute-done.17.recv_ref
  99.0 6.3 %chain.1 = (bf16[96,768]{1,0:T(8,128)(2,1)S(1)}, bf16[192,768]{1,0:T(8,128)(2,1)S(1)}, bf16[192,3072]{1,0:T(8,128)(2,1)S(1)}, f32[192,3072]{1,0:T(8,128)S(1)}, b...) custom-call(s32[2]{0:T(128)S(1)} %bitcast.34, ...), custom_call_target="tpu_custom_call" | custom-call | flops 4529848320 | bytes 7077888 | tf_op jit(solution)/shard_map/chain/pallas_call | solution.py:740
  105.3 1.3 collective-permute-start.18
  106.6 1.5 collective-permute-start.19
  108.2 1.9 output.1.beside
  110.0 7.8 %collective-permute-done.18.some_ref = bf16[96,768]{1,0:T(8,128)(2,1)S(1)} collective-permute-done((bf16[96,768]{1,0:T(8,128)(2,1)S(1)}, bf16[96,768]{1,0:T(8,128)(2,1)S(1)}, u32[]{:S(2)}, u32[]{:S(2)}) %collective-permute-start.18) | collective-permute-done | bytes 147488 | tf_op jit(solution)/shard_map/ppermute | solution.py:998
  117.9 4.4 %collective-permute-done.19.other_ref = bf16[96,768]{1,0:T(8,128)(2,1)S(1)} collective-permute-done((bf16[96,768]{1,0:T(8,128)(2,1)S(1)}, bf16[96,768]{1,0:T(8,128)(2,1)S(1)}, u32[]{:S(2)}, u32[]{:S(2)}) %collective-permute-start.19) | collective-permute-done | bytes 147488 | tf_op jit(solution)/shard_map/ppermute | solution.py:998
  122.3 5.7 %mlp_back.1 = (bf16[192,3072]{1,0:T(8,128)(2,1)}, f32[16,768]{1,0:T(8,128)S(1)}, bf16[16,8,48,768]{3,2,1,0:T(8,128)(2,1)}) custom-call(s32[1]{0:T(128)} %bitcast.flag, bf16[192,768]{1,0:T(8,128)(2,1)} %output.1.beside, bf16[96,768]{1,0:T(8,128)(2,1)S(1)} %collective-permute-done.18.some_ref, bf16[96,768]{1,0:T(8,128)(2,1)S(1)} %collective-permute-done.19.other_ref, ...), custom_call_target="tpu_custom_call" | custom-call | flops 3623878656 | bytes 9437184 | tf_op jit(solution)/shard_map/mlp_back/pallas_call | solution.py:740
  128.1 18.7 %rest.1 = (f32[192,768]{1,0:T(8,128)}, f32[16,768]{1,0:T(8,128)}, bf16[8,208,768]{2,1,0:T(8,128)(2,1)}, bf16[8,208,768]{2,1,0:T(8,128)(2,1)}, bf16[1,208,768]{2,1,0:T(8,128)(2,1)}) custom-call(s32[1]{0:T(128)} %bitcast.flag, s32[16]{0:T(128)S(1)} %pad_add_fusion.devs, s32[2]{0:T(128)S(1)} %bitcast.36, bf16[96,768]{1,0:T(8,128)(2,1)S(1)} %collective-permute-done.18.some_ref, ...), custom_call_target="tpu_custom_call" | custom-call | flops 2717908992 | bytes 14155776 | tf_op jit(solution)/shard_map/rest/pallas_call | solution.py:740
  146.8 1.8 collective-permute-done.20.refs_1_.refs_3_
  148.8 1.2 add.77
  150.1 1.9 collective-permute-start.22
  152.0 6.0 %collective-permute-done.22.refs_2_ = bf16[96,768]{1,0:T(8,128)(2,1)S(1)} collective-permute-done((bf16[96,768]{1,0:T(8,128)(2,1)S(1)}, bf16[96,768]{1,0:T(8,128)(2,1)S(1)}, u32[]{:S(2)}, u32[]{:S(2)}) %collective-permute-start.22) | collective-permute-done | bytes 147488 | tf_op jit(solution)/shard_map/ppermute | solution.py:1026
  158.0 0.8 collective-permute-done.23.refs_5_
  158.8 1.3 add.78
  160.1 1.4 collective-permute-start.24
  162.2 11.2 %collective-permute-done.24.refs_2_ = bf16[208,768]{1,0:T(8,128)(2,1)S(1)} collective-permute-done((bf16[208,768]{1,0:T(8,128)(2,1)S(1)}, bf16[208,768]{1,0:T(8,128)(2,1)S(1)}, u32[]{:S(2)}, u32[]{:S(2)}) %collective-permute-start.24) | collective-permute-done | bytes 319520 | tf_op jit(solution)/shard_map/ppermute | solution.py:1026
  173.4 1.2 collective-permute-done.25.refs_5_
  174.6 1.3 add.79
  175.9 1.7 collective-permute-start.26
  178.0 10.7 %collective-permute-done.26.refs_2_ = bf16[208,768]{1,0:T(8,128)(2,1)S(1)} collective-permute-done((bf16[208,768]{1,0:T(8,128)(2,1)S(1)}, bf16[208,768]{1,0:T(8,128)(2,1)S(1)}, u32[]{:S(2)}, u32[]{:S(2)}) %collective-permute-start.26) | collective-permute-done | bytes 319520 | tf_op jit(solution)/shard_map/ppermute | solution.py:1026
  188.7 1.6 collective-permute-done.27.refs_5_
  190.3 1.3 add.80
  191.6 1.6 collective-permute-start.28
  193.7 10.0 %collective-permute-done.28.ahead = bf16[208,768]{1,0:T(8,128)(2,1)S(1)} collective-permute-done((bf16[208,768]{1,0:T(8,128)(2,1)S(1)}, bf16[208,768]{1,0:T(8,128)(2,1)S(1)}, u32[]{:S(2)}, u32[]{:S(2)}) %collective-permute-start.28) | collective-permute-done | bytes 319520 | tf_op jit(solution)/shard_map/ppermute | solution.py:1026
  203.7 1.5 collective-permute-done.29.behind
  205.2 2.0 total.1
  207.2 2.4 %reduce-scatter.2.cloned.1.call-done.grads_ref = bf16[8,48,768]{2,1,0:T(8,128)(2,1)} async-done(((bf16[128,48,768]{2,1,0:T(8,128)(2,1)}), bf16[8,48,768]{2,1,0:T(8,128)(2,1)}) %reduce-scatter.2.cloned.1.call-update) | async-done | bytes 589840 | tf_op jit(solution)/shard_map/reduce_scatter | solution.py:1155
  209.6 2.1 unpack.1
  (72 shorter events, 7.4 us)
Async XLA Ops:
  7.2 64.9 %copy-start.3 = (s32[2,1]{0,1:T(1,128)S(1)}, s32[2,1]{0,1:T(1,128)}, u32[]{:S(2)}) copy-start(s32[2,1]{0,1:T(1,128)} %param.21) | copy-start | bytes 28
  7.2 78.4 %all-gather.2.cloned.1.call-start = ((), (), s32[]{:S(2)}) async-start(), calls=%async_computation.1 | async-start | bytes 10027008 | tf_op jit(solution)/shard_map/all_gather | solution.py:1099
  9.9 199.7 %reduce-scatter.2.cloned.1.call-start = ((), (), s32[]{:S(2)}) async-start(), calls=%async_computation.2 | async-start | bytes 10027008 | tf_op jit(solution)/shard_map/reduce_scatter | solution.py:1155
  9.9 11.5 %collective-permute-start.1 = (bf16[208,768]{1,0:T(8,128)(2,1)}, bf16[208,768]{1,0:T(8,128)(2,1)S(1)}, u32[]{:S(2)}, u32[]{:S(2)}) collective-permute-start(bf16[208,768]{1,0:T(8,128)(2,1)} %get-tuple-element.75.refs_0_.refs_6_), channel_id=1, source_target_pairs={{0,4},{1,5},{4,8},{5,9},{8,12},{9,13},{12,14},{13,15},{14,10},{15,... | collective-permute-start | bytes 958472 | tf_op jit(solution)/shard_map/ppermute | solution.py:1026
  13.0 10.6 %collective-permute-start = (bf16[208,768]{1,0:T(8,128)(2,1)}, bf16[208,768]{1,0:T(8,128)(2,1)S(1)}, u32[]{:S(2)}, u32[]{:S(2)}) collective-permute-start(bf16[208,768]{1,0:T(8,128)(2,1)} %get-tuple-element.75.refs_0_.refs_6_), channel_id=1, source_target_pairs={{4,0},{5,1},{8,4},{9,5},{12,8},{13,9},{14,12},{15,13},{10,14},{11,... | collective-permute-start | bytes 958472 | tf_op jit(solution)/shard_map/ppermute | solution.py:1026
  21.4 50.6 %copy-start.6 = (bf16[208,768]{1,0:T(8,128)(2,1)}, bf16[208,768]{1,0:T(8,128)(2,1)S(1)}, u32[]{:S(2)}) copy-start(bf16[208,768]{1,0:T(8,128)(2,1)S(1)} %collective-permute-done.1.refs_8_.refs_14_) | copy-start | bytes 958468
  23.6 48.4 %copy-start.7 = (bf16[208,768]{1,0:T(8,128)(2,1)}, bf16[208,768]{1,0:T(8,128)(2,1)S(1)}, u32[]{:S(2)}) copy-start(bf16[208,768]{1,0:T(8,128)(2,1)S(1)} %collective-permute-done.refs_1_.refs_7_) | copy-start | bytes 958468
  23.6 16.2 %collective-permute-start.2 = (bf16[208,768]{1,0:T(8,128)(2,1)S(1)}, bf16[208,768]{1,0:T(8,128)(2,1)S(1)}, u32[]{:S(2)}, u32[]{:S(2)}) collective-permute-start(bf16[208,768]{1,0:T(8,128)(2,1)S(1)} %collective-permute-done.refs_1_.refs_7_), channel_id=1, source_target_pairs={{4,0},{5,1},{8,4},{9,5},{12,8},{13,9},{14,12},{15,13},{10,14},{11,... | collective-permute-start | bytes 958472 | tf_op jit(solution)/shard_map/ppermute | solution.py:1026
  23.9 16.0 %collective-permute-start.3 = (bf16[208,768]{1,0:T(8,128)(2,1)S(1)}, bf16[208,768]{1,0:T(8,128)(2,1)S(1)}, u32[]{:S(2)}, u32[]{:S(2)}) collective-permute-start(bf16[208,768]{1,0:T(8,128)(2,1)S(1)} %collective-permute-done.1.refs_8_.refs_14_), channel_id=1, source_target_pairs={{0,4},{1,5},{4,8},{5,9},{8,12},{9,13},{12,14},{13,15},{14,10},{15,... | collective-permute-start | bytes 958472 | tf_op jit(solution)/shard_map/ppermute | solution.py:1026
  39.8 32.2 %copy-start.8 = (bf16[208,768]{1,0:T(8,128)(2,1)}, bf16[208,768]{1,0:T(8,128)(2,1)S(1)}, u32[]{:S(2)}) copy-start(bf16[208,768]{1,0:T(8,128)(2,1)S(1)} %collective-permute-done.2.refs_2_.refs_8_) | copy-start | bytes 958468
  39.9 32.1 %copy-start.9 = (bf16[208,768]{1,0:T(8,128)(2,1)}, bf16[208,768]{1,0:T(8,128)(2,1)S(1)}, u32[]{:S(2)}) copy-start(bf16[208,768]{1,0:T(8,128)(2,1)S(1)} %collective-permute-done.3.refs_7_.refs_13_) | copy-start | bytes 958468
  39.9 15.8 %collective-permute-start.4 = (bf16[208,768]{1,0:T(8,128)(2,1)S(1)}, bf16[208,768]{1,0:T(8,128)(2,1)S(1)}, u32[]{:S(2)}, u32[]{:S(2)}) collective-permute-start(bf16[208,768]{1,0:T(8,128)(2,1)S(1)} %collective-permute-done.2.refs_2_.refs_8_), channel_id=1, source_target_pairs={{4,0},{5,1},{8,4},{9,5},{12,8},{13,9},{14,12},{15,13},{10,14},{11,... | collective-permute-start | bytes 958472 | tf_op jit(solution)/shard_map/ppermute | solution.py:1026
  41.5 15.6 %collective-permute-start.5 = (bf16[208,768]{1,0:T(8,128)(2,1)S(1)}, bf16[208,768]{1,0:T(8,128)(2,1)S(1)}, u32[]{:S(2)}, u32[]{:S(2)}) collective-permute-start(bf16[208,768]{1,0:T(8,128)(2,1)S(1)} %collective-permute-done.3.refs_7_.refs_13_), channel_id=1, source_target_pairs={{0,4},{1,5},{4,8},{5,9},{8,12},{9,13},{12,14},{13,15},{14,10},{15,... | collective-permute-start | bytes 958472 | tf_op jit(solution)/shard_map/ppermute | solution.py:1026
  41.9 18.2 %collective-permute-start.8 = (bf16[208,768]{1,0:T(8,128)(2,1)}, bf16[208,768]{1,0:T(8,128)(2,1)S(1)}, u32[]{:S(2)}, u32[]{:S(2)}) collective-permute-start(bf16[208,768]{1,0:T(8,128)(2,1)} %get-tuple-element.75.refs_0_.refs_6_), channel_id=1, source_target_pairs={{0,1},{1,0},{2,3},{3,2},{4,5},{5,4},{6,7},{7,6},{8,9},{9,8},{10,11... | collective-permute-start | bytes 958472 | tf_op jit(solution)/shard_map/ppermute | solution.py:1040
  41.9 18.6 %collective-permute-start.16 = (bf16[208,768]{1,0:T(8,128)(2,1)S(1)}, bf16[208,768]{1,0:T(8,128)(2,1)S(1)}, u32[]{:S(2)}, u32[]{:S(2)}) collective-permute-start(bf16[208,768]{1,0:T(8,128)(2,1)S(1)} %collective-permute-done.1.refs_8_.refs_14_), channel_id=1, source_target_pairs={{0,1},{1,0},{2,3},{3,2},{4,5},{5,4},{6,7},{7,6},{8,9},{9,8},{10,11... | collective-permute-start | bytes 958472 | tf_op jit(solution)/shard_map/ppermute | solution.py:1040
  42.4 18.1 %collective-permute-start.9 = (bf16[208,768]{1,0:T(8,128)(2,1)S(1)}, bf16[208,768]{1,0:T(8,128)(2,1)S(1)}, u32[]{:S(2)}, u32[]{:S(2)}) collective-permute-start(bf16[208,768]{1,0:T(8,128)(2,1)S(1)} %collective-permute-done.refs_1_.refs_7_), channel_id=1, source_target_pairs={{0,1},{1,0},{2,3},{3,2},{4,5},{5,4},{6,7},{7,6},{8,9},{9,8},{10,11... | collective-permute-start | bytes 958472 | tf_op jit(solution)/shard_map/ppermute | solution.py:1040
  55.7 16.3 %copy-start.4 = (bf16[208,768]{1,0:T(8,128)(2,1)}, bf16[208,768]{1,0:T(8,128)(2,1)S(1)}, u32[]{:S(2)}) copy-start(bf16[208,768]{1,0:T(8,128)(2,1)S(1)} %collective-permute-done.4.refs_3_.refs_9_) | copy-start | bytes 958468
  55.7 5.3 %collective-permute-start.10 = (bf16[208,768]{1,0:T(8,128)(2,1)S(1)}, bf16[208,768]{1,0:T(8,128)(2,1)S(1)}, u32[]{:S(2)}, u32[]{:S(2)}) collective-permute-start(bf16[208,768]{1,0:T(8,128)(2,1)S(1)} %collective-permute-done.2.refs_2_.refs_8_), channel_id=1, source_target_pairs={{0,1},{1,0},{2,3},{3,2},{4,5},{5,4},{6,7},{7,6},{8,9},{9,8},{10,11... | collective-permute-start | bytes 958472 | tf_op jit(solution)/shard_map/ppermute | solution.py:1040
  57.1 14.9 %copy-start.5 = (bf16[208,768]{1,0:T(8,128)(2,1)}, bf16[208,768]{1,0:T(8,128)(2,1)S(1)}, u32[]{:S(2)}) copy-start(bf16[208,768]{1,0:T(8,128)(2,1)S(1)} %collective-permute-done.5.refs_6_.refs_12_) | copy-start | bytes 958468
  57.8 11.7 %collective-permute-start.7 = (bf16[112,768]{1,0:T(8,128)(2,1)}, bf16[112,768]{1,0:T(8,128)(2,1)S(1)}, u32[]{:S(2)}, u32[]{:S(2)}) collective-permute-start(bf16[112,768]{1,0:T(8,128)(2,1)} %slice.7), channel_id=1, source_target_pairs={{4,0},{5,1},{8,4},{9,5},{12,8},{13,9},{14,12},{15,13},{10,14},{11,... | collective-permute-start | bytes 516104 | tf_op jit(solution)/shard_map/ppermute | solution.py:1026
  60.1 11.9 %copy-start.10 = (bf16[208,768]{1,0:T(8,128)(2,1)}, bf16[208,768]{1,0:T(8,128)(2,1)S(1)}, u32[]{:S(2)}) copy-start(bf16[208,768]{1,0:T(8,128)(2,1)S(1)} %collective-permute-done.8.refs_9_.refs_15_) | copy-start | bytes 958468
  60.1 9.4 %collective-permute-start.6 = (bf16[96,768]{1,0:T(8,128)(2,1)}, bf16[96,768]{1,0:T(8,128)(2,1)}, u32[]{:S(2)}, u32[]{:S(2)}) collective-permute-start(bf16[96,768]{1,0:T(8,128)(2,1)} %slice.6), channel_id=1, source_target_pairs={{0,4},{1,5},{4,8},{5,9},{8,12},{9,13},{12,14},{13,15},{14,10},{15,... | collective-permute-start | bytes 442376 | tf_op jit(solution)/shard_map/ppermute | solution.py:1026
  60.5 11.5 %copy-start.11 = (bf16[208,768]{1,0:T(8,128)(2,1)}, bf16[208,768]{1,0:T(8,128)(2,1)S(1)}, u32[]{:S(2)}) copy-start(bf16[208,768]{1,0:T(8,128)(2,1)S(1)} %collective-permute-done.16.refs_17_.refs_23_) | copy-start | bytes 958468
  60.5 9.6 %collective-permute-start.15 = (bf16[208,768]{1,0:T(8,128)(2,1)S(1)}, bf16[208,768]{1,0:T(8,128)(2,1)S(1)}, u32[]{:S(2)}, u32[]{:S(2)}) collective-permute-start(bf16[208,768]{1,0:T(8,128)(2,1)S(1)} %collective-permute-done.3.refs_7_.refs_13_), channel_id=1, source_target_pairs={{0,1},{1,0},{2,3},{3,2},{4,5},{5,4},{6,7},{7,6},{8,9},{9,8},{10,11... | collective-permute-start | bytes 958472 | tf_op jit(solution)/shard_map/ppermute | solution.py:1040
  60.6 0.8 copy-start.12
  60.6 10.7 %collective-permute-start.11 = (bf16[208,768]{1,0:T(8,128)(2,1)S(1)}, bf16[208,768]{1,0:T(8,128)(2,1)S(1)}, u32[]{:S(2)}, u32[]{:S(2)}) collective-permute-start(bf16[208,768]{1,0:T(8,128)(2,1)S(1)} %collective-permute-done.4.refs_3_.refs_9_), channel_id=1, source_target_pairs={{0,1},{1,0},{2,3},{3,2},{4,5},{5,4},{6,7},{7,6},{8,9},{9,8},{10,11... | collective-permute-start | bytes 958472 | tf_op jit(solution)/shard_map/ppermute | solution.py:1040
  61.4 0.7 copy-start.13
  61.4 9.9 %collective-permute-start.14 = (bf16[208,768]{1,0:T(8,128)(2,1)S(1)}, bf16[208,768]{1,0:T(8,128)(2,1)}, u32[]{:S(2)}, u32[]{:S(2)}) collective-permute-start(bf16[208,768]{1,0:T(8,128)(2,1)S(1)} %collective-permute-done.5.refs_6_.refs_12_), channel_id=1, source_target_pairs={{0,1},{1,0},{2,3},{3,2},{4,5},{5,4},{6,7},{7,6},{8,9},{9,8},{10,11... | collective-permute-start | bytes 958472 | tf_op jit(solution)/shard_map/ppermute | solution.py:1040
  69.6 1.7 collective-permute-start.12
  69.6 2.5 %copy-start.16 = (bf16[112,768]{1,0:T(8,128)(2,1)}, bf16[112,768]{1,0:T(8,128)(2,1)S(1)}, u32[]{:S(2)}) copy-start(bf16[112,768]{1,0:T(8,128)(2,1)S(1)} %collective-permute-done.7.refs_5_.refs_11_) | copy-start | bytes 516100
  69.6 1.9 collective-permute-start.13
  70.2 1.3 copy-start.14
  72.1 2.9 %copy-start.1 = (bf16[2,1,96,768]{3,2,1,0:T(8,128)(2,1)S(1)}, bf16[2,1,96,768]{3,2,1,0:T(8,128)(2,1)}, u32[]{:S(2)}) copy-start(bf16[2,1,96,768]{3,2,1,0:T(8,128)(2,1)} %param.18) | copy-start | bytes 884740
  72.1 2.9 %copy-start.2 = (s32[2,1]{0,1:T(1,128)S(1)}, s32[2,1]{0,1:T(1,128)}, u32[]{:S(2)}) copy-start(s32[2,1]{0,1:T(1,128)} %param.20) | copy-start | bytes 28
  85.6 6.6 %copy-start = (bf16[2,1,96,768]{3,2,1,0:T(8,128)(2,1)S(1)}, bf16[2,1,96,768]{3,2,1,0:T(8,128)(2,1)}, u32[]{:S(2)}) copy-start(bf16[2,1,96,768]{3,2,1,0:T(8,128)(2,1)} %param.19) | copy-start | bytes 884740
  90.7 8.2 %collective-permute-start.17 = (bf16[192,768]{1,0:T(8,128)(2,1)S(1)}, bf16[192,768]{1,0:T(8,128)(2,1)S(1)}, u32[]{:S(2)}, u32[]{:S(2)}) collective-permute-start(bf16[192,768]{1,0:T(8,128)(2,1)S(1)} %mlp.1.after), channel_id=1, source_target_pairs={{0,16},{1,17},{2,18},{3,19},{4,20},{5,21},{6,22},{7,23},{8,24},{9,... | collective-permute-start | bytes 884744 | tf_op jit(solution)/shard_map/ppermute | solution.py:998
  105.3 12.5 %collective-permute-start.18 = (bf16[96,768]{1,0:T(8,128)(2,1)S(1)}, bf16[96,768]{1,0:T(8,128)(2,1)S(1)}, u32[]{:S(2)}, u32[]{:S(2)}) collective-permute-start(bf16[96,768]{1,0:T(8,128)(2,1)S(1)} %get-tuple-element.90), channel_id=1, source_target_pairs={{16,0},{17,1},{18,2},{19,3},{20,4},{21,5},{22,6},{23,7},{24,8},{25... | collective-permute-start | bytes 442376 | tf_op jit(solution)/shard_map/ppermute | solution.py:998
  106.6 15.6 %collective-permute-start.19 = (bf16[96,768]{1,0:T(8,128)(2,1)S(1)}, bf16[96,768]{1,0:T(8,128)(2,1)S(1)}, u32[]{:S(2)}, u32[]{:S(2)}) collective-permute-start(bf16[96,768]{1,0:T(8,128)(2,1)S(1)} %chain_end.1), channel_id=1, source_target_pairs={{16,0},{17,1},{18,2},{19,3},{20,4},{21,5},{22,6},{23,7},{24,8},{25... | collective-permute-start | bytes 442376 | tf_op jit(solution)/shard_map/ppermute | solution.py:998
  146.7 1.9 collective-permute-start.20
  148.6 10.2 %collective-permute-start.21 = (bf16[8,208,768]{2,1,0:T(8,128)(2,1)}, bf16[8,208,768]{2,1,0:T(8,128)(2,1)S(1)}, u32[]{:S(2)}, u32[]{:S(2)}) collective-permute-start(bf16[8,208,768]{2,1,0:T(8,128)(2,1)} %get-tuple-element.110), channel_id=1, source_target_pairs={{0,1},{1,0},{2,3},{3,2},{4,5},{5,4},{6,7},{7,6},{8,9},{9,8},{10,11... | collective-permute-start | bytes 7667720 | tf_op jit(solution)/shard_map/ppermute | solution.py:1040
  149.9 8.9 %collective-permute-start.23 = (bf16[112,768]{1,0:T(8,128)(2,1)S(1)}, bf16[112,768]{1,0:T(8,128)(2,1)S(1)}, u32[]{:S(2)}, u32[]{:S(2)}) collective-permute-start(bf16[112,768]{1,0:T(8,128)(2,1)S(1)} %get-tuple-element.112), channel_id=1, source_target_pairs={{4,0},{5,1},{8,4},{9,5},{12,8},{13,9},{14,12},{15,13},{10,14},{11,... | collective-permute-start | bytes 516104 | tf_op jit(solution)/shard_map/ppermute | solution.py:1026
  150.1 8.0 %collective-permute-start.22 = (bf16[96,768]{1,0:T(8,128)(2,1)S(1)}, bf16[96,768]{1,0:T(8,128)(2,1)S(1)}, u32[]{:S(2)}, u32[]{:S(2)}) collective-permute-start(bf16[96,768]{1,0:T(8,128)(2,1)S(1)} %get-tuple-element.111), channel_id=1, source_target_pairs={{0,4},{1,5},{4,8},{5,9},{8,12},{9,13},{12,14},{13,15},{14,10},{15,... | collective-permute-start | bytes 442376 | tf_op jit(solution)/shard_map/ppermute | solution.py:1026
  160.1 13.3 %collective-permute-start.24 = (bf16[208,768]{1,0:T(8,128)(2,1)S(1)}, bf16[208,768]{1,0:T(8,128)(2,1)S(1)}, u32[]{:S(2)}, u32[]{:S(2)}) collective-permute-start(bf16[208,768]{1,0:T(8,128)(2,1)S(1)} %get-tuple-element.113), channel_id=1, source_target_pairs={{0,4},{1,5},{4,8},{5,9},{8,12},{9,13},{12,14},{13,15},{14,10},{15,... | collective-permute-start | bytes 958472 | tf_op jit(solution)/shard_map/ppermute | solution.py:1026
  161.5 13.1 %collective-permute-start.25 = (bf16[208,768]{1,0:T(8,128)(2,1)S(1)}, bf16[208,768]{1,0:T(8,128)(2,1)S(1)}, u32[]{:S(2)}, u32[]{:S(2)}) collective-permute-start(bf16[208,768]{1,0:T(8,128)(2,1)S(1)} %get-tuple-element.114), channel_id=1, source_target_pairs={{4,0},{5,1},{8,4},{9,5},{12,8},{13,9},{14,12},{15,13},{10,14},{11,... | collective-permute-start | bytes 958472 | tf_op jit(solution)/shard_map/ppermute | solution.py:1026
  175.9 12.8 %collective-permute-start.26 = (bf16[208,768]{1,0:T(8,128)(2,1)S(1)}, bf16[208,768]{1,0:T(8,128)(2,1)S(1)}, u32[]{:S(2)}, u32[]{:S(2)}) collective-permute-start(bf16[208,768]{1,0:T(8,128)(2,1)S(1)} %get-tuple-element.115), channel_id=1, source_target_pairs={{0,4},{1,5},{4,8},{5,9},{8,12},{9,13},{12,14},{13,15},{14,10},{15,... | collective-permute-start | bytes 958472 | tf_op jit(solution)/shard_map/ppermute | solution.py:1026
  177.6 12.6 %collective-permute-start.27 = (bf16[208,768]{1,0:T(8,128)(2,1)S(1)}, bf16[208,768]{1,0:T(8,128)(2,1)S(1)}, u32[]{:S(2)}, u32[]{:S(2)}) collective-permute-start(bf16[208,768]{1,0:T(8,128)(2,1)S(1)} %get-tuple-element.116), channel_id=1, source_target_pairs={{4,0},{5,1},{8,4},{9,5},{12,8},{13,9},{14,12},{15,13},{10,14},{11,... | collective-permute-start | bytes 958472 | tf_op jit(solution)/shard_map/ppermute | solution.py:1026
  191.6 12.1 %collective-permute-start.28 = (bf16[208,768]{1,0:T(8,128)(2,1)S(1)}, bf16[208,768]{1,0:T(8,128)(2,1)S(1)}, u32[]{:S(2)}, u32[]{:S(2)}) collective-permute-start(bf16[208,768]{1,0:T(8,128)(2,1)S(1)} %get-tuple-element.117), channel_id=1, source_target_pairs={{0,4},{1,5},{4,8},{5,9},{8,12},{9,13},{12,14},{13,15},{14,10},{15,... | collective-permute-start | bytes 958472 | tf_op jit(solution)/shard_map/ppermute | solution.py:1026
  193.1 12.0 %collective-permute-start.29 = (bf16[208,768]{1,0:T(8,128)(2,1)S(1)}, bf16[208,768]{1,0:T(8,128)(2,1)S(1)}, u32[]{:S(2)}, u32[]{:S(2)}) collective-permute-start(bf16[208,768]{1,0:T(8,128)(2,1)S(1)} %get-tuple-element.118), channel_id=1, source_target_pairs={{4,0},{5,1},{8,4},{9,5},{12,8},{13,9},{14,12},{15,13},{10,14},{11,... | collective-permute-start | bytes 958472 | tf_op jit(solution)/shard_map/ppermute | solution.py:1026
  (1 other events, 0.7 us)
Sparse Core Ops, SparseCore 0:
  10.2 75.3 all-gather.1
  128.2 81.3 reduce-scatter.1

commit v8 on v7

--- a/solution.py
+++ b/solution.py
@@ -291,8 +291,8 @@
         y_ref[...] = (middle_ref[...] + total).astype(BF16)
 
 
-def load_kernel(plan, devs, after, cot_ref, gathered, *refs):
-    firsts, (held1, held2, grad_act, sems, down_sems) = refs[:-5], refs[-5:]
+def load_kernel(plan, devs, flag, after, cot_ref, gathered, *refs):
+    firsts, (held1, held2, grad_act, turned, sems, down_sems) = refs[:-6], refs[-6:]
     ups, downs = second_pieces(plan, gathered)
     start_all([copy for _, copy in down_copies(plan, downs, plan.order, held2, down_sems)])
     start_all(block_copies(ups, plan.order, held2, sems.at[1], pl.ds(0, QUART)))
@@ -305,20 +305,27 @@
     wait_bytes(held2.at[pl.ds(0, QUART)], sems.at[1])
     wait_bytes(held1, sems.at[0])
 
-
-def input_grad(plan, items, vec, held1, xin_ref, qkv, probs, grad_middle, grad_attended, grad_rows, dx_ref):
+    @pl.when(flag[0] == 1)
+    def _():
+        for block in range(FIRST):
+            turned[block] = block_of(plan, held1, block).T
+        for part in range(QUART):
+            turned[FIRST + part] = block_of(plan, held2, part).T
+
+
+def input_grad(plan, items, vec, turned, xin_ref, qkv, probs, grad_middle, grad_attended, grad_rows, dx_ref):
     attention_back(plan, probs, qkv, grad_attended, grad_rows, items)
     rows = slice(items.start * plan.length, items.stop * plan.length)
     grad_normed = None
     for part in range(OUT):
-        term = mm_nt(grad_rows[rows, columns_of(plan, part)], block_of(plan, held1, part))
+        term = mm(grad_rows[rows, columns_of(plan, part)], turned[part])
         grad_normed = term if grad_normed is None else grad_normed + term
     xhat, rstd = normalised(xin_ref[rows, :].astype(F32))
     dx_ref[...] = (grad_middle[rows, :] + norm_back(grad_normed, xhat, rstd, vec[0:1, :])).astype(BF16)
 
 
 def chain_kernel(
-    plan, lengths, flag, x_ref, recv_ref, cot_ref, vec, held1, held2, grad_act,
+    plan, lengths, flag, x_ref, recv_ref, cot_ref, vec, held1, held2, grad_act, turned,
     dx_ref, hidden, act, slope, xin_ref, qkv, probs, grad_middle, grad_attended, middle, *refs,
 ):
     outs, (normed, attended, grad_rows, sems) = refs[:6], refs[6:]
@@ -342,24 +349,24 @@
         grad_hidden = None
         for part in range(QUART):
             grad_pre = (slope[:, columns_of(plan, part)] * grad_act[:, columns_of(plan, part)]).astype(BF16)
-            term = mm_nt(grad_pre, block_of(plan, held2, part))
+            term = mm(grad_pre, turned[FIRST + part])
             grad_hidden = term if grad_hidden is None else grad_hidden + term
         xhat, rstd = normalised(middle[...])
         grad_middle[...] = branch.astype(F32) + norm_back(grad_hidden, xhat, rstd, vec[5:6, :])
-        grad_attended[...] = mm_nt(grad_middle[...].astype(BF16), block_of(plan, held1, OUT)).astype(BF16)
+        grad_attended[...] = mm(grad_middle[...].astype(BF16), turned[OUT]).astype(BF16)
         input_grad(
-            plan, range(plan.items // 2), vec, held1, xin_ref, qkv, probs, grad_middle, grad_attended, grad_rows, dx_ref
+            plan, range(plan.items // 2), vec, turned, xin_ref, qkv, probs, grad_middle, grad_attended, grad_rows, dx_ref
         )
 
     for copy in copies:
         copy.wait()
 
 
-def chain_end_kernel(plan, flag, vec, held1, xin_ref, qkv, probs, grad_middle, grad_attended, dx_ref, grad_rows):
+def chain_end_kernel(plan, flag, vec, turned, xin_ref, qkv, probs, grad_middle, grad_attended, dx_ref, grad_rows):
     @pl.when(flag[0] == 1)
     def _():
         input_grad(
-            plan, range(plan.items // 2, plan.items), vec, held1, xin_ref, qkv, probs, grad_middle, grad_attended,
+            plan, range(plan.items // 2, plan.items), vec, turned, xin_ref, qkv, probs, grad_middle, grad_attended,
             grad_rows, dx_ref,
         )
 
@@ -807,22 +814,23 @@
     )
 
 
-def run_load(plan, devs, after, cot, firsts, gathered):
+def run_load(plan, devs, flag, after, cot, firsts, gathered):
     block = plan.width * plan.width
     return call(
         functools.partial(load_kernel, plan),
-        [held_blocks(plan, FIRST), held_blocks(plan, SECOND), inside(kept_shapes(plan)[7])],
-        [SMEM, ANY, VMEM] + [HBM] * (1 + len(firsts)),
-        [VMEM] * 3,
+        [held_blocks(plan, FIRST), held_blocks(plan, SECOND), inside(kept_shapes(plan)[7])]
+        + [pltpu.VMEM((FIRST + QUART, plan.width, plan.width), BF16)],
+        [SMEM, SMEM, ANY, VMEM] + [HBM] * (1 + len(firsts)),
+        [VMEM] * 4,
         [pltpu.SemaphoreType.DMA((2,)), pltpu.SemaphoreType.DMA((QUART,))],
         "load",
         (QUART * block * plan.tokens, (FIRST + SECOND) * block * 4),
         4,
-        (devs, after, cot, gathered, *firsts),
-    )
-
-
-def run_chain(plan, lengths, flag, x, recv, cot, vec, held1, held2, grad_act):
+        (devs, flag, after, cot, gathered, *firsts),
+    )
+
+
+def run_chain(plan, lengths, flag, x, recv, cot, vec, held1, held2, grad_act, turned):
     shapes = kept_shapes(plan)
     block = plan.width * plan.width
     rest = [shapes[index] for index in (0, 0, 1, 2, 3, 5)]
@@ -832,14 +840,14 @@
         [of(some)]
         + [inside(shapes[index]) for index in (4, 6, 7, 0, 1, 5, 3, 0, 3)]
         + [pltpu.HBM(*shape) for shape in rest],
-        [SMEM] * 2 + [VMEM] * 7,
+        [SMEM] * 2 + [VMEM] * 8,
         [VMEM] * 10 + [HBM] * len(rest),
         [inside(shapes[index]) for index in (0, 2, 1)]
         + [pltpu.SemaphoreType.DMA((len(rest),))],
         "chain",
         (20 * block * plan.tokens, 12 * block),
         12,
-        (lengths, flag, x, recv, cot, vec, held1, held2, grad_act),
+        (lengths, flag, x, recv, cot, vec, held1, held2, grad_act, turned),
     )
     return results[0], results[1:4], results[4:9], results[9], results[10:]
 
@@ -859,7 +867,7 @@
     )
 
 
-def run_chain_end(plan, flag, vec, held1, end):
+def run_chain_end(plan, flag, vec, turned, end):
     shapes = kept_shapes(plan)
     block = plan.width * plan.width
     left = plan.items - plan.items // 2
@@ -872,7 +880,7 @@
         "chain_end",
         (2 * block * plan.tokens, 3 * block),
         6,
-        (flag, vec, held1, *end),
+        (flag, vec, turned, *end),
     )
 
 
@@ -1132,11 +1140,11 @@
     middle, hidden = run_attend(plan, lens, flag, devs, x, vec, firsts)
     first_out = run_mlp(plan, flag, middle, hidden, vec, gathered)
     recv = shifted(first_out, "section", 1)
-    held1, held2, grad_act = run_load(plan, devs, first_out, cot, firsts, gathered)
+    held1, held2, grad_act, turned = run_load(plan, devs, flag, first_out, cot, firsts, gathered)
     some_grad, (hidden, act, slope), end, middle, kept = run_chain(
-        plan, lens, flag, x, recv, cot, vec, held1, held2, grad_act
-    )
-    other_grad = run_chain_end(plan, flag, vec, held1, end)
+        plan, lens, flag, x, recv, cot, vec, held1, held2, grad_act, turned
+    )
+    other_grad = run_chain_end(plan, flag, vec, turned, end)
     arriving = [shifted(grad, "section", -1) for grad in (some_grad, other_grad)]
     output = run_output(plan, flag, act, middle, vec, held2)
     grad_pre, sums, grads2 = run_mlp_back(

time: 219 us -> 217 us (level)
  no operation moved by 1% of the time
where the time goes in v8:
time: 217 us
  waiting for transfers between devices  112 us (52%)
  Pallas kernels  63.6 us (29%)
  starting transfers between devices  23.8 us (11%)
  between operations  14.3 us (7%)
  local copies, waits for them, and re-layouts  2.55 us (1%)
    ppermute x8, waiting for transfers between devices, step(): lax.ppermute(ahead, 'dp', self.onward)  55.2 us
    pallas_call x9, Pallas kernels, call(): pl.pallas_call(kernel, out_shape=outs, in_specs=in_specs, out_specs=out_s...  51.8 us
    ppermute x8, waiting for transfers between devices, step(): lax.ppermute(behind, 'dp', self.back)  34.8 us
    ppermute x8, starting transfers between devices, step(): lax.ppermute(ahead, 'dp', self.onward)  12.4 us
    ppermute x3, waiting for transfers between devices, shifted(): lax.ppermute(value, axis, [(source, source + steps) for source in range(f...  11.9 us
    ppermute x8, starting transfers between devices, step(): lax.ppermute(behind, 'dp', self.back)  5.12 us
    pallas_call x4, Pallas kernels, run_add(): pl.pallas_call(functools.partial(add_kernel, plans), out_shape=[jax.Shape...  5.07 us
    all_gather x1, waiting for transfers between devices, body(): lax.all_gather(second, 'dp', axis=0, tiled=True, axis_index_groups=[ring....  5.04 us
  transfers between devices with their start and end apart: 32, of which 23 were waited for; matrix products, arithmetic and copies ran while one was open for 1% of the time, Pallas kernels for 19%

profile of v8, /device:TPU:0, one launch (start us, length us, event | category | flops | bytes accessed | tf_op | source)
XLA Modules:
  0.0 216.8 jit_solution(12932917372864610183)
XLA Ops:
  7.2 2.6 %pack.1 = (bf16[208,768]{1,0:T(8,128)(2,1)}, bf16[8,48,768]{2,1,0:T(8,128)(2,1)}) custom-call(f32[48,2304]{1,0:T(8,128)} %bitcast.44, f32[48,768]{1,0:T(8,128)} %bitcast.45, f32[48,3072]{1,0:T(8,128)} %bitcast.42, f32[192,768]{1,0:T(8,128)} %bitcast.43, f32[1,48]{1,0:T(1,128)} %refs_0_.1, f32[1,48]{1,0:T(1,128)} %refs_1_.1, f32[1,48]{1,0:T(1,128)} %refs_2_.1, ...), custom_call_target="tpu_custom_call" | custom-call | tf_op jit(solution)/shard_map/pack/pallas_call | solution.py:1098
  9.9 3.1 %collective-permute-start.1 = (bf16[208,768]{1,0:T(8,128)(2,1)}, bf16[208,768]{1,0:T(8,128)(2,1)S(1)}, u32[]{:S(2)}, u32[]{:S(2)}) collective-permute-start(bf16[208,768]{1,0:T(8,128)(2,1)} %get-tuple-element.76.refs_0_.refs_6_), channel_id=1, source_target_pairs={{0,4},{1,5},{4,8},{5,9},{8,12},{9,13},{12,14},{13,15},{14,10},{15,... | collective-permute-start | bytes 958472 | tf_op jit(solution)/shard_map/ppermute | solution.py:1034
  13.0 8.4 %collective-permute-done.1.refs_8_.refs_14_ = bf16[208,768]{1,0:T(8,128)(2,1)S(1)} collective-permute-done((bf16[208,768]{1,0:T(8,128)(2,1)}, bf16[208,768]{1,0:T(8,128)(2,1)S(1)}, u32[]{:S(2)}, u32[]{:S(2)}) %collective-permute-start.1) | collective-permute-done | bytes 319520 | tf_op jit(solution)/shard_map/ppermute | solution.py:1034
  21.4 2.2 %collective-permute-done.refs_1_.refs_7_ = bf16[208,768]{1,0:T(8,128)(2,1)S(1)} collective-permute-done((bf16[208,768]{1,0:T(8,128)(2,1)}, bf16[208,768]{1,0:T(8,128)(2,1)S(1)}, u32[]{:S(2)}, u32[]{:S(2)}) %collective-permute-start) | collective-permute-done | bytes 319520 | tf_op jit(solution)/shard_map/ppermute | solution.py:1034
  23.9 1.7 collective-permute-start.3
  25.7 14.1 %collective-permute-done.2.refs_2_.refs_8_ = bf16[208,768]{1,0:T(8,128)(2,1)S(1)} collective-permute-done((bf16[208,768]{1,0:T(8,128)(2,1)S(1)}, bf16[208,768]{1,0:T(8,128)(2,1)S(1)}, u32[]{:S(2)}, u32[]{:S(2)}) %collective-permute-start.2) | collective-permute-done | bytes 319520 | tf_op jit(solution)/shard_map/ppermute | solution.py:1034
  39.9 1.5 collective-permute-start.4
  42.5 13.3 %collective-permute-done.4.refs_3_.refs_9_ = bf16[208,768]{1,0:T(8,128)(2,1)S(1)} collective-permute-done((bf16[208,768]{1,0:T(8,128)(2,1)S(1)}, bf16[208,768]{1,0:T(8,128)(2,1)S(1)}, u32[]{:S(2)}, u32[]{:S(2)}) %collective-permute-start.4) | collective-permute-done | bytes 319520 | tf_op jit(solution)/shard_map/ppermute | solution.py:1034
  55.7 1.4 collective-permute-done.5.refs_6_.refs_12_
  57.8 1.6 collective-permute-start.7
  62.1 7.4 %collective-permute-done.6.refs_4_.refs_10_ = bf16[96,768]{1,0:T(8,128)(2,1)} collective-permute-done((bf16[96,768]{1,0:T(8,128)(2,1)}, bf16[96,768]{1,0:T(8,128)(2,1)}, u32[]{:S(2)}, u32[]{:S(2)}) %collective-permute-start.6) | collective-permute-done | bytes 147488 | tf_op jit(solution)/shard_map/ppermute | solution.py:1034
  70.2 1.1 collective-permute-done.12.refs_13_.refs_19_
  72.1 2.9 %vectors.1.vec = f32[16,768]{1,0:T(8,128)S(1)} custom-call(s32[16]{0:T(128)S(1)} %pad_add_fusion.devs, s32[2]{0:T(128)S(1)} %bitcast.35, bf16[208,768]{1,0:T(8,128)(2,1)} %get-tuple-element.76.refs_0_.refs_6_, bf16[208,768]{1,0:T(8,128)(2,1)} %copy-done.7, bf16[208,768]{1,0:T(8,128)(2,1)} %copy-done.8, bf16[208,768]{1,0:T(8,128)(2,1)} %copy-done.4, ...), custom_call_target="tpu_custom_call" | custom-call | flops 56623104 | bytes 2359296 | tf_op jit(solution)/shard_map/vectors/pallas_call | solution.py:747
  75.0 5.5 %attend.1 = (f32[192,768]{1,0:T(8,128)S(1)}, bf16[192,768]{1,0:T(8,128)(2,1)S(1)}) custom-call(s32[2]{0:T(128)S(1)} %bitcast.33, s32[1]{0:T(128)} %bitcast.flag, s32[16]{0:T(128)S(1)} %pad_add_fusion.devs, bf16[192,768]{1,0:T(8,128)(2,1)S(1)} %bitcast.31, f32[16,768]{1,0:T(8,128)S(1)} %vectors.1.vec, bf16[208,768]{1,0:T(8,128)(2,1)} %get-tuple-element.76.refs_0_.refs_6_, ...), custom_call_target="tpu_custom_call" | custom-call | flops 905969664 | bytes 4718592 | tf_op jit(solution)/shard_map/attend/pallas_call | solution.py:747
  80.5 5.0 %all-gather.2.cloned.1.call-done = bf16[128,48,768]{2,1,0:T(8,128)(2,1)} async-done(((bf16[8,48,768]{2,1,0:T(8,128)(2,1)}), bf16[128,48,768]{2,1,0:T(8,128)(2,1)}) %all-gather.2.cloned.1.call-update) | async-done | bytes 9437200 | tf_op jit(solution)/shard_map/all_gather | solution.py:1107
  85.6 5.1 %mlp.1.after = bf16[192,768]{1,0:T(8,128)(2,1)S(1)} custom-call(s32[1]{0:T(128)} %bitcast.flag, f32[192,768]{1,0:T(8,128)S(1)} %get-tuple-element.83.middle_ref, bf16[192,768]{1,0:T(8,128)(2,1)S(1)} %get-tuple-element.84.hidden_ref, f32[16,768]{1,0:T(8,128)S(1)} %vectors.1.vec, bf16[16,8,48,768]{3,2,1,0:T(8,128)(2,1)} %bitcast.37), custom_call_target="tpu_custom_call" | custom-call | flops 1811939328 | bytes 9437184 | tf_op jit(solution)/shard_map/mlp/pallas_call | solution.py:747
  90.7 1.3 collective-permute-start.17
  92.0 5.6 %load.1 = (bf16[4,16,48,768]{3,2,1,0:T(8,128)(2,1)S(1)}, bf16[8,16,48,768]{3,2,1,0:T(8,128)(2,1)S(1)}, f32[192,3072]{1,0:T(8,128)S(1)}, bf16[8,768,768]{2,1,0:T(8,128)(2,1)S(1)}) custom-call(s32[16]{0:T(128)S(1)} %pad_add_fusion.devs, s32[1]{0:T(128)} %bitcast.flag, bf16[192,768]{1,0:T(8,128)(2,1)S(1)} %mlp.1.after, bf16[192,768]{1,0:T(8,128)(2,1)S(1)} %bitcast.27, ...), custom_call_target="tpu_custom_call" | custom-call | flops 905969664 | bytes 28311552 | tf_op jit(solution)/shard_map/load/pallas_call | solution.py:747
  97.6 1.3 collective-permute-done.17.recv_ref
  99.0 6.4 %chain.1 = (bf16[96,768]{1,0:T(8,128)(2,1)S(1)}, bf16[192,768]{1,0:T(8,128)(2,1)S(1)}, bf16[192,3072]{1,0:T(8,128)(2,1)S(1)}, f32[192,3072]{1,0:T(8,128)S(1)}, b...) custom-call(s32[2]{0:T(128)S(1)} %bitcast.34, ...), custom_call_target="tpu_custom_call" | custom-call | flops 4529848320 | bytes 7077888 | tf_op jit(solution)/shard_map/chain/pallas_call | solution.py:747
  105.3 1.3 collective-permute-start.18
  106.6 1.5 collective-permute-start.19
  108.2 1.8 output.1.beside
  110.0 6.5 %collective-permute-done.18.some_ref = bf16[96,768]{1,0:T(8,128)(2,1)S(1)} collective-permute-done((bf16[96,768]{1,0:T(8,128)(2,1)S(1)}, bf16[96,768]{1,0:T(8,128)(2,1)S(1)}, u32[]{:S(2)}, u32[]{:S(2)}) %collective-permute-start.18) | collective-permute-done | bytes 147488 | tf_op jit(solution)/shard_map/ppermute | solution.py:1006
  116.5 4.0 %collective-permute-done.19.other_ref = bf16[96,768]{1,0:T(8,128)(2,1)S(1)} collective-permute-done((bf16[96,768]{1,0:T(8,128)(2,1)S(1)}, bf16[96,768]{1,0:T(8,128)(2,1)S(1)}, u32[]{:S(2)}, u32[]{:S(2)}) %collective-permute-start.19) | collective-permute-done | bytes 147488 | tf_op jit(solution)/shard_map/ppermute | solution.py:1006
  120.5 5.7 %mlp_back.1 = (bf16[192,3072]{1,0:T(8,128)(2,1)}, f32[16,768]{1,0:T(8,128)S(1)}, bf16[16,8,48,768]{3,2,1,0:T(8,128)(2,1)}) custom-call(s32[1]{0:T(128)} %bitcast.flag, bf16[192,768]{1,0:T(8,128)(2,1)} %output.1.beside, bf16[96,768]{1,0:T(8,128)(2,1)S(1)} %collective-permute-done.18.some_ref, bf16[96,768]{1,0:T(8,128)(2,1)S(1)} %collective-permute-done.19.other_ref, ...), custom_call_target="tpu_custom_call" | custom-call | flops 3623878656 | bytes 9437184 | tf_op jit(solution)/shard_map/mlp_back/pallas_call | solution.py:747
  126.3 18.7 %rest.1 = (f32[192,768]{1,0:T(8,128)}, f32[16,768]{1,0:T(8,128)}, bf16[8,208,768]{2,1,0:T(8,128)(2,1)}, bf16[8,208,768]{2,1,0:T(8,128)(2,1)}, bf16[1,208,768]{2,1,0:T(8,128)(2,1)}) custom-call(s32[1]{0:T(128)} %bitcast.flag, s32[16]{0:T(128)S(1)} %pad_add_fusion.devs, s32[2]{0:T(128)S(1)} %bitcast.36, bf16[96,768]{1,0:T(8,128)(2,1)S(1)} %collective-permute-done.18.some_ref, ...), custom_call_target="tpu_custom_call" | custom-call | flops 2717908992 | bytes 14155776 | tf_op jit(solution)/shard_map/rest/pallas_call | solution.py:747
  145.1 1.8 collective-permute-done.20.refs_1_.refs_3_
  147.0 1.2 add.77
  148.3 1.9 collective-permute-start.22
  150.3 6.0 %collective-permute-done.22.refs_2_ = bf16[96,768]{1,0:T(8,128)(2,1)S(1)} collective-permute-done((bf16[96,768]{1,0:T(8,128)(2,1)S(1)}, bf16[96,768]{1,0:T(8,128)(2,1)S(1)}, u32[]{:S(2)}, u32[]{:S(2)}) %collective-permute-start.22) | collective-permute-done | bytes 147488 | tf_op jit(solution)/shard_map/ppermute | solution.py:1034
  156.2 0.8 collective-permute-done.23.refs_5_
  157.1 1.3 add.78
  158.3 1.3 collective-permute-start.24
  159.6 0.8 collective-permute-start.25
  160.4 11.2 %collective-permute-done.24.refs_2_ = bf16[208,768]{1,0:T(8,128)(2,1)S(1)} collective-permute-done((bf16[208,768]{1,0:T(8,128)(2,1)S(1)}, bf16[208,768]{1,0:T(8,128)(2,1)S(1)}, u32[]{:S(2)}, u32[]{:S(2)}) %collective-permute-start.24) | collective-permute-done | bytes 319520 | tf_op jit(solution)/shard_map/ppermute | solution.py:1034
  171.7 1.1 collective-permute-done.25.refs_5_
  172.7 1.3 add.79
  174.1 1.8 collective-permute-start.26
  176.1 10.7 %collective-permute-done.26.refs_2_ = bf16[208,768]{1,0:T(8,128)(2,1)S(1)} collective-permute-done((bf16[208,768]{1,0:T(8,128)(2,1)S(1)}, bf16[208,768]{1,0:T(8,128)(2,1)S(1)}, u32[]{:S(2)}, u32[]{:S(2)}) %collective-permute-start.26) | collective-permute-done | bytes 319520 | tf_op jit(solution)/shard_map/ppermute | solution.py:1034
  186.8 1.6 collective-permute-done.27.refs_5_
  188.4 1.3 add.80
  189.8 1.7 collective-permute-start.28
  191.8 10.0 %collective-permute-done.28.ahead = bf16[208,768]{1,0:T(8,128)(2,1)S(1)} collective-permute-done((bf16[208,768]{1,0:T(8,128)(2,1)S(1)}, bf16[208,768]{1,0:T(8,128)(2,1)S(1)}, u32[]{:S(2)}, u32[]{:S(2)}) %collective-permute-start.28) | collective-permute-done | bytes 319520 | tf_op jit(solution)/shard_map/ppermute | solution.py:1034
  201.9 1.6 collective-permute-done.29.behind
  203.5 2.0 total.1
  205.5 2.3 %reduce-scatter.2.cloned.1.call-done.grads_ref = bf16[8,48,768]{2,1,0:T(8,128)(2,1)} async-done(((bf16[128,48,768]{2,1,0:T(8,128)(2,1)}), bf16[8,48,768]{2,1,0:T(8,128)(2,1)}) %reduce-scatter.2.cloned.1.call-update) | async-done | bytes 589840 | tf_op jit(solution)/shard_map/reduce_scatter | solution.py:1163
  207.8 2.1 unpack.1
  (72 shorter events, 7.3 us)
Async XLA Ops:
  7.2 64.9 %copy-start.3 = (s32[2,1]{0,1:T(1,128)S(1)}, s32[2,1]{0,1:T(1,128)}, u32[]{:S(2)}) copy-start(s32[2,1]{0,1:T(1,128)} %param.21) | copy-start | bytes 28
  7.2 78.4 %all-gather.2.cloned.1.call-start = ((), (), s32[]{:S(2)}) async-start(), calls=%async_computation.1 | async-start | bytes 10027008 | tf_op jit(solution)/shard_map/all_gather | solution.py:1107
  9.9 197.9 %reduce-scatter.2.cloned.1.call-start = ((), (), s32[]{:S(2)}) async-start(), calls=%async_computation.2 | async-start | bytes 10027008 | tf_op jit(solution)/shard_map/reduce_scatter | solution.py:1163
  9.9 11.5 %collective-permute-start.1 = (bf16[208,768]{1,0:T(8,128)(2,1)}, bf16[208,768]{1,0:T(8,128)(2,1)S(1)}, u32[]{:S(2)}, u32[]{:S(2)}) collective-permute-start(bf16[208,768]{1,0:T(8,128)(2,1)} %get-tuple-element.76.refs_0_.refs_6_), channel_id=1, source_target_pairs={{0,4},{1,5},{4,8},{5,9},{8,12},{9,13},{12,14},{13,15},{14,10},{15,... | collective-permute-start | bytes 958472 | tf_op jit(solution)/shard_map/ppermute | solution.py:1034
  13.0 10.6 %collective-permute-start = (bf16[208,768]{1,0:T(8,128)(2,1)}, bf16[208,768]{1,0:T(8,128)(2,1)S(1)}, u32[]{:S(2)}, u32[]{:S(2)}) collective-permute-start(bf16[208,768]{1,0:T(8,128)(2,1)} %get-tuple-element.76.refs_0_.refs_6_), channel_id=1, source_target_pairs={{4,0},{5,1},{8,4},{9,5},{12,8},{13,9},{14,12},{15,13},{10,14},{11,... | collective-permute-start | bytes 958472 | tf_op jit(solution)/shard_map/ppermute | solution.py:1034
  21.4 50.6 %copy-start.6 = (bf16[208,768]{1,0:T(8,128)(2,1)}, bf16[208,768]{1,0:T(8,128)(2,1)S(1)}, u32[]{:S(2)}) copy-start(bf16[208,768]{1,0:T(8,128)(2,1)S(1)} %collective-permute-done.1.refs_8_.refs_14_) | copy-start | bytes 958468
  23.6 48.4 %copy-start.7 = (bf16[208,768]{1,0:T(8,128)(2,1)}, bf16[208,768]{1,0:T(8,128)(2,1)S(1)}, u32[]{:S(2)}) copy-start(bf16[208,768]{1,0:T(8,128)(2,1)S(1)} %collective-permute-done.refs_1_.refs_7_) | copy-start | bytes 958468
  23.6 16.2 %collective-permute-start.2 = (bf16[208,768]{1,0:T(8,128)(2,1)S(1)}, bf16[208,768]{1,0:T(8,128)(2,1)S(1)}, u32[]{:S(2)}, u32[]{:S(2)}) collective-permute-start(bf16[208,768]{1,0:T(8,128)(2,1)S(1)} %collective-permute-done.refs_1_.refs_7_), channel_id=1, source_target_pairs={{4,0},{5,1},{8,4},{9,5},{12,8},{13,9},{14,12},{15,13},{10,14},{11,... | collective-permute-start | bytes 958472 | tf_op jit(solution)/shard_map/ppermute | solution.py:1034
  23.9 16.0 %collective-permute-start.3 = (bf16[208,768]{1,0:T(8,128)(2,1)S(1)}, bf16[208,768]{1,0:T(8,128)(2,1)S(1)}, u32[]{:S(2)}, u32[]{:S(2)}) collective-permute-start(bf16[208,768]{1,0:T(8,128)(2,1)S(1)} %collective-permute-done.1.refs_8_.refs_14_), channel_id=1, source_target_pairs={{0,4},{1,5},{4,8},{5,9},{8,12},{9,13},{12,14},{13,15},{14,10},{15,... | collective-permute-start | bytes 958472 | tf_op jit(solution)/shard_map/ppermute | solution.py:1034
  39.8 32.2 %copy-start.8 = (bf16[208,768]{1,0:T(8,128)(2,1)}, bf16[208,768]{1,0:T(8,128)(2,1)S(1)}, u32[]{:S(2)}) copy-start(bf16[208,768]{1,0:T(8,128)(2,1)S(1)} %collective-permute-done.2.refs_2_.refs_8_) | copy-start | bytes 958468
  39.9 32.1 %copy-start.9 = (bf16[208,768]{1,0:T(8,128)(2,1)}, bf16[208,768]{1,0:T(8,128)(2,1)S(1)}, u32[]{:S(2)}) copy-start(bf16[208,768]{1,0:T(8,128)(2,1)S(1)} %collective-permute-done.3.refs_7_.refs_13_) | copy-start | bytes 958468
  39.9 15.8 %collective-permute-start.4 = (bf16[208,768]{1,0:T(8,128)(2,1)S(1)}, bf16[208,768]{1,0:T(8,128)(2,1)S(1)}, u32[]{:S(2)}, u32[]{:S(2)}) collective-permute-start(bf16[208,768]{1,0:T(8,128)(2,1)S(1)} %collective-permute-done.2.refs_2_.refs_8_), channel_id=1, source_target_pairs={{4,0},{5,1},{8,4},{9,5},{12,8},{13,9},{14,12},{15,13},{10,14},{11,... | collective-permute-start | bytes 958472 | tf_op jit(solution)/shard_map/ppermute | solution.py:1034
  41.5 15.6 %collective-permute-start.5 = (bf16[208,768]{1,0:T(8,128)(2,1)S(1)}, bf16[208,768]{1,0:T(8,128)(2,1)S(1)}, u32[]{:S(2)}, u32[]{:S(2)}) collective-permute-start(bf16[208,768]{1,0:T(8,128)(2,1)S(1)} %collective-permute-done.3.refs_7_.refs_13_), channel_id=1, source_target_pairs={{0,4},{1,5},{4,8},{5,9},{8,12},{9,13},{12,14},{13,15},{14,10},{15,... | collective-permute-start | bytes 958472 | tf_op jit(solution)/shard_map/ppermute | solution.py:1034
  41.9 18.2 %collective-permute-start.8 = (bf16[208,768]{1,0:T(8,128)(2,1)}, bf16[208,768]{1,0:T(8,128)(2,1)S(1)}, u32[]{:S(2)}, u32[]{:S(2)}) collective-permute-start(bf16[208,768]{1,0:T(8,128)(2,1)} %get-tuple-element.76.refs_0_.refs_6_), channel_id=1, source_target_pairs={{0,1},{1,0},{2,3},{3,2},{4,5},{5,4},{6,7},{7,6},{8,9},{9,8},{10,11... | collective-permute-start | bytes 958472 | tf_op jit(solution)/shard_map/ppermute | solution.py:1048
  41.9 18.6 %collective-permute-start.16 = (bf16[208,768]{1,0:T(8,128)(2,1)S(1)}, bf16[208,768]{1,0:T(8,128)(2,1)S(1)}, u32[]{:S(2)}, u32[]{:S(2)}) collective-permute-start(bf16[208,768]{1,0:T(8,128)(2,1)S(1)} %collective-permute-done.1.refs_8_.refs_14_), channel_id=1, source_target_pairs={{0,1},{1,0},{2,3},{3,2},{4,5},{5,4},{6,7},{7,6},{8,9},{9,8},{10,11... | collective-permute-start | bytes 958472 | tf_op jit(solution)/shard_map/ppermute | solution.py:1048
  42.4 18.1 %collective-permute-start.9 = (bf16[208,768]{1,0:T(8,128)(2,1)S(1)}, bf16[208,768]{1,0:T(8,128)(2,1)S(1)}, u32[]{:S(2)}, u32[]{:S(2)}) collective-permute-start(bf16[208,768]{1,0:T(8,128)(2,1)S(1)} %collective-permute-done.refs_1_.refs_7_), channel_id=1, source_target_pairs={{0,1},{1,0},{2,3},{3,2},{4,5},{5,4},{6,7},{7,6},{8,9},{9,8},{10,11... | collective-permute-start | bytes 958472 | tf_op jit(solution)/shard_map/ppermute | solution.py:1048
  55.7 16.3 %copy-start.4 = (bf16[208,768]{1,0:T(8,128)(2,1)}, bf16[208,768]{1,0:T(8,128)(2,1)S(1)}, u32[]{:S(2)}) copy-start(bf16[208,768]{1,0:T(8,128)(2,1)S(1)} %collective-permute-done.4.refs_3_.refs_9_) | copy-start | bytes 958468
  55.7 5.3 %collective-permute-start.10 = (bf16[208,768]{1,0:T(8,128)(2,1)S(1)}, bf16[208,768]{1,0:T(8,128)(2,1)S(1)}, u32[]{:S(2)}, u32[]{:S(2)}) collective-permute-start(bf16[208,768]{1,0:T(8,128)(2,1)S(1)} %collective-permute-done.2.refs_2_.refs_8_), channel_id=1, source_target_pairs={{0,1},{1,0},{2,3},{3,2},{4,5},{5,4},{6,7},{7,6},{8,9},{9,8},{10,11... | collective-permute-start | bytes 958472 | tf_op jit(solution)/shard_map/ppermute | solution.py:1048
  57.1 14.9 %copy-start.5 = (bf16[208,768]{1,0:T(8,128)(2,1)}, bf16[208,768]{1,0:T(8,128)(2,1)S(1)}, u32[]{:S(2)}) copy-start(bf16[208,768]{1,0:T(8,128)(2,1)S(1)} %collective-permute-done.5.refs_6_.refs_12_) | copy-start | bytes 958468
  57.8 11.7 %collective-permute-start.7 = (bf16[112,768]{1,0:T(8,128)(2,1)}, bf16[112,768]{1,0:T(8,128)(2,1)S(1)}, u32[]{:S(2)}, u32[]{:S(2)}) collective-permute-start(bf16[112,768]{1,0:T(8,128)(2,1)} %slice.7), channel_id=1, source_target_pairs={{4,0},{5,1},{8,4},{9,5},{12,8},{13,9},{14,12},{15,13},{10,14},{11,... | collective-permute-start | bytes 516104 | tf_op jit(solution)/shard_map/ppermute | solution.py:1034
  60.1 11.9 %copy-start.10 = (bf16[208,768]{1,0:T(8,128)(2,1)}, bf16[208,768]{1,0:T(8,128)(2,1)S(1)}, u32[]{:S(2)}) copy-start(bf16[208,768]{1,0:T(8,128)(2,1)S(1)} %collective-permute-done.8.refs_9_.refs_15_) | copy-start | bytes 958468
  60.1 9.4 %collective-permute-start.6 = (bf16[96,768]{1,0:T(8,128)(2,1)}, bf16[96,768]{1,0:T(8,128)(2,1)}, u32[]{:S(2)}, u32[]{:S(2)}) collective-permute-start(bf16[96,768]{1,0:T(8,128)(2,1)} %slice.6), channel_id=1, source_target_pairs={{0,4},{1,5},{4,8},{5,9},{8,12},{9,13},{12,14},{13,15},{14,10},{15,... | collective-permute-start | bytes 442376 | tf_op jit(solution)/shard_map/ppermute | solution.py:1034
  60.5 11.5 %copy-start.11 = (bf16[208,768]{1,0:T(8,128)(2,1)}, bf16[208,768]{1,0:T(8,128)(2,1)S(1)}, u32[]{:S(2)}) copy-start(bf16[208,768]{1,0:T(8,128)(2,1)S(1)} %collective-permute-done.16.refs_17_.refs_23_) | copy-start | bytes 958468
  60.5 9.6 %collective-permute-start.15 = (bf16[208,768]{1,0:T(8,128)(2,1)S(1)}, bf16[208,768]{1,0:T(8,128)(2,1)S(1)}, u32[]{:S(2)}, u32[]{:S(2)}) collective-permute-start(bf16[208,768]{1,0:T(8,128)(2,1)S(1)} %collective-permute-done.3.refs_7_.refs_13_), channel_id=1, source_target_pairs={{0,1},{1,0},{2,3},{3,2},{4,5},{5,4},{6,7},{7,6},{8,9},{9,8},{10,11... | collective-permute-start | bytes 958472 | tf_op jit(solution)/shard_map/ppermute | solution.py:1048
  60.6 0.8 copy-start.12
  60.6 10.7 %collective-permute-start.11 = (bf16[208,768]{1,0:T(8,128)(2,1)S(1)}, bf16[208,768]{1,0:T(8,128)(2,1)S(1)}, u32[]{:S(2)}, u32[]{:S(2)}) collective-permute-start(bf16[208,768]{1,0:T(8,128)(2,1)S(1)} %collective-permute-done.4.refs_3_.refs_9_), channel_id=1, source_target_pairs={{0,1},{1,0},{2,3},{3,2},{4,5},{5,4},{6,7},{7,6},{8,9},{9,8},{10,11... | collective-permute-start | bytes 958472 | tf_op jit(solution)/shard_map/ppermute | solution.py:1048
  61.4 0.7 copy-start.13
  61.4 9.9 %collective-permute-start.14 = (bf16[208,768]{1,0:T(8,128)(2,1)S(1)}, bf16[208,768]{1,0:T(8,128)(2,1)}, u32[]{:S(2)}, u32[]{:S(2)}) collective-permute-start(bf16[208,768]{1,0:T(8,128)(2,1)S(1)} %collective-permute-done.5.refs_6_.refs_12_), channel_id=1, source_target_pairs={{0,1},{1,0},{2,3},{3,2},{4,5},{5,4},{6,7},{7,6},{8,9},{9,8},{10,11... | collective-permute-start | bytes 958472 | tf_op jit(solution)/shard_map/ppermute | solution.py:1048
  69.5 1.7 collective-permute-start.12
  69.5 2.5 %copy-start.16 = (bf16[112,768]{1,0:T(8,128)(2,1)}, bf16[112,768]{1,0:T(8,128)(2,1)S(1)}, u32[]{:S(2)}) copy-start(bf16[112,768]{1,0:T(8,128)(2,1)S(1)} %collective-permute-done.7.refs_5_.refs_11_) | copy-start | bytes 516100
  69.6 1.9 collective-permute-start.13
  70.2 1.3 copy-start.14
  72.1 2.9 %copy-start.1 = (bf16[2,1,96,768]{3,2,1,0:T(8,128)(2,1)S(1)}, bf16[2,1,96,768]{3,2,1,0:T(8,128)(2,1)}, u32[]{:S(2)}) copy-start(bf16[2,1,96,768]{3,2,1,0:T(8,128)(2,1)} %param.18) | copy-start | bytes 884740
  72.1 2.9 %copy-start.2 = (s32[2,1]{0,1:T(1,128)S(1)}, s32[2,1]{0,1:T(1,128)}, u32[]{:S(2)}) copy-start(s32[2,1]{0,1:T(1,128)} %param.20) | copy-start | bytes 28
  85.6 6.4 %copy-start = (bf16[2,1,96,768]{3,2,1,0:T(8,128)(2,1)S(1)}, bf16[2,1,96,768]{3,2,1,0:T(8,128)(2,1)}, u32[]{:S(2)}) copy-start(bf16[2,1,96,768]{3,2,1,0:T(8,128)(2,1)} %param.19) | copy-start | bytes 884740
  90.7 8.2 %collective-permute-start.17 = (bf16[192,768]{1,0:T(8,128)(2,1)S(1)}, bf16[192,768]{1,0:T(8,128)(2,1)S(1)}, u32[]{:S(2)}, u32[]{:S(2)}) collective-permute-start(bf16[192,768]{1,0:T(8,128)(2,1)S(1)} %mlp.1.after), channel_id=1, source_target_pairs={{0,16},{1,17},{2,18},{3,19},{4,20},{5,21},{6,22},{7,23},{8,24},{9,... | collective-permute-start | bytes 884744 | tf_op jit(solution)/shard_map/ppermute | solution.py:1006
  105.3 11.2 %collective-permute-start.18 = (bf16[96,768]{1,0:T(8,128)(2,1)S(1)}, bf16[96,768]{1,0:T(8,128)(2,1)S(1)}, u32[]{:S(2)}, u32[]{:S(2)}) collective-permute-start(bf16[96,768]{1,0:T(8,128)(2,1)S(1)} %get-tuple-element.92), channel_id=1, source_target_pairs={{16,0},{17,1},{18,2},{19,3},{20,4},{21,5},{22,6},{23,7},{24,8},{25... | collective-permute-start | bytes 442376 | tf_op jit(solution)/shard_map/ppermute | solution.py:1006
  106.6 13.9 %collective-permute-start.19 = (bf16[96,768]{1,0:T(8,128)(2,1)S(1)}, bf16[96,768]{1,0:T(8,128)(2,1)S(1)}, u32[]{:S(2)}, u32[]{:S(2)}) collective-permute-start(bf16[96,768]{1,0:T(8,128)(2,1)S(1)} %chain_end.1), channel_id=1, source_target_pairs={{16,0},{17,1},{18,2},{19,3},{20,4},{21,5},{22,6},{23,7},{24,8},{25... | collective-permute-start | bytes 442376 | tf_op jit(solution)/shard_map/ppermute | solution.py:1006
  145.0 1.9 collective-permute-start.20
  146.9 10.2 %collective-permute-start.21 = (bf16[8,208,768]{2,1,0:T(8,128)(2,1)}, bf16[8,208,768]{2,1,0:T(8,128)(2,1)S(1)}, u32[]{:S(2)}, u32[]{:S(2)}) collective-permute-start(bf16[8,208,768]{2,1,0:T(8,128)(2,1)} %get-tuple-element.112), channel_id=1, source_target_pairs={{0,1},{1,0},{2,3},{3,2},{4,5},{5,4},{6,7},{7,6},{8,9},{9,8},{10,11... | collective-permute-start | bytes 7667720 | tf_op jit(solution)/shard_map/ppermute | solution.py:1048
  148.2 8.9 %collective-permute-start.23 = (bf16[112,768]{1,0:T(8,128)(2,1)S(1)}, bf16[112,768]{1,0:T(8,128)(2,1)S(1)}, u32[]{:S(2)}, u32[]{:S(2)}) collective-permute-start(bf16[112,768]{1,0:T(8,128)(2,1)S(1)} %get-tuple-element.114), channel_id=1, source_target_pairs={{4,0},{5,1},{8,4},{9,5},{12,8},{13,9},{14,12},{15,13},{10,14},{11,... | collective-permute-start | bytes 516104 | tf_op jit(solution)/shard_map/ppermute | solution.py:1034
  148.3 7.9 %collective-permute-start.22 = (bf16[96,768]{1,0:T(8,128)(2,1)S(1)}, bf16[96,768]{1,0:T(8,128)(2,1)S(1)}, u32[]{:S(2)}, u32[]{:S(2)}) collective-permute-start(bf16[96,768]{1,0:T(8,128)(2,1)S(1)} %get-tuple-element.113), channel_id=1, source_target_pairs={{0,4},{1,5},{4,8},{5,9},{8,12},{9,13},{12,14},{13,15},{14,10},{15,... | collective-permute-start | bytes 442376 | tf_op jit(solution)/shard_map/ppermute | solution.py:1034
  158.3 13.3 %collective-permute-start.24 = (bf16[208,768]{1,0:T(8,128)(2,1)S(1)}, bf16[208,768]{1,0:T(8,128)(2,1)S(1)}, u32[]{:S(2)}, u32[]{:S(2)}) collective-permute-start(bf16[208,768]{1,0:T(8,128)(2,1)S(1)} %get-tuple-element.115), channel_id=1, source_target_pairs={{0,4},{1,5},{4,8},{5,9},{8,12},{9,13},{12,14},{13,15},{14,10},{15,... | collective-permute-start | bytes 958472 | tf_op jit(solution)/shard_map/ppermute | solution.py:1034
  159.6 13.1 %collective-permute-start.25 = (bf16[208,768]{1,0:T(8,128)(2,1)S(1)}, bf16[208,768]{1,0:T(8,128)(2,1)S(1)}, u32[]{:S(2)}, u32[]{:S(2)}) collective-permute-start(bf16[208,768]{1,0:T(8,128)(2,1)S(1)} %get-tuple-element.116), channel_id=1, source_target_pairs={{4,0},{5,1},{8,4},{9,5},{12,8},{13,9},{14,12},{15,13},{10,14},{11,... | collective-permute-start | bytes 958472 | tf_op jit(solution)/shard_map/ppermute | solution.py:1034
  174.1 12.8 %collective-permute-start.26 = (bf16[208,768]{1,0:T(8,128)(2,1)S(1)}, bf16[208,768]{1,0:T(8,128)(2,1)S(1)}, u32[]{:S(2)}, u32[]{:S(2)}) collective-permute-start(bf16[208,768]{1,0:T(8,128)(2,1)S(1)} %get-tuple-element.117), channel_id=1, source_target_pairs={{0,4},{1,5},{4,8},{5,9},{8,12},{9,13},{12,14},{13,15},{14,10},{15,... | collective-permute-start | bytes 958472 | tf_op jit(solution)/shard_map/ppermute | solution.py:1034
  175.9 12.6 %collective-permute-start.27 = (bf16[208,768]{1,0:T(8,128)(2,1)S(1)}, bf16[208,768]{1,0:T(8,128)(2,1)S(1)}, u32[]{:S(2)}, u32[]{:S(2)}) collective-permute-start(bf16[208,768]{1,0:T(8,128)(2,1)S(1)} %get-tuple-element.118), channel_id=1, source_target_pairs={{4,0},{5,1},{8,4},{9,5},{12,8},{13,9},{14,12},{15,13},{10,14},{11,... | collective-permute-start | bytes 958472 | tf_op jit(solution)/shard_map/ppermute | solution.py:1034
  189.8 12.1 %collective-permute-start.28 = (bf16[208,768]{1,0:T(8,128)(2,1)S(1)}, bf16[208,768]{1,0:T(8,128)(2,1)S(1)}, u32[]{:S(2)}, u32[]{:S(2)}) collective-permute-start(bf16[208,768]{1,0:T(8,128)(2,1)S(1)} %get-tuple-element.119), channel_id=1, source_target_pairs={{0,4},{1,5},{4,8},{5,9},{8,12},{9,13},{12,14},{13,15},{14,10},{15,... | collective-permute-start | bytes 958472 | tf_op jit(solution)/shard_map/ppermute | solution.py:1034
  191.4 12.1 %collective-permute-start.29 = (bf16[208,768]{1,0:T(8,128)(2,1)S(1)}, bf16[208,768]{1,0:T(8,128)(2,1)S(1)}, u32[]{:S(2)}, u32[]{:S(2)}) collective-permute-start(bf16[208,768]{1,0:T(8,128)(2,1)S(1)} %get-tuple-element.120), channel_id=1, source_target_pairs={{4,0},{5,1},{8,4},{9,5},{12,8},{13,9},{14,12},{15,13},{10,14},{11,... | collective-permute-start | bytes 958472 | tf_op jit(solution)/shard_map/ppermute | solution.py:1034
  (1 other events, 0.7 us)
Sparse Core Ops, SparseCore 0:
  10.2 75.3 all-gather.1
  126.4 81.3 reduce-scatter.1

commit v9 on v8

--- a/solution.py
+++ b/solution.py
@@ -400,7 +400,7 @@
 
 def mlp_back_kernel(
     plan, flag, beside, some_ref, other_ref, cot_ref, held2, hidden, act, slope,
-    grad_pre_out, small_ref, grads, grad_pre_ref, stage, stage_sems, pre_sem,
+    grad_pre_ref, small_ref, grads, stage, stage_sems,
 ):
     arrived = jnp.concatenate([some_ref[...], other_ref[...]], 0)
     branch = jnp.where(flag[0] == 0, arrived, cot_ref[...])
@@ -442,14 +442,11 @@
         grad_pre_ref[:, columns] = grad_pre
         out.put(mm_tn(act[:, columns], branch), copies_of_down(part))
         out.put(mm_tn(hidden[...], grad_pre), copies_of_up(part))
-    copy = pltpu.make_async_copy(grad_pre_ref, grad_pre_out, pre_sem.at[0])
-    copy.start()
     small_ref[...] = jnp.zeros_like(small_ref)
     small_ref[7:8, :] = column_sum(branch)
     for part in range(QUART):
         small_ref[8 + part : 9 + part, :] = column_sum(grad_pre_ref[:, columns_of(plan, part)])
     out.drain()
-    copy.wait()
 
 
 def slot_target(plan, grads, slot):
@@ -510,17 +507,15 @@
 
 
 def rest_kernel(
-    plan, many, flag, devs, lead, some_ref, other_ref, cot_ref, small_in, vec, gathered, grad_pre_in, *refs,
+    plan, many, flag, devs, lead, some_ref, other_ref, cot_ref, small_in, vec, grad_pre, gathered, *refs,
 ):
     count = plan.shards + (2 if plan.parts > 1 else 0)
     kept_in, pieces, refs = refs[:6], refs[6 : 6 + count], refs[6 + count :]
     dx_ref, small_ref = refs[:2]
     grads, refs = refs[2 : 2 + plan.parts], refs[2 + plan.parts :]
-    kept, (held2, grad_pre, up_sems, pre_sem), refs = refs[:6], refs[6:10], refs[10:]
+    kept, (held2, up_sems), refs = refs[:6], refs[6:8], refs[8:]
     held, grad_middle_ref, grad_attended, grad_rows, sems, kept_sems, stage, stage_sems, out_sem, stack, lines, packed = refs
     xin_ref, normed, qkv, attended, middle_ref, probs = kept
-    pre_copy = pltpu.make_async_copy(grad_pre_in, grad_pre, pre_sem.at[0])
-    pre_copy.start()
     for part in range(QUART):
         start_all(up_copies(plan, gathered, held2, up_sems.at[part], part))
     start_all(first_copies(plan, pieces, devs, held, sems.at[1], pl.ds(OUT, 1)))
@@ -536,7 +531,6 @@
     branch = jnp.where(flag[0] == 0, arrived, cot_ref[...])
     out = Stage(plan, stage, stage_sems)
     small_ref[...] = small_in[...]
-    pre_copy.wait()
     grad_hidden = None
     for part in range(QUART):
         wait_bytes(held2.at[part], up_sems.at[part])
@@ -907,13 +901,13 @@
     return call(
         functools.partial(mlp_back_kernel, plan),
         [
-            pltpu.HBM(*shapes[6]),
+            inside(shapes[6]),
             jax.ShapeDtypeStruct((16, plan.width), F32),
             pltpu.HBM((plan.shards, SECOND, plan.rows, plan.width), BF16),
         ],
         [SMEM, HBM] + [VMEM] * 7,
-        [HBM, VMEM, HBM],
-        [inside(shapes[6])] + stage_scratch(plan, SECOND) + [pltpu.SemaphoreType.DMA((1,))],
+        [VMEM, VMEM, HBM],
+        stage_scratch(plan, SECOND),
         "mlp_back",
         (2 * SECOND * block * plan.tokens, SECOND * block * 2),
         16,
@@ -931,11 +925,10 @@
     input_grad, small, *grads = call(
         functools.partial(rest_kernel, plan, many),
         [of(shapes[3]), jax.ShapeDtypeStruct((16, plan.width), F32)] + grad_shapes(plan),
-        [SMEM] * 3 + [VMEM] * 5 + [HBM] * (2 + len(rest) + len(pieces)),
+        [SMEM] * 3 + [VMEM] * 6 + [HBM] * (1 + len(rest) + len(pieces)),
         [VMEM] * 2 + [HBM] * plan.parts,
         [inside(shape) for shape in rest]
-        + [held_blocks(plan, QUART), inside(shapes[6])]
-        + [pltpu.SemaphoreType.DMA((QUART,)), pltpu.SemaphoreType.DMA((1,))]
+        + [held_blocks(plan, QUART), pltpu.SemaphoreType.DMA((QUART,))]
         + [held_blocks(plan, FIRST)]
         + [inside(shapes[index]) for index in (3, 0, 1)]
         + [pltpu.SemaphoreType.DMA((2,)), pltpu.SemaphoreType.DMA((len(rest),))]
@@ -945,7 +938,7 @@
         "rest",
         (3 * FIRST * block * plan.tokens, 3 * FIRST * block * 2),
         34,
-        (flag, devs, lead, *arriving, cot, small, vec, gathered, grad_pre, *kept, *pieces),
+        (flag, devs, lead, *arriving, cot, small, vec, grad_pre, gathered, *kept, *pieces),
     )
     return input_grad, small, grads
 

time: 217 us -> 217 us (level)
  waiting for transfers between devices: 112 us -> 115 us
  Pallas kernels: 63.6 us -> 61.2 us
    pallas_call x9, Pallas kernels: 51.8 us -> 49.3 us  [call(): pl.pallas_call(kernel, out_shape=outs, in_specs=in_specs, out_specs=out_s...]
    reduce_scatter x1, waiting for transfers between devices: 2.3 us -> 4.64 us  [body(): lax.psum_scatter(grads2.reshape(count * SECOND, rows, width), 'dp', scatt...]
  transfers between devices with their start and end apart: 32 -> 32, of which waited for: 23 -> 23; matrix products, arithmetic and copies ran while one was open for 1% -> 1% of each run, Pallas kernels for 19% -> 18%
where the time goes in v9:
time: 217 us
  waiting for transfers between devices  115 us (53%)
  Pallas kernels  61.2 us (28%)
  starting transfers between devices  23.9 us (11%)
  between operations  14.3 us (7%)
  local copies, waits for them, and re-layouts  2.5 us (1%)
    ppermute x8, waiting for transfers between devices, step(): lax.ppermute(ahead, 'dp', self.onward)  55.3 us
    pallas_call x9, Pallas kernels, call(): pl.pallas_call(kernel, out_shape=outs, in_specs=in_specs, out_specs=out_s...  49.3 us
    ppermute x8, waiting for transfers between devices, step(): lax.ppermute(behind, 'dp', self.back)  34.6 us
    ppermute x8, starting transfers between devices, step(): lax.ppermute(ahead, 'dp', self.onward)  12.2 us
    ppermute x3, waiting for transfers between devices, shifted(): lax.ppermute(value, axis, [(source, source + steps) for source in range(f...  11.9 us
    ppermute x8, starting transfers between devices, step(): lax.ppermute(behind, 'dp', self.back)  5.31 us
    pallas_call x4, Pallas kernels, run_add(): pl.pallas_call(functools.partial(add_kernel, plans), out_shape=[jax.Shape...  5.08 us
    all_gather x1, waiting for transfers between devices, body(): lax.all_gather(second, 'dp', axis=0, tiled=True, axis_index_groups=[ring....  5.02 us
  transfers between devices with their start and end apart: 32, of which 23 were waited for; matrix products, arithmetic and copies ran while one was open for 1% of the time, Pallas kernels for 18%

profile of v9, /device:TPU:0, one launch (start us, length us, event | category | flops | bytes accessed | tf_op | source)
XLA Modules:
  0.0 216.6 jit_solution(5035920397246126139)
XLA Ops:
  7.2 2.6 %pack.1 = (bf16[208,768]{1,0:T(8,128)(2,1)}, bf16[8,48,768]{2,1,0:T(8,128)(2,1)}) custom-call(f32[48,2304]{1,0:T(8,128)} %bitcast.44, f32[48,768]{1,0:T(8,128)} %bitcast.45, f32[48,3072]{1,0:T(8,128)} %bitcast.42, f32[192,768]{1,0:T(8,128)} %bitcast.43, f32[1,48]{1,0:T(1,128)} %refs_0_.1, f32[1,48]{1,0:T(1,128)} %refs_1_.1, f32[1,48]{1,0:T(1,128)} %refs_2_.1, ...), custom_call_target="tpu_custom_call" | custom-call | tf_op jit(solution)/shard_map/pack/pallas_call | solution.py:1091
  9.9 3.1 %collective-permute-start.1 = (bf16[208,768]{1,0:T(8,128)(2,1)}, bf16[208,768]{1,0:T(8,128)(2,1)S(1)}, u32[]{:S(2)}, u32[]{:S(2)}) collective-permute-start(bf16[208,768]{1,0:T(8,128)(2,1)} %get-tuple-element.76.refs_0_.refs_6_), channel_id=1, source_target_pairs={{0,4},{1,5},{4,8},{5,9},{8,12},{9,13},{12,14},{13,15},{14,10},{15,... | collective-permute-start | bytes 958472 | tf_op jit(solution)/shard_map/ppermute | solution.py:1027
  13.0 8.4 %collective-permute-done.1.refs_8_.refs_14_ = bf16[208,768]{1,0:T(8,128)(2,1)S(1)} collective-permute-done((bf16[208,768]{1,0:T(8,128)(2,1)}, bf16[208,768]{1,0:T(8,128)(2,1)S(1)}, u32[]{:S(2)}, u32[]{:S(2)}) %collective-permute-start.1) | collective-permute-done | bytes 319520 | tf_op jit(solution)/shard_map/ppermute | solution.py:1027
  21.4 2.2 %collective-permute-done.refs_1_.refs_7_ = bf16[208,768]{1,0:T(8,128)(2,1)S(1)} collective-permute-done((bf16[208,768]{1,0:T(8,128)(2,1)}, bf16[208,768]{1,0:T(8,128)(2,1)S(1)}, u32[]{:S(2)}, u32[]{:S(2)}) %collective-permute-start) | collective-permute-done | bytes 319520 | tf_op jit(solution)/shard_map/ppermute | solution.py:1027
  23.9 1.7 collective-permute-start.3
  25.7 14.1 %collective-permute-done.2.refs_2_.refs_8_ = bf16[208,768]{1,0:T(8,128)(2,1)S(1)} collective-permute-done((bf16[208,768]{1,0:T(8,128)(2,1)S(1)}, bf16[208,768]{1,0:T(8,128)(2,1)S(1)}, u32[]{:S(2)}, u32[]{:S(2)}) %collective-permute-start.2) | collective-permute-done | bytes 319520 | tf_op jit(solution)/shard_map/ppermute | solution.py:1027
  39.9 1.5 collective-permute-start.4
  42.5 13.3 %collective-permute-done.4.refs_3_.refs_9_ = bf16[208,768]{1,0:T(8,128)(2,1)S(1)} collective-permute-done((bf16[208,768]{1,0:T(8,128)(2,1)S(1)}, bf16[208,768]{1,0:T(8,128)(2,1)S(1)}, u32[]{:S(2)}, u32[]{:S(2)}) %collective-permute-start.4) | collective-permute-done | bytes 319520 | tf_op jit(solution)/shard_map/ppermute | solution.py:1027
  55.7 1.4 collective-permute-done.5.refs_6_.refs_12_
  57.1 0.7 slice.7
  57.8 1.6 collective-permute-start.7
  59.5 0.7 slice.6
  62.1 7.5 %collective-permute-done.6.refs_4_.refs_10_ = bf16[96,768]{1,0:T(8,128)(2,1)} collective-permute-done((bf16[96,768]{1,0:T(8,128)(2,1)}, bf16[96,768]{1,0:T(8,128)(2,1)}, u32[]{:S(2)}, u32[]{:S(2)}) %collective-permute-start.6) | collective-permute-done | bytes 147488 | tf_op jit(solution)/shard_map/ppermute | solution.py:1027
  70.2 1.1 collective-permute-done.12.refs_13_.refs_19_
  72.1 2.9 %vectors.1.vec = f32[16,768]{1,0:T(8,128)S(1)} custom-call(s32[16]{0:T(128)S(1)} %pad_add_fusion.devs, s32[2]{0:T(128)S(1)} %bitcast.35, bf16[208,768]{1,0:T(8,128)(2,1)} %get-tuple-element.76.refs_0_.refs_6_, bf16[208,768]{1,0:T(8,128)(2,1)} %copy-done.7, bf16[208,768]{1,0:T(8,128)(2,1)} %copy-done.8, bf16[208,768]{1,0:T(8,128)(2,1)} %copy-done.4, ...), custom_call_target="tpu_custom_call" | custom-call | flops 56623104 | bytes 2359296 | tf_op jit(solution)/shard_map/vectors/pallas_call | solution.py:741
  75.0 5.5 %attend.1 = (f32[192,768]{1,0:T(8,128)S(1)}, bf16[192,768]{1,0:T(8,128)(2,1)S(1)}) custom-call(s32[2]{0:T(128)S(1)} %bitcast.33, s32[1]{0:T(128)} %bitcast.flag, s32[16]{0:T(128)S(1)} %pad_add_fusion.devs, bf16[192,768]{1,0:T(8,128)(2,1)S(1)} %bitcast.31, f32[16,768]{1,0:T(8,128)S(1)} %vectors.1.vec, bf16[208,768]{1,0:T(8,128)(2,1)} %get-tuple-element.76.refs_0_.refs_6_, ...), custom_call_target="tpu_custom_call" | custom-call | flops 905969664 | bytes 4718592 | tf_op jit(solution)/shard_map/attend/pallas_call | solution.py:741
  80.6 5.0 %all-gather.2.cloned.1.call-done = bf16[128,48,768]{2,1,0:T(8,128)(2,1)} async-done(((bf16[8,48,768]{2,1,0:T(8,128)(2,1)}), bf16[128,48,768]{2,1,0:T(8,128)(2,1)}) %all-gather.2.cloned.1.call-update) | async-done | bytes 9437200 | tf_op jit(solution)/shard_map/all_gather | solution.py:1100
  85.6 5.1 %mlp.1.after = bf16[192,768]{1,0:T(8,128)(2,1)S(1)} custom-call(s32[1]{0:T(128)} %bitcast.flag, f32[192,768]{1,0:T(8,128)S(1)} %get-tuple-element.83.middle_ref, bf16[192,768]{1,0:T(8,128)(2,1)S(1)} %get-tuple-element.84.hidden_ref, f32[16,768]{1,0:T(8,128)S(1)} %vectors.1.vec, bf16[16,8,48,768]{3,2,1,0:T(8,128)(2,1)} %bitcast.37), custom_call_target="tpu_custom_call" | custom-call | flops 1811939328 | bytes 9437184 | tf_op jit(solution)/shard_map/mlp/pallas_call | solution.py:741
  90.7 1.3 collective-permute-start.17
  92.0 5.6 %load.1 = (bf16[4,16,48,768]{3,2,1,0:T(8,128)(2,1)S(1)}, bf16[8,16,48,768]{3,2,1,0:T(8,128)(2,1)S(1)}, f32[192,3072]{1,0:T(8,128)S(1)}, bf16[8,768,768]{2,1,0:T(8,128)(2,1)S(1)}) custom-call(s32[16]{0:T(128)S(1)} %pad_add_fusion.devs, s32[1]{0:T(128)} %bitcast.flag, bf16[192,768]{1,0:T(8,128)(2,1)S(1)} %mlp.1.after, bf16[192,768]{1,0:T(8,128)(2,1)S(1)} %bitcast.27, ...), custom_call_target="tpu_custom_call" | custom-call | flops 905969664 | bytes 28311552 | tf_op jit(solution)/shard_map/load/pallas_call | solution.py:741
  97.6 1.3 collective-permute-done.17.recv_ref
  99.0 6.4 %chain.1 = (bf16[96,768]{1,0:T(8,128)(2,1)S(1)}, bf16[192,768]{1,0:T(8,128)(2,1)S(1)}, bf16[192,3072]{1,0:T(8,128)(2,1)S(1)}, f32[192,3072]{1,0:T(8,128)S(1)}, b...) custom-call(s32[2]{0:T(128)S(1)} %bitcast.34, ...), custom_call_target="tpu_custom_call" | custom-call | flops 4529848320 | bytes 7077888 | tf_op jit(solution)/shard_map/chain/pallas_call | solution.py:741
  105.3 1.3 collective-permute-start.18
  106.6 1.5 collective-permute-start.19
  108.2 1.8 output.1.beside
  110.0 6.5 %collective-permute-done.18.some_ref = bf16[96,768]{1,0:T(8,128)(2,1)S(1)} collective-permute-done((bf16[96,768]{1,0:T(8,128)(2,1)S(1)}, bf16[96,768]{1,0:T(8,128)(2,1)S(1)}, u32[]{:S(2)}, u32[]{:S(2)}) %collective-permute-start.18) | collective-permute-done | bytes 147488 | tf_op jit(solution)/shard_map/ppermute | solution.py:999
  116.5 4.0 %collective-permute-done.19.other_ref = bf16[96,768]{1,0:T(8,128)(2,1)S(1)} collective-permute-done((bf16[96,768]{1,0:T(8,128)(2,1)S(1)}, bf16[96,768]{1,0:T(8,128)(2,1)S(1)}, u32[]{:S(2)}, u32[]{:S(2)}) %collective-permute-start.19) | collective-permute-done | bytes 147488 | tf_op jit(solution)/shard_map/ppermute | solution.py:999
  120.5 5.5 %mlp_back.1 = (bf16[192,3072]{1,0:T(8,128)(2,1)S(1)}, f32[16,768]{1,0:T(8,128)S(1)}, bf16[16,8,48,768]{3,2,1,0:T(8,128)(2,1)}) custom-call(s32[1]{0:T(128)} %bitcast.flag, bf16[192,768]{1,0:T(8,128)(2,1)} %output.1.beside, bf16[96,768]{1,0:T(8,128)(2,1)S(1)} %collective-permute-done.18.some_ref, bf16[96,768]{1,0:T(8,128)(2,1)S(1)} %collective-permute-done.19.other_ref, ...), custom_call_target="tpu_custom_call" | custom-call | flops 3623878656 | bytes 9437184 | tf_op jit(solution)/shard_map/mlp_back/pallas_call | solution.py:741
  126.0 16.5 %rest.1 = (f32[192,768]{1,0:T(8,128)}, f32[16,768]{1,0:T(8,128)}, bf16[8,208,768]{2,1,0:T(8,128)(2,1)}, bf16[8,208,768]{2,1,0:T(8,128)(2,1)}, bf16[1,208,768]{2,1,0:T(8,128)(2,1)}) custom-call(s32[1]{0:T(128)} %bitcast.flag, s32[16]{0:T(128)S(1)} %pad_add_fusion.devs, s32[2]{0:T(128)S(1)} %bitcast.36, bf16[96,768]{1,0:T(8,128)(2,1)S(1)} %collective-permute-done.18.some_ref, ...), custom_call_target="tpu_custom_call" | custom-call | flops 2717908992 | bytes 14155776 | tf_op jit(solution)/shard_map/rest/pallas_call | solution.py:741
  142.6 1.8 collective-permute-done.20.refs_1_.refs_3_
  144.6 1.2 add.77
  146.2 1.7 collective-permute-start.22
  147.9 6.1 %collective-permute-done.22.refs_2_ = bf16[96,768]{1,0:T(8,128)(2,1)S(1)} collective-permute-done((bf16[96,768]{1,0:T(8,128)(2,1)S(1)}, bf16[96,768]{1,0:T(8,128)(2,1)S(1)}, u32[]{:S(2)}, u32[]{:S(2)}) %collective-permute-start.22) | collective-permute-done | bytes 147488 | tf_op jit(solution)/shard_map/ppermute | solution.py:1027
  154.6 1.3 add.78
  155.9 1.7 collective-permute-start.24
  158.0 11.1 %collective-permute-done.24.refs_2_ = bf16[208,768]{1,0:T(8,128)(2,1)S(1)} collective-permute-done((bf16[208,768]{1,0:T(8,128)(2,1)S(1)}, bf16[208,768]{1,0:T(8,128)(2,1)S(1)}, u32[]{:S(2)}, u32[]{:S(2)}) %collective-permute-start.24) | collective-permute-done | bytes 319520 | tf_op jit(solution)/shard_map/ppermute | solution.py:1027
  169.1 1.6 collective-permute-done.25.refs_5_
  170.7 1.3 add.79
  172.0 1.6 collective-permute-start.26
  174.1 10.7 %collective-permute-done.26.refs_2_ = bf16[208,768]{1,0:T(8,128)(2,1)S(1)} collective-permute-done((bf16[208,768]{1,0:T(8,128)(2,1)S(1)}, bf16[208,768]{1,0:T(8,128)(2,1)S(1)}, u32[]{:S(2)}, u32[]{:S(2)}) %collective-permute-start.26) | collective-permute-done | bytes 319520 | tf_op jit(solution)/shard_map/ppermute | solution.py:1027
  184.8 1.3 collective-permute-done.27.refs_5_
  186.1 1.3 add.80
  187.5 1.6 collective-permute-start.28
  189.5 10.1 %collective-permute-done.28.ahead = bf16[208,768]{1,0:T(8,128)(2,1)S(1)} collective-permute-done((bf16[208,768]{1,0:T(8,128)(2,1)S(1)}, bf16[208,768]{1,0:T(8,128)(2,1)S(1)}, u32[]{:S(2)}, u32[]{:S(2)}) %collective-permute-start.28) | collective-permute-done | bytes 319520 | tf_op jit(solution)/shard_map/ppermute | solution.py:1027
  199.6 1.4 collective-permute-done.29.behind
  201.0 2.0 total.1
  203.0 4.6 %reduce-scatter.2.cloned.1.call-done.grads_ref = bf16[8,48,768]{2,1,0:T(8,128)(2,1)} async-done(((bf16[128,48,768]{2,1,0:T(8,128)(2,1)}), bf16[8,48,768]{2,1,0:T(8,128)(2,1)}) %reduce-scatter.2.cloned.1.call-update) | async-done | bytes 589840 | tf_op jit(solution)/shard_map/reduce_scatter | solution.py:1156
  207.6 2.1 unpack.1
  (72 shorter events, 7.5 us)
Async XLA Ops:
  7.2 64.9 %copy-start.3 = (s32[2,1]{0,1:T(1,128)S(1)}, s32[2,1]{0,1:T(1,128)}, u32[]{:S(2)}) copy-start(s32[2,1]{0,1:T(1,128)} %param.21) | copy-start | bytes 28
  7.2 78.4 %all-gather.2.cloned.1.call-start = ((), (), s32[]{:S(2)}) async-start(), calls=%async_computation.1 | async-start | bytes 10027008 | tf_op jit(solution)/shard_map/all_gather | solution.py:1100
  9.9 197.7 %reduce-scatter.2.cloned.1.call-start = ((), (), s32[]{:S(2)}) async-start(), calls=%async_computation.2 | async-start | bytes 10027008 | tf_op jit(solution)/shard_map/reduce_scatter | solution.py:1156
  9.9 11.5 %collective-permute-start.1 = (bf16[208,768]{1,0:T(8,128)(2,1)}, bf16[208,768]{1,0:T(8,128)(2,1)S(1)}, u32[]{:S(2)}, u32[]{:S(2)}) collective-permute-start(bf16[208,768]{1,0:T(8,128)(2,1)} %get-tuple-element.76.refs_0_.refs_6_), channel_id=1, source_target_pairs={{0,4},{1,5},{4,8},{5,9},{8,12},{9,13},{12,14},{13,15},{14,10},{15,... | collective-permute-start | bytes 958472 | tf_op jit(solution)/shard_map/ppermute | solution.py:1027
  13.0 10.6 %collective-permute-start = (bf16[208,768]{1,0:T(8,128)(2,1)}, bf16[208,768]{1,0:T(8,128)(2,1)S(1)}, u32[]{:S(2)}, u32[]{:S(2)}) collective-permute-start(bf16[208,768]{1,0:T(8,128)(2,1)} %get-tuple-element.76.refs_0_.refs_6_), channel_id=1, source_target_pairs={{4,0},{5,1},{8,4},{9,5},{12,8},{13,9},{14,12},{15,13},{10,14},{11,... | collective-permute-start | bytes 958472 | tf_op jit(solution)/shard_map/ppermute | solution.py:1027
  21.4 50.6 %copy-start.6 = (bf16[208,768]{1,0:T(8,128)(2,1)}, bf16[208,768]{1,0:T(8,128)(2,1)S(1)}, u32[]{:S(2)}) copy-start(bf16[208,768]{1,0:T(8,128)(2,1)S(1)} %collective-permute-done.1.refs_8_.refs_14_) | copy-start | bytes 958468
  23.6 48.4 %copy-start.7 = (bf16[208,768]{1,0:T(8,128)(2,1)}, bf16[208,768]{1,0:T(8,128)(2,1)S(1)}, u32[]{:S(2)}) copy-start(bf16[208,768]{1,0:T(8,128)(2,1)S(1)} %collective-permute-done.refs_1_.refs_7_) | copy-start | bytes 958468
  23.6 16.2 %collective-permute-start.2 = (bf16[208,768]{1,0:T(8,128)(2,1)S(1)}, bf16[208,768]{1,0:T(8,128)(2,1)S(1)}, u32[]{:S(2)}, u32[]{:S(2)}) collective-permute-start(bf16[208,768]{1,0:T(8,128)(2,1)S(1)} %collective-permute-done.refs_1_.refs_7_), channel_id=1, source_target_pairs={{4,0},{5,1},{8,4},{9,5},{12,8},{13,9},{14,12},{15,13},{10,14},{11,... | collective-permute-start | bytes 958472 | tf_op jit(solution)/shard_map/ppermute | solution.py:1027
  23.9 16.0 %collective-permute-start.3 = (bf16[208,768]{1,0:T(8,128)(2,1)S(1)}, bf16[208,768]{1,0:T(8,128)(2,1)S(1)}, u32[]{:S(2)}, u32[]{:S(2)}) collective-permute-start(bf16[208,768]{1,0:T(8,128)(2,1)S(1)} %collective-permute-done.1.refs_8_.refs_14_), channel_id=1, source_target_pairs={{0,4},{1,5},{4,8},{5,9},{8,12},{9,13},{12,14},{13,15},{14,10},{15,... | collective-permute-start | bytes 958472 | tf_op jit(solution)/shard_map/ppermute | solution.py:1027
  39.8 32.2 %copy-start.8 = (bf16[208,768]{1,0:T(8,128)(2,1)}, bf16[208,768]{1,0:T(8,128)(2,1)S(1)}, u32[]{:S(2)}) copy-start(bf16[208,768]{1,0:T(8,128)(2,1)S(1)} %collective-permute-done.2.refs_2_.refs_8_) | copy-start | bytes 958468
  39.9 32.1 %copy-start.9 = (bf16[208,768]{1,0:T(8,128)(2,1)}, bf16[208,768]{1,0:T(8,128)(2,1)S(1)}, u32[]{:S(2)}) copy-start(bf16[208,768]{1,0:T(8,128)(2,1)S(1)} %collective-permute-done.3.refs_7_.refs_13_) | copy-start | bytes 958468
  39.9 15.8 %collective-permute-start.4 = (bf16[208,768]{1,0:T(8,128)(2,1)S(1)}, bf16[208,768]{1,0:T(8,128)(2,1)S(1)}, u32[]{:S(2)}, u32[]{:S(2)}) collective-permute-start(bf16[208,768]{1,0:T(8,128)(2,1)S(1)} %collective-permute-done.2.refs_2_.refs_8_), channel_id=1, source_target_pairs={{4,0},{5,1},{8,4},{9,5},{12,8},{13,9},{14,12},{15,13},{10,14},{11,... | collective-permute-start | bytes 958472 | tf_op jit(solution)/shard_map/ppermute | solution.py:1027
  41.5 15.6 %collective-permute-start.5 = (bf16[208,768]{1,0:T(8,128)(2,1)S(1)}, bf16[208,768]{1,0:T(8,128)(2,1)S(1)}, u32[]{:S(2)}, u32[]{:S(2)}) collective-permute-start(bf16[208,768]{1,0:T(8,128)(2,1)S(1)} %collective-permute-done.3.refs_7_.refs_13_), channel_id=1, source_target_pairs={{0,4},{1,5},{4,8},{5,9},{8,12},{9,13},{12,14},{13,15},{14,10},{15,... | collective-permute-start | bytes 958472 | tf_op jit(solution)/shard_map/ppermute | solution.py:1027
  41.9 18.2 %collective-permute-start.8 = (bf16[208,768]{1,0:T(8,128)(2,1)}, bf16[208,768]{1,0:T(8,128)(2,1)S(1)}, u32[]{:S(2)}, u32[]{:S(2)}) collective-permute-start(bf16[208,768]{1,0:T(8,128)(2,1)} %get-tuple-element.76.refs_0_.refs_6_), channel_id=1, source_target_pairs={{0,1},{1,0},{2,3},{3,2},{4,5},{5,4},{6,7},{7,6},{8,9},{9,8},{10,11... | collective-permute-start | bytes 958472 | tf_op jit(solution)/shard_map/ppermute | solution.py:1041
  41.9 18.6 %collective-permute-start.16 = (bf16[208,768]{1,0:T(8,128)(2,1)S(1)}, bf16[208,768]{1,0:T(8,128)(2,1)S(1)}, u32[]{:S(2)}, u32[]{:S(2)}) collective-permute-start(bf16[208,768]{1,0:T(8,128)(2,1)S(1)} %collective-permute-done.1.refs_8_.refs_14_), channel_id=1, source_target_pairs={{0,1},{1,0},{2,3},{3,2},{4,5},{5,4},{6,7},{7,6},{8,9},{9,8},{10,11... | collective-permute-start | bytes 958472 | tf_op jit(solution)/shard_map/ppermute | solution.py:1041
  42.4 18.1 %collective-permute-start.9 = (bf16[208,768]{1,0:T(8,128)(2,1)S(1)}, bf16[208,768]{1,0:T(8,128)(2,1)S(1)}, u32[]{:S(2)}, u32[]{:S(2)}) collective-permute-start(bf16[208,768]{1,0:T(8,128)(2,1)S(1)} %collective-permute-done.refs_1_.refs_7_), channel_id=1, source_target_pairs={{0,1},{1,0},{2,3},{3,2},{4,5},{5,4},{6,7},{7,6},{8,9},{9,8},{10,11... | collective-permute-start | bytes 958472 | tf_op jit(solution)/shard_map/ppermute | solution.py:1041
  55.7 16.3 %copy-start.4 = (bf16[208,768]{1,0:T(8,128)(2,1)}, bf16[208,768]{1,0:T(8,128)(2,1)S(1)}, u32[]{:S(2)}) copy-start(bf16[208,768]{1,0:T(8,128)(2,1)S(1)} %collective-permute-done.4.refs_3_.refs_9_) | copy-start | bytes 958468
  55.7 5.3 %collective-permute-start.10 = (bf16[208,768]{1,0:T(8,128)(2,1)S(1)}, bf16[208,768]{1,0:T(8,128)(2,1)S(1)}, u32[]{:S(2)}, u32[]{:S(2)}) collective-permute-start(bf16[208,768]{1,0:T(8,128)(2,1)S(1)} %collective-permute-done.2.refs_2_.refs_8_), channel_id=1, source_target_pairs={{0,1},{1,0},{2,3},{3,2},{4,5},{5,4},{6,7},{7,6},{8,9},{9,8},{10,11... | collective-permute-start | bytes 958472 | tf_op jit(solution)/shard_map/ppermute | solution.py:1041
  57.1 14.9 %copy-start.5 = (bf16[208,768]{1,0:T(8,128)(2,1)}, bf16[208,768]{1,0:T(8,128)(2,1)S(1)}, u32[]{:S(2)}) copy-start(bf16[208,768]{1,0:T(8,128)(2,1)S(1)} %collective-permute-done.5.refs_6_.refs_12_) | copy-start | bytes 958468
  57.8 11.7 %collective-permute-start.7 = (bf16[112,768]{1,0:T(8,128)(2,1)}, bf16[112,768]{1,0:T(8,128)(2,1)S(1)}, u32[]{:S(2)}, u32[]{:S(2)}) collective-permute-start(bf16[112,768]{1,0:T(8,128)(2,1)} %slice.7), channel_id=1, source_target_pairs={{4,0},{5,1},{8,4},{9,5},{12,8},{13,9},{14,12},{15,13},{10,14},{11,... | collective-permute-start | bytes 516104 | tf_op jit(solution)/shard_map/ppermute | solution.py:1027
  60.1 11.9 %copy-start.10 = (bf16[208,768]{1,0:T(8,128)(2,1)}, bf16[208,768]{1,0:T(8,128)(2,1)S(1)}, u32[]{:S(2)}) copy-start(bf16[208,768]{1,0:T(8,128)(2,1)S(1)} %collective-permute-done.8.refs_9_.refs_15_) | copy-start | bytes 958468
  60.1 9.4 %collective-permute-start.6 = (bf16[96,768]{1,0:T(8,128)(2,1)}, bf16[96,768]{1,0:T(8,128)(2,1)}, u32[]{:S(2)}, u32[]{:S(2)}) collective-permute-start(bf16[96,768]{1,0:T(8,128)(2,1)} %slice.6), channel_id=1, source_target_pairs={{0,4},{1,5},{4,8},{5,9},{8,12},{9,13},{12,14},{13,15},{14,10},{15,... | collective-permute-start | bytes 442376 | tf_op jit(solution)/shard_map/ppermute | solution.py:1027
  60.5 11.5 %copy-start.11 = (bf16[208,768]{1,0:T(8,128)(2,1)}, bf16[208,768]{1,0:T(8,128)(2,1)S(1)}, u32[]{:S(2)}) copy-start(bf16[208,768]{1,0:T(8,128)(2,1)S(1)} %collective-permute-done.16.refs_17_.refs_23_) | copy-start | bytes 958468
  60.5 9.6 %collective-permute-start.15 = (bf16[208,768]{1,0:T(8,128)(2,1)S(1)}, bf16[208,768]{1,0:T(8,128)(2,1)S(1)}, u32[]{:S(2)}, u32[]{:S(2)}) collective-permute-start(bf16[208,768]{1,0:T(8,128)(2,1)S(1)} %collective-permute-done.3.refs_7_.refs_13_), channel_id=1, source_target_pairs={{0,1},{1,0},{2,3},{3,2},{4,5},{5,4},{6,7},{7,6},{8,9},{9,8},{10,11... | collective-permute-start | bytes 958472 | tf_op jit(solution)/shard_map/ppermute | solution.py:1041
  60.6 0.8 copy-start.12
  60.6 10.7 %collective-permute-start.11 = (bf16[208,768]{1,0:T(8,128)(2,1)S(1)}, bf16[208,768]{1,0:T(8,128)(2,1)S(1)}, u32[]{:S(2)}, u32[]{:S(2)}) collective-permute-start(bf16[208,768]{1,0:T(8,128)(2,1)S(1)} %collective-permute-done.4.refs_3_.refs_9_), channel_id=1, source_target_pairs={{0,1},{1,0},{2,3},{3,2},{4,5},{5,4},{6,7},{7,6},{8,9},{9,8},{10,11... | collective-permute-start | bytes 958472 | tf_op jit(solution)/shard_map/ppermute | solution.py:1041
  61.3 9.9 %collective-permute-start.14 = (bf16[208,768]{1,0:T(8,128)(2,1)S(1)}, bf16[208,768]{1,0:T(8,128)(2,1)}, u32[]{:S(2)}, u32[]{:S(2)}) collective-permute-start(bf16[208,768]{1,0:T(8,128)(2,1)S(1)} %collective-permute-done.5.refs_6_.refs_12_), channel_id=1, source_target_pairs={{0,1},{1,0},{2,3},{3,2},{4,5},{5,4},{6,7},{7,6},{8,9},{9,8},{10,11... | collective-permute-start | bytes 958472 | tf_op jit(solution)/shard_map/ppermute | solution.py:1041
  69.5 1.7 collective-permute-start.12
  69.5 2.5 %copy-start.16 = (bf16[112,768]{1,0:T(8,128)(2,1)}, bf16[112,768]{1,0:T(8,128)(2,1)S(1)}, u32[]{:S(2)}) copy-start(bf16[112,768]{1,0:T(8,128)(2,1)S(1)} %collective-permute-done.7.refs_5_.refs_11_) | copy-start | bytes 516100
  69.5 1.9 collective-permute-start.13
  70.2 1.3 copy-start.14
  71.3 0.7 copy-start.15
  72.1 2.9 %copy-start.1 = (bf16[2,1,96,768]{3,2,1,0:T(8,128)(2,1)S(1)}, bf16[2,1,96,768]{3,2,1,0:T(8,128)(2,1)}, u32[]{:S(2)}) copy-start(bf16[2,1,96,768]{3,2,1,0:T(8,128)(2,1)} %param.18) | copy-start | bytes 884740
  72.1 2.9 %copy-start.2 = (s32[2,1]{0,1:T(1,128)S(1)}, s32[2,1]{0,1:T(1,128)}, u32[]{:S(2)}) copy-start(s32[2,1]{0,1:T(1,128)} %param.20) | copy-start | bytes 28
  85.6 6.4 %copy-start = (bf16[2,1,96,768]{3,2,1,0:T(8,128)(2,1)S(1)}, bf16[2,1,96,768]{3,2,1,0:T(8,128)(2,1)}, u32[]{:S(2)}) copy-start(bf16[2,1,96,768]{3,2,1,0:T(8,128)(2,1)} %param.19) | copy-start | bytes 884740
  90.7 8.2 %collective-permute-start.17 = (bf16[192,768]{1,0:T(8,128)(2,1)S(1)}, bf16[192,768]{1,0:T(8,128)(2,1)S(1)}, u32[]{:S(2)}, u32[]{:S(2)}) collective-permute-start(bf16[192,768]{1,0:T(8,128)(2,1)S(1)} %mlp.1.after), channel_id=1, source_target_pairs={{0,16},{1,17},{2,18},{3,19},{4,20},{5,21},{6,22},{7,23},{8,24},{9,... | collective-permute-start | bytes 884744 | tf_op jit(solution)/shard_map/ppermute | solution.py:999
  105.3 11.2 %collective-permute-start.18 = (bf16[96,768]{1,0:T(8,128)(2,1)S(1)}, bf16[96,768]{1,0:T(8,128)(2,1)S(1)}, u32[]{:S(2)}, u32[]{:S(2)}) collective-permute-start(bf16[96,768]{1,0:T(8,128)(2,1)S(1)} %get-tuple-element.92), channel_id=1, source_target_pairs={{16,0},{17,1},{18,2},{19,3},{20,4},{21,5},{22,6},{23,7},{24,8},{25... | collective-permute-start | bytes 442376 | tf_op jit(solution)/shard_map/ppermute | solution.py:999
  106.6 13.9 %collective-permute-start.19 = (bf16[96,768]{1,0:T(8,128)(2,1)S(1)}, bf16[96,768]{1,0:T(8,128)(2,1)S(1)}, u32[]{:S(2)}, u32[]{:S(2)}) collective-permute-start(bf16[96,768]{1,0:T(8,128)(2,1)S(1)} %chain_end.1), channel_id=1, source_target_pairs={{16,0},{17,1},{18,2},{19,3},{20,4},{21,5},{22,6},{23,7},{24,8},{25... | collective-permute-start | bytes 442376 | tf_op jit(solution)/shard_map/ppermute | solution.py:999
  142.6 1.9 collective-permute-start.20
  144.5 10.1 %collective-permute-start.21 = (bf16[8,208,768]{2,1,0:T(8,128)(2,1)}, bf16[8,208,768]{2,1,0:T(8,128)(2,1)S(1)}, u32[]{:S(2)}, u32[]{:S(2)}) collective-permute-start(bf16[8,208,768]{2,1,0:T(8,128)(2,1)} %get-tuple-element.112), channel_id=1, source_target_pairs={{0,1},{1,0},{2,3},{3,2},{4,5},{5,4},{6,7},{7,6},{8,9},{9,8},{10,11... | collective-permute-start | bytes 7667720 | tf_op jit(solution)/shard_map/ppermute | solution.py:1041
  145.8 8.8 %collective-permute-start.23 = (bf16[112,768]{1,0:T(8,128)(2,1)S(1)}, bf16[112,768]{1,0:T(8,128)(2,1)S(1)}, u32[]{:S(2)}, u32[]{:S(2)}) collective-permute-start(bf16[112,768]{1,0:T(8,128)(2,1)S(1)} %get-tuple-element.114), channel_id=1, source_target_pairs={{4,0},{5,1},{8,4},{9,5},{12,8},{13,9},{14,12},{15,13},{10,14},{11,... | collective-permute-start | bytes 516104 | tf_op jit(solution)/shard_map/ppermute | solution.py:1027
  146.2 7.8 %collective-permute-start.22 = (bf16[96,768]{1,0:T(8,128)(2,1)S(1)}, bf16[96,768]{1,0:T(8,128)(2,1)S(1)}, u32[]{:S(2)}, u32[]{:S(2)}) collective-permute-start(bf16[96,768]{1,0:T(8,128)(2,1)S(1)} %get-tuple-element.113), channel_id=1, source_target_pairs={{0,4},{1,5},{4,8},{5,9},{8,12},{9,13},{12,14},{13,15},{14,10},{15,... | collective-permute-start | bytes 442376 | tf_op jit(solution)/shard_map/ppermute | solution.py:1027
  155.9 13.2 %collective-permute-start.24 = (bf16[208,768]{1,0:T(8,128)(2,1)S(1)}, bf16[208,768]{1,0:T(8,128)(2,1)S(1)}, u32[]{:S(2)}, u32[]{:S(2)}) collective-permute-start(bf16[208,768]{1,0:T(8,128)(2,1)S(1)} %get-tuple-element.115), channel_id=1, source_target_pairs={{0,4},{1,5},{4,8},{5,9},{8,12},{9,13},{12,14},{13,15},{14,10},{15,... | collective-permute-start | bytes 958472 | tf_op jit(solution)/shard_map/ppermute | solution.py:1027
  157.6 13.1 %collective-permute-start.25 = (bf16[208,768]{1,0:T(8,128)(2,1)S(1)}, bf16[208,768]{1,0:T(8,128)(2,1)S(1)}, u32[]{:S(2)}, u32[]{:S(2)}) collective-permute-start(bf16[208,768]{1,0:T(8,128)(2,1)S(1)} %get-tuple-element.116), channel_id=1, source_target_pairs={{4,0},{5,1},{8,4},{9,5},{12,8},{13,9},{14,12},{15,13},{10,14},{11,... | collective-permute-start | bytes 958472 | tf_op jit(solution)/shard_map/ppermute | solution.py:1027
  172.0 12.8 %collective-permute-start.26 = (bf16[208,768]{1,0:T(8,128)(2,1)S(1)}, bf16[208,768]{1,0:T(8,128)(2,1)S(1)}, u32[]{:S(2)}, u32[]{:S(2)}) collective-permute-start(bf16[208,768]{1,0:T(8,128)(2,1)S(1)} %get-tuple-element.117), channel_id=1, source_target_pairs={{0,4},{1,5},{4,8},{5,9},{8,12},{9,13},{12,14},{13,15},{14,10},{15,... | collective-permute-start | bytes 958472 | tf_op jit(solution)/shard_map/ppermute | solution.py:1027
  173.6 12.6 %collective-permute-start.27 = (bf16[208,768]{1,0:T(8,128)(2,1)S(1)}, bf16[208,768]{1,0:T(8,128)(2,1)S(1)}, u32[]{:S(2)}, u32[]{:S(2)}) collective-permute-start(bf16[208,768]{1,0:T(8,128)(2,1)S(1)} %get-tuple-element.118), channel_id=1, source_target_pairs={{4,0},{5,1},{8,4},{9,5},{12,8},{13,9},{14,12},{15,13},{10,14},{11,... | collective-permute-start | bytes 958472 | tf_op jit(solution)/shard_map/ppermute | solution.py:1027
  187.5 12.1 %collective-permute-start.28 = (bf16[208,768]{1,0:T(8,128)(2,1)S(1)}, bf16[208,768]{1,0:T(8,128)(2,1)S(1)}, u32[]{:S(2)}, u32[]{:S(2)}) collective-permute-start(bf16[208,768]{1,0:T(8,128)(2,1)S(1)} %get-tuple-element.119), channel_id=1, source_target_pairs={{0,4},{1,5},{4,8},{5,9},{8,12},{9,13},{12,14},{13,15},{14,10},{15,... | collective-permute-start | bytes 958472 | tf_op jit(solution)/shard_map/ppermute | solution.py:1027
  189.0 12.0 %collective-permute-start.29 = (bf16[208,768]{1,0:T(8,128)(2,1)S(1)}, bf16[208,768]{1,0:T(8,128)(2,1)S(1)}, u32[]{:S(2)}, u32[]{:S(2)}) collective-permute-start(bf16[208,768]{1,0:T(8,128)(2,1)S(1)} %get-tuple-element.120), channel_id=1, source_target_pairs={{4,0},{5,1},{8,4},{9,5},{12,8},{13,9},{14,12},{15,13},{10,14},{11,... | collective-permute-start | bytes 958472 | tf_op jit(solution)/shard_map/ppermute | solution.py:1027
  (1 other events, 0.7 us)
Sparse Core Ops, SparseCore 0:
  10.2 75.3 all-gather.1
  126.2 81.4 reduce-scatter.1
